TPU v7x, 256 devices: a whole 4x4x8 slice. The times are simulated.
256 devices in a mesh: tile: 32 (over x, y, z_hi), fsdp: 8 (over z_lo, core).
Axes of the slice: x: 4, y: 4, z: 8 (z_hi: 2, z_lo: 4; z = z_hi * 4 + z_lo), core: 2. Of those that a mesh axis runs over, the one named last changes fastest.
Arguments:
- image: bfloat16 [128, 256, 640], P('tile', 'fsdp'), may hold values from -6 to 6
- conv_weight: bfloat16 [640, 9, 640], P('fsdp'), may hold values from -0.078125 to 0.078125
- group_weight: bfloat16 [9, 128, 640], P(None, None, 'fsdp'), may hold values from -0.1875 to 0.1875
- cotangent: bfloat16 [64, 128, 640], P('tile', 'fsdp'), may hold values from -6 to 6
Outputs:
- image_grad: bfloat16 [128, 256, 640], P('tile', 'fsdp')
- conv_weight_grad: float32 [640, 9, 640], P('fsdp', None, 'tile')
- group_weight_grad: float32 [9, 128, 640], P(None, 'fsdp', 'tile')
All inputs are finite; a program needn't handle non-finite values.
Results may differ from a plain program's by a relative error of at most 0.0049.
Values may be sent and summed in bfloat16 or wider, within the bound.
No kernel may reach another device: no remote copies, remote signals or barrier semaphores. Data moves between devices by JAX's collectives and lax.ppermute only.
A program may use at most 64 MiB of HBM per device.

v0:
```python
import math

import jax
import jax.numpy as jnp
from jax import lax
from jax.sharding import PartitionSpec as P


def shifted_2(block, axis, distance):
    devices = range(lax.axis_size(axis))
    route = [(i - distance, i) for i in devices if i - distance in devices]
    return lax.ppermute(block, axis, route)


def padded_2(cells, sides, width):
    for axis, dim in sides:
        count = lax.axis_size(axis)
        ends = count - 1
        head = lax.slice_in_dim(cells, 0, width, axis=dim)
        tail = lax.slice_in_dim(cells, cells.shape[dim] - width, cells.shape[dim], axis=dim)
        cells = jnp.concatenate(
            [
                lax.ppermute(tail, axis, [(i, (i + 1) % count) for i in range(ends)]),
                cells,
                lax.ppermute(head, axis, [((i + 1) % count, i) for i in range(ends)]),
            ],
            axis=dim,
        )
    return cells


def normal_terms(hidden_pre):
    cumul = 0.5 * (1.0 + lax.erf(hidden_pre * (1.0 / math.sqrt(2.0))))
    density = jnp.exp(-0.5 * hidden_pre * hidden_pre) * (1.0 / math.sqrt(2.0 * math.pi))
    return (cumul, density)


def per_device(image, conv_weight, group_weight, cotangent):
    in_rows, in_cols, in_channels = image.shape
    out_rows, out_cols = (in_rows // 2, in_cols // 2)
    out_channels = cotangent.shape[2]
    group_width = group_weight.shape[1]
    group_count = out_channels // group_width
    cells = out_rows * out_cols
    top_rim = shifted_2(image[in_rows - 1 :], "tile", 1)
    taller = jnp.concatenate([top_rim, image], axis=0)
    left_rim = shifted_2(taller[:, in_cols - 1 :], "fsdp", 1)
    padded = jnp.concatenate([left_rim, taller], axis=1)
    windows = jnp.stack(
        [
            padded[
                position // 3 : position // 3 + in_rows : 2,
                position % 3 : position % 3 + in_cols : 2,
            ]
            for position in range(9)
        ],
        axis=0,
    )
    weights = lax.all_gather(conv_weight, "fsdp", axis=0, tiled=True)
    hidden_pre = jnp.einsum("thwc,cto->hwo", windows, weights, preferred_element_type=jnp.float32)
    cumul, density = normal_terms(hidden_pre)
    activation = (hidden_pre * cumul).astype(jnp.bfloat16)
    slopes = cumul + hidden_pre * density
    grad_pad = padded_2(cotangent, (("tile", 0), ("fsdp", 1)), 1)
    act_pad = padded_2(activation, (("tile", 0), ("fsdp", 1)), 1)
    group_full = lax.all_gather(group_weight, "fsdp", axis=2, tiled=True)
    group_full = group_full.reshape(9, group_width, group_count, group_width)
    grad_groups = cotangent.reshape(cells, group_count, group_width)
    act_grad = jnp.zeros((out_rows, out_cols, group_count, group_width), jnp.float32)
    group_terms = []
    for position in range(9):
        row_step, col_step = (position // 3 - 1, position % 3 - 1)
        moved = grad_pad[
            1 - row_step : 1 - row_step + out_rows, 1 - col_step : 1 - col_step + out_cols
        ]
        moved = moved.reshape(out_rows, out_cols, group_count, group_width)
        act_grad = act_grad + jnp.einsum(
            "hwgj,igj->hwgi", moved, group_full[position], preferred_element_type=jnp.float32
        )
        shifted = act_pad[
            1 + row_step : 1 + row_step + out_rows, 1 + col_step : 1 + col_step + out_cols
        ]
        shifted = shifted.reshape(cells, group_count, group_width)
        group_terms.append(
            jnp.einsum(
                "pgi,pgj->igj", shifted, grad_groups, preferred_element_type=jnp.float32
            ).reshape(group_width, out_channels)
        )
    group_partial = jnp.stack(group_terms, axis=0)
    group_rows = lax.psum_scatter(group_partial, "tile", scatter_dimension=2, tiled=True)
    group_weight_grad = lax.psum_scatter(group_rows, "fsdp", scatter_dimension=1, tiled=True)
    pre_grad = (act_grad.reshape(out_rows, out_cols, out_channels) * slopes).astype(jnp.bfloat16)
    below_rim = shifted_2(pre_grad[:1], "tile", -1)
    grad_tall = jnp.concatenate([pre_grad, below_rim], axis=0)
    right_rim = shifted_2(grad_tall[:, :1], "fsdp", -1)
    grad_ext = jnp.concatenate([grad_tall, right_rim], axis=1)
    parity = (1, 0, 1)
    offsets = (1, 0, 0)
    parts = [
        [jnp.zeros((out_rows, out_cols, in_channels), jnp.float32) for side in range(2)]
        for level in range(2)
    ]
    for position in range(9):
        row_tap, col_tap = (position // 3, position % 3)
        row_start, col_start = (offsets[row_tap], offsets[col_tap])
        source = grad_ext[row_start : row_start + out_rows, col_start : col_start + out_cols]
        term = jnp.einsum(
            "hwo,co->hwc", source, weights[:, position, :], preferred_element_type=jnp.float32
        )
        parts[parity[row_tap]][parity[col_tap]] = parts[parity[row_tap]][parity[col_tap]] + term
    rounded = [[parts[level][side].astype(jnp.bfloat16) for side in range(2)] for level in range(2)]
    row_sets = [jnp.stack([rounded[level][0], rounded[level][1]], axis=2) for level in range(2)]
    image_grad = jnp.stack(row_sets, axis=1).reshape(in_rows, in_cols, in_channels)
    owned = lax.all_to_all(windows, "fsdp", split_axis=3, concat_axis=2, tiled=True)
    band_sums = jnp.einsum(
        "thwc,hwo->cto",
        owned,
        lax.all_gather(pre_grad, "fsdp", axis=1, tiled=True),
        preferred_element_type=jnp.float32,
    )
    conv_weight_grad = lax.psum_scatter(band_sums, "tile", scatter_dimension=2, tiled=True)
    return (image_grad, conv_weight_grad, group_weight_grad)


def solution(mesh):
    placed = (
        P("tile", "fsdp", None),
        P("fsdp", None, None),
        P(None, None, "fsdp"),
        P("tile", "fsdp", None),
    )
    return jax.shard_map(
        per_device,
        mesh=mesh,
        in_specs=placed,
        out_specs=(P("tile", "fsdp", None), P("fsdp", None, "tile"), P(None, "fsdp", "tile")),
        check_vma=False,
    )
```

profile of v0, /device:TPU:1, one launch (start us, length us, event | category | flops | bytes accessed | tf_op | source)
XLA Modules:
  0.0 784.3 jit_solution(9655546912076006844)
XLA Ops:
  9.4 9.6 %collective-permute-start = (bf16[1,16,640]{2,1,0:T(8,128)(2,1)S(1)}, bf16[1,16,640]{2,1,0:T(8,128)(2,1)S(1)}, u32[]{:S(2)}, u32[]{:S(2)}) collective-permute-start(bf16[1,16,640]{2,1,0:T(8,128)(2,1)S(1)} %get-tuple-element.55), channel_id=1, source_target_pairs={{0,8},{8,16},{16,24},{24,32},{32,40},{40,48},{48,56},{56,64},{64,7... | collective-permute-start | bytes 61448 | tf_op jit(solution)/shard_map/ppermute | solution.py:23
  19.1 1.3 collective-permute-start.1
  21.2 7.9 %collective-permute-start.4 = (bf16[1,32,640]{2,1,0:T(8,128)(2,1)S(1)}, bf16[1,32,640]{2,1,0:T(8,128)(2,1)S(1)}, u32[]{:S(2)}, u32[]{:S(2)}) collective-permute-start(bf16[1,32,640]{2,1,0:T(8,128)(2,1)S(1)} %slice.222), channel_id=1, source_target_pairs={{0,8},{8,16},{16,24},{24,32},{32,40},{40,48},{48,56},{56,64},{64,7... | collective-permute-start | bytes 122888 | tf_op jit(solution)/shard_map/ppermute | solution.py:12
  29.9 1.0 slice.228
  30.8 1.0 slice.229
  31.8 1.0 slice.231
  32.8 1.0 slice.232
  33.8 0.8 reshape.100
  35.5 4.1 collective-permute-start.3
  39.6 1.9 collective-permute-start.2
  41.6 0.9 constant_dynamic-update-slice_fusion.3
  42.5 3.6 collective-permute-start.5
  47.6 2.4 all-gather.3.cloned.1.call-done
  50.0 1.5 fusion.86
  53.1 81.8 %all-gather.5.cloned.1.call-done = bf16[640,9,640]{2,0,1:T(8,128)(2,1)} async-done(((bf16[80,9,640]{2,0,1:T(8,128)(2,1)}), bf16[640,9,640]{2,0,1:T(8,128)(2,1)}) %all-gather.5.cloned.1.call-update) | async-done | bytes 7372816 | tf_op jit(solution)/shard_map/all_gather | solution.py:59
  134.9 4.5 multiply_convert_fusion
  139.5 1.3 collective-permute-start.9
  140.8 7.9 %collective-permute-start.8 = (bf16[1,16,640]{2,1,0:T(8,128)(2,1)S(1)}, bf16[1,16,640]{2,1,0:T(8,128)(2,1)S(1)}, u32[]{:S(2)}, u32[]{:S(2)}) collective-permute-start(bf16[1,16,640]{2,1,0:T(8,128)(2,1)S(1)} %get-tuple-element.49), channel_id=1, source_target_pairs={{0,8},{8,16},{16,24},{24,32},{32,40},{40,48},{48,56},{56,64},{64,7... | collective-permute-start | bytes 61448 | tf_op jit(solution)/shard_map/ppermute | solution.py:23
  149.6 6.1 collective-permute-start.11
  155.7 1.9 collective-permute-start.10
  160.8 10.0 %stack.79 = f32[9,128,640]{1,0,2:T(8,128)} concatenate(f32[1,128,640]{1,0,2:T(1,128)S(1)} %bitcast.292, f32[1,128,640]{1,0,2:T(1,128)S(1)} %bitcast.290, f32[1,128,640]{1,0,2:T(1,128)S(1)} %bitcast.293, f32[1,128,640]{1,0,2:T(1,128)S(1)} %bitcast.294, f32[1,128,640]{1,0,2:T(1,128)S(1)} %bitcast.289, f32[1,128,640]{1,0,2:T(1,128)S(1)} %bitcast.295, f32[1,128,640]{1,0,2:T(1,128)S(1)} %bitcast.296, ...), dimensions={0} | concatenate | bytes 5898240 | tf_op jit(solution)/shard_map/stack | solution.py:89
  170.9 3.7 copy.176
  174.6 2.3 reshape.132
  176.9 21.4 %all_to_all.18 = bf16[8,2,11520]{2,1,0:T(2,128)(2,1)} all-to-all(bf16[8,2,11520]{2,1,0:T(2,128)(2,1)S(1)} %reshape.132), channel_id=1, replica_groups=mesh['tile'=32,'fsdp'=8] {'fsdp'}, dimensions={0} | all-to-all | bytes 737280 | tf_op jit(solution)/shard_map/all_to_all | solution.py:114
  198.2 9.5 %reshape.133 = bf16[640,9,2,16]{3,2,1,0:T(2,128)(2,1)S(1)} reshape(bf16[8,2,11520]{2,1,0:T(2,128)(2,1)} %all_to_all.18) | data formatting | bytes 737280
  207.7 3.7 copy.177
  211.4 20.2 %all_gather.11 = bf16[2,128,640]{2,1,0:T(8,128)(2,1)S(1)} all-gather(bf16[2,16,640]{2,1,0:T(8,128)(2,1)S(1)} %get-tuple-element.41), channel_id=1, replica_groups=mesh['tile'=32,'fsdp'=8] {'fsdp'}, dimensions={1}, use_global_device_ids=true | all-gather | bytes 368640 | tf_op jit(solution)/shard_map/all_gather | solution.py:118
  231.6 1.6 convolution_bitcast_fusion
  233.2 4.7 copy.179
  238.0 1.3 collective-permute-start.6
  239.3 1.5 fusion.25
  240.8 1.5 fusion.21
  242.3 1.5 fusion.24
  243.8 1.5 fusion.17
  245.4 5.9 collective-permute-done.6
  251.3 2.6 collective-permute-start.7
  253.9 1.5 fusion.23
  255.4 1.5 fusion.18
  256.9 2.7 collective-permute-done.7
  259.6 1.5 fusion.20
  261.1 1.5 fusion.22
  262.6 1.5 fusion.19
  264.1 171.1 %reduce-scatter.6.cloned.1.call-done = f32[9,128,20]{1,0,2:T(8,128)} async-done(((f32[9,128,640]{1,0,2:T(8,128)}), f32[9,128,20]{1,0,2:T(8,128)}) %reduce-scatter.6.cloned.1.call-update) | async-done | bytes 92176 | tf_op jit(solution)/shard_map/reduce_scatter | solution.py:90
  435.2 2.3 copy.207
  438.5 279.7 %reduce-scatter.4.cloned.1.call-done = f32[80,9,20]{0,1,2:T(8,128)} async-done(((f32[80,9,640]{0,1,2:T(8,128)}), f32[80,9,20]{0,1,2:T(8,128)}) %reduce-scatter.4.cloned.1.call-update) | async-done | bytes 57616 | tf_op jit(solution)/shard_map/reduce_scatter | solution.py:121
  718.3 1.6 copy.208
  719.9 56.3 %reduce-scatter.8.cloned.1.call-done = f32[9,16,20]{2,0,1:T(8,128)} async-done(((f32[9,128,20]{2,0,1:T(8,128)}), f32[9,16,20]{2,0,1:T(8,128)}) %reduce-scatter.8.cloned.1.call-update) | async-done | bytes 11536 | tf_op jit(solution)/shard_map/reduce_scatter | solution.py:91
  776.2 1.6 copy.209
  (84 shorter events, 12.7 us)
Async XLA Ops:
  7.2 42.9 %all-gather.3.cloned.1.call-start = ((), (), s32[]{:S(2)}) async-start(), calls=%async_computation.4 | async-start | bytes 1658880 | tf_op jit(solution)/shard_map/all_gather | solution.py:66
  7.9 127.0 %all-gather.5.cloned.1.call-start = ((), (), s32[]{:S(2)}) async-start(), calls=%async_computation.5 | async-start | bytes 8294400 | tf_op jit(solution)/shard_map/all_gather | solution.py:59
  8.6 426.6 %reduce-scatter.6.cloned.1.call-start = ((), (), s32[]{:S(2)}) async-start(), calls=%async_computation.7 | async-start | bytes 5406720 | tf_op jit(solution)/shard_map/reduce_scatter | solution.py:90
  9.4 25.2 %collective-permute-start = (bf16[1,16,640]{2,1,0:T(8,128)(2,1)S(1)}, bf16[1,16,640]{2,1,0:T(8,128)(2,1)S(1)}, u32[]{:S(2)}, u32[]{:S(2)}) collective-permute-start(bf16[1,16,640]{2,1,0:T(8,128)(2,1)S(1)} %get-tuple-element.55), channel_id=1, source_target_pairs={{0,8},{8,16},{16,24},{24,32},{32,40},{40,48},{48,56},{56,64},{64,7... | collective-permute-start | bytes 61448 | tf_op jit(solution)/shard_map/ppermute | solution.py:23
  19.1 15.6 %collective-permute-start.1 = (bf16[1,16,640]{2,1,0:T(8,128)(2,1)S(1)}, bf16[1,16,640]{2,1,0:T(8,128)(2,1)S(1)}, u32[]{:S(2)}, u32[]{:S(2)}) collective-permute-start(bf16[1,16,640]{2,1,0:T(8,128)(2,1)S(1)} %get-tuple-element.54), channel_id=1, source_target_pairs={{8,0},{16,8},{24,16},{32,24},{40,32},{48,40},{56,48},{64,56},{72,6... | collective-permute-start | bytes 61448 | tf_op jit(solution)/shard_map/ppermute | solution.py:25
  21.2 20.4 %collective-permute-start.4 = (bf16[1,32,640]{2,1,0:T(8,128)(2,1)S(1)}, bf16[1,32,640]{2,1,0:T(8,128)(2,1)S(1)}, u32[]{:S(2)}, u32[]{:S(2)}) collective-permute-start(bf16[1,32,640]{2,1,0:T(8,128)(2,1)S(1)} %slice.222), channel_id=1, source_target_pairs={{0,8},{8,16},{16,24},{24,32},{32,40},{40,48},{48,56},{56,64},{64,7... | collective-permute-start | bytes 122888 | tf_op jit(solution)/shard_map/ppermute | solution.py:12
  35.5 10.6 %collective-permute-start.3 = (bf16[4,1,640]{2,1,0:T(2,128)(2,1)S(1)}, bf16[4,1,640]{2,1,0:T(2,128)(2,1)S(1)}, u32[]{:S(2)}, u32[]{:S(2)}) collective-permute-start(bf16[4,1,640]{2,1,0:T(2,128)(2,1)S(1)} %get-tuple-element.45), channel_id=1, source_target_pairs={{0,1},{1,2},{2,3},{3,4},{4,5},{5,6},{6,7},{8,9},{9,10},{10,11},{11... | collective-permute-start | bytes 15368 | tf_op jit(solution)/shard_map/ppermute | solution.py:23
  39.6 6.6 collective-permute-start.2
  42.5 4.5 collective-permute-start.5
  139.5 9.5 %collective-permute-start.9 = (bf16[1,16,640]{2,1,0:T(8,128)(2,1)S(1)}, bf16[1,16,640]{2,1,0:T(8,128)(2,1)S(1)}, u32[]{:S(2)}, u32[]{:S(2)}) collective-permute-start(bf16[1,16,640]{2,1,0:T(8,128)(2,1)S(1)} %get-tuple-element.50), channel_id=1, source_target_pairs={{8,0},{16,8},{24,16},{32,24},{40,32},{48,40},{56,48},{64,56},{72,6... | collective-permute-start | bytes 61448 | tf_op jit(solution)/shard_map/ppermute | solution.py:25
  140.8 8.8 %collective-permute-start.8 = (bf16[1,16,640]{2,1,0:T(8,128)(2,1)S(1)}, bf16[1,16,640]{2,1,0:T(8,128)(2,1)S(1)}, u32[]{:S(2)}, u32[]{:S(2)}) collective-permute-start(bf16[1,16,640]{2,1,0:T(8,128)(2,1)S(1)} %get-tuple-element.49), channel_id=1, source_target_pairs={{0,8},{8,16},{16,24},{24,32},{32,40},{40,48},{48,56},{56,64},{64,7... | collective-permute-start | bytes 61448 | tf_op jit(solution)/shard_map/ppermute | solution.py:23
  149.6 8.7 %collective-permute-start.11 = (bf16[4,1,640]{2,1,0:T(2,128)(2,1)S(1)}, bf16[4,1,640]{2,1,0:T(2,128)(2,1)S(1)}, u32[]{:S(2)}, u32[]{:S(2)}) collective-permute-start(bf16[4,1,640]{2,1,0:T(2,128)(2,1)S(1)} %get-tuple-element.38), channel_id=1, source_target_pairs={{1,0},{2,1},{3,2},{4,3},{5,4},{6,5},{7,6},{9,8},{10,9},{11,10},{12... | collective-permute-start | bytes 15368 | tf_op jit(solution)/shard_map/ppermute | solution.py:25
  155.7 3.1 collective-permute-start.10
  170.9 547.4 %reduce-scatter.4.cloned.1.call-start = ((), (), s32[]{:S(2)}) async-start(), calls=%async_computation.6 | async-start | bytes 5406720 | tf_op jit(solution)/shard_map/reduce_scatter | solution.py:121
  238.0 538.2 %reduce-scatter.8.cloned.1.call-start = ((), (), s32[]{:S(2)}) async-start(), calls=%async_computation.8 | async-start | bytes 1179648 | tf_op jit(solution)/shard_map/reduce_scatter | solution.py:91
  238.0 13.2 %collective-permute-start.6 = (bf16[1,16,640]{2,1,0:T(8,128)(2,1)S(1)}, bf16[1,16,640]{2,1,0:T(8,128)(2,1)S(1)}, u32[]{:S(2)}, u32[]{:S(2)}) collective-permute-start(bf16[1,16,640]{2,1,0:T(8,128)(2,1)S(1)} %slice.280), channel_id=1, source_target_pairs={{8,0},{16,8},{24,16},{32,24},{40,32},{48,40},{56,48},{64,56},{72,6... | collective-permute-start | bytes 61448 | tf_op jit(solution)/shard_map/ppermute | solution.py:12
  251.3 8.3 %collective-permute-start.7 = (bf16[3,1,640]{2,1,0:T(2,128)(2,1)S(1)}, bf16[3,1,640]{2,1,0:T(2,128)(2,1)S(1)}, u32[]{:S(2)}, u32[]{:S(2)}) collective-permute-start(bf16[3,1,640]{2,1,0:T(2,128)(2,1)S(1)} %pad_maximum_fusion.20), channel_id=1, source_target_pairs={{1,0},{2,1},{3,2},{4,3},{5,4},{6,5},{7,6},{9,8},{10,9},{11,10},{12... | collective-permute-start | bytes 11528 | tf_op jit(solution)/shard_map/ppermute | solution.py:12
Sparse Core Ops, SparseCore 0:
  9.8 40.2 all-gather.2
  51.8 83.0 all-gather.4
  171.0 264.2 reduce-scatter.5
  437.6 280.5 reduce-scatter.3
  720.7 55.5 reduce-scatter.7
where the time goes:
time: 788 us; the launch traced here: 784 us
  waiting for transfers between devices  603 us (77%)
  local copies, waits for them, and re-layouts  51.2 us (6%)
  starting transfers between devices  49.8 us (6%)
  blocking collectives  41.5 us (5%)
  matrix products  23.4 us (3%)
  between operations  14.4 us (2%)
    reduce_scatter x1, waiting for transfers between devices, per_device(): lax.psum_scatter(band_sums, 'tile', scatter_dimension=2, tiled=True)  280 us
    reduce_scatter x1, waiting for transfers between devices, per_device(): lax.psum_scatter(group_partial, 'tile', scatter_dimension=2, tiled=True)  171 us
    all_gather x1, waiting for transfers between devices, per_device(): weights = lax.all_gather(conv_weight, 'fsdp', axis=0, tiled=True)  81.8 us
    reduce_scatter x1, waiting for transfers between devices, per_device(): lax.psum_scatter(group_rows, 'fsdp', scatter_dimension=1, tiled=True)  56.3 us
    ppermute x4, starting transfers between devices, padded_2(): lax.ppermute(tail, axis, [(i, (i + 1) % count) for i in range(ends)])  23.5 us
    all_to_all x1, blocking collectives, per_device(): lax.all_to_all(windows, 'fsdp', split_axis=3, concat_axis=2, tiled=True)  21.4 us
    all_gather x1, blocking collectives, per_device(): lax.all_gather(pre_grad, 'fsdp', axis=1, tiled=True)  20.2 us
  transfers between devices with their start and end apart: 17, of which 10 were waited for; matrix products, arithmetic and copies ran while one was open for 7% of the time, Pallas kernels for 0%

commit v1 on v0

v1 whole, which is shorter than its diff:
```python
import functools
import math

import jax
import jax.numpy as jnp
from jax import lax
from jax.experimental import pallas as pl
from jax.experimental.pallas import tpu as pltpu
from jax.sharding import PartitionSpec as P

F32 = jnp.float32
BF16 = jnp.bfloat16
PARAMS = pltpu.CompilerParams(vmem_limit_bytes=48 * 1024 * 1024)


def nn(a, b):
    return lax.dot_general(a, b, (((1,), (0,)), ((), ())), preferred_element_type=F32)


def nt(a, b):
    return lax.dot_general(a, b, (((1,), (1,)), ((), ())), preferred_element_type=F32)


def tn(a, b):
    return lax.dot_general(a, b, (((0,), (0,)), ((), ())), preferred_element_type=F32)


def iota(shape, dim):
    return lax.broadcasted_iota(jnp.int32, shape, dim)


def from_left(x):
    return jnp.where(iota(x.shape, 1) == 0, 0.0, pltpu.roll(x, 1, 1))


def from_right(x):
    width = x.shape[1]
    return jnp.where(iota(x.shape, 1) == width - 1, 0.0, pltpu.roll(x, width - 1, 1))


def swap_blocks(arrays):
    arrays = list(arrays)
    lane = iota(arrays[0].shape, 1) // 16
    for step in (1, 2, 4):
        upper = (lane & step) != 0
        for low in range(8):
            if low & step:
                continue
            a, b = arrays[low], arrays[low | step]
            arrays[low] = jnp.where(upper, pltpu.roll(b, 16 * step, 1), a)
            arrays[low | step] = jnp.where(upper, b, pltpu.roll(a, 128 - 16 * step, 1))
    return arrays


def cell_of_lane(lane):
    return (lane // 32) * 32 + 2 * (lane % 16) + (lane // 16) % 2


def pack_kernel(image_ref, rim_ref, group_ref, cot_ref, send_ref):
    cells = jnp.concatenate([image_ref[...], rim_ref[...]], axis=0)
    lane = iota((160, 384), 1)
    pick = jnp.where((cell_of_lane(lane) == iota((160, 384), 0)) & (lane < 160), 1.0, 0.0)
    pixels = tn(cells, pick.astype(BF16))
    spread = jnp.where(iota((32, 256), 1) % 32 == iota((32, 256), 0), 1.0, 0.0)
    wide = tn(cot_ref[...], spread.astype(BF16))
    block = iota((80, 256), 1) // 32
    cot = wide[0:80]
    for b in range(1, 8):
        cot = jnp.where(block == b, wide[80 * b : 80 * b + 80], cot)
    cot = cot.astype(BF16)
    eye = jnp.where(iota((80, 80), 0) == iota((80, 80), 1), 1.0, 0.0).astype(BF16)
    above, below = jnp.zeros((160, 80), BF16), jnp.zeros((80, 80), BF16)
    for p in range(8):
        taps = [group_ref[t, 16 * p : 16 * p + 16, :] for t in range(9)]
        slab = nt(eye, jnp.concatenate([above, *taps, below], axis=0))
        send_ref[p, :, 0:384] = (pixels[80 * p : 80 * p + 80] + slab).astype(BF16)
        send_ref[p, :, 384:640] = cot


def forward_kernel(recv_ref, weight_ref, hid_ref, win_ref, own_ref, up_ref, down_ref, cot_ref, gw_ref):
    def tile(start):
        return swap_blocks([recv_ref[q, :, start : start + 128].astype(F32) for q in range(8)])

    inner = tile(0)
    rim = tile(128)
    even = [rim[0]] + [inner[2 * r] for r in range(4)]
    odd = [rim[1]] + [inner[2 * r + 1] for r in range(4)]
    left = [from_left(odd[r]).astype(BF16) for r in range(4)] + [None]
    even = [x.astype(BF16) for x in even]
    odd = [x.astype(BF16) for x in odd]
    for a in range(3):
        for b in range(3):
            t = 3 * a + b
            for i in range(2):
                r = 2 * i + a
                part = (left, even, odd)[b][r] if not (b == 0 and r == 4) else from_left(odd[4].astype(F32)).astype(BF16)
                win_ref[80 * t : 80 * t + 80, 128 * i : 128 * i + 128] = part
    hidden = tn(weight_ref[...], win_ref[...]).astype(BF16)
    for p in range(8):
        for g in range(5):
            hid_ref[p, 16 * g : 16 * g + 16, :] = hidden[128 * g + 16 * p : 128 * g + 16 * p + 16]
    for half in range(2):
        blocks = tile(384 + 128 * half)
        for k in range(8):
            b, i = 4 * half + k // 2, k % 2
            cot_ref[80 * b : 80 * b + 80, 128 * i : 128 * i + 128] = blocks[k].astype(BF16)
    for q in range(8):
        gw_ref[80 * q : 80 * q + 80, :] = recv_ref[q, :, 128:384]
    for g in range(5):
        rows = slice(128 * g, 128 * g + 128)
        terms = tn(gw_ref[rows, :], cot_ref[rows, :])
        sums = []
        for u in range(3):
            base = 32 + 48 * u
            by_row = []
            for i in range(2):
                lanes = slice(128 * i, 128 * i + 128)
                by_row.append(
                    from_right(terms[base : base + 16, lanes])
                    + terms[base + 16 : base + 32, lanes]
                    + from_left(terms[base + 32 : base + 48, lanes])
                )
            sums.append(by_row)
        here = slice(16 * g, 16 * g + 16)
        own_ref[here, 0:128] = sums[1][0] + sums[0][1]
        own_ref[here, 128:256] = sums[1][1] + sums[2][0]
        up_ref[here, :] = sums[0][0]
        down_ref[here, :] = sums[2][1]


def middle_kernel(hid_ref, own_ref, above_ref, below_ref, act_ref, pre_ref):
    hidden = hid_ref[0].astype(F32)
    for q in range(1, 8):
        hidden = hidden + hid_ref[q].astype(F32)
    cumul = 0.5 * (1.0 + lax.erf(hidden * (1.0 / math.sqrt(2.0))))
    density = jnp.exp(-0.5 * hidden * hidden) * (1.0 / math.sqrt(2.0 * math.pi))
    act_ref[...] = (hidden * cumul).astype(BF16)
    slopes = cumul + hidden * density
    act_grad = own_ref[...] + jnp.concatenate([above_ref[...], below_ref[...]], axis=1)
    pre_ref[...] = (act_grad * slopes).astype(BF16)


def backward_kernel(
    all_ref, weight_ref, win_ref, cot_ref, act_ref, above_ref, below_ref,
    img_ref, up_ref, red_ref, pre_ref, shift_ref,
):
    for p in range(8):
        for g in range(5):
            pre_ref[128 * g + 16 * p : 128 * g + 16 * p + 16, :] = all_ref[p, 16 * g : 16 * g + 16, :]
    pre = pre_ref[...]
    back = nn(weight_ref[...], pre)

    def term(a, b, i):
        t = 3 * a + b
        return back[80 * t : 80 * t + 80, 128 * i : 128 * i + 128]

    for i in range(2):
        img_ref[4 * i] = term(1, 1, i)
        img_ref[4 * i + 1] = term(1, 2, i) + from_right(term(1, 0, i))
    upper_even = [term(0, 1, i) for i in range(2)]
    upper_odd = [term(0, 2, i) + from_right(term(0, 0, i)) for i in range(2)]
    lower_odd = [term(2, 2, i) + from_right(term(2, 0, i)) for i in range(2)]
    img_ref[2] = term(2, 1, 0) + upper_even[1]
    img_ref[3] = lower_odd[0] + upper_odd[1]
    img_ref[6] = term(2, 1, 1)
    img_ref[7] = lower_odd[1]
    up_ref[0] = upper_even[0]
    up_ref[1] = upper_odd[0]

    red_ref[:, 0:640] = nt(pre, win_ref[0:640, :]).astype(BF16)
    rows = [above_ref[...].astype(F32), act_ref[:, 0:128].astype(F32), act_ref[:, 128:256].astype(F32), below_ref[...].astype(F32)]
    moved = [[from_left(x).astype(BF16) for x in rows], [x.astype(BF16) for x in rows], [from_right(x).astype(BF16) for x in rows]]
    for g in range(5):
        shift_ref[g, 0:80, :] = jnp.zeros((80, 256), BF16)
        shift_ref[g, 224:256, :] = jnp.zeros((32, 256), BF16)
        for u in range(3):
            for v in range(3):
                base = 80 + 16 * (3 * u + v)
                for i in range(2):
                    shift_ref[g, base : base + 16, 128 * i : 128 * i + 128] = moved[v][i + u][16 * g : 16 * g + 16]
    tail = jnp.concatenate([win_ref[640:720, :], jnp.zeros((176, 256), BF16)], axis=0)
    last = nt(pre, tail)
    for g in range(5):
        here = slice(128 * g, 128 * g + 128)
        red_ref[here, 640:896] = (last[here] + nt(cot_ref[here, :], shift_ref[g])).astype(BF16)


def fold_kernel(high_ref, red_ref, img_ref, below_ref, keep_ref, give_ref, send_ref):
    total = red_ref[0].astype(F32)
    for q in range(1, 16):
        total = total + red_ref[q].astype(F32)
    first, second = total[0:20], total[20:40]
    high = high_ref[0] == 1
    keep_ref[...] = jnp.where(high, second, first)
    give_ref[...] = jnp.where(high, first, second)
    parts = [img_ref[k] for k in range(8)]
    parts[6] = parts[6] + below_ref[0]
    parts[7] = parts[7] + below_ref[1]
    for q, x in enumerate(swap_blocks(parts)):
        send_ref[q] = x.astype(BF16)


def unpack_kernel(recv_ref, out_ref):
    lane = iota((128, 128), 1)
    pick = jnp.where(cell_of_lane(lane) == iota((128, 128), 0), 1.0, 0.0).astype(BF16)
    for p in range(5):
        out_ref[:, 128 * p : 128 * p + 128] = nt(pick, recv_ref[128 * p : 128 * p + 128, :]).astype(BF16)


def call(kernel, outs, *args, scratch=(), smem=0):
    whole = [pl.BlockSpec(memory_space=pltpu.SMEM)] * smem
    whole += [pl.BlockSpec(memory_space=pltpu.VMEM)] * (len(args) - smem)
    return pl.pallas_call(
        kernel,
        out_shape=[jax.ShapeDtypeStruct(shape, dtype) for shape, dtype in outs],
        in_specs=whole,
        out_specs=[pl.BlockSpec(memory_space=pltpu.VMEM)] * len(outs),
        scratch_shapes=list(scratch),
        compiler_params=PARAMS,
    )(*args)


def per_device(image, conv_weight, group_weight, cotangent):
    tiles = lax.axis_size("tile")
    downward = [(i, i + 1) for i in range(tiles - 1)]
    upward = [(i + 1, i) for i in range(tiles - 1)]
    partners = [(i, i ^ 1) for i in range(tiles)]
    planes = [[2 * i + z for i in range(tiles // 2)] for z in range(2)]

    rim = lax.ppermute(image[3:4], "tile", downward).reshape(32, 640)
    weights = conv_weight.transpose(1, 0, 2).reshape(720, 640)
    (send,) = call(
        pack_kernel, [((8, 80, 640), BF16)],
        image.reshape(128, 640), rim, group_weight, cotangent.reshape(32, 640),
    )
    recv = lax.all_to_all(send, "fsdp", 0, 0, tiled=True)
    hid, windows, own, up, down, cot = call(
        forward_kernel,
        [((8, 80, 256), BF16), ((720, 256), BF16), ((80, 256), F32), ((80, 128), F32), ((80, 128), F32), ((640, 256), BF16)],
        recv, weights,
        scratch=[pltpu.VMEM((640, 256), BF16)],
    )
    from_above = lax.ppermute(down, "tile", downward)
    from_below = lax.ppermute(up, "tile", upward)
    hid = lax.all_to_all(hid, "fsdp", 0, 0, tiled=True)
    act, pre = call(
        middle_kernel, [((80, 256), BF16), ((80, 256), BF16)], hid, own, from_above, from_below
    )
    act_above = lax.ppermute(act[:, 128:], "tile", downward)
    act_below = lax.ppermute(act[:, :128], "tile", upward)
    pre_all = lax.all_gather(pre, "fsdp", axis=0, tiled=False)
    img, img_up, red = call(
        backward_kernel,
        [((8, 80, 128), F32), ((2, 80, 128), F32), ((640, 896), BF16)],
        pre_all, weights, windows, cot, act, act_above, act_below,
        scratch=[pltpu.VMEM((640, 256), BF16), pltpu.VMEM((5, 256, 256), BF16)],
    )
    img_below = lax.ppermute(img_up, "tile", upward)
    red = lax.all_to_all(
        red.reshape(16, 40, 896), "tile", 0, 0, tiled=True, axis_index_groups=planes
    )
    high = (lax.axis_index("tile") % 2).astype(jnp.int32).reshape(1)
    keep, give, back = call(
        fold_kernel, [((20, 896), F32), ((20, 896), F32), ((8, 80, 128), BF16)],
        high, red, img, img_below, smem=1,
    )
    given = lax.ppermute(give, "tile", partners)
    back = lax.all_to_all(back, "fsdp", 0, 0, tiled=True)
    (image_grad,) = call(unpack_kernel, [((128, 640), BF16)], back.reshape(640, 128))
    total = keep + given
    conv_weight_grad = total[:, :720].reshape(20, 9, 80).transpose(2, 1, 0)
    group_weight_grad = total[:, 720:864].reshape(20, 9, 16).transpose(1, 2, 0)
    return (image_grad.reshape(4, 32, 640), conv_weight_grad, group_weight_grad)


def solution(mesh):
    placed = (
        P("tile", "fsdp", None),
        P("fsdp", None, None),
        P(None, None, "fsdp"),
        P("tile", "fsdp", None),
    )
    return jax.shard_map(
        per_device,
        mesh=mesh,
        in_specs=placed,
        out_specs=(P("tile", "fsdp", None), P("fsdp", None, "tile"), P(None, "fsdp", "tile")),
        check_vma=False,
    )
```

time: 788 us -> 140 us (0.18)
  waiting for transfers between devices: 603 us -> 29.1 us
  local copies, waits for them, and re-layouts: 51.2 us -> 5.23 us
  matrix products: 23.4 us -> 0 us
  between operations: 14.4 us -> 0.77 us
    reduce_scatter x3 -> x0, waiting for transfers between devices: 507 us -> none  [the longest x1 280 us: per_device(): lax.psum_scatter(band_sums, 'tile', scatter_dimension=2, tiled=True)]
    all_gather x2 -> x0, waiting for transfers between devices: 84.2 us -> none  [the longest x1 81.8 us: per_device(): weights = lax.all_gather(conv_weight, 'fsdp', axis=0, tiled=True)]
    dot_general x28 -> x0, matrix products: 23.2 us -> none  [the longest x9 13.5 us: per_device(): jnp.einsum('hwo,co->hwc', source, weights[:, position, :], preferred_elem...]
    all_to_all x0 -> x3, starting transfers between devices: none -> 21.2 us  [the longest x1 10.1 us: per_device(): lax.all_to_all(red.reshape(16, 40, 896), 'tile', 0, 0, tiled=True, axis_i...]
    ppermute x12 -> x7, starting transfers between devices: 49.6 us -> 32.9 us  [the longest x1 9.63 us: per_device(): rim = lax.ppermute(image[3:4], 'tile', downward).reshape(32, 640)]
    another operation x4 -> x0, local copies, waits for them, and re-layouts: 13.8 us -> none  [the longest x1 10 us: per_device(): group_partial = jnp.stack(group_terms, axis=0)]
    unnamed x14 -> x8, local copies, waits for them, and re-layouts: 15 us -> 3.51 us
    ppermute x12 -> x7, waiting for transfers between devices: 10.1 us -> 21.2 us  [the longest x1 8.08 us: per_device(): img_below = lax.ppermute(img_up, 'tile', upward)]
  transfers between devices with their start and end apart: 17 -> 10, of which waited for: 10 -> 4; matrix products, arithmetic and copies ran while one was open for 7% -> 2% of each run, Pallas kernels for 0% -> 0%
where the time goes in v1:
time: 140 us; the launch traced here: 139 us
  starting transfers between devices  54.1 us (39%)
  blocking collectives  42.7 us (30%)
  waiting for transfers between devices  29.1 us (21%)
  Pallas kernels  7.23 us (5%)
  local copies, waits for them, and re-layouts  5.23 us (4%)
    all_to_all x1, blocking collectives, per_device(): recv = lax.all_to_all(send, 'fsdp', 0, 0, tiled=True)  25.7 us
    all_gather x1, blocking collectives, per_device(): pre_all = lax.all_gather(pre, 'fsdp', axis=0, tiled=False)  17 us
    all_to_all x1, starting transfers between devices, per_device(): lax.all_to_all(red.reshape(16, 40, 896), 'tile', 0, 0, tiled=True, axis_i...  10.1 us
    ppermute x1, starting transfers between devices, per_device(): rim = lax.ppermute(image[3:4], 'tile', downward).reshape(32, 640)  9.63 us
    ppermute x1, waiting for transfers between devices, per_device(): img_below = lax.ppermute(img_up, 'tile', upward)  8.08 us
    all_to_all x1, waiting for transfers between devices, per_device(): lax.all_to_all(red.reshape(16, 40, 896), 'tile', 0, 0, tiled=True, axis_i...  7.95 us
    ppermute x1, starting transfers between devices, per_device(): from_above = lax.ppermute(down, 'tile', downward)  7.84 us
    ppermute x1, waiting for transfers between devices, per_device(): from_below = lax.ppermute(up, 'tile', upward)  7.37 us
  transfers between devices with their start and end apart: 10, of which 4 were waited for; matrix products, arithmetic and copies ran while one was open for 2% of the time, Pallas kernels for 0%

profile of v1, /device:TPU:1, one launch (start us, length us, event | category | flops | bytes accessed | tf_op | source)
XLA Modules:
  0.0 139.2 jit_solution(2819733494621933587)
XLA Ops:
  0.6 0.8 slice.15
  1.4 9.6 %collective-permute-start = (bf16[1,32,640]{2,1,0:T(8,128)(2,1)S(1)}, bf16[1,32,640]{2,1,0:T(8,128)(2,1)S(1)}, u32[]{:S(2)}, u32[]{:S(2)}) collective-permute-start(bf16[1,32,640]{2,1,0:T(8,128)(2,1)S(1)} %slice.15), channel_id=1, source_target_pairs={{0,8},{8,16},{16,24},{24,32},{32,40},{40,48},{48,56},{56,64},{64,7... | collective-permute-start | bytes 122888 | tf_op jit(solution)/shard_map/ppermute | solution.py:230
  11.1 1.1 copy.10.group_ref
  12.2 0.0 collective-permute-done
  12.2 0.0 copy-start.1
  12.2 0.9 copy-done.1
  13.1 0.0 copy-start.2
  13.1 0.8 copy-done.2
  13.9 0.7 shard_map.67
  14.6 0.0 copy-start
  14.6 25.7 %all_to_all.20.recv_ref = bf16[8,80,640]{2,1,0:T(8,128)(2,1)S(1)} all-to-all(bf16[8,80,640]{2,1,0:T(8,128)(2,1)S(1)} %shard_map.67), channel_id=1, replica_groups=mesh['tile'=32,'fsdp'=8] {'fsdp'}, dimensions={0} | all-to-all | bytes 1638400 | tf_op jit(solution)/shard_map/all_to_all | solution.py:236
  40.3 0.0 copy-done
  40.3 2.6 %shard_map.68 = (bf16[8,80,256]{2,1,0:T(8,128)(2,1)}, bf16[720,256]{1,0:T(8,128)(2,1)S(1)}, f32[80,256]{1,0:T(8,128)S(1)}, f32[80,128]{1,0:T(8,128)S(1)}, f32[80...) custom-call(bf16[8,80,640]{2,1,0:T(8,128)(2,1)S(1)} %all_to_all.20.recv_ref, bf16[720,640]{1,0:T(8,128)(2,1)S(1)} %bitcast.15), custom_call_target="tpu_custom_call" | custom-call | tf_op jit(solution)/shard_map/pallas_call | solution.py:213
  42.9 3.9 %all-to-all-start.1 = ((bf16[8,80,256]{2,1,0:T(8,128)(2,1)}), bf16[8,80,256]{2,1,0:T(8,128)(2,1)S(1)}, u32[]{:S(2)}, u32[]{:S(2)}) async-start(bf16[8,80,256]{2,1,0:T(8,128)(2,1)} %get-tuple-element.17), calls=%async_computation.1 | async-start | bytes 655360 | tf_op jit(solution)/shard_map/all_to_all | solution.py:245
  46.8 7.8 %collective-permute-start.1 = (f32[80,128]{1,0:T(8,128)S(1)}, f32[80,128]{1,0:T(8,128)S(1)}, u32[]{:S(2)}, u32[]{:S(2)}) collective-permute-start(f32[80,128]{1,0:T(8,128)S(1)} %get-tuple-element.19), channel_id=1, source_target_pairs={{0,8},{8,16},{16,24},{24,32},{32,40},{40,48},{48,56},{56,64},{64,7... | collective-permute-start | bytes 122888 | tf_op jit(solution)/shard_map/ppermute | solution.py:243
  54.7 1.3 collective-permute-start.2
  56.0 0.0 collective-permute-done.1.above_ref
  56.0 7.4 %collective-permute-done.2.below_ref = f32[80,128]{1,0:T(8,128)S(1)} collective-permute-done((f32[80,128]{1,0:T(8,128)S(1)}, f32[80,128]{1,0:T(8,128)S(1)}, u32[]{:S(2)}, u32[]{:S(2)}) %collective-permute-start.2) | collective-permute-done | bytes 40992 | tf_op jit(solution)/shard_map/ppermute | solution.py:244
  63.3 0.0 all-to-all-done.1.hid_ref
  63.3 0.1 shard_map.69
  63.4 6.1 %collective-permute-start.3 = (bf16[80,128]{1,0:T(8,128)(2,1)S(1)}, bf16[80,128]{1,0:T(8,128)(2,1)S(1)}, u32[]{:S(2)}, u32[]{:S(2)}) collective-permute-start(bf16[80,128]{1,0:T(8,128)(2,1)S(1)} %get-tuple-element.35), channel_id=1, source_target_pairs={{0,8},{8,16},{16,24},{24,32},{32,40},{40,48},{48,56},{56,64},{64,7... | collective-permute-start | bytes 61448 | tf_op jit(solution)/shard_map/ppermute | solution.py:249
  69.6 1.3 collective-permute-start.4
  70.9 17.0 %all-gather = bf16[640,256]{1,0:T(8,128)(2,1)S(1)} all-gather(bf16[80,256]{1,0:T(8,128)(2,1)S(1)} %get-tuple-element.21), channel_id=2, replica_groups=mesh['tile'=32,'fsdp'=8] {'fsdp'}, dimensions={0}, use_global_device_ids=true | all-gather | bytes 368640 | tf_op jit(solution)/shard_map/all_gather | solution.py:251
  87.9 0.0 collective-permute-done.3.above_ref
  87.9 0.0 collective-permute-done.4.below_ref
  87.9 2.0 %shard_map.70 = (f32[8,80,128]{2,1,0:T(8,128)S(1)}, f32[2,80,128]{2,1,0:T(8,128)S(1)}, bf16[640,896]{1,0:T(8,128)(2,1)}) custom-call(bf16[8,80,256]{2,1,0:T(8,128)(2,1)S(1)} %bitcast.17, bf16[720,640]{1,0:T(8,128)(2,1)S(1)} %bitcast.16, bf16[720,256]{1,0:T(8,128)(2,1)S(1)} %get-tuple-element.22.win_ref, bf16[640,256]{1,0:T(8,128)(2,1)S(1)} %get-tuple-element.23.cot_ref, ...), custom_call_target="tpu_custom_call" | custom-call | tf_op jit(solution)/shard_map/pallas_call | solution.py:213
  89.9 10.1 %all-to-all-start.2 = ((bf16[16,40,896]{2,1,0:T(8,128)(2,1)}), bf16[16,40,896]{2,1,0:T(8,128)(2,1)S(1)}, u32[]{:S(2)}, u32[]{:S(2)}) async-start(bf16[16,40,896]{2,1,0:T(8,128)(2,1)} %bitcast.7), calls=%async_computation.2 | async-start | bytes 2293760 | tf_op jit(solution)/shard_map/all_to_all | solution.py:259
  100.0 1.3 collective-permute-start.5
  101.4 8.1 %collective-permute-done.5.below_ref = f32[2,80,128]{2,1,0:T(8,128)S(1)} collective-permute-done((f32[2,80,128]{2,1,0:T(8,128)S(1)}, f32[2,80,128]{2,1,0:T(8,128)S(1)}, u32[]{:S(2)}, u32[]{:S(2)}) %collective-permute-start.5) | collective-permute-done | bytes 81952 | tf_op jit(solution)/shard_map/ppermute | solution.py:258
  109.4 7.9 %all-to-all-done.2.red_ref = bf16[16,40,896]{2,1,0:T(8,128)(2,1)S(1)} async-done(((bf16[16,40,896]{2,1,0:T(8,128)(2,1)}), bf16[16,40,896]{2,1,0:T(8,128)(2,1)S(1)}, u32[]{:S(2)}, u32[]{:S(2)}) %all-to-all-start.2) | async-done | bytes 1146912 | tf_op jit(solution)/shard_map/all_to_all | solution.py:259
  117.4 1.0 shard_map.71
  118.3 7.2 %all-to-all-start.3 = ((bf16[8,80,128]{2,1,0:T(8,128)(2,1)}), bf16[8,80,128]{2,1,0:T(8,128)(2,1)S(1)}, u32[]{:S(2)}, u32[]{:S(2)}) async-start(bf16[8,80,128]{2,1,0:T(8,128)(2,1)} %get-tuple-element.28), calls=%async_computation.3 | async-start | bytes 327680 | tf_op jit(solution)/shard_map/all_to_all | solution.py:268
  125.5 5.4 %collective-permute-start.6 = (f32[20,896]{1,0:T(8,128)S(1)}, f32[20,896]{1,0:T(8,128)S(1)}, u32[]{:S(2)}, u32[]{:S(2)}) collective-permute-start(f32[20,896]{1,0:T(8,128)S(1)} %get-tuple-element.30), channel_id=1, source_target_pairs={{0,8},{8,0},{16,24},{24,16},{32,40},{40,32},{48,56},{56,48},{64,72... | collective-permute-start | bytes 215048 | tf_op jit(solution)/shard_map/ppermute | solution.py:267
  130.9 5.7 %collective-permute-done.6 = f32[20,896]{1,0:T(8,128)S(1)} collective-permute-done((f32[20,896]{1,0:T(8,128)S(1)}, f32[20,896]{1,0:T(8,128)S(1)}, u32[]{:S(2)}, u32[]{:S(2)}) %collective-permute-start.6) | collective-permute-done | bytes 71712 | tf_op jit(solution)/shard_map/ppermute | solution.py:267
  136.6 0.1 slice.21
  136.7 0.1 reshape.44
  136.8 0.7 copy.12
  137.5 0.7 copy.11
  138.2 0.0 all-to-all-done.3
  138.3 0.9 shard_map.72
  (3 shorter events, 0.0 us)
Async XLA Ops:
  1.4 10.8 %collective-permute-start = (bf16[1,32,640]{2,1,0:T(8,128)(2,1)S(1)}, bf16[1,32,640]{2,1,0:T(8,128)(2,1)S(1)}, u32[]{:S(2)}, u32[]{:S(2)}) collective-permute-start(bf16[1,32,640]{2,1,0:T(8,128)(2,1)S(1)} %slice.15), channel_id=1, source_target_pairs={{0,8},{8,16},{16,24},{24,32},{32,40},{40,48},{48,56},{56,64},{64,7... | collective-permute-start | bytes 122888 | tf_op jit(solution)/shard_map/ppermute | solution.py:230
  12.2 0.9 copy-start.1
  13.1 0.8 copy-start.2
  14.6 25.7 %copy-start = (bf16[80,9,640]{2,0,1:T(8,128)(2,1)S(1)}, bf16[80,9,640]{2,0,1:T(8,128)(2,1)}, u32[]{:S(2)}) copy-start(bf16[80,9,640]{2,0,1:T(8,128)(2,1)} %param.5) | copy-start | bytes 2764804
  42.9 20.4 %all-to-all-start.1 = ((bf16[8,80,256]{2,1,0:T(8,128)(2,1)}), bf16[8,80,256]{2,1,0:T(8,128)(2,1)S(1)}, u32[]{:S(2)}, u32[]{:S(2)}) async-start(bf16[8,80,256]{2,1,0:T(8,128)(2,1)} %get-tuple-element.17), calls=%async_computation.1 | async-start | bytes 655360 | tf_op jit(solution)/shard_map/all_to_all | solution.py:245
  46.8 9.2 %collective-permute-start.1 = (f32[80,128]{1,0:T(8,128)S(1)}, f32[80,128]{1,0:T(8,128)S(1)}, u32[]{:S(2)}, u32[]{:S(2)}) collective-permute-start(f32[80,128]{1,0:T(8,128)S(1)} %get-tuple-element.19), channel_id=1, source_target_pairs={{0,8},{8,16},{16,24},{24,32},{32,40},{40,48},{48,56},{56,64},{64,7... | collective-permute-start | bytes 122888 | tf_op jit(solution)/shard_map/ppermute | solution.py:243
  54.7 8.7 %collective-permute-start.2 = (f32[80,128]{1,0:T(8,128)S(1)}, f32[80,128]{1,0:T(8,128)S(1)}, u32[]{:S(2)}, u32[]{:S(2)}) collective-permute-start(f32[80,128]{1,0:T(8,128)S(1)} %get-tuple-element.20), channel_id=1, source_target_pairs={{8,0},{16,8},{24,16},{32,24},{40,32},{48,40},{56,48},{64,56},{72,6... | collective-permute-start | bytes 122888 | tf_op jit(solution)/shard_map/ppermute | solution.py:244
  63.4 24.5 %collective-permute-start.3 = (bf16[80,128]{1,0:T(8,128)(2,1)S(1)}, bf16[80,128]{1,0:T(8,128)(2,1)S(1)}, u32[]{:S(2)}, u32[]{:S(2)}) collective-permute-start(bf16[80,128]{1,0:T(8,128)(2,1)S(1)} %get-tuple-element.35), channel_id=1, source_target_pairs={{0,8},{8,16},{16,24},{24,32},{32,40},{40,48},{48,56},{56,64},{64,7... | collective-permute-start | bytes 61448 | tf_op jit(solution)/shard_map/ppermute | solution.py:249
  69.6 18.3 %collective-permute-start.4 = (bf16[80,128]{1,0:T(8,128)(2,1)S(1)}, bf16[80,128]{1,0:T(8,128)(2,1)S(1)}, u32[]{:S(2)}, u32[]{:S(2)}) collective-permute-start(bf16[80,128]{1,0:T(8,128)(2,1)S(1)} %get-tuple-element.34), channel_id=1, source_target_pairs={{8,0},{16,8},{24,16},{32,24},{40,32},{48,40},{56,48},{64,56},{72,6... | collective-permute-start | bytes 61448 | tf_op jit(solution)/shard_map/ppermute | solution.py:250
  89.9 27.5 %all-to-all-start.2 = ((bf16[16,40,896]{2,1,0:T(8,128)(2,1)}), bf16[16,40,896]{2,1,0:T(8,128)(2,1)S(1)}, u32[]{:S(2)}, u32[]{:S(2)}) async-start(bf16[16,40,896]{2,1,0:T(8,128)(2,1)} %bitcast.7), calls=%async_computation.2 | async-start | bytes 2293760 | tf_op jit(solution)/shard_map/all_to_all | solution.py:259
  100.0 9.4 %collective-permute-start.5 = (f32[2,80,128]{2,1,0:T(8,128)S(1)}, f32[2,80,128]{2,1,0:T(8,128)S(1)}, u32[]{:S(2)}, u32[]{:S(2)}) collective-permute-start(f32[2,80,128]{2,1,0:T(8,128)S(1)} %get-tuple-element.27), channel_id=1, source_target_pairs={{8,0},{16,8},{24,16},{32,24},{40,32},{48,40},{56,48},{64,56},{72,6... | collective-permute-start | bytes 245768 | tf_op jit(solution)/shard_map/ppermute | solution.py:258
  118.3 19.9 %all-to-all-start.3 = ((bf16[8,80,128]{2,1,0:T(8,128)(2,1)}), bf16[8,80,128]{2,1,0:T(8,128)(2,1)S(1)}, u32[]{:S(2)}, u32[]{:S(2)}) async-start(bf16[8,80,128]{2,1,0:T(8,128)(2,1)} %get-tuple-element.28), calls=%async_computation.3 | async-start | bytes 327680 | tf_op jit(solution)/shard_map/all_to_all | solution.py:268
  125.5 11.1 %collective-permute-start.6 = (f32[20,896]{1,0:T(8,128)S(1)}, f32[20,896]{1,0:T(8,128)S(1)}, u32[]{:S(2)}, u32[]{:S(2)}) collective-permute-start(f32[20,896]{1,0:T(8,128)S(1)} %get-tuple-element.30), channel_id=1, source_target_pairs={{0,8},{8,0},{16,24},{24,16},{32,40},{40,32},{48,56},{56,48},{64,72... | collective-permute-start | bytes 215048 | tf_op jit(solution)/shard_map/ppermute | solution.py:267

commit v2 on v1

v2 whole, which is shorter than its diff:
```python
import functools
import math

import jax
import jax.numpy as jnp
from jax import lax
from jax.experimental import pallas as pl
from jax.experimental.pallas import tpu as pltpu
from jax.sharding import PartitionSpec as P

F32 = jnp.float32
BF16 = jnp.bfloat16
PARAMS = pltpu.CompilerParams(vmem_limit_bytes=48 * 1024 * 1024)


def nn(a, b):
    return lax.dot_general(a, b, (((1,), (0,)), ((), ())), preferred_element_type=F32)


def nt(a, b):
    return lax.dot_general(a, b, (((1,), (1,)), ((), ())), preferred_element_type=F32)


def tn(a, b):
    return lax.dot_general(a, b, (((0,), (0,)), ((), ())), preferred_element_type=F32)


def iota(shape, dim):
    return lax.broadcasted_iota(jnp.int32, shape, dim)


def from_left(x):
    return jnp.where(iota(x.shape, 1) == 0, 0.0, pltpu.roll(x, 1, 1))


def from_right(x):
    width = x.shape[1]
    return jnp.where(iota(x.shape, 1) == width - 1, 0.0, pltpu.roll(x, width - 1, 1))


def swap_blocks(arrays):
    arrays = list(arrays)
    lane = iota(arrays[0].shape, 1) // 16
    for step in (1, 2, 4):
        upper = (lane & step) != 0
        for low in range(8):
            if low & step:
                continue
            a, b = arrays[low], arrays[low | step]
            arrays[low] = jnp.where(upper, pltpu.roll(b, 16 * step, 1), a)
            arrays[low | step] = jnp.where(upper, b, pltpu.roll(a, 128 - 16 * step, 1))
    return arrays


def cell_of_lane(lane):
    return (lane // 32) * 32 + 2 * (lane % 16) + (lane // 16) % 2


def pack_kernel(image_ref, group_ref, send_ref):
    pick = jnp.where(cell_of_lane(iota((128, 128), 1)) == iota((128, 128), 0), 1.0, 0.0)
    pixels = tn(image_ref[...], pick.astype(BF16)).astype(BF16)
    eye = jnp.where(iota((80, 80), 0) == iota((80, 80), 1), 1.0, 0.0).astype(BF16)
    above, below = jnp.zeros((32, 80), BF16), jnp.zeros((80, 80), BF16)
    for p in range(8):
        taps = [group_ref[t, 16 * p : 16 * p + 16, :] for t in range(9)]
        send_ref[p, :, 0:128] = pixels[80 * p : 80 * p + 80]
        send_ref[p, :, 128:384] = nt(eye, jnp.concatenate([above, *taps, below], axis=0)).astype(BF16)


def rim_kernel(base_ref, rim_ref, send_ref):
    lane = iota((32, 128), 1)
    pick = jnp.where((cell_of_lane(lane) == iota((32, 128), 0)) & (lane < 32), 1.0, 0.0)
    pixels = tn(rim_ref[...], pick.astype(BF16)).astype(BF16)
    here = iota((80, 128), 1) < 32
    for p in range(8):
        send_ref[p, :, 0:128] = base_ref[p, :, 0:128]
        send_ref[p, :, 128:256] = jnp.where(here, pixels[80 * p : 80 * p + 80], base_ref[p, :, 128:256])
        send_ref[p, :, 256:384] = base_ref[p, :, 256:384]


def forward_kernel(recv_ref, weight_ref, above_ref, cells_ref, below_ref, hid_ref, win_ref, share_ref):
    share_ref[0:16, :] = above_ref[...]
    share_ref[16:48, :] = cells_ref[...]
    share_ref[48:64, :] = below_ref[...]

    def tile(start):
        return swap_blocks([recv_ref[q, :, start : start + 128].astype(F32) for q in range(8)])

    inner = tile(0)
    rim = tile(128)
    even = [rim[0]] + [inner[2 * r] for r in range(4)]
    odd = [rim[1]] + [inner[2 * r + 1] for r in range(4)]
    left = [from_left(odd[r]).astype(BF16) for r in range(4)] + [None]
    even = [x.astype(BF16) for x in even]
    odd = [x.astype(BF16) for x in odd]
    for a in range(3):
        for b in range(3):
            t = 3 * a + b
            for i in range(2):
                r = 2 * i + a
                part = (left, even, odd)[b][r] if not (b == 0 and r == 4) else from_left(odd[4].astype(F32)).astype(BF16)
                win_ref[80 * t : 80 * t + 80, 128 * i : 128 * i + 128] = part
    hidden = tn(weight_ref[...], win_ref[...]).astype(BF16)
    for p in range(8):
        for g in range(5):
            hid_ref[p, 16 * g : 16 * g + 16, :] = hidden[128 * g + 16 * p : 128 * g + 16 * p + 16]


def group_kernel(recv_ref, all_ref, grad_ref, cot_ref, cell_ref, gw_ref):
    for q in range(8):
        gw_ref[80 * q : 80 * q + 80, :] = recv_ref[q, :, 128:384]
        for r in range(4):
            cell_ref[128 * r + 16 * q : 128 * r + 16 * q + 16, :] = all_ref[q, 16 * r : 16 * r + 16, :]
    eye = jnp.where(iota((128, 128), 0) == iota((128, 128), 1), 1.0, 0.0).astype(BF16)
    for g in range(5):
        rows = slice(128 * g, 128 * g + 128)
        cot = nt(eye, cell_ref[:, rows]).astype(BF16)
        cot_ref[rows, :] = cot
        terms = tn(gw_ref[rows, :], cot)
        for i in range(2):
            total = None
            for u in range(3):
                base = 32 + 48 * u
                lanes = slice(128 * (i + 2 - u), 128 * (i + 2 - u) + 128)
                part = (
                    from_right(terms[base : base + 16, lanes])
                    + terms[base + 16 : base + 32, lanes]
                    + from_left(terms[base + 32 : base + 48, lanes])
                )
                total = part if total is None else total + part
            grad_ref[16 * g : 16 * g + 16, 128 * i : 128 * i + 128] = total


def middle_kernel(hid_ref, grad_ref, act_ref, pre_ref):
    hidden = hid_ref[0].astype(F32)
    for q in range(1, 8):
        hidden = hidden + hid_ref[q].astype(F32)
    cumul = 0.5 * (1.0 + lax.erf(hidden * (1.0 / math.sqrt(2.0))))
    density = jnp.exp(-0.5 * hidden * hidden) * (1.0 / math.sqrt(2.0 * math.pi))
    act_ref[...] = (hidden * cumul).astype(BF16)
    slopes = cumul + hidden * density
    pre_ref[...] = (grad_ref[...] * slopes).astype(BF16)


def backward_kernel(
    all_ref, weight_ref, win_ref, cot_ref, act_ref, img_ref, up_ref, red_ref, pre_ref, shift_ref
):
    for p in range(8):
        for g in range(5):
            pre_ref[128 * g + 16 * p : 128 * g + 16 * p + 16, :] = all_ref[p, 16 * g : 16 * g + 16, :]
    pre = pre_ref[...]
    back = nn(weight_ref[...], pre)

    def term(a, b, i):
        t = 3 * a + b
        return back[80 * t : 80 * t + 80, 128 * i : 128 * i + 128]

    for i in range(2):
        img_ref[4 * i] = term(1, 1, i)
        img_ref[4 * i + 1] = term(1, 2, i) + from_right(term(1, 0, i))
    upper_even = [term(0, 1, i) for i in range(2)]
    upper_odd = [term(0, 2, i) + from_right(term(0, 0, i)) for i in range(2)]
    lower_odd = [term(2, 2, i) + from_right(term(2, 0, i)) for i in range(2)]
    img_ref[2] = term(2, 1, 0) + upper_even[1]
    img_ref[3] = lower_odd[0] + upper_odd[1]
    img_ref[6] = term(2, 1, 1)
    img_ref[7] = lower_odd[1]
    up_ref[0] = upper_even[0]
    up_ref[1] = upper_odd[0]

    red_ref[:, 0:640] = nt(pre, win_ref[0:640, :]).astype(BF16)
    rows = [act_ref[:, 128 * i : 128 * i + 128].astype(F32) for i in range(2)]
    moved = [[move(x).astype(BF16) for x in rows] for move in (from_left, lambda x: x, from_right)]
    shift_ref[...] = jnp.zeros((5, 256, 512), BF16)
    for g in range(5):
        for u in range(3):
            for v in range(3):
                base = 80 + 16 * (3 * u + v)
                for i in range(2):
                    lanes = slice(128 * (i + 2 - u), 128 * (i + 2 - u) + 128)
                    shift_ref[g, base : base + 16, lanes] = moved[v][i][16 * g : 16 * g + 16]
    tail = jnp.concatenate([win_ref[640:720, :], jnp.zeros((176, 256), BF16)], axis=0)
    last = nt(pre, tail)
    for g in range(5):
        here = slice(128 * g, 128 * g + 128)
        red_ref[here, 640:896] = (last[here] + nt(cot_ref[here, :], shift_ref[g])).astype(BF16)


def return_kernel(img_ref, below_ref, send_ref):
    parts = [img_ref[k] for k in range(8)]
    parts[6] = parts[6] + below_ref[0]
    parts[7] = parts[7] + below_ref[1]
    for q, x in enumerate(swap_blocks(parts)):
        send_ref[q] = x.astype(BF16)


def fold_kernel(high_ref, red_ref, keep_ref, give_ref):
    total = red_ref[0].astype(F32)
    for q in range(1, 16):
        total = total + red_ref[q].astype(F32)
    first, second = total[0:20], total[20:40]
    high = high_ref[0] == 1
    keep_ref[...] = jnp.where(high, second, first)
    give_ref[...] = jnp.where(high, first, second)


def unpack_kernel(recv_ref, out_ref):
    lane = iota((128, 128), 1)
    pick = jnp.where(cell_of_lane(lane) == iota((128, 128), 0), 1.0, 0.0).astype(BF16)
    for p in range(5):
        out_ref[:, 128 * p : 128 * p + 128] = nt(pick, recv_ref[128 * p : 128 * p + 128, :]).astype(BF16)


def finish_kernel(keep_ref, given_ref, conv_ref, group_ref):
    total = keep_ref[...] + given_ref[...]
    for t in range(9):
        conv_ref[t] = total[:, 80 * t : 80 * t + 80]
    group_ref[...] = jnp.transpose(total[:, 640:896])[80:224]


def call(kernel, outs, *args, scratch=(), smem=0):
    whole = [pl.BlockSpec(memory_space=pltpu.SMEM)] * smem
    whole += [pl.BlockSpec(memory_space=pltpu.VMEM)] * (len(args) - smem)
    return pl.pallas_call(
        kernel,
        out_shape=[jax.ShapeDtypeStruct(shape, dtype) for shape, dtype in outs],
        in_specs=whole,
        out_specs=[pl.BlockSpec(memory_space=pltpu.VMEM)] * len(outs),
        scratch_shapes=list(scratch),
        compiler_params=PARAMS,
    )(*args)


def per_device(image, conv_weight, group_weight, cotangent):
    tiles = lax.axis_size("tile")
    downward = [(i, i + 1) for i in range(tiles - 1)]
    upward = [(i + 1, i) for i in range(tiles - 1)]
    partners = [(i, i ^ 1) for i in range(tiles)]
    planes = [[2 * i + z for i in range(tiles // 2)] for z in range(2)]

    cells = cotangent.reshape(32, 640)
    rim = lax.ppermute(image[3:4], "tile", downward).reshape(32, 640)
    above = lax.ppermute(cotangent[1], "tile", downward)
    below = lax.ppermute(cotangent[0], "tile", upward)
    weights = conv_weight.transpose(1, 0, 2).reshape(720, 640)
    (base,) = call(pack_kernel, [((8, 80, 384), BF16)], image.reshape(128, 640), group_weight)
    (send,) = call(rim_kernel, [((8, 80, 384), BF16)], base, rim)
    recv = lax.all_to_all(send, "fsdp", 0, 0, tiled=True)
    hid, windows, share = call(
        forward_kernel,
        [((8, 80, 256), BF16), ((720, 256), BF16), ((64, 640), BF16)],
        recv, weights, above, cells, below,
    )
    cot_all = lax.all_gather(share, "fsdp", axis=0, tiled=False)
    grad, cot = call(
        group_kernel,
        [((80, 256), F32), ((640, 512), BF16)],
        recv, cot_all,
        scratch=[pltpu.VMEM((512, 640), BF16), pltpu.VMEM((640, 256), BF16)],
    )
    hid = lax.all_to_all(hid, "fsdp", 0, 0, tiled=True)
    act, pre = call(middle_kernel, [((80, 256), BF16), ((80, 256), BF16)], hid, grad)
    pre_all = lax.all_gather(pre, "fsdp", axis=0, tiled=False)
    img, img_up, red = call(
        backward_kernel,
        [((8, 80, 128), F32), ((2, 80, 128), F32), ((640, 896), BF16)],
        pre_all, weights, windows, cot, act,
        scratch=[pltpu.VMEM((640, 256), BF16), pltpu.VMEM((5, 256, 512), BF16)],
    )
    img_below = lax.ppermute(img_up, "tile", upward)
    red = lax.all_to_all(
        red.reshape(16, 40, 896), "tile", 0, 0, tiled=True, axis_index_groups=planes
    )
    (back,) = call(return_kernel, [((8, 80, 128), BF16)], img, img_below)
    back = lax.all_to_all(back, "fsdp", 0, 0, tiled=True)
    high = (lax.axis_index("tile") % 2).astype(jnp.int32).reshape(1)
    keep, give = call(fold_kernel, [((20, 896), F32), ((20, 896), F32)], high, red, smem=1)
    given = lax.ppermute(give, "tile", partners)
    (image_grad,) = call(unpack_kernel, [((128, 640), BF16)], back.reshape(640, 128))
    conv_weight_grad, group_weight_grad = call(
        finish_kernel, [((9, 20, 80), F32), ((144, 20), F32)], keep, given
    )
    conv_weight_grad = conv_weight_grad.transpose(2, 0, 1)
    group_weight_grad = group_weight_grad.reshape(9, 16, 20)
    return (image_grad.reshape(4, 32, 640), conv_weight_grad, group_weight_grad)


def solution(mesh):
    placed = (
        P("tile", "fsdp", None),
        P("fsdp", None, None),
        P(None, None, "fsdp"),
        P("tile", "fsdp", None),
    )
    return jax.shard_map(
        per_device,
        mesh=mesh,
        in_specs=placed,
        out_specs=(P("tile", "fsdp", None), P("fsdp", None, "tile"), P(None, "fsdp", "tile")),
        check_vma=False,
    )
```

time: 140 us -> 126 us (0.900)
  blocking collectives: 42.7 us -> 34.5 us
  starting transfers between devices: 54.1 us -> 50.2 us
  Pallas kernels: 7.23 us -> 9.65 us
  local copies, waits for them, and re-layouts: 5.23 us -> 2.86 us
  waiting for transfers between devices: 29.1 us -> 26.8 us
    all_to_all x1 -> x0, blocking collectives: 25.7 us -> none  [per_device(): recv = lax.all_to_all(send, 'fsdp', 0, 0, tiled=True)]
    all_gather x0 -> x1, blocking collectives: none -> 20.1 us  [per_device(): cot_all = lax.all_gather(share, 'fsdp', axis=0, tiled=False)]
    ppermute x4 -> x2, starting transfers between devices: 16.6 us -> 8.73 us  [the longest x1 7.44 us: per_device(): above = lax.ppermute(cotangent[1], 'tile', downward)]
    all_to_all x0 -> x1, starting transfers between devices: none -> 4.34 us  [per_device(): recv = lax.all_to_all(send, 'fsdp', 0, 0, tiled=True)]
    all_to_all x1, starting transfers between devices: 10.1 us -> 6.31 us  [per_device(): lax.all_to_all(red.reshape(16, 40, 896), 'tile', 0, 0, tiled=True, axis_i...]
    all_to_all x1, starting transfers between devices: 3.91 us -> 7.1 us  [per_device(): hid = lax.all_to_all(hid, 'fsdp', 0, 0, tiled=True)]
    all_gather x1, blocking collectives: 17 us -> 14.3 us  [per_device(): pre_all = lax.all_gather(pre, 'fsdp', axis=0, tiled=False)]
    pallas_call x6 -> x10, Pallas kernels: 7.23 us -> 9.65 us  [call(): pl.pallas_call(kernel, out_shape=[jax.ShapeDtypeStruct(shape, dtype) for...]
  transfers between devices with their start and end apart: 10 -> 9, of which waited for: 4 -> 5; matrix products, arithmetic and copies ran while one was open for 2% -> 1% of each run, Pallas kernels for 0% -> 3%
where the time goes in v2:
time: 126 us; the launch traced here: 125 us
  starting transfers between devices  50.2 us (40%)
  blocking collectives  34.5 us (27%)
  waiting for transfers between devices  26.8 us (21%)
  Pallas kernels  9.65 us (8%)
  local copies, waits for them, and re-layouts  2.86 us (2%)
    all_gather x1, blocking collectives, per_device(): cot_all = lax.all_gather(share, 'fsdp', axis=0, tiled=False)  20.1 us
    all_gather x1, blocking collectives, per_device(): pre_all = lax.all_gather(pre, 'fsdp', axis=0, tiled=False)  14.3 us
    pallas_call x10, Pallas kernels, call(): pl.pallas_call(kernel, out_shape=[jax.ShapeDtypeStruct(shape, dtype) for...  9.65 us
    ppermute x1, starting transfers between devices, per_device(): rim = lax.ppermute(image[3:4], 'tile', downward).reshape(32, 640)  9.63 us
    ppermute x1, waiting for transfers between devices, per_device(): img_below = lax.ppermute(img_up, 'tile', upward)  9.57 us
    ppermute x1, starting transfers between devices, per_device(): above = lax.ppermute(cotangent[1], 'tile', downward)  7.44 us
    all_to_all x1, starting transfers between devices, per_device(): hid = lax.all_to_all(hid, 'fsdp', 0, 0, tiled=True)  7.1 us
    ppermute x1, waiting for transfers between devices, per_device(): below = lax.ppermute(cotangent[0], 'tile', upward)  7.03 us
  transfers between devices with their start and end apart: 9, of which 5 were waited for; matrix products, arithmetic and copies ran while one was open for 1% of the time, Pallas kernels for 3%

profile of v2, /device:TPU:1, one launch (start us, length us, event | category | flops | bytes accessed | tf_op | source)
XLA Modules:
  0.0 124.8 jit_solution(4084761067672520512)
XLA Ops:
  0.6 0.8 slice.9
  1.4 9.6 %collective-permute-start = (bf16[1,32,640]{2,1,0:T(8,128)(2,1)S(1)}, bf16[1,32,640]{2,1,0:T(8,128)(2,1)S(1)}, u32[]{:S(2)}, u32[]{:S(2)}) collective-permute-start(bf16[1,32,640]{2,1,0:T(8,128)(2,1)S(1)} %slice.9), channel_id=1, source_target_pairs={{0,8},{8,16},{16,24},{24,32},{32,40},{40,48},{48,56},{56,64},{64,7... | collective-permute-start | bytes 122888 | tf_op jit(solution)/shard_map/ppermute | solution.py:242
  11.1 1.1 copy.7.group_ref
  12.2 0.0 copy-start.1
  12.2 0.9 copy-done.1
  13.1 0.4 shard_map.67.base_ref
  13.6 0.0 copy-start.2
  13.6 0.0 copy-start
  13.6 0.0 collective-permute-done
  13.6 1.0 shard_map.68
  14.6 4.3 %all-to-all-start = ((bf16[8,80,384]{2,1,0:T(8,128)(2,1)}), bf16[8,80,384]{2,1,0:T(8,128)(2,1)S(1)}, u32[]{:S(2)}, u32[]{:S(2)}) async-start(bf16[8,80,384]{2,1,0:T(8,128)(2,1)} %shard_map.68), calls=%async_computation | async-start | bytes 983040 | tf_op jit(solution)/shard_map/all_to_all | solution.py:248
  18.9 0.0 copy-done.2
  18.9 7.4 %collective-permute-start.1 = (bf16[16,640]{1,0:T(8,128)(2,1)S(1)}, bf16[16,640]{1,0:T(8,128)(2,1)S(1)}, u32[]{:S(2)}, u32[]{:S(2)}) collective-permute-start(bf16[16,640]{1,0:T(8,128)(2,1)S(1)} %get-tuple-element.32), channel_id=1, source_target_pairs={{0,8},{8,16},{16,24},{24,32},{32,40},{40,48},{48,56},{56,64},{64,7... | collective-permute-start | bytes 61448 | tf_op jit(solution)/shard_map/ppermute | solution.py:243
  26.4 1.3 %collective-permute-start.2 = (bf16[16,640]{1,0:T(8,128)(2,1)S(1)}, bf16[16,640]{1,0:T(8,128)(2,1)S(1)}, u32[]{:S(2)}, u32[]{:S(2)}) collective-permute-start(bf16[16,640]{1,0:T(8,128)(2,1)S(1)} %get-tuple-element.31), channel_id=1, source_target_pairs={{8,0},{16,8},{24,16},{32,24},{40,32},{48,40},{56,48},{64,56},{72,6... | collective-permute-start | bytes 61448 | tf_op jit(solution)/shard_map/ppermute | solution.py:244
  27.7 0.1 collective-permute-done.1.above_ref
  27.8 7.0 %collective-permute-done.2.below_ref = bf16[16,640]{1,0:T(8,128)(2,1)S(1)} collective-permute-done((bf16[16,640]{1,0:T(8,128)(2,1)S(1)}, bf16[16,640]{1,0:T(8,128)(2,1)S(1)}, u32[]{:S(2)}, u32[]{:S(2)}) %collective-permute-start.2) | collective-permute-done | bytes 20512 | tf_op jit(solution)/shard_map/ppermute | solution.py:244
  34.8 0.0 all-to-all-done.recv_ref
  34.8 0.0 copy-done
  34.8 1.7 %shard_map.69 = (bf16[8,80,256]{2,1,0:T(8,128)(2,1)}, bf16[720,256]{1,0:T(8,128)(2,1)S(1)}, bf16[64,640]{1,0:T(8,128)(2,1)S(1)}) custom-call(bf16[8,80,384]{2,1,0:T(8,128)(2,1)S(1)} %all-to-all-done.recv_ref, bf16[720,640]{1,0:T(8,128)(2,1)S(1)} %bitcast.18, bf16[16,640]{1,0:T(8,128)(2,1)S(1)} %collective-permute-done.1.above_ref, ...), custom_call_target="tpu_custom_call" | custom-call | tf_op jit(solution)/shard_map/pallas_call | solution.py:224
  36.5 7.1 %all-to-all-start.1 = ((bf16[8,80,256]{2,1,0:T(8,128)(2,1)}), bf16[8,80,256]{2,1,0:T(8,128)(2,1)S(1)}, u32[]{:S(2)}, u32[]{:S(2)}) async-start(bf16[8,80,256]{2,1,0:T(8,128)(2,1)} %get-tuple-element.17), calls=%async_computation.1 | async-start | bytes 655360 | tf_op jit(solution)/shard_map/all_to_all | solution.py:261
  43.6 20.1 %all-gather = bf16[512,640]{1,0:T(8,128)(2,1)S(1)} all-gather(bf16[64,640]{1,0:T(8,128)(2,1)S(1)} %get-tuple-element.18), channel_id=2, replica_groups=mesh['tile'=32,'fsdp'=8] {'fsdp'}, dimensions={0}, use_global_device_ids=true | all-gather | bytes 737280 | tf_op jit(solution)/shard_map/all_gather | solution.py:254
  63.8 1.4 %shard_map.70 = (f32[80,256]{1,0:T(8,128)S(1)}, bf16[640,512]{1,0:T(8,128)(2,1)S(1)}) custom-call(bf16[8,80,384]{2,1,0:T(8,128)(2,1)S(1)} %all-to-all-done.recv_ref, bf16[8,64,640]{2,1,0:T(8,128)(2,1)S(1)} %bitcast.20), custom_call_target="tpu_custom_call" | custom-call | tf_op jit(solution)/shard_map/pallas_call | solution.py:224
  65.2 0.0 all-to-all-done.1.hid_ref
  65.2 0.1 shard_map.71
  65.3 14.3 %all-gather.1 = bf16[640,256]{1,0:T(8,128)(2,1)S(1)} all-gather(bf16[80,256]{1,0:T(8,128)(2,1)S(1)} %get-tuple-element.20), channel_id=3, replica_groups=mesh['tile'=32,'fsdp'=8] {'fsdp'}, dimensions={0}, use_global_device_ids=true | all-gather | bytes 368640 | tf_op jit(solution)/shard_map/all_gather | solution.py:263
  79.6 2.2 %shard_map.72 = (f32[8,80,128]{2,1,0:T(8,128)S(1)}, f32[2,80,128]{2,1,0:T(8,128)S(1)}, bf16[640,896]{1,0:T(8,128)(2,1)}) custom-call(bf16[8,80,256]{2,1,0:T(8,128)(2,1)S(1)} %bitcast.21, bf16[720,640]{1,0:T(8,128)(2,1)S(1)} %bitcast.19, bf16[720,256]{1,0:T(8,128)(2,1)S(1)} %get-tuple-element.21.win_ref, bf16[640,512]{1,0:T(8,128)(2,1)S(1)} %get-tuple-element.22.cot_ref, ...), custom_call_target="tpu_custom_call" | custom-call | tf_op jit(solution)/shard_map/pallas_call | solution.py:224
  81.8 6.3 %all-to-all-start.3 = ((bf16[16,40,896]{2,1,0:T(8,128)(2,1)}), bf16[16,40,896]{2,1,0:T(8,128)(2,1)S(1)}, u32[]{:S(2)}, u32[]{:S(2)}) async-start(bf16[16,40,896]{2,1,0:T(8,128)(2,1)} %bitcast.12), calls=%async_computation.3 | async-start | bytes 2293760 | tf_op jit(solution)/shard_map/all_to_all | solution.py:271
  88.1 1.3 %collective-permute-start.3 = (f32[2,80,128]{2,1,0:T(8,128)S(1)}, f32[2,80,128]{2,1,0:T(8,128)S(1)}, u32[]{:S(2)}, u32[]{:S(2)}) collective-permute-start(f32[2,80,128]{2,1,0:T(8,128)S(1)} %get-tuple-element.25), channel_id=1, source_target_pairs={{8,0},{16,8},{24,16},{32,24},{40,32},{48,40},{56,48},{64,56},{72,6... | collective-permute-start | bytes 245768 | tf_op jit(solution)/shard_map/ppermute | solution.py:270
  89.4 9.6 %collective-permute-done.3.below_ref = f32[2,80,128]{2,1,0:T(8,128)S(1)} collective-permute-done((f32[2,80,128]{2,1,0:T(8,128)S(1)}, f32[2,80,128]{2,1,0:T(8,128)S(1)}, u32[]{:S(2)}, u32[]{:S(2)}) %collective-permute-start.3) | collective-permute-done | bytes 81952 | tf_op jit(solution)/shard_map/ppermute | solution.py:270
  99.0 0.9 shard_map.73
  99.9 5.5 %all-to-all-done.3.red_ref = bf16[16,40,896]{2,1,0:T(8,128)(2,1)S(1)} async-done(((bf16[16,40,896]{2,1,0:T(8,128)(2,1)}), bf16[16,40,896]{2,1,0:T(8,128)(2,1)S(1)}, u32[]{:S(2)}, u32[]{:S(2)}) %all-to-all-start.3) | async-done | bytes 1146912 | tf_op jit(solution)/shard_map/all_to_all | solution.py:271
  105.5 6.2 %all-to-all-start.2 = ((bf16[8,80,128]{2,1,0:T(8,128)(2,1)}), bf16[8,80,128]{2,1,0:T(8,128)(2,1)S(1)}, u32[]{:S(2)}, u32[]{:S(2)}) async-start(bf16[8,80,128]{2,1,0:T(8,128)(2,1)} %shard_map.73), calls=%async_computation.2 | async-start | bytes 327680 | tf_op jit(solution)/shard_map/all_to_all | solution.py:275
  111.7 0.2 shard_map.75
  111.9 6.6 %collective-permute-start.4 = (f32[20,896]{1,0:T(8,128)S(1)}, f32[20,896]{1,0:T(8,128)S(1)}, u32[]{:S(2)}, u32[]{:S(2)}) collective-permute-start(f32[20,896]{1,0:T(8,128)S(1)} %get-tuple-element.28), channel_id=1, source_target_pairs={{0,8},{8,0},{16,24},{24,16},{32,40},{40,32},{48,56},{56,48},{64,72... | collective-permute-start | bytes 215048 | tf_op jit(solution)/shard_map/ppermute | solution.py:278
  118.5 0.0 all-to-all-done.2
  118.5 0.9 shard_map.74
  119.4 4.6 %collective-permute-done.4.given_ref = f32[20,896]{1,0:T(8,128)S(1)} collective-permute-done((f32[20,896]{1,0:T(8,128)S(1)}, f32[20,896]{1,0:T(8,128)S(1)}, u32[]{:S(2)}, u32[]{:S(2)}) %collective-permute-start.4) | collective-permute-done | bytes 71712 | tf_op jit(solution)/shard_map/ppermute | solution.py:278
  124.0 0.8 shard_map.76
  (1 shorter events, 0.0 us)
Async XLA Ops:
  1.4 12.1 %collective-permute-start = (bf16[1,32,640]{2,1,0:T(8,128)(2,1)S(1)}, bf16[1,32,640]{2,1,0:T(8,128)(2,1)S(1)}, u32[]{:S(2)}, u32[]{:S(2)}) collective-permute-start(bf16[1,32,640]{2,1,0:T(8,128)(2,1)S(1)} %slice.9), channel_id=1, source_target_pairs={{0,8},{8,16},{16,24},{24,32},{32,40},{40,48},{48,56},{56,64},{64,7... | collective-permute-start | bytes 122888 | tf_op jit(solution)/shard_map/ppermute | solution.py:242
  12.2 0.9 copy-start.1
  13.6 5.4 %copy-start.2 = (bf16[2,16,640]{2,1,0:T(8,128)(2,1)S(1)}, bf16[2,16,640]{2,1,0:T(8,128)(2,1)}, u32[]{:S(2)}) copy-start(bf16[2,16,640]{2,1,0:T(8,128)(2,1)} %param.7) | copy-start | bytes 122884
  13.6 21.3 %copy-start = (bf16[80,9,640]{2,0,1:T(8,128)(2,1)S(1)}, bf16[80,9,640]{2,0,1:T(8,128)(2,1)}, u32[]{:S(2)}) copy-start(bf16[80,9,640]{2,0,1:T(8,128)(2,1)} %param.5) | copy-start | bytes 2764804
  14.6 20.2 %all-to-all-start = ((bf16[8,80,384]{2,1,0:T(8,128)(2,1)}), bf16[8,80,384]{2,1,0:T(8,128)(2,1)S(1)}, u32[]{:S(2)}, u32[]{:S(2)}) async-start(bf16[8,80,384]{2,1,0:T(8,128)(2,1)} %shard_map.68), calls=%async_computation | async-start | bytes 983040 | tf_op jit(solution)/shard_map/all_to_all | solution.py:248
  18.9 8.9 %collective-permute-start.1 = (bf16[16,640]{1,0:T(8,128)(2,1)S(1)}, bf16[16,640]{1,0:T(8,128)(2,1)S(1)}, u32[]{:S(2)}, u32[]{:S(2)}) collective-permute-start(bf16[16,640]{1,0:T(8,128)(2,1)S(1)} %get-tuple-element.32), channel_id=1, source_target_pairs={{0,8},{8,16},{16,24},{24,32},{32,40},{40,48},{48,56},{56,64},{64,7... | collective-permute-start | bytes 61448 | tf_op jit(solution)/shard_map/ppermute | solution.py:243
  26.4 8.4 %collective-permute-start.2 = (bf16[16,640]{1,0:T(8,128)(2,1)S(1)}, bf16[16,640]{1,0:T(8,128)(2,1)S(1)}, u32[]{:S(2)}, u32[]{:S(2)}) collective-permute-start(bf16[16,640]{1,0:T(8,128)(2,1)S(1)} %get-tuple-element.31), channel_id=1, source_target_pairs={{8,0},{16,8},{24,16},{32,24},{40,32},{48,40},{56,48},{64,56},{72,6... | collective-permute-start | bytes 61448 | tf_op jit(solution)/shard_map/ppermute | solution.py:244
  36.5 28.6 %all-to-all-start.1 = ((bf16[8,80,256]{2,1,0:T(8,128)(2,1)}), bf16[8,80,256]{2,1,0:T(8,128)(2,1)S(1)}, u32[]{:S(2)}, u32[]{:S(2)}) async-start(bf16[8,80,256]{2,1,0:T(8,128)(2,1)} %get-tuple-element.17), calls=%async_computation.1 | async-start | bytes 655360 | tf_op jit(solution)/shard_map/all_to_all | solution.py:261
  81.8 23.7 %all-to-all-start.3 = ((bf16[16,40,896]{2,1,0:T(8,128)(2,1)}), bf16[16,40,896]{2,1,0:T(8,128)(2,1)S(1)}, u32[]{:S(2)}, u32[]{:S(2)}) async-start(bf16[16,40,896]{2,1,0:T(8,128)(2,1)} %bitcast.12), calls=%async_computation.3 | async-start | bytes 2293760 | tf_op jit(solution)/shard_map/all_to_all | solution.py:271
  88.1 10.9 %collective-permute-start.3 = (f32[2,80,128]{2,1,0:T(8,128)S(1)}, f32[2,80,128]{2,1,0:T(8,128)S(1)}, u32[]{:S(2)}, u32[]{:S(2)}) collective-permute-start(f32[2,80,128]{2,1,0:T(8,128)S(1)} %get-tuple-element.25), channel_id=1, source_target_pairs={{8,0},{16,8},{24,16},{32,24},{40,32},{48,40},{56,48},{64,56},{72,6... | collective-permute-start | bytes 245768 | tf_op jit(solution)/shard_map/ppermute | solution.py:270
  105.5 13.0 %all-to-all-start.2 = ((bf16[8,80,128]{2,1,0:T(8,128)(2,1)}), bf16[8,80,128]{2,1,0:T(8,128)(2,1)S(1)}, u32[]{:S(2)}, u32[]{:S(2)}) async-start(bf16[8,80,128]{2,1,0:T(8,128)(2,1)} %shard_map.73), calls=%async_computation.2 | async-start | bytes 327680 | tf_op jit(solution)/shard_map/all_to_all | solution.py:275
  111.9 12.1 %collective-permute-start.4 = (f32[20,896]{1,0:T(8,128)S(1)}, f32[20,896]{1,0:T(8,128)S(1)}, u32[]{:S(2)}, u32[]{:S(2)}) collective-permute-start(f32[20,896]{1,0:T(8,128)S(1)} %get-tuple-element.28), channel_id=1, source_target_pairs={{0,8},{8,0},{16,24},{24,16},{32,40},{40,32},{48,56},{56,48},{64,72... | collective-permute-start | bytes 215048 | tf_op jit(solution)/shard_map/ppermute | solution.py:278

commit v3 on v2

--- a/solution.py
+++ b/solution.py
@@ -56,82 +56,89 @@
     return (lane // 32) * 32 + 2 * (lane % 16) + (lane // 16) % 2
 
 
-def pack_kernel(image_ref, group_ref, send_ref):
+def pack_kernel(image_ref, group_ref, cot_ref, send_ref):
     pick = jnp.where(cell_of_lane(iota((128, 128), 1)) == iota((128, 128), 0), 1.0, 0.0)
     pixels = tn(image_ref[...], pick.astype(BF16)).astype(BF16)
-    eye = jnp.where(iota((80, 80), 0) == iota((80, 80), 1), 1.0, 0.0).astype(BF16)
-    above, below = jnp.zeros((32, 80), BF16), jnp.zeros((80, 80), BF16)
+    taps = swap_blocks([group_ref[t].astype(F32) for t in range(8)])
+    last = [group_ref[8, 16 * b : 16 * b + 16, :].astype(F32) for b in range(5)]
+    last = swap_blocks(last + [jnp.zeros((16, 128), F32)] * 3)
     for p in range(8):
-        taps = [group_ref[t, 16 * p : 16 * p + 16, :] for t in range(9)]
-        send_ref[p, :, 0:128] = pixels[80 * p : 80 * p + 80]
-        send_ref[p, :, 128:384] = nt(eye, jnp.concatenate([above, *taps, below], axis=0)).astype(BF16)
-
-
-def rim_kernel(base_ref, rim_ref, send_ref):
-    lane = iota((32, 128), 1)
-    pick = jnp.where((cell_of_lane(lane) == iota((32, 128), 0)) & (lane < 32), 1.0, 0.0)
-    pixels = tn(rim_ref[...], pick.astype(BF16)).astype(BF16)
-    here = iota((80, 128), 1) < 32
-    for p in range(8):
-        send_ref[p, :, 0:128] = base_ref[p, :, 0:128]
-        send_ref[p, :, 128:256] = jnp.where(here, pixels[80 * p : 80 * p + 80], base_ref[p, :, 128:256])
-        send_ref[p, :, 256:384] = base_ref[p, :, 256:384]
-
-
-def forward_kernel(recv_ref, weight_ref, above_ref, cells_ref, below_ref, hid_ref, win_ref, share_ref):
-    share_ref[0:16, :] = above_ref[...]
-    share_ref[16:48, :] = cells_ref[...]
-    share_ref[48:64, :] = below_ref[...]
-
-    def tile(start):
-        return swap_blocks([recv_ref[q, :, start : start + 128].astype(F32) for q in range(8)])
-
-    inner = tile(0)
-    rim = tile(128)
-    even = [rim[0]] + [inner[2 * r] for r in range(4)]
-    odd = [rim[1]] + [inner[2 * r + 1] for r in range(4)]
-    left = [from_left(odd[r]).astype(BF16) for r in range(4)] + [None]
-    even = [x.astype(BF16) for x in even]
-    odd = [x.astype(BF16) for x in odd]
-    for a in range(3):
+        send_ref[p, 0:80, :] = pixels[80 * p : 80 * p + 80]
+        send_ref[p, 80:160, :] = taps[p].astype(BF16)
+        send_ref[p, 160:176, :] = last[p].astype(BF16)
+        for k in range(5):
+            send_ref[p, 176 + 32 * k : 208 + 32 * k, :] = cot_ref[:, 128 * k : 128 * k + 128]
+
+
+def spread_kernel(
+    recv_ref, above_ref, below_ref,
+    win_ref, down_ref, up_ref, own_ref, cot_ref, halo_ref, cell_ref, tap_ref,
+):
+    pixels = swap_blocks([recv_ref[q, 0:80, :].astype(F32) for q in range(8)])
+    for r in range(4):
+        columns = (from_left(pixels[2 * r + 1]), pixels[2 * r], pixels[2 * r + 1])
         for b in range(3):
-            t = 3 * a + b
+            part = columns[b].astype(BF16)
             for i in range(2):
-                r = 2 * i + a
-                part = (left, even, odd)[b][r] if not (b == 0 and r == 4) else from_left(odd[4].astype(F32)).astype(BF16)
-                win_ref[80 * t : 80 * t + 80, 128 * i : 128 * i + 128] = part
-    hidden = tn(weight_ref[...], win_ref[...]).astype(BF16)
-    for p in range(8):
-        for g in range(5):
-            hid_ref[p, 16 * g : 16 * g + 16, :] = hidden[128 * g + 16 * p : 128 * g + 16 * p + 16]
-
-
-def group_kernel(recv_ref, all_ref, grad_ref, cot_ref, cell_ref, gw_ref):
+                a = r + 1 - 2 * i
+                if 0 <= a < 3:
+                    t = 3 * a + b
+                    win_ref[80 * t : 80 * t + 80, 128 * i : 128 * i + 128] = part
+    win_ref[0:240, 0:128] = jnp.zeros((240, 128), BF16)
+    down_ref[:, 0:128] = pixels[6].astype(BF16)
+    down_ref[:, 128:256] = pixels[7].astype(BF16)
     for q in range(8):
-        gw_ref[80 * q : 80 * q + 80, :] = recv_ref[q, :, 128:384]
-        for r in range(4):
-            cell_ref[128 * r + 16 * q : 128 * r + 16 * q + 16, :] = all_ref[q, 16 * r : 16 * r + 16, :]
+        tap_ref[80 * q : 80 * q + 80, 0:128] = recv_ref[q, 80:160, :]
+        last = recv_ref[q, 160:176, :].astype(F32)
+        for b in range(5):
+            moved = last if b == 0 else pltpu.roll(last, 128 - 16 * b, 1)
+            tap_ref[80 * q + 16 * b : 80 * q + 16 * b + 16, 128:256] = moved.astype(BF16)
+        for k in range(5):
+            for i in range(2):
+                start = 176 + 32 * k + 16 * i
+                cell_ref[128 * i + 16 * q : 128 * i + 16 * q + 16, 128 * k : 128 * k + 128] = recv_ref[q, start : start + 16, :]
     eye = jnp.where(iota((128, 128), 0) == iota((128, 128), 1), 1.0, 0.0).astype(BF16)
     for g in range(5):
         rows = slice(128 * g, 128 * g + 128)
         cot = nt(eye, cell_ref[:, rows]).astype(BF16)
         cot_ref[rows, :] = cot
-        terms = tn(gw_ref[rows, :], cot)
-        for i in range(2):
-            total = None
-            for u in range(3):
-                base = 32 + 48 * u
-                lanes = slice(128 * (i + 2 - u), 128 * (i + 2 - u) + 128)
-                part = (
+        terms = tn(tap_ref[rows, :], cot)
+        sums = []
+        for u in range(3):
+            base = 48 * u
+            by_row = []
+            for i in range(2):
+                lanes = slice(128 * i, 128 * i + 128)
+                by_row.append(
                     from_right(terms[base : base + 16, lanes])
                     + terms[base + 16 : base + 32, lanes]
                     + from_left(terms[base + 32 : base + 48, lanes])
                 )
-                total = part if total is None else total + part
-            grad_ref[16 * g : 16 * g + 16, 128 * i : 128 * i + 128] = total
-
-
-def middle_kernel(hid_ref, grad_ref, act_ref, pre_ref):
+            sums.append(by_row)
+        here = slice(16 * g, 16 * g + 16)
+        own_ref[here, 0:128] = sums[1][0] + sums[0][1]
+        own_ref[here, 128:256] = sums[1][1] + sums[2][0]
+        up_ref[here, :] = sums[0][0]
+        down_ref[here, 256:384] = sums[2][1].astype(BF16)
+        halo_ref[here, 0:128] = above_ref[:, rows]
+        halo_ref[here, 128:256] = below_ref[:, rows]
+
+
+def forward_kernel(part_ref, down_ref, up_ref, weight_ref, hid_ref, win_ref, pass_ref):
+    even = down_ref[:, 0:128]
+    odd = down_ref[:, 128:256]
+    win_ref[...] = part_ref[...]
+    win_ref[0:80, 0:128] = from_left(odd.astype(F32)).astype(BF16)
+    win_ref[80:160, 0:128] = even
+    win_ref[160:240, 0:128] = odd
+    pass_ref[...] = up_ref[...]
+    hidden = tn(weight_ref[...], win_ref[...]).astype(BF16)
+    for p in range(8):
+        for g in range(5):
+            hid_ref[p, 16 * g : 16 * g + 16, :] = hidden[128 * g + 16 * p : 128 * g + 16 * p + 16]
+
+
+def middle_kernel(hid_ref, own_ref, down_ref, up_ref, halo_ref, act_ref, share_ref):
     hidden = hid_ref[0].astype(F32)
     for q in range(1, 8):
         hidden = hidden + hid_ref[q].astype(F32)
@@ -139,11 +146,14 @@
     density = jnp.exp(-0.5 * hidden * hidden) * (1.0 / math.sqrt(2.0 * math.pi))
     act_ref[...] = (hidden * cumul).astype(BF16)
     slopes = cumul + hidden * density
-    pre_ref[...] = (grad_ref[...] * slopes).astype(BF16)
+    act_grad = own_ref[...] + jnp.concatenate([down_ref[:, 256:384].astype(F32), up_ref[...]], axis=1)
+    share_ref[0:80, :] = (act_grad * slopes).astype(BF16)
+    share_ref[80:160, :] = halo_ref[...]
 
 
 def backward_kernel(
-    all_ref, weight_ref, win_ref, cot_ref, act_ref, img_ref, up_ref, red_ref, pre_ref, shift_ref
+    all_ref, weight_ref, win_ref, cot_ref, act_ref,
+    img_ref, up_ref, red_ref, pre_ref, shift_ref, cell_ref,
 ):
     for p in range(8):
         for g in range(5):
@@ -179,11 +189,20 @@
                 for i in range(2):
                     lanes = slice(128 * (i + 2 - u), 128 * (i + 2 - u) + 128)
                     shift_ref[g, base : base + 16, lanes] = moved[v][i][16 * g : 16 * g + 16]
+    for q in range(8):
+        for k in range(5):
+            for side in range(2):
+                cell_ref[128 * side + 16 * q : 128 * side + 16 * q + 16, 128 * k : 128 * k + 128] = all_ref[
+                    q, 80 + 16 * k : 96 + 16 * k, 128 * side : 128 * side + 128
+                ]
+    eye = jnp.where(iota((128, 128), 0) == iota((128, 128), 1), 1.0, 0.0).astype(BF16)
     tail = jnp.concatenate([win_ref[640:720, :], jnp.zeros((176, 256), BF16)], axis=0)
     last = nt(pre, tail)
     for g in range(5):
         here = slice(128 * g, 128 * g + 128)
-        red_ref[here, 640:896] = (last[here] + nt(cot_ref[here, :], shift_ref[g])).astype(BF16)
+        rims = nt(eye, cell_ref[:, here]).astype(BF16)
+        cot = jnp.concatenate([rims[:, 0:128], cot_ref[here, :], rims[:, 128:256]], axis=1)
+        red_ref[here, 640:896] = (last[here] + nt(cot, shift_ref[g])).astype(BF16)
 
 
 def return_kernel(img_ref, below_ref, send_ref):
@@ -239,33 +258,37 @@
     planes = [[2 * i + z for i in range(tiles // 2)] for z in range(2)]
 
     cells = cotangent.reshape(32, 640)
-    rim = lax.ppermute(image[3:4], "tile", downward).reshape(32, 640)
     above = lax.ppermute(cotangent[1], "tile", downward)
     below = lax.ppermute(cotangent[0], "tile", upward)
     weights = conv_weight.transpose(1, 0, 2).reshape(720, 640)
-    (base,) = call(pack_kernel, [((8, 80, 384), BF16)], image.reshape(128, 640), group_weight)
-    (send,) = call(rim_kernel, [((8, 80, 384), BF16)], base, rim)
+    (send,) = call(
+        pack_kernel, [((8, 336, 128), BF16)],
+        image.reshape(128, 640), group_weight.transpose(0, 2, 1), cells,
+    )
     recv = lax.all_to_all(send, "fsdp", 0, 0, tiled=True)
-    hid, windows, share = call(
+    windows, down, up, own, cot, halo = call(
+        spread_kernel,
+        [((720, 256), BF16), ((80, 384), BF16), ((80, 128), F32), ((80, 256), F32), ((640, 256), BF16), ((80, 256), BF16)],
+        recv, above, below,
+        scratch=[pltpu.VMEM((256, 640), BF16), pltpu.VMEM((640, 256), BF16)],
+    )
+    down = lax.ppermute(down, "tile", downward)
+    hid, windows, up = call(
         forward_kernel,
-        [((8, 80, 256), BF16), ((720, 256), BF16), ((64, 640), BF16)],
-        recv, weights, above, cells, below,
-    )
-    cot_all = lax.all_gather(share, "fsdp", axis=0, tiled=False)
-    grad, cot = call(
-        group_kernel,
-        [((80, 256), F32), ((640, 512), BF16)],
-        recv, cot_all,
-        scratch=[pltpu.VMEM((512, 640), BF16), pltpu.VMEM((640, 256), BF16)],
-    )
+        [((8, 80, 256), BF16), ((720, 256), BF16), ((80, 128), F32)],
+        windows, down, up, weights,
+    )
+    up = lax.ppermute(up, "tile", upward)
     hid = lax.all_to_all(hid, "fsdp", 0, 0, tiled=True)
-    act, pre = call(middle_kernel, [((80, 256), BF16), ((80, 256), BF16)], hid, grad)
-    pre_all = lax.all_gather(pre, "fsdp", axis=0, tiled=False)
+    act, share = call(
+        middle_kernel, [((80, 256), BF16), ((160, 256), BF16)], hid, own, down, up, halo
+    )
+    share_all = lax.all_gather(share, "fsdp", axis=0, tiled=False)
     img, img_up, red = call(
         backward_kernel,
         [((8, 80, 128), F32), ((2, 80, 128), F32), ((640, 896), BF16)],
-        pre_all, weights, windows, cot, act,
-        scratch=[pltpu.VMEM((640, 256), BF16), pltpu.VMEM((5, 256, 512), BF16)],
+        share_all, weights, windows, cot, act,
+        scratch=[pltpu.VMEM((640, 256), BF16), pltpu.VMEM((5, 256, 512), BF16), pltpu.VMEM((256, 640), BF16)],
     )
     img_below = lax.ppermute(img_up, "tile", upward)
     red = lax.all_to_all(

time: 126 us -> 125 us (level)
  blocking collectives: 34.5 us -> 15.8 us
  waiting for transfers between devices: 26.8 us -> 44.7 us
    all_gather x2 -> x1, blocking collectives: 34.5 us -> 15.8 us  [per_device(): share_all = lax.all_gather(share, 'fsdp', axis=0, tiled=False)]
    ppermute x1 -> x2, waiting for transfers between devices: 0.01 us -> 13.4 us  [the longest x1 12.1 us: per_device(): up = lax.ppermute(up, 'tile', upward)]
    ppermute x1, waiting for transfers between devices: 0.11 us -> 4.39 us  [per_device(): above = lax.ppermute(cotangent[1], 'tile', downward)]
    all_to_all x1, starting transfers between devices: 6.31 us -> 10.2 us  [per_device(): lax.all_to_all(red.reshape(16, 40, 896), 'tile', 0, 0, tiled=True, axis_i...]
    all_to_all x1, starting transfers between devices: 4.34 us -> 7.53 us  [per_device(): recv = lax.all_to_all(send, 'fsdp', 0, 0, tiled=True)]
    all_to_all x1, starting transfers between devices: 7.1 us -> 5.06 us  [per_device(): hid = lax.all_to_all(hid, 'fsdp', 0, 0, tiled=True)]
    ppermute x1 -> x2, starting transfers between devices: 9.63 us -> 7.66 us  [the longest x1 6.38 us: per_device(): down = lax.ppermute(down, 'tile', downward)]
    all_to_all x1, waiting for transfers between devices: 0.01 us -> 1.5 us  [per_device(): recv = lax.all_to_all(send, 'fsdp', 0, 0, tiled=True)]
  transfers between devices with their start and end apart: 9 -> 10, of which waited for: 5 -> 8; matrix products, arithmetic and copies ran while one was open for 1% -> 0% of each run, Pallas kernels for 3% -> 2%
where the time goes in v3:
time: 125 us; the launch traced here: 124 us
  starting transfers between devices  51.2 us (41%)
  waiting for transfers between devices  44.7 us (36%)
  blocking collectives  15.8 us (13%)
  Pallas kernels  9.12 us (7%)
  local copies, waits for them, and re-layouts  2.62 us (2%)
    all_gather x1, blocking collectives, per_device(): share_all = lax.all_gather(share, 'fsdp', axis=0, tiled=False)  15.8 us
    ppermute x1, waiting for transfers between devices, per_device(): up = lax.ppermute(up, 'tile', upward)  12.1 us
    all_to_all x1, starting transfers between devices, per_device(): lax.all_to_all(red.reshape(16, 40, 896), 'tile', 0, 0, tiled=True, axis_i...  10.2 us
    pallas_call x9, Pallas kernels, call(): pl.pallas_call(kernel, out_shape=[jax.ShapeDtypeStruct(shape, dtype) for...  9.12 us
    ppermute x1, waiting for transfers between devices, per_device(): img_below = lax.ppermute(img_up, 'tile', upward)  8.09 us
    all_to_all x1, starting transfers between devices, per_device(): recv = lax.all_to_all(send, 'fsdp', 0, 0, tiled=True)  7.53 us
    all_to_all x1, waiting for transfers between devices, per_device(): lax.all_to_all(red.reshape(16, 40, 896), 'tile', 0, 0, tiled=True, axis_i...  7.04 us
    ppermute x1, starting transfers between devices, per_device(): down = lax.ppermute(down, 'tile', downward)  6.38 us
  transfers between devices with their start and end apart: 10, of which 8 were waited for; matrix products, arithmetic and copies ran while one was open for 0% of the time, Pallas kernels for 2%

profile of v3, /device:TPU:1, one launch (start us, length us, event | category | flops | bytes accessed | tf_op | source)
XLA Modules:
  0.0 124.1 jit_solution(5611015765694673631)
XLA Ops:
  0.6 0.0 copy-start.1
  0.6 0.9 copy-done.1
  1.6 0.0 copy-start.2
  1.6 0.8 copy-done.2
  2.3 0.0 copy-start.4
  2.3 0.9 copy-done.4
  3.2 0.0 copy-start.3
  3.3 1.3 %shard_map.67 = bf16[8,336,128]{2,1,0:T(8,128)(2,1)} custom-call(bf16[128,640]{1,0:T(8,128)(2,1)S(1)} %bitcast.23, bf16[9,80,128]{2,1,0:T(8,128)(2,1)S(1)} %bitcast.21, bf16[32,640]{1,0:T(8,128)(2,1)S(1)} %bitcast.22), custom_call_target="tpu_custom_call" | custom-call | tf_op jit(solution)/shard_map/pallas_call | solution.py:243
  4.6 0.0 copy-start
  4.6 7.5 %all-to-all-start = ((bf16[8,336,128]{2,1,0:T(8,128)(2,1)}), bf16[8,336,128]{2,1,0:T(8,128)(2,1)S(1)}, u32[]{:S(2)}, u32[]{:S(2)}) async-start(bf16[8,336,128]{2,1,0:T(8,128)(2,1)} %shard_map.67), calls=%async_computation | async-start | bytes 1376256 | tf_op jit(solution)/shard_map/all_to_all | solution.py:268
  12.1 0.0 copy-done.3
  12.1 6.4 %collective-permute-start = (bf16[16,640]{1,0:T(8,128)(2,1)S(1)}, bf16[16,640]{1,0:T(8,128)(2,1)S(1)}, u32[]{:S(2)}, u32[]{:S(2)}) collective-permute-start(bf16[16,640]{1,0:T(8,128)(2,1)S(1)} %get-tuple-element.40), channel_id=1, source_target_pairs={{0,8},{8,16},{16,24},{24,32},{32,40},{40,48},{48,56},{56,64},{64,7... | collective-permute-start | bytes 61448 | tf_op jit(solution)/shard_map/ppermute | solution.py:261
  18.5 1.3 %collective-permute-start.1 = (bf16[16,640]{1,0:T(8,128)(2,1)S(1)}, bf16[16,640]{1,0:T(8,128)(2,1)S(1)}, u32[]{:S(2)}, u32[]{:S(2)}) collective-permute-start(bf16[16,640]{1,0:T(8,128)(2,1)S(1)} %get-tuple-element.39), channel_id=1, source_target_pairs={{8,0},{16,8},{24,16},{32,24},{40,32},{48,40},{56,48},{64,56},{72,6... | collective-permute-start | bytes 61448 | tf_op jit(solution)/shard_map/ppermute | solution.py:262
  19.8 4.4 %collective-permute-done.above_ref = bf16[16,640]{1,0:T(8,128)(2,1)S(1)} collective-permute-done((bf16[16,640]{1,0:T(8,128)(2,1)S(1)}, bf16[16,640]{1,0:T(8,128)(2,1)S(1)}, u32[]{:S(2)}, u32[]{:S(2)}) %collective-permute-start) | collective-permute-done | bytes 20512 | tf_op jit(solution)/shard_map/ppermute | solution.py:261
  24.2 5.8 %collective-permute-done.1.below_ref = bf16[16,640]{1,0:T(8,128)(2,1)S(1)} collective-permute-done((bf16[16,640]{1,0:T(8,128)(2,1)S(1)}, bf16[16,640]{1,0:T(8,128)(2,1)S(1)}, u32[]{:S(2)}, u32[]{:S(2)}) %collective-permute-start.1) | collective-permute-done | bytes 20512 | tf_op jit(solution)/shard_map/ppermute | solution.py:262
  29.9 1.5 %all-to-all-done.recv_ref = bf16[8,336,128]{2,1,0:T(8,128)(2,1)S(1)} async-done(((bf16[8,336,128]{2,1,0:T(8,128)(2,1)}), bf16[8,336,128]{2,1,0:T(8,128)(2,1)S(1)}, u32[]{:S(2)}, u32[]{:S(2)}) %all-to-all-start) | async-done | bytes 688160 | tf_op jit(solution)/shard_map/all_to_all | solution.py:268
  31.4 0.8 shard_map.68
  32.2 6.4 %collective-permute-start.2 = (bf16[80,384]{1,0:T(8,128)(2,1)S(1)}, bf16[80,384]{1,0:T(8,128)(2,1)S(1)}, u32[]{:S(2)}, u32[]{:S(2)}) collective-permute-start(bf16[80,384]{1,0:T(8,128)(2,1)S(1)} %get-tuple-element.22), channel_id=1, source_target_pairs={{0,8},{8,16},{16,24},{24,32},{32,40},{40,48},{48,56},{56,64},{64,7... | collective-permute-start | bytes 184328 | tf_op jit(solution)/shard_map/ppermute | solution.py:275
  38.6 1.3 %collective-permute-done.2.down_ref = bf16[80,384]{1,0:T(8,128)(2,1)S(1)} collective-permute-done((bf16[80,384]{1,0:T(8,128)(2,1)S(1)}, bf16[80,384]{1,0:T(8,128)(2,1)S(1)}, u32[]{:S(2)}, u32[]{:S(2)}) %collective-permute-start.2) | collective-permute-done | bytes 61472 | tf_op jit(solution)/shard_map/ppermute | solution.py:275
  39.9 0.0 copy-done
  39.9 1.2 shard_map.69
  41.1 5.1 %all-to-all-start.1 = ((bf16[8,80,256]{2,1,0:T(8,128)(2,1)}), bf16[8,80,256]{2,1,0:T(8,128)(2,1)S(1)}, u32[]{:S(2)}, u32[]{:S(2)}) async-start(bf16[8,80,256]{2,1,0:T(8,128)(2,1)} %get-tuple-element.24), calls=%async_computation.1 | async-start | bytes 655360 | tf_op jit(solution)/shard_map/all_to_all | solution.py:282
  46.2 1.3 %collective-permute-start.3 = (f32[80,128]{1,0:T(8,128)S(1)}, f32[80,128]{1,0:T(8,128)S(1)}, u32[]{:S(2)}, u32[]{:S(2)}) collective-permute-start(f32[80,128]{1,0:T(8,128)S(1)} %get-tuple-element.26), channel_id=1, source_target_pairs={{8,0},{16,8},{24,16},{32,24},{40,32},{48,40},{56,48},{64,56},{72,6... | collective-permute-start | bytes 122888 | tf_op jit(solution)/shard_map/ppermute | solution.py:281
  47.5 12.1 %collective-permute-done.3.up_ref = f32[80,128]{1,0:T(8,128)S(1)} collective-permute-done((f32[80,128]{1,0:T(8,128)S(1)}, f32[80,128]{1,0:T(8,128)S(1)}, u32[]{:S(2)}, u32[]{:S(2)}) %collective-permute-start.3) | collective-permute-done | bytes 40992 | tf_op jit(solution)/shard_map/ppermute | solution.py:281
  59.6 0.0 all-to-all-done.1.hid_ref
  59.6 0.1 shard_map.70
  59.7 15.8 %all-gather = bf16[1280,256]{1,0:T(8,128)(2,1)S(1)} all-gather(bf16[160,256]{1,0:T(8,128)(2,1)S(1)} %get-tuple-element.28), channel_id=2, replica_groups=mesh['tile'=32,'fsdp'=8] {'fsdp'}, dimensions={0}, use_global_device_ids=true | all-gather | bytes 737280 | tf_op jit(solution)/shard_map/all_gather | solution.py:286
  75.5 2.9 %shard_map.71 = (f32[8,80,128]{2,1,0:T(8,128)S(1)}, f32[2,80,128]{2,1,0:T(8,128)S(1)}, bf16[640,896]{1,0:T(8,128)(2,1)}) custom-call(bf16[8,160,256]{2,1,0:T(8,128)(2,1)S(1)} %bitcast.19, bf16[720,640]{1,0:T(8,128)(2,1)S(1)} %bitcast.18, bf16[720,256]{1,0:T(8,128)(2,1)S(1)} %get-tuple-element.29.win_ref, bf16[640,256]{1,0:T(8,128)(2,1)S(1)} %get-tuple-element.30.cot_ref, ...), custom_call_target="tpu_custom_call" | custom-call | tf_op jit(solution)/shard_map/pallas_call | solution.py:243
  78.3 10.2 %all-to-all-start.3 = ((bf16[16,40,896]{2,1,0:T(8,128)(2,1)}), bf16[16,40,896]{2,1,0:T(8,128)(2,1)S(1)}, u32[]{:S(2)}, u32[]{:S(2)}) async-start(bf16[16,40,896]{2,1,0:T(8,128)(2,1)} %bitcast.11), calls=%async_computation.3 | async-start | bytes 2293760 | tf_op jit(solution)/shard_map/all_to_all | solution.py:294
  88.6 1.3 %collective-permute-start.4 = (f32[2,80,128]{2,1,0:T(8,128)S(1)}, f32[2,80,128]{2,1,0:T(8,128)S(1)}, u32[]{:S(2)}, u32[]{:S(2)}) collective-permute-start(f32[2,80,128]{2,1,0:T(8,128)S(1)} %get-tuple-element.33), channel_id=1, source_target_pairs={{8,0},{16,8},{24,16},{32,24},{40,32},{48,40},{56,48},{64,56},{72,6... | collective-permute-start | bytes 245768 | tf_op jit(solution)/shard_map/ppermute | solution.py:293
  89.9 8.1 %collective-permute-done.4.below_ref = f32[2,80,128]{2,1,0:T(8,128)S(1)} collective-permute-done((f32[2,80,128]{2,1,0:T(8,128)S(1)}, f32[2,80,128]{2,1,0:T(8,128)S(1)}, u32[]{:S(2)}, u32[]{:S(2)}) %collective-permute-start.4) | collective-permute-done | bytes 81952 | tf_op jit(solution)/shard_map/ppermute | solution.py:293
  98.0 0.9 shard_map.72
  98.9 7.0 %all-to-all-done.3.red_ref = bf16[16,40,896]{2,1,0:T(8,128)(2,1)S(1)} async-done(((bf16[16,40,896]{2,1,0:T(8,128)(2,1)}), bf16[16,40,896]{2,1,0:T(8,128)(2,1)S(1)}, u32[]{:S(2)}, u32[]{:S(2)}) %all-to-all-start.3) | async-done | bytes 1146912 | tf_op jit(solution)/shard_map/all_to_all | solution.py:294
  106.0 5.8 %all-to-all-start.2 = ((bf16[8,80,128]{2,1,0:T(8,128)(2,1)}), bf16[8,80,128]{2,1,0:T(8,128)(2,1)S(1)}, u32[]{:S(2)}, u32[]{:S(2)}) async-start(bf16[8,80,128]{2,1,0:T(8,128)(2,1)} %shard_map.72), calls=%async_computation.2 | async-start | bytes 327680 | tf_op jit(solution)/shard_map/all_to_all | solution.py:298
  111.8 0.2 shard_map.74
  111.9 5.9 %collective-permute-start.5 = (f32[20,896]{1,0:T(8,128)S(1)}, f32[20,896]{1,0:T(8,128)S(1)}, u32[]{:S(2)}, u32[]{:S(2)}) collective-permute-start(f32[20,896]{1,0:T(8,128)S(1)} %get-tuple-element.36), channel_id=1, source_target_pairs={{0,8},{8,0},{16,24},{24,16},{32,40},{40,32},{48,56},{56,48},{64,72... | collective-permute-start | bytes 215048 | tf_op jit(solution)/shard_map/ppermute | solution.py:301
  117.9 0.0 all-to-all-done.2
  117.9 0.9 shard_map.73
  118.8 4.6 %collective-permute-done.5.given_ref = f32[20,896]{1,0:T(8,128)S(1)} collective-permute-done((f32[20,896]{1,0:T(8,128)S(1)}, f32[20,896]{1,0:T(8,128)S(1)}, u32[]{:S(2)}, u32[]{:S(2)}) %collective-permute-start.5) | collective-permute-done | bytes 71712 | tf_op jit(solution)/shard_map/ppermute | solution.py:301
  123.3 0.8 shard_map.75
  (1 shorter events, 0.0 us)
Async XLA Ops:
  0.6 0.9 copy-start.1
  1.6 0.8 copy-start.2
  2.3 0.9 copy-start.4
  3.2 8.9 %copy-start.3 = (bf16[2,16,640]{2,1,0:T(8,128)(2,1)S(1)}, bf16[2,16,640]{2,1,0:T(8,128)(2,1)}, u32[]{:S(2)}) copy-start(bf16[2,16,640]{2,1,0:T(8,128)(2,1)} %param.7) | copy-start | bytes 122884
  4.6 35.3 %copy-start = (bf16[80,9,640]{2,0,1:T(8,128)(2,1)S(1)}, bf16[80,9,640]{2,0,1:T(8,128)(2,1)}, u32[]{:S(2)}) copy-start(bf16[80,9,640]{2,0,1:T(8,128)(2,1)} %param.5) | copy-start | bytes 2764804
  4.6 26.9 %all-to-all-start = ((bf16[8,336,128]{2,1,0:T(8,128)(2,1)}), bf16[8,336,128]{2,1,0:T(8,128)(2,1)S(1)}, u32[]{:S(2)}, u32[]{:S(2)}) async-start(bf16[8,336,128]{2,1,0:T(8,128)(2,1)} %shard_map.67), calls=%async_computation | async-start | bytes 1376256 | tf_op jit(solution)/shard_map/all_to_all | solution.py:268
  12.1 12.1 %collective-permute-start = (bf16[16,640]{1,0:T(8,128)(2,1)S(1)}, bf16[16,640]{1,0:T(8,128)(2,1)S(1)}, u32[]{:S(2)}, u32[]{:S(2)}) collective-permute-start(bf16[16,640]{1,0:T(8,128)(2,1)S(1)} %get-tuple-element.40), channel_id=1, source_target_pairs={{0,8},{8,16},{16,24},{24,32},{32,40},{40,48},{48,56},{56,64},{64,7... | collective-permute-start | bytes 61448 | tf_op jit(solution)/shard_map/ppermute | solution.py:261
  18.5 11.4 %collective-permute-start.1 = (bf16[16,640]{1,0:T(8,128)(2,1)S(1)}, bf16[16,640]{1,0:T(8,128)(2,1)S(1)}, u32[]{:S(2)}, u32[]{:S(2)}) collective-permute-start(bf16[16,640]{1,0:T(8,128)(2,1)S(1)} %get-tuple-element.39), channel_id=1, source_target_pairs={{8,0},{16,8},{24,16},{32,24},{40,32},{48,40},{56,48},{64,56},{72,6... | collective-permute-start | bytes 61448 | tf_op jit(solution)/shard_map/ppermute | solution.py:262
  32.2 7.7 %collective-permute-start.2 = (bf16[80,384]{1,0:T(8,128)(2,1)S(1)}, bf16[80,384]{1,0:T(8,128)(2,1)S(1)}, u32[]{:S(2)}, u32[]{:S(2)}) collective-permute-start(bf16[80,384]{1,0:T(8,128)(2,1)S(1)} %get-tuple-element.22), channel_id=1, source_target_pairs={{0,8},{8,16},{16,24},{24,32},{32,40},{40,48},{48,56},{56,64},{64,7... | collective-permute-start | bytes 184328 | tf_op jit(solution)/shard_map/ppermute | solution.py:275
  41.1 18.5 %all-to-all-start.1 = ((bf16[8,80,256]{2,1,0:T(8,128)(2,1)}), bf16[8,80,256]{2,1,0:T(8,128)(2,1)S(1)}, u32[]{:S(2)}, u32[]{:S(2)}) async-start(bf16[8,80,256]{2,1,0:T(8,128)(2,1)} %get-tuple-element.24), calls=%async_computation.1 | async-start | bytes 655360 | tf_op jit(solution)/shard_map/all_to_all | solution.py:282
  46.2 13.4 %collective-permute-start.3 = (f32[80,128]{1,0:T(8,128)S(1)}, f32[80,128]{1,0:T(8,128)S(1)}, u32[]{:S(2)}, u32[]{:S(2)}) collective-permute-start(f32[80,128]{1,0:T(8,128)S(1)} %get-tuple-element.26), channel_id=1, source_target_pairs={{8,0},{16,8},{24,16},{32,24},{40,32},{48,40},{56,48},{64,56},{72,6... | collective-permute-start | bytes 122888 | tf_op jit(solution)/shard_map/ppermute | solution.py:281
  78.3 27.6 %all-to-all-start.3 = ((bf16[16,40,896]{2,1,0:T(8,128)(2,1)}), bf16[16,40,896]{2,1,0:T(8,128)(2,1)S(1)}, u32[]{:S(2)}, u32[]{:S(2)}) async-start(bf16[16,40,896]{2,1,0:T(8,128)(2,1)} %bitcast.11), calls=%async_computation.3 | async-start | bytes 2293760 | tf_op jit(solution)/shard_map/all_to_all | solution.py:294
  88.6 9.4 %collective-permute-start.4 = (f32[2,80,128]{2,1,0:T(8,128)S(1)}, f32[2,80,128]{2,1,0:T(8,128)S(1)}, u32[]{:S(2)}, u32[]{:S(2)}) collective-permute-start(f32[2,80,128]{2,1,0:T(8,128)S(1)} %get-tuple-element.33), channel_id=1, source_target_pairs={{8,0},{16,8},{24,16},{32,24},{40,32},{48,40},{56,48},{64,56},{72,6... | collective-permute-start | bytes 245768 | tf_op jit(solution)/shard_map/ppermute | solution.py:293
  106.0 11.9 %all-to-all-start.2 = ((bf16[8,80,128]{2,1,0:T(8,128)(2,1)}), bf16[8,80,128]{2,1,0:T(8,128)(2,1)S(1)}, u32[]{:S(2)}, u32[]{:S(2)}) async-start(bf16[8,80,128]{2,1,0:T(8,128)(2,1)} %shard_map.72), calls=%async_computation.2 | async-start | bytes 327680 | tf_op jit(solution)/shard_map/all_to_all | solution.py:298
  111.9 11.4 %collective-permute-start.5 = (f32[20,896]{1,0:T(8,128)S(1)}, f32[20,896]{1,0:T(8,128)S(1)}, u32[]{:S(2)}, u32[]{:S(2)}) collective-permute-start(f32[20,896]{1,0:T(8,128)S(1)} %get-tuple-element.36), channel_id=1, source_target_pairs={{0,8},{8,0},{16,24},{24,16},{32,40},{40,32},{48,56},{56,48},{64,72... | collective-permute-start | bytes 215048 | tf_op jit(solution)/shard_map/ppermute | solution.py:301

commit v4 on v3

--- a/solution.py
+++ b/solution.py
@@ -10,7 +10,8 @@
 
 F32 = jnp.float32
 BF16 = jnp.bfloat16
-PARAMS = pltpu.CompilerParams(vmem_limit_bytes=48 * 1024 * 1024)
+USUAL = 48 * 1024 * 1024
+LARGE = 64 * 1024 * 1024 - 256 * 1024
 
 
 def nn(a, b):
@@ -56,7 +57,16 @@
     return (lane // 32) * 32 + 2 * (lane % 16) + (lane // 16) % 2
 
 
-def pack_kernel(image_ref, group_ref, cot_ref, send_ref):
+def pack_kernel(image_hbm, group_hbm, cot_hbm, send_ref, image_ref, group_ref, cot_ref, sems):
+    copies = [
+        pltpu.make_async_copy(group_hbm, group_ref, sems.at[0]),
+        pltpu.make_async_copy(image_hbm, image_ref, sems.at[1]),
+        pltpu.make_async_copy(cot_hbm, cot_ref, sems.at[2]),
+    ]
+    for copy in copies:
+        copy.start()
+    for copy in copies:
+        copy.wait()
     pick = jnp.where(cell_of_lane(iota((128, 128), 1)) == iota((128, 128), 0), 1.0, 0.0)
     pixels = tn(image_ref[...], pick.astype(BF16)).astype(BF16)
     taps = swap_blocks([group_ref[t].astype(F32) for t in range(8)])
@@ -71,8 +81,7 @@
 
 
 def spread_kernel(
-    recv_ref, above_ref, below_ref,
-    win_ref, down_ref, up_ref, own_ref, cot_ref, halo_ref, cell_ref, tap_ref,
+    recv_ref, raw_ref, win_ref, down_ref, up_ref, own_ref, cot_ref, cell_ref, tap_ref
 ):
     pixels = swap_blocks([recv_ref[q, 0:80, :].astype(F32) for q in range(8)])
     for r in range(4):
@@ -118,10 +127,10 @@
         here = slice(16 * g, 16 * g + 16)
         own_ref[here, 0:128] = sums[1][0] + sums[0][1]
         own_ref[here, 128:256] = sums[1][1] + sums[2][0]
-        up_ref[here, :] = sums[0][0]
+        up_ref[here, 0:128] = sums[0][0].astype(BF16)
+        up_ref[here, 128:256] = raw_ref[0:16, rows]
         down_ref[here, 256:384] = sums[2][1].astype(BF16)
-        halo_ref[here, 0:128] = above_ref[:, rows]
-        halo_ref[here, 128:256] = below_ref[:, rows]
+        down_ref[here, 384:512] = raw_ref[16:32, rows]
 
 
 def forward_kernel(part_ref, down_ref, up_ref, weight_ref, hid_ref, win_ref, pass_ref):
@@ -138,7 +147,7 @@
             hid_ref[p, 16 * g : 16 * g + 16, :] = hidden[128 * g + 16 * p : 128 * g + 16 * p + 16]
 
 
-def middle_kernel(hid_ref, own_ref, down_ref, up_ref, halo_ref, act_ref, share_ref):
+def middle_kernel(hid_ref, own_ref, down_ref, up_ref, act_ref, share_ref):
     hidden = hid_ref[0].astype(F32)
     for q in range(1, 8):
         hidden = hidden + hid_ref[q].astype(F32)
@@ -146,38 +155,19 @@
     density = jnp.exp(-0.5 * hidden * hidden) * (1.0 / math.sqrt(2.0 * math.pi))
     act_ref[...] = (hidden * cumul).astype(BF16)
     slopes = cumul + hidden * density
-    act_grad = own_ref[...] + jnp.concatenate([down_ref[:, 256:384].astype(F32), up_ref[...]], axis=1)
+    act_grad = own_ref[...] + jnp.concatenate(
+        [down_ref[:, 256:384].astype(F32), up_ref[:, 0:128].astype(F32)], axis=1
+    )
     share_ref[0:80, :] = (act_grad * slopes).astype(BF16)
-    share_ref[80:160, :] = halo_ref[...]
-
-
-def backward_kernel(
-    all_ref, weight_ref, win_ref, cot_ref, act_ref,
-    img_ref, up_ref, red_ref, pre_ref, shift_ref, cell_ref,
-):
+    share_ref[80:160, 0:128] = down_ref[:, 384:512]
+    share_ref[80:160, 128:256] = up_ref[:, 128:256]
+
+
+def weight_grad_kernel(all_ref, win_ref, cot_ref, act_ref, red_ref, pre_ref, shift_ref, cell_ref):
     for p in range(8):
         for g in range(5):
             pre_ref[128 * g + 16 * p : 128 * g + 16 * p + 16, :] = all_ref[p, 16 * g : 16 * g + 16, :]
     pre = pre_ref[...]
-    back = nn(weight_ref[...], pre)
-
-    def term(a, b, i):
-        t = 3 * a + b
-        return back[80 * t : 80 * t + 80, 128 * i : 128 * i + 128]
-
-    for i in range(2):
-        img_ref[4 * i] = term(1, 1, i)
-        img_ref[4 * i + 1] = term(1, 2, i) + from_right(term(1, 0, i))
-    upper_even = [term(0, 1, i) for i in range(2)]
-    upper_odd = [term(0, 2, i) + from_right(term(0, 0, i)) for i in range(2)]
-    lower_odd = [term(2, 2, i) + from_right(term(2, 0, i)) for i in range(2)]
-    img_ref[2] = term(2, 1, 0) + upper_even[1]
-    img_ref[3] = lower_odd[0] + upper_odd[1]
-    img_ref[6] = term(2, 1, 1)
-    img_ref[7] = lower_odd[1]
-    up_ref[0] = upper_even[0]
-    up_ref[1] = upper_odd[0]
-
     red_ref[:, 0:640] = nt(pre, win_ref[0:640, :]).astype(BF16)
     rows = [act_ref[:, 128 * i : 128 * i + 128].astype(F32) for i in range(2)]
     moved = [[move(x).astype(BF16) for x in rows] for move in (from_left, lambda x: x, from_right)]
@@ -205,6 +195,28 @@
         red_ref[here, 640:896] = (last[here] + nt(cot, shift_ref[g])).astype(BF16)
 
 
+def image_grad_kernel(pre_ref, weight_ref, img_ref, up_ref):
+    pre = pre_ref[...]
+    back = nn(weight_ref[...], pre)
+
+    def term(a, b, i):
+        t = 3 * a + b
+        return back[80 * t : 80 * t + 80, 128 * i : 128 * i + 128]
+
+    for i in range(2):
+        img_ref[4 * i] = term(1, 1, i)
+        img_ref[4 * i + 1] = term(1, 2, i) + from_right(term(1, 0, i))
+    upper_even = [term(0, 1, i) for i in range(2)]
+    upper_odd = [term(0, 2, i) + from_right(term(0, 0, i)) for i in range(2)]
+    lower_odd = [term(2, 2, i) + from_right(term(2, 0, i)) for i in range(2)]
+    img_ref[2] = term(2, 1, 0) + upper_even[1]
+    img_ref[3] = lower_odd[0] + upper_odd[1]
+    img_ref[6] = term(2, 1, 1)
+    img_ref[7] = lower_odd[1]
+    up_ref[0] = upper_even[0]
+    up_ref[1] = upper_odd[0]
+
+
 def return_kernel(img_ref, below_ref, send_ref):
     parts = [img_ref[k] for k in range(8)]
     parts[6] = parts[6] + below_ref[0]
@@ -220,7 +232,7 @@
     first, second = total[0:20], total[20:40]
     high = high_ref[0] == 1
     keep_ref[...] = jnp.where(high, second, first)
-    give_ref[...] = jnp.where(high, first, second)
+    give_ref[...] = jnp.where(high, first, second).astype(BF16)
 
 
 def unpack_kernel(recv_ref, out_ref):
@@ -231,22 +243,22 @@
 
 
 def finish_kernel(keep_ref, given_ref, conv_ref, group_ref):
-    total = keep_ref[...] + given_ref[...]
+    total = keep_ref[...] + given_ref[...].astype(F32)
     for t in range(9):
         conv_ref[t] = total[:, 80 * t : 80 * t + 80]
     group_ref[...] = jnp.transpose(total[:, 640:896])[80:224]
 
 
-def call(kernel, outs, *args, scratch=(), smem=0):
+def call(kernel, outs, *args, scratch=(), smem=0, space=pltpu.VMEM, limit=USUAL):
     whole = [pl.BlockSpec(memory_space=pltpu.SMEM)] * smem
-    whole += [pl.BlockSpec(memory_space=pltpu.VMEM)] * (len(args) - smem)
+    whole += [pl.BlockSpec(memory_space=space)] * (len(args) - smem)
     return pl.pallas_call(
         kernel,
         out_shape=[jax.ShapeDtypeStruct(shape, dtype) for shape, dtype in outs],
         in_specs=whole,
         out_specs=[pl.BlockSpec(memory_space=pltpu.VMEM)] * len(outs),
         scratch_shapes=list(scratch),
-        compiler_params=PARAMS,
+        compiler_params=pltpu.CompilerParams(vmem_limit_bytes=limit),
     )(*args)
 
 
@@ -258,37 +270,41 @@
     planes = [[2 * i + z for i in range(tiles // 2)] for z in range(2)]
 
     cells = cotangent.reshape(32, 640)
-    above = lax.ppermute(cotangent[1], "tile", downward)
-    below = lax.ppermute(cotangent[0], "tile", upward)
     weights = conv_weight.transpose(1, 0, 2).reshape(720, 640)
     (send,) = call(
         pack_kernel, [((8, 336, 128), BF16)],
         image.reshape(128, 640), group_weight.transpose(0, 2, 1), cells,
+        scratch=[pltpu.VMEM((128, 640), BF16), pltpu.VMEM((9, 80, 128), BF16), pltpu.VMEM((32, 640), BF16), pltpu.SemaphoreType.DMA((3,))],
+        space=pl.ANY,
+        limit=LARGE,
     )
     recv = lax.all_to_all(send, "fsdp", 0, 0, tiled=True)
-    windows, down, up, own, cot, halo = call(
+    windows, down, up, own, cot = call(
         spread_kernel,
-        [((720, 256), BF16), ((80, 384), BF16), ((80, 128), F32), ((80, 256), F32), ((640, 256), BF16), ((80, 256), BF16)],
-        recv, above, below,
+        [((720, 256), BF16), ((80, 512), BF16), ((80, 256), BF16), ((80, 256), F32), ((640, 256), BF16)],
+        recv, cells,
         scratch=[pltpu.VMEM((256, 640), BF16), pltpu.VMEM((640, 256), BF16)],
     )
     down = lax.ppermute(down, "tile", downward)
     hid, windows, up = call(
         forward_kernel,
-        [((8, 80, 256), BF16), ((720, 256), BF16), ((80, 128), F32)],
+        [((8, 80, 256), BF16), ((720, 256), BF16), ((80, 256), BF16)],
         windows, down, up, weights,
     )
     up = lax.ppermute(up, "tile", upward)
     hid = lax.all_to_all(hid, "fsdp", 0, 0, tiled=True)
     act, share = call(
-        middle_kernel, [((80, 256), BF16), ((160, 256), BF16)], hid, own, down, up, halo
+        middle_kernel, [((80, 256), BF16), ((160, 256), BF16)], hid, own, down, up
     )
     share_all = lax.all_gather(share, "fsdp", axis=0, tiled=False)
-    img, img_up, red = call(
-        backward_kernel,
-        [((8, 80, 128), F32), ((2, 80, 128), F32), ((640, 896), BF16)],
-        share_all, weights, windows, cot, act,
-        scratch=[pltpu.VMEM((640, 256), BF16), pltpu.VMEM((5, 256, 512), BF16), pltpu.VMEM((256, 640), BF16)],
+    red, pre = call(
+        weight_grad_kernel,
+        [((640, 896), BF16), ((640, 256), BF16)],
+        share_all, windows, cot, act,
+        scratch=[pltpu.VMEM((5, 256, 512), BF16), pltpu.VMEM((256, 640), BF16)],
+    )
+    img, img_up = call(
+        image_grad_kernel, [((8, 80, 128), F32), ((2, 80, 128), F32)], pre, weights
     )
     img_below = lax.ppermute(img_up, "tile", upward)
     red = lax.all_to_all(
@@ -297,7 +313,7 @@
     (back,) = call(return_kernel, [((8, 80, 128), BF16)], img, img_below)
     back = lax.all_to_all(back, "fsdp", 0, 0, tiled=True)
     high = (lax.axis_index("tile") % 2).astype(jnp.int32).reshape(1)
-    keep, give = call(fold_kernel, [((20, 896), F32), ((20, 896), F32)], high, red, smem=1)
+    keep, give = call(fold_kernel, [((20, 896), F32), ((20, 896), BF16)], high, red, smem=1)
     given = lax.ppermute(give, "tile", partners)
     (image_grad,) = call(unpack_kernel, [((128, 640), BF16)], back.reshape(640, 128))
     conv_weight_grad, group_weight_grad = call(

time: 125 us -> 120 us (0.960)
  blocking collectives: 15.8 us -> 41.3 us
  starting transfers between devices: 51.2 us -> 33.6 us
  waiting for transfers between devices: 44.7 us -> 33.3 us
  local copies, waits for them, and re-layouts: 2.62 us -> 0.01 us
  Pallas kernels: 9.12 us -> 10.4 us
    all_to_all x0 -> x1, blocking collectives: none -> 25.5 us  [per_device(): recv = lax.all_to_all(send, 'fsdp', 0, 0, tiled=True)]
    ppermute x2 -> x0, waiting for transfers between devices: 10.1 us -> none  [the longest x1 5.76 us: per_device(): below = lax.ppermute(cotangent[0], 'tile', upward)]
    ppermute x2 -> x0, starting transfers between devices: 7.65 us -> none  [the longest x1 6.36 us: per_device(): above = lax.ppermute(cotangent[1], 'tile', downward)]
    all_to_all x1 -> x0, starting transfers between devices: 7.53 us -> none  [per_device(): recv = lax.all_to_all(send, 'fsdp', 0, 0, tiled=True)]
    unnamed x10 -> x4, local copies, waits for them, and re-layouts: 2.62 us -> 0.01 us
    all_to_all x1 -> x0, waiting for transfers between devices: 1.5 us -> none  [per_device(): recv = lax.all_to_all(send, 'fsdp', 0, 0, tiled=True)]
    ppermute x1, waiting for transfers between devices: 1.27 us -> 2.76 us  [per_device(): down = lax.ppermute(down, 'tile', downward)]
    all_to_all x1, starting transfers between devices: 10.2 us -> 8.98 us  [per_device(): lax.all_to_all(red.reshape(16, 40, 896), 'tile', 0, 0, tiled=True, axis_i...]
  transfers between devices with their start and end apart: 10 -> 7, of which waited for: 8 -> 6; matrix products, arithmetic and copies ran while one was open for 0% -> 0% of each run, Pallas kernels for 2% -> 2%
where the time goes in v4:
time: 120 us; the launch traced here: 119 us
  blocking collectives  41.3 us (34%)
  starting transfers between devices  33.6 us (28%)
  waiting for transfers between devices  33.3 us (28%)
  Pallas kernels  10.4 us (9%)
    all_to_all x1, blocking collectives, per_device(): recv = lax.all_to_all(send, 'fsdp', 0, 0, tiled=True)  25.5 us
    all_gather x1, blocking collectives, per_device(): share_all = lax.all_gather(share, 'fsdp', axis=0, tiled=False)  15.8 us
    ppermute x1, waiting for transfers between devices, per_device(): up = lax.ppermute(up, 'tile', upward)  12.2 us
    pallas_call x10, Pallas kernels, call(): pl.pallas_call(kernel, out_shape=[jax.ShapeDtypeStruct(shape, dtype) for...  10.4 us
    all_to_all x1, starting transfers between devices, per_device(): lax.all_to_all(red.reshape(16, 40, 896), 'tile', 0, 0, tiled=True, axis_i...  8.98 us
    ppermute x1, waiting for transfers between devices, per_device(): img_below = lax.ppermute(img_up, 'tile', upward)  8.09 us
    all_to_all x1, waiting for transfers between devices, per_device(): lax.all_to_all(red.reshape(16, 40, 896), 'tile', 0, 0, tiled=True, axis_i...  6.55 us
    ppermute x1, starting transfers between devices, per_device(): down = lax.ppermute(down, 'tile', downward)  6.36 us
  transfers between devices with their start and end apart: 7, of which 6 were waited for; matrix products, arithmetic and copies ran while one was open for 0% of the time, Pallas kernels for 2%

profile of v4, /device:TPU:1, one launch (start us, length us, event | category | flops | bytes accessed | tf_op | source)
XLA Modules:
  0.0 119.2 jit_solution(12091063403877990475)
XLA Ops:
  0.6 0.0 copy-start.1
  0.6 2.4 %shard_map.67 = bf16[8,336,128]{2,1,0:T(8,128)(2,1)} custom-call(bf16[128,640]{1,0:T(8,128)(2,1)} %bitcast.21, bf16[9,80,128]{2,1,0:T(8,128)(2,1)} %bitcast.19, bf16[32,640]{1,0:T(8,128)(2,1)} %bitcast.17), custom_call_target="tpu_custom_call" | custom-call | tf_op jit(solution)/shard_map/pallas_call | solution.py:255
  3.0 0.0 copy-start
  3.0 25.5 %all_to_all.20.recv_ref = bf16[8,336,128]{2,1,0:T(8,128)(2,1)S(1)} all-to-all(bf16[8,336,128]{2,1,0:T(8,128)(2,1)} %shard_map.67), channel_id=1, replica_groups=mesh['tile'=32,'fsdp'=8] {'fsdp'}, dimensions={0} | all-to-all | bytes 1376256 | tf_op jit(solution)/shard_map/all_to_all | solution.py:281
  28.5 0.0 copy-done.1
  28.5 0.8 shard_map.68
  29.3 6.4 %collective-permute-start = (bf16[80,512]{1,0:T(8,128)(2,1)S(1)}, bf16[80,512]{1,0:T(8,128)(2,1)S(1)}, u32[]{:S(2)}, u32[]{:S(2)}) collective-permute-start(bf16[80,512]{1,0:T(8,128)(2,1)S(1)} %get-tuple-element.22), channel_id=1, source_target_pairs={{0,8},{8,16},{16,24},{24,32},{32,40},{40,48},{48,56},{56,64},{64,7... | collective-permute-start | bytes 245768 | tf_op jit(solution)/shard_map/ppermute | solution.py:288
  35.7 2.8 %collective-permute-done.down_ref = bf16[80,512]{1,0:T(8,128)(2,1)S(1)} collective-permute-done((bf16[80,512]{1,0:T(8,128)(2,1)S(1)}, bf16[80,512]{1,0:T(8,128)(2,1)S(1)}, u32[]{:S(2)}, u32[]{:S(2)}) %collective-permute-start) | collective-permute-done | bytes 81952 | tf_op jit(solution)/shard_map/ppermute | solution.py:288
  38.5 0.0 copy-done
  38.5 1.2 %shard_map.69 = (bf16[8,80,256]{2,1,0:T(8,128)(2,1)}, bf16[720,256]{1,0:T(8,128)(2,1)S(1)}, bf16[80,256]{1,0:T(8,128)(2,1)S(1)}) custom-call(bf16[720,256]{1,0:T(8,128)(2,1)S(1)} %get-tuple-element.21.part_ref, bf16[80,512]{1,0:T(8,128)(2,1)S(1)} %collective-permute-done.down_ref, bf16[80,256]{1,0:T(8,128)(2,1)S(1)} %get-tuple-element.23.up_ref, ...), custom_call_target="tpu_custom_call" | custom-call | tf_op jit(solution)/shard_map/pallas_call | solution.py:255
  39.7 4.2 %all-to-all-start.1 = ((bf16[8,80,256]{2,1,0:T(8,128)(2,1)}), bf16[8,80,256]{2,1,0:T(8,128)(2,1)S(1)}, u32[]{:S(2)}, u32[]{:S(2)}) async-start(bf16[8,80,256]{2,1,0:T(8,128)(2,1)} %get-tuple-element.24), calls=%async_computation.1 | async-start | bytes 655360 | tf_op jit(solution)/shard_map/all_to_all | solution.py:295
  43.9 1.3 %collective-permute-start.1 = (bf16[80,256]{1,0:T(8,128)(2,1)S(1)}, bf16[80,256]{1,0:T(8,128)(2,1)S(1)}, u32[]{:S(2)}, u32[]{:S(2)}) collective-permute-start(bf16[80,256]{1,0:T(8,128)(2,1)S(1)} %get-tuple-element.26), channel_id=1, source_target_pairs={{8,0},{16,8},{24,16},{32,24},{40,32},{48,40},{56,48},{64,56},{72,6... | collective-permute-start | bytes 122888 | tf_op jit(solution)/shard_map/ppermute | solution.py:294
  45.2 12.2 %collective-permute-done.1.up_ref = bf16[80,256]{1,0:T(8,128)(2,1)S(1)} collective-permute-done((bf16[80,256]{1,0:T(8,128)(2,1)S(1)}, bf16[80,256]{1,0:T(8,128)(2,1)S(1)}, u32[]{:S(2)}, u32[]{:S(2)}) %collective-permute-start.1) | collective-permute-done | bytes 40992 | tf_op jit(solution)/shard_map/ppermute | solution.py:294
  57.4 0.0 all-to-all-done.1.hid_ref
  57.4 0.1 shard_map.70
  57.5 15.8 %all-gather = bf16[1280,256]{1,0:T(8,128)(2,1)S(1)} all-gather(bf16[160,256]{1,0:T(8,128)(2,1)S(1)} %get-tuple-element.27), channel_id=2, replica_groups=mesh['tile'=32,'fsdp'=8] {'fsdp'}, dimensions={0}, use_global_device_ids=true | all-gather | bytes 737280 | tf_op jit(solution)/shard_map/all_gather | solution.py:299
  73.3 2.6 %shard_map.71 = (bf16[640,896]{1,0:T(8,128)(2,1)}, bf16[640,256]{1,0:T(8,128)(2,1)S(1)}) custom-call(bf16[8,160,256]{2,1,0:T(8,128)(2,1)S(1)} %bitcast.15, bf16[720,256]{1,0:T(8,128)(2,1)S(1)} %get-tuple-element.28.win_ref, bf16[640,256]{1,0:T(8,128)(2,1)S(1)} %get-tuple-element.29.cot_ref, bf16[80,256]{1,0:T(8,128)(2,1)S(1)} %get-tuple-element.30.act_ref), custom_call_target="tpu_custom_call" | custom-call | tf_op jit(solution)/shard_map/pallas_call | solution.py:255
  75.9 9.0 %all-to-all-start.3 = ((bf16[16,40,896]{2,1,0:T(8,128)(2,1)}), bf16[16,40,896]{2,1,0:T(8,128)(2,1)S(1)}, u32[]{:S(2)}, u32[]{:S(2)}) async-start(bf16[16,40,896]{2,1,0:T(8,128)(2,1)} %bitcast.9), calls=%async_computation.3 | async-start | bytes 2293760 | tf_op jit(solution)/shard_map/all_to_all | solution.py:310
  84.9 0.5 shard_map.72
  85.3 1.3 %collective-permute-start.2 = (f32[2,80,128]{2,1,0:T(8,128)S(1)}, f32[2,80,128]{2,1,0:T(8,128)S(1)}, u32[]{:S(2)}, u32[]{:S(2)}) collective-permute-start(f32[2,80,128]{2,1,0:T(8,128)S(1)} %get-tuple-element.33), channel_id=1, source_target_pairs={{8,0},{16,8},{24,16},{32,24},{40,32},{48,40},{56,48},{64,56},{72,6... | collective-permute-start | bytes 245768 | tf_op jit(solution)/shard_map/ppermute | solution.py:309
  86.6 8.1 %collective-permute-done.2.below_ref = f32[2,80,128]{2,1,0:T(8,128)S(1)} collective-permute-done((f32[2,80,128]{2,1,0:T(8,128)S(1)}, f32[2,80,128]{2,1,0:T(8,128)S(1)}, u32[]{:S(2)}, u32[]{:S(2)}) %collective-permute-start.2) | collective-permute-done | bytes 81952 | tf_op jit(solution)/shard_map/ppermute | solution.py:309
  94.7 0.9 shard_map.73
  95.7 6.5 %all-to-all-done.3.red_ref = bf16[16,40,896]{2,1,0:T(8,128)(2,1)S(1)} async-done(((bf16[16,40,896]{2,1,0:T(8,128)(2,1)}), bf16[16,40,896]{2,1,0:T(8,128)(2,1)S(1)}, u32[]{:S(2)}, u32[]{:S(2)}) %all-to-all-start.3) | async-done | bytes 1146912 | tf_op jit(solution)/shard_map/all_to_all | solution.py:310
  102.2 5.8 %all-to-all-start.2 = ((bf16[8,80,128]{2,1,0:T(8,128)(2,1)}), bf16[8,80,128]{2,1,0:T(8,128)(2,1)S(1)}, u32[]{:S(2)}, u32[]{:S(2)}) async-start(bf16[8,80,128]{2,1,0:T(8,128)(2,1)} %shard_map.73), calls=%async_computation.2 | async-start | bytes 327680 | tf_op jit(solution)/shard_map/all_to_all | solution.py:314
  108.0 0.2 shard_map.75
  108.2 5.7 %collective-permute-start.3 = (bf16[20,896]{1,0:T(8,128)(2,1)S(1)}, bf16[20,896]{1,0:T(8,128)(2,1)S(1)}, u32[]{:S(2)}, u32[]{:S(2)}) collective-permute-start(bf16[20,896]{1,0:T(8,128)(2,1)S(1)} %get-tuple-element.36), channel_id=1, source_target_pairs={{0,8},{8,0},{16,24},{24,16},{32,40},{40,32},{48,56},{56,48},{64,72... | collective-permute-start | bytes 107528 | tf_op jit(solution)/shard_map/ppermute | solution.py:317
  113.9 0.2 all-to-all-done.2
  114.0 0.9 shard_map.74
  114.9 3.5 %collective-permute-done.3.given_ref = bf16[20,896]{1,0:T(8,128)(2,1)S(1)} collective-permute-done((bf16[20,896]{1,0:T(8,128)(2,1)S(1)}, bf16[20,896]{1,0:T(8,128)(2,1)S(1)}, u32[]{:S(2)}, u32[]{:S(2)}) %collective-permute-start.3) | collective-permute-done | bytes 35872 | tf_op jit(solution)/shard_map/ppermute | solution.py:317
  118.4 0.8 shard_map.76
Async XLA Ops:
  0.6 27.9 %copy-start.1 = (bf16[2,16,640]{2,1,0:T(8,128)(2,1)S(1)}, bf16[2,16,640]{2,1,0:T(8,128)(2,1)}, u32[]{:S(2)}) copy-start(bf16[2,16,640]{2,1,0:T(8,128)(2,1)} %param.7) | copy-start | bytes 122884
  3.0 35.5 %copy-start = (bf16[80,9,640]{2,0,1:T(8,128)(2,1)S(1)}, bf16[80,9,640]{2,0,1:T(8,128)(2,1)}, u32[]{:S(2)}) copy-start(bf16[80,9,640]{2,0,1:T(8,128)(2,1)} %param.5) | copy-start | bytes 2764804
  29.3 9.1 %collective-permute-start = (bf16[80,512]{1,0:T(8,128)(2,1)S(1)}, bf16[80,512]{1,0:T(8,128)(2,1)S(1)}, u32[]{:S(2)}, u32[]{:S(2)}) collective-permute-start(bf16[80,512]{1,0:T(8,128)(2,1)S(1)} %get-tuple-element.22), channel_id=1, source_target_pairs={{0,8},{8,16},{16,24},{24,32},{32,40},{40,48},{48,56},{56,64},{64,7... | collective-permute-start | bytes 245768 | tf_op jit(solution)/shard_map/ppermute | solution.py:288
  39.7 17.7 %all-to-all-start.1 = ((bf16[8,80,256]{2,1,0:T(8,128)(2,1)}), bf16[8,80,256]{2,1,0:T(8,128)(2,1)S(1)}, u32[]{:S(2)}, u32[]{:S(2)}) async-start(bf16[8,80,256]{2,1,0:T(8,128)(2,1)} %get-tuple-element.24), calls=%async_computation.1 | async-start | bytes 655360 | tf_op jit(solution)/shard_map/all_to_all | solution.py:295
  43.9 13.5 %collective-permute-start.1 = (bf16[80,256]{1,0:T(8,128)(2,1)S(1)}, bf16[80,256]{1,0:T(8,128)(2,1)S(1)}, u32[]{:S(2)}, u32[]{:S(2)}) collective-permute-start(bf16[80,256]{1,0:T(8,128)(2,1)S(1)} %get-tuple-element.26), channel_id=1, source_target_pairs={{8,0},{16,8},{24,16},{32,24},{40,32},{48,40},{56,48},{64,56},{72,6... | collective-permute-start | bytes 122888 | tf_op jit(solution)/shard_map/ppermute | solution.py:294
  75.9 26.4 %all-to-all-start.3 = ((bf16[16,40,896]{2,1,0:T(8,128)(2,1)}), bf16[16,40,896]{2,1,0:T(8,128)(2,1)S(1)}, u32[]{:S(2)}, u32[]{:S(2)}) async-start(bf16[16,40,896]{2,1,0:T(8,128)(2,1)} %bitcast.9), calls=%async_computation.3 | async-start | bytes 2293760 | tf_op jit(solution)/shard_map/all_to_all | solution.py:310
  85.3 9.4 %collective-permute-start.2 = (f32[2,80,128]{2,1,0:T(8,128)S(1)}, f32[2,80,128]{2,1,0:T(8,128)S(1)}, u32[]{:S(2)}, u32[]{:S(2)}) collective-permute-start(f32[2,80,128]{2,1,0:T(8,128)S(1)} %get-tuple-element.33), channel_id=1, source_target_pairs={{8,0},{16,8},{24,16},{32,24},{40,32},{48,40},{56,48},{64,56},{72,6... | collective-permute-start | bytes 245768 | tf_op jit(solution)/shard_map/ppermute | solution.py:309
  102.2 11.8 %all-to-all-start.2 = ((bf16[8,80,128]{2,1,0:T(8,128)(2,1)}), bf16[8,80,128]{2,1,0:T(8,128)(2,1)S(1)}, u32[]{:S(2)}, u32[]{:S(2)}) async-start(bf16[8,80,128]{2,1,0:T(8,128)(2,1)} %shard_map.73), calls=%async_computation.2 | async-start | bytes 327680 | tf_op jit(solution)/shard_map/all_to_all | solution.py:314
  108.2 10.2 %collective-permute-start.3 = (bf16[20,896]{1,0:T(8,128)(2,1)S(1)}, bf16[20,896]{1,0:T(8,128)(2,1)S(1)}, u32[]{:S(2)}, u32[]{:S(2)}) collective-permute-start(bf16[20,896]{1,0:T(8,128)(2,1)S(1)} %get-tuple-element.36), channel_id=1, source_target_pairs={{0,8},{8,0},{16,24},{24,16},{32,40},{40,32},{48,56},{56,48},{64,72... | collective-permute-start | bytes 107528 | tf_op jit(solution)/shard_map/ppermute | solution.py:317

commit v5 on v4

--- a/solution.py
+++ b/solution.py
@@ -10,8 +10,7 @@
 
 F32 = jnp.float32
 BF16 = jnp.bfloat16
-USUAL = 48 * 1024 * 1024
-LARGE = 64 * 1024 * 1024 - 256 * 1024
+FORWARD_FLOPS = 12_000_000_000
 
 
 def nn(a, b):
@@ -57,33 +56,28 @@
     return (lane // 32) * 32 + 2 * (lane % 16) + (lane // 16) % 2
 
 
-def pack_kernel(image_hbm, group_hbm, cot_hbm, send_ref, image_ref, group_ref, cot_ref, sems):
-    copies = [
-        pltpu.make_async_copy(group_hbm, group_ref, sems.at[0]),
-        pltpu.make_async_copy(image_hbm, image_ref, sems.at[1]),
-        pltpu.make_async_copy(cot_hbm, cot_ref, sems.at[2]),
-    ]
-    for copy in copies:
-        copy.start()
-    for copy in copies:
-        copy.wait()
+def pack_kernel(slot_ref, image_ref, group_ref, cot_ref, *refs):
+    *send_refs, block_ref = refs
     pick = jnp.where(cell_of_lane(iota((128, 128), 1)) == iota((128, 128), 0), 1.0, 0.0)
     pixels = tn(image_ref[...], pick.astype(BF16)).astype(BF16)
     taps = swap_blocks([group_ref[t].astype(F32) for t in range(8)])
     last = [group_ref[8, 16 * b : 16 * b + 16, :].astype(F32) for b in range(5)]
     last = swap_blocks(last + [jnp.zeros((16, 128), F32)] * 3)
     for p in range(8):
-        send_ref[p, 0:80, :] = pixels[80 * p : 80 * p + 80]
-        send_ref[p, 80:160, :] = taps[p].astype(BF16)
-        send_ref[p, 160:176, :] = last[p].astype(BF16)
-        for k in range(5):
-            send_ref[p, 176 + 32 * k : 208 + 32 * k, :] = cot_ref[:, 128 * k : 128 * k + 128]
-
-
-def spread_kernel(
-    recv_ref, raw_ref, win_ref, down_ref, up_ref, own_ref, cot_ref, cell_ref, tap_ref
-):
-    pixels = swap_blocks([recv_ref[q, 0:80, :].astype(F32) for q in range(8)])
+        block_ref[p, 0:80, :] = pixels[80 * p : 80 * p + 80]
+        block_ref[p, 80:160, :] = taps[p].astype(BF16)
+        block_ref[p, 160:176, :] = last[p].astype(BF16)
+    for k in range(8):
+        send_refs[k][0:176, :] = block_ref[slot_ref[0] ^ k]
+        for j in range(5):
+            send_refs[k][176 + 32 * j : 208 + 32 * j, :] = cot_ref[:, 128 * j : 128 * j + 128]
+
+
+def spread_kernel(slot_ref, raw_ref, *refs):
+    *recv_refs, win_ref, down_ref, up_ref, own_ref, cot_ref, cell_ref, tap_ref, block_ref = refs
+    for k in range(8):
+        block_ref[slot_ref[0] ^ k] = recv_refs[k][...]
+    pixels = swap_blocks([block_ref[q, 0:80, :].astype(F32) for q in range(8)])
     for r in range(4):
         columns = (from_left(pixels[2 * r + 1]), pixels[2 * r], pixels[2 * r + 1])
         for b in range(3):
@@ -97,15 +91,15 @@
     down_ref[:, 0:128] = pixels[6].astype(BF16)
     down_ref[:, 128:256] = pixels[7].astype(BF16)
     for q in range(8):
-        tap_ref[80 * q : 80 * q + 80, 0:128] = recv_ref[q, 80:160, :]
-        last = recv_ref[q, 160:176, :].astype(F32)
+        tap_ref[80 * q : 80 * q + 80, 0:128] = block_ref[q, 80:160, :]
+        last = block_ref[q, 160:176, :].astype(F32)
         for b in range(5):
             moved = last if b == 0 else pltpu.roll(last, 128 - 16 * b, 1)
             tap_ref[80 * q + 16 * b : 80 * q + 16 * b + 16, 128:256] = moved.astype(BF16)
         for k in range(5):
             for i in range(2):
                 start = 176 + 32 * k + 16 * i
-                cell_ref[128 * i + 16 * q : 128 * i + 16 * q + 16, 128 * k : 128 * k + 128] = recv_ref[q, start : start + 16, :]
+                cell_ref[128 * i + 16 * q : 128 * i + 16 * q + 16, 128 * k : 128 * k + 128] = block_ref[q, start : start + 16, :]
     eye = jnp.where(iota((128, 128), 0) == iota((128, 128), 1), 1.0, 0.0).astype(BF16)
     for g in range(5):
         rows = slice(128 * g, 128 * g + 128)
@@ -133,24 +127,26 @@
         down_ref[here, 384:512] = raw_ref[16:32, rows]
 
 
-def forward_kernel(part_ref, down_ref, up_ref, weight_ref, hid_ref, win_ref, pass_ref):
-    even = down_ref[:, 0:128]
+def forward_kernel(slot_ref, part_ref, down_ref, weight_ref, *refs):
+    *hid_refs, win_ref, block_ref = refs
     odd = down_ref[:, 128:256]
     win_ref[...] = part_ref[...]
     win_ref[0:80, 0:128] = from_left(odd.astype(F32)).astype(BF16)
-    win_ref[80:160, 0:128] = even
+    win_ref[80:160, 0:128] = down_ref[:, 0:128]
     win_ref[160:240, 0:128] = odd
-    pass_ref[...] = up_ref[...]
     hidden = tn(weight_ref[...], win_ref[...]).astype(BF16)
     for p in range(8):
         for g in range(5):
-            hid_ref[p, 16 * g : 16 * g + 16, :] = hidden[128 * g + 16 * p : 128 * g + 16 * p + 16]
-
-
-def middle_kernel(hid_ref, own_ref, down_ref, up_ref, act_ref, share_ref):
-    hidden = hid_ref[0].astype(F32)
-    for q in range(1, 8):
-        hidden = hidden + hid_ref[q].astype(F32)
+            block_ref[p, 16 * g : 16 * g + 16, :] = hidden[128 * g + 16 * p : 128 * g + 16 * p + 16]
+    for k in range(8):
+        hid_refs[k][...] = block_ref[slot_ref[0] ^ k]
+
+
+def middle_kernel(own_ref, down_ref, up_ref, *refs):
+    *hid_refs, act_ref, share_ref = refs
+    hidden = hid_refs[0][...].astype(F32)
+    for k in range(1, 8):
+        hidden = hidden + hid_refs[k][...].astype(F32)
     cumul = 0.5 * (1.0 + lax.erf(hidden * (1.0 / math.sqrt(2.0))))
     density = jnp.exp(-0.5 * hidden * hidden) * (1.0 / math.sqrt(2.0 * math.pi))
     act_ref[...] = (hidden * cumul).astype(BF16)
@@ -217,12 +213,15 @@
     up_ref[1] = upper_odd[0]
 
 
-def return_kernel(img_ref, below_ref, send_ref):
+def return_kernel(slot_ref, img_ref, below_ref, *refs):
+    *send_refs, slot_blocks = refs
     parts = [img_ref[k] for k in range(8)]
     parts[6] = parts[6] + below_ref[0]
     parts[7] = parts[7] + below_ref[1]
     for q, x in enumerate(swap_blocks(parts)):
-        send_ref[q] = x.astype(BF16)
+        slot_blocks[slot_ref[0] ^ q] = x.astype(BF16)
+    for k in range(8):
+        send_refs[k][...] = slot_blocks[k]
 
 
 def fold_kernel(high_ref, red_ref, keep_ref, give_ref):
@@ -235,11 +234,15 @@
     give_ref[...] = jnp.where(high, first, second).astype(BF16)
 
 
-def unpack_kernel(recv_ref, out_ref):
+def unpack_kernel(slot_ref, *refs):
+    *recv_refs, out_ref, block_ref = refs
+    for k in range(8):
+        block_ref[slot_ref[0] ^ k] = recv_refs[k][...]
     lane = iota((128, 128), 1)
     pick = jnp.where(cell_of_lane(lane) == iota((128, 128), 0), 1.0, 0.0).astype(BF16)
+    blocks = block_ref[...].reshape(640, 128)
     for p in range(5):
-        out_ref[:, 128 * p : 128 * p + 128] = nt(pick, recv_ref[128 * p : 128 * p + 128, :]).astype(BF16)
+        out_ref[:, 128 * p : 128 * p + 128] = nt(pick, blocks[128 * p : 128 * p + 128]).astype(BF16)
 
 
 def finish_kernel(keep_ref, given_ref, conv_ref, group_ref):
@@ -249,17 +252,25 @@
     group_ref[...] = jnp.transpose(total[:, 640:896])[80:224]
 
 
-def call(kernel, outs, *args, scratch=(), smem=0, space=pltpu.VMEM, limit=USUAL):
+def call(kernel, outs, *args, scratch=(), smem=0, flops=0):
     whole = [pl.BlockSpec(memory_space=pltpu.SMEM)] * smem
-    whole += [pl.BlockSpec(memory_space=space)] * (len(args) - smem)
+    whole += [pl.BlockSpec(memory_space=pltpu.VMEM)] * (len(args) - smem)
     return pl.pallas_call(
         kernel,
         out_shape=[jax.ShapeDtypeStruct(shape, dtype) for shape, dtype in outs],
         in_specs=whole,
         out_specs=[pl.BlockSpec(memory_space=pltpu.VMEM)] * len(outs),
         scratch_shapes=list(scratch),
-        compiler_params=pltpu.CompilerParams(vmem_limit_bytes=limit),
+        compiler_params=pltpu.CompilerParams(vmem_limit_bytes=48 * 1024 * 1024),
+        cost_estimate=pl.CostEstimate(flops=flops, bytes_accessed=0, transcendentals=0) if flops else None,
     )(*args)
+
+
+def trade(blocks):
+    devices = range(8)
+    return [blocks[0]] + [
+        lax.ppermute(blocks[k], "fsdp", [(i, i ^ k) for i in devices]) for k in devices[1:]
+    ]
 
 
 def per_device(image, conv_weight, group_weight, cotangent):
@@ -270,31 +281,32 @@
     planes = [[2 * i + z for i in range(tiles // 2)] for z in range(2)]
 
     cells = cotangent.reshape(32, 640)
+    slot = lax.axis_index("fsdp").astype(jnp.int32).reshape(1)
     weights = conv_weight.transpose(1, 0, 2).reshape(720, 640)
-    (send,) = call(
-        pack_kernel, [((8, 336, 128), BF16)],
-        image.reshape(128, 640), group_weight.transpose(0, 2, 1), cells,
-        scratch=[pltpu.VMEM((128, 640), BF16), pltpu.VMEM((9, 80, 128), BF16), pltpu.VMEM((32, 640), BF16), pltpu.SemaphoreType.DMA((3,))],
-        space=pl.ANY,
-        limit=LARGE,
-    )
-    recv = lax.all_to_all(send, "fsdp", 0, 0, tiled=True)
+    parts = trade(
+        call(
+            pack_kernel, [((336, 128), BF16)] * 8,
+            slot, image.reshape(128, 640), group_weight.transpose(0, 2, 1), cells,
+            scratch=[pltpu.VMEM((8, 176, 128), BF16)], smem=1,
+        )
+    )
     windows, down, up, own, cot = call(
         spread_kernel,
         [((720, 256), BF16), ((80, 512), BF16), ((80, 256), BF16), ((80, 256), F32), ((640, 256), BF16)],
-        recv, cells,
-        scratch=[pltpu.VMEM((256, 640), BF16), pltpu.VMEM((640, 256), BF16)],
+        slot, cells, *parts,
+        scratch=[pltpu.VMEM((256, 640), BF16), pltpu.VMEM((640, 256), BF16), pltpu.VMEM((8, 336, 128), BF16)],
+        smem=1,
     )
     down = lax.ppermute(down, "tile", downward)
-    hid, windows, up = call(
-        forward_kernel,
-        [((8, 80, 256), BF16), ((720, 256), BF16), ((80, 256), BF16)],
-        windows, down, up, weights,
-    )
+    *hid, windows = call(
+        forward_kernel, [((80, 256), BF16)] * 8 + [((720, 256), BF16)],
+        slot, windows, down, weights,
+        scratch=[pltpu.VMEM((8, 80, 256), BF16)], smem=1, flops=FORWARD_FLOPS,
+    )
+    hid = trade(hid)
     up = lax.ppermute(up, "tile", upward)
-    hid = lax.all_to_all(hid, "fsdp", 0, 0, tiled=True)
     act, share = call(
-        middle_kernel, [((80, 256), BF16), ((160, 256), BF16)], hid, own, down, up
+        middle_kernel, [((80, 256), BF16), ((160, 256), BF16)], own, down, up, *hid
     )
     share_all = lax.all_gather(share, "fsdp", axis=0, tiled=False)
     red, pre = call(
@@ -310,12 +322,19 @@
     red = lax.all_to_all(
         red.reshape(16, 40, 896), "tile", 0, 0, tiled=True, axis_index_groups=planes
     )
-    (back,) = call(return_kernel, [((8, 80, 128), BF16)], img, img_below)
-    back = lax.all_to_all(back, "fsdp", 0, 0, tiled=True)
+    back = trade(
+        call(
+            return_kernel, [((80, 128), BF16)] * 8, slot, img, img_below,
+            scratch=[pltpu.VMEM((8, 80, 128), BF16)], smem=1,
+        )
+    )
     high = (lax.axis_index("tile") % 2).astype(jnp.int32).reshape(1)
     keep, give = call(fold_kernel, [((20, 896), F32), ((20, 896), BF16)], high, red, smem=1)
     given = lax.ppermute(give, "tile", partners)
-    (image_grad,) = call(unpack_kernel, [((128, 640), BF16)], back.reshape(640, 128))
+    (image_grad,) = call(
+        unpack_kernel, [((128, 640), BF16)], slot, *back,
+        scratch=[pltpu.VMEM((8, 80, 128), BF16)], smem=1,
+    )
     conv_weight_grad, group_weight_grad = call(
         finish_kernel, [((9, 20, 80), F32), ((144, 20), F32)], keep, given
     )

time: 120 us -> 114 us (0.950)
  blocking collectives: 41.3 us -> 15.1 us
  starting transfers between devices: 33.6 us -> 54.8 us
  local copies, waits for them, and re-layouts: 0.01 us -> 3.47 us
  Pallas kernels: 10.4 us -> 7.2 us
  waiting for transfers between devices: 33.3 us -> 31.9 us
    ppermute x0 -> x21, starting transfers between devices: none -> 34.2 us  [trade(): lax.ppermute(blocks[k], 'fsdp', [(i, i ^ k) for i in devices])]
    all_to_all x1 -> x0, blocking collectives: 25.5 us -> none  [per_device(): recv = lax.all_to_all(send, 'fsdp', 0, 0, tiled=True)]
    ppermute x0 -> x21, waiting for transfers between devices: none -> 17.5 us  [trade(): lax.ppermute(blocks[k], 'fsdp', [(i, i ^ k) for i in devices])]
    ppermute x1, waiting for transfers between devices: 12.2 us -> 1.82 us  [per_device(): up = lax.ppermute(up, 'tile', upward)]
    all_to_all x2 -> x0, starting transfers between devices: 9.99 us -> none  [the longest x1 5.79 us: per_device(): back = lax.all_to_all(back, 'fsdp', 0, 0, tiled=True)]
    ppermute x1, waiting for transfers between devices: 3.48 us -> 0.01 us  [per_device(): given = lax.ppermute(give, 'tile', partners)]
    unnamed x4 -> x10, local copies, waits for them, and re-layouts: 0.01 us -> 3.47 us
    pallas_call x10, Pallas kernels: 10.4 us -> 7.2 us  [call(): pl.pallas_call(kernel, out_shape=[jax.ShapeDtypeStruct(shape, dtype) for...]
  transfers between devices with their start and end apart: 7 -> 26, of which waited for: 6 -> 11; matrix products, arithmetic and copies ran while one was open for 0% -> 0% of each run, Pallas kernels for 2% -> 2%
where the time goes in v5:
time: 114 us; the launch traced here: 113 us
  starting transfers between devices  54.8 us (48%)
  waiting for transfers between devices  31.9 us (28%)
  blocking collectives  15.1 us (13%)
  Pallas kernels  7.2 us (6%)
  local copies, waits for them, and re-layouts  3.47 us (3%)
    ppermute x21, starting transfers between devices, trade(): lax.ppermute(blocks[k], 'fsdp', [(i, i ^ k) for i in devices])  34.2 us
    ppermute x21, waiting for transfers between devices, trade(): lax.ppermute(blocks[k], 'fsdp', [(i, i ^ k) for i in devices])  17.5 us
    all_gather x1, blocking collectives, per_device(): share_all = lax.all_gather(share, 'fsdp', axis=0, tiled=False)  15.1 us
    ppermute x1, waiting for transfers between devices, per_device(): img_below = lax.ppermute(img_up, 'tile', upward)  7.91 us
    ppermute x1, starting transfers between devices, per_device(): down = lax.ppermute(down, 'tile', downward)  7.3 us
    pallas_call x10, Pallas kernels, call(): pl.pallas_call(kernel, out_shape=[jax.ShapeDtypeStruct(shape, dtype) for...  7.2 us
    all_to_all x1, starting transfers between devices, per_device(): lax.all_to_all(red.reshape(16, 40, 896), 'tile', 0, 0, tiled=True, axis_i...  6.71 us
    all_to_all x1, waiting for transfers between devices, per_device(): lax.all_to_all(red.reshape(16, 40, 896), 'tile', 0, 0, tiled=True, axis_i...  3.96 us
  transfers between devices with their start and end apart: 26, of which 11 were waited for; matrix products, arithmetic and copies ran while one was open for 0% of the time, Pallas kernels for 2%

profile of v5, /device:TPU:1, one launch (start us, length us, event | category | flops | bytes accessed | tf_op | source)
XLA Modules:
  0.0 113.2 jit_solution(17642495037962956601)
XLA Ops:
  0.7 1.0 copy-done.1
  1.7 0.8 copy-done.2
  2.4 0.9 copy-done.4
  3.3 0.5 shard_map.67
  3.8 3.3 %collective-permute-start = (bf16[336,128]{1,0:T(8,128)(2,1)S(1)}, bf16[336,128]{1,0:T(8,128)(2,1)S(1)}, u32[]{:S(2)}, u32[]{:S(2)}) collective-permute-start(bf16[336,128]{1,0:T(8,128)(2,1)S(1)} %get-tuple-element.44), channel_id=1, source_target_pairs={{0,1},{1,0},{2,3},{3,2},{4,5},{5,4},{6,7},{7,6},{8,9},{9,8},{10,11... | collective-permute-start | bytes 258056 | tf_op jit(solution)/shard_map/ppermute | solution.py:272
  7.2 1.7 %collective-permute-start.2 = (bf16[336,128]{1,0:T(8,128)(2,1)S(1)}, bf16[336,128]{1,0:T(8,128)(2,1)S(1)}, u32[]{:S(2)}, u32[]{:S(2)}) collective-permute-start(bf16[336,128]{1,0:T(8,128)(2,1)S(1)} %get-tuple-element.46), channel_id=1, source_target_pairs={{0,3},{1,2},{2,1},{3,0},{4,7},{5,6},{6,5},{7,4},{8,11},{9,10},{10,... | collective-permute-start | bytes 258056 | tf_op jit(solution)/shard_map/ppermute | solution.py:272
  8.9 1.3 %collective-permute-start.3 = (bf16[336,128]{1,0:T(8,128)(2,1)S(1)}, bf16[336,128]{1,0:T(8,128)(2,1)S(1)}, u32[]{:S(2)}, u32[]{:S(2)}) collective-permute-start(bf16[336,128]{1,0:T(8,128)(2,1)S(1)} %get-tuple-element.47), channel_id=1, source_target_pairs={{0,4},{1,5},{2,6},{3,7},{4,0},{5,1},{6,2},{7,3},{8,12},{9,13},{10,... | collective-permute-start | bytes 258056 | tf_op jit(solution)/shard_map/ppermute | solution.py:272
  10.1 1.4 %collective-permute-start.4 = (bf16[336,128]{1,0:T(8,128)(2,1)S(1)}, bf16[336,128]{1,0:T(8,128)(2,1)S(1)}, u32[]{:S(2)}, u32[]{:S(2)}) collective-permute-start(bf16[336,128]{1,0:T(8,128)(2,1)S(1)} %get-tuple-element.48), channel_id=1, source_target_pairs={{0,5},{1,4},{2,7},{3,6},{4,1},{5,0},{6,3},{7,2},{8,13},{9,12},{10,... | collective-permute-start | bytes 258056 | tf_op jit(solution)/shard_map/ppermute | solution.py:272
  11.6 2.6 %collective-permute-start.5 = (bf16[336,128]{1,0:T(8,128)(2,1)S(1)}, bf16[336,128]{1,0:T(8,128)(2,1)S(1)}, u32[]{:S(2)}, u32[]{:S(2)}) collective-permute-start(bf16[336,128]{1,0:T(8,128)(2,1)S(1)} %get-tuple-element.49), channel_id=1, source_target_pairs={{0,6},{1,7},{2,4},{3,5},{4,2},{5,3},{6,0},{7,1},{8,14},{9,15},{10,... | collective-permute-start | bytes 258056 | tf_op jit(solution)/shard_map/ppermute | solution.py:272
  14.2 0.9 collective-permute-start.6
  15.1 0.7 collective-permute-done.2.refs_3_
  15.8 7.7 %collective-permute-done.4.refs_5_ = bf16[336,128]{1,0:T(8,128)(2,1)S(1)} collective-permute-done((bf16[336,128]{1,0:T(8,128)(2,1)S(1)}, bf16[336,128]{1,0:T(8,128)(2,1)S(1)}, u32[]{:S(2)}, u32[]{:S(2)}) %collective-permute-start.4) | collective-permute-done | bytes 86048 | tf_op jit(solution)/shard_map/ppermute | solution.py:272
  23.5 0.8 copy-done.3
  24.3 0.8 shard_map.68
  25.1 7.3 %collective-permute-start.7 = (bf16[80,512]{1,0:T(8,128)(2,1)S(1)}, bf16[80,512]{1,0:T(8,128)(2,1)S(1)}, u32[]{:S(2)}, u32[]{:S(2)}) collective-permute-start(bf16[80,512]{1,0:T(8,128)(2,1)S(1)} %get-tuple-element.52), channel_id=1, source_target_pairs={{0,8},{8,16},{16,24},{24,32},{32,40},{40,48},{48,56},{56,64},{64,7... | collective-permute-start | bytes 245768 | tf_op jit(solution)/shard_map/ppermute | solution.py:300
  32.4 1.3 %collective-permute-start.8 = (bf16[80,256]{1,0:T(8,128)(2,1)S(1)}, bf16[80,256]{1,0:T(8,128)(2,1)S(1)}, u32[]{:S(2)}, u32[]{:S(2)}) collective-permute-start(bf16[80,256]{1,0:T(8,128)(2,1)S(1)} %get-tuple-element.53), channel_id=1, source_target_pairs={{8,0},{16,8},{24,16},{32,24},{40,32},{48,40},{56,48},{64,56},{72,6... | collective-permute-start | bytes 122888 | tf_op jit(solution)/shard_map/ppermute | solution.py:307
  33.7 0.7 collective-permute-done.7.down_ref
  34.4 0.5 shard_map.69
  34.9 0.8 collective-permute-start.9
  35.7 3.6 %collective-permute-start.10 = (bf16[80,256]{1,0:T(8,128)(2,1)S(1)}, bf16[80,256]{1,0:T(8,128)(2,1)S(1)}, u32[]{:S(2)}, u32[]{:S(2)}) collective-permute-start(bf16[80,256]{1,0:T(8,128)(2,1)S(1)} %get-tuple-element.57), channel_id=1, source_target_pairs={{0,2},{1,3},{2,0},{3,1},{4,6},{5,7},{6,4},{7,5},{8,10},{9,11},{10,... | collective-permute-start | bytes 122888 | tf_op jit(solution)/shard_map/ppermute | solution.py:272
  39.3 2.1 %collective-permute-start.12 = (bf16[80,256]{1,0:T(8,128)(2,1)S(1)}, bf16[80,256]{1,0:T(8,128)(2,1)S(1)}, u32[]{:S(2)}, u32[]{:S(2)}) collective-permute-start(bf16[80,256]{1,0:T(8,128)(2,1)S(1)} %get-tuple-element.59), channel_id=1, source_target_pairs={{0,4},{1,5},{2,6},{3,7},{4,0},{5,1},{6,2},{7,3},{8,12},{9,13},{10,... | collective-permute-start | bytes 122888 | tf_op jit(solution)/shard_map/ppermute | solution.py:272
  41.4 1.8 %collective-permute-done.8.up_ref = bf16[80,256]{1,0:T(8,128)(2,1)S(1)} collective-permute-done((bf16[80,256]{1,0:T(8,128)(2,1)S(1)}, bf16[80,256]{1,0:T(8,128)(2,1)S(1)}, u32[]{:S(2)}, u32[]{:S(2)}) %collective-permute-start.8) | collective-permute-done | bytes 40992 | tf_op jit(solution)/shard_map/ppermute | solution.py:307
  43.3 3.4 %collective-permute-start.13 = (bf16[80,256]{1,0:T(8,128)(2,1)S(1)}, bf16[80,256]{1,0:T(8,128)(2,1)S(1)}, u32[]{:S(2)}, u32[]{:S(2)}) collective-permute-start(bf16[80,256]{1,0:T(8,128)(2,1)S(1)} %get-tuple-element.60), channel_id=1, source_target_pairs={{0,5},{1,4},{2,7},{3,6},{4,1},{5,0},{6,3},{7,2},{8,13},{9,12},{10,... | collective-permute-start | bytes 122888 | tf_op jit(solution)/shard_map/ppermute | solution.py:272
  46.7 1.6 %collective-permute-start.14 = (bf16[80,256]{1,0:T(8,128)(2,1)S(1)}, bf16[80,256]{1,0:T(8,128)(2,1)S(1)}, u32[]{:S(2)}, u32[]{:S(2)}) collective-permute-start(bf16[80,256]{1,0:T(8,128)(2,1)S(1)} %get-tuple-element.61), channel_id=1, source_target_pairs={{0,6},{1,7},{2,4},{3,5},{4,2},{5,3},{6,0},{7,1},{8,14},{9,15},{10,... | collective-permute-start | bytes 122888 | tf_op jit(solution)/shard_map/ppermute | solution.py:272
  48.3 1.1 collective-permute-start.15
  49.5 2.2 %collective-permute-done.14.refs_6_ = bf16[80,256]{1,0:T(8,128)(2,1)S(1)} collective-permute-done((bf16[80,256]{1,0:T(8,128)(2,1)S(1)}, bf16[80,256]{1,0:T(8,128)(2,1)S(1)}, u32[]{:S(2)}, u32[]{:S(2)}) %collective-permute-start.14) | collective-permute-done | bytes 40992 | tf_op jit(solution)/shard_map/ppermute | solution.py:272
  51.7 1.9 %collective-permute-done.15.refs_7_ = bf16[80,256]{1,0:T(8,128)(2,1)S(1)} collective-permute-done((bf16[80,256]{1,0:T(8,128)(2,1)S(1)}, bf16[80,256]{1,0:T(8,128)(2,1)S(1)}, u32[]{:S(2)}, u32[]{:S(2)}) %collective-permute-start.15) | collective-permute-done | bytes 40992 | tf_op jit(solution)/shard_map/ppermute | solution.py:272
  53.6 0.1 shard_map.70
  53.7 15.1 %all-gather = bf16[1280,256]{1,0:T(8,128)(2,1)S(1)} all-gather(bf16[160,256]{1,0:T(8,128)(2,1)S(1)} %get-tuple-element.63), channel_id=2, replica_groups=mesh['tile'=32,'fsdp'=8] {'fsdp'}, dimensions={0}, use_global_device_ids=true | all-gather | bytes 737280 | tf_op jit(solution)/shard_map/all_gather | solution.py:311
  68.7 2.6 %shard_map.71 = (bf16[640,896]{1,0:T(8,128)(2,1)}, bf16[640,256]{1,0:T(8,128)(2,1)S(1)}) custom-call(bf16[8,160,256]{2,1,0:T(8,128)(2,1)S(1)} %bitcast.13, bf16[720,256]{1,0:T(8,128)(2,1)S(1)} %get-tuple-element.64.win_ref, bf16[640,256]{1,0:T(8,128)(2,1)S(1)} %get-tuple-element.65.cot_ref, bf16[80,256]{1,0:T(8,128)(2,1)S(1)} %get-tuple-element.66.act_ref), custom_call_target="tpu_custom_call" | custom-call | tf_op jit(solution)/shard_map/pallas_call | solution.py:258
  71.3 6.7 %all-to-all-start = ((bf16[16,40,896]{2,1,0:T(8,128)(2,1)}), bf16[16,40,896]{2,1,0:T(8,128)(2,1)S(1)}, u32[]{:S(2)}, u32[]{:S(2)}) async-start(bf16[16,40,896]{2,1,0:T(8,128)(2,1)} %bitcast.9), calls=%async_computation | async-start | bytes 2293760 | tf_op jit(solution)/shard_map/all_to_all | solution.py:322
  78.1 0.5 shard_map.72
  78.6 1.5 %collective-permute-start.16 = (f32[2,80,128]{2,1,0:T(8,128)S(1)}, f32[2,80,128]{2,1,0:T(8,128)S(1)}, u32[]{:S(2)}, u32[]{:S(2)}) collective-permute-start(f32[2,80,128]{2,1,0:T(8,128)S(1)} %get-tuple-element.69), channel_id=1, source_target_pairs={{8,0},{16,8},{24,16},{32,24},{40,32},{48,40},{56,48},{64,56},{72,6... | collective-permute-start | bytes 245768 | tf_op jit(solution)/shard_map/ppermute | solution.py:321
  80.0 7.9 %collective-permute-done.16.below_ref = f32[2,80,128]{2,1,0:T(8,128)S(1)} collective-permute-done((f32[2,80,128]{2,1,0:T(8,128)S(1)}, f32[2,80,128]{2,1,0:T(8,128)S(1)}, u32[]{:S(2)}, u32[]{:S(2)}) %collective-permute-start.16) | collective-permute-done | bytes 81952 | tf_op jit(solution)/shard_map/ppermute | solution.py:321
  88.0 0.3 shard_map.73
  88.3 1.5 %collective-permute-start.17 = (bf16[80,128]{1,0:T(8,128)(2,1)S(1)}, bf16[80,128]{1,0:T(8,128)(2,1)S(1)}, u32[]{:S(2)}, u32[]{:S(2)}) collective-permute-start(bf16[80,128]{1,0:T(8,128)(2,1)S(1)} %get-tuple-element.71), channel_id=1, source_target_pairs={{0,1},{1,0},{2,3},{3,2},{4,5},{5,4},{6,7},{7,6},{8,9},{9,8},{10,11... | collective-permute-start | bytes 61448 | tf_op jit(solution)/shard_map/ppermute | solution.py:272
  89.7 1.7 %collective-permute-start.19 = (bf16[80,128]{1,0:T(8,128)(2,1)S(1)}, bf16[80,128]{1,0:T(8,128)(2,1)S(1)}, u32[]{:S(2)}, u32[]{:S(2)}) collective-permute-start(bf16[80,128]{1,0:T(8,128)(2,1)S(1)} %get-tuple-element.73), channel_id=1, source_target_pairs={{0,3},{1,2},{2,1},{3,0},{4,7},{5,6},{6,5},{7,4},{8,11},{9,10},{10,... | collective-permute-start | bytes 61448 | tf_op jit(solution)/shard_map/ppermute | solution.py:272
  91.4 4.0 %all-to-all-done.red_ref = bf16[16,40,896]{2,1,0:T(8,128)(2,1)S(1)} async-done(((bf16[16,40,896]{2,1,0:T(8,128)(2,1)}), bf16[16,40,896]{2,1,0:T(8,128)(2,1)S(1)}, u32[]{:S(2)}, u32[]{:S(2)}) %all-to-all-start) | async-done | bytes 1146912 | tf_op jit(solution)/shard_map/all_to_all | solution.py:322
  95.4 0.2 shard_map.75
  95.6 3.9 %collective-permute-start.24 = (bf16[20,896]{1,0:T(8,128)(2,1)S(1)}, bf16[20,896]{1,0:T(8,128)(2,1)S(1)}, u32[]{:S(2)}, u32[]{:S(2)}) collective-permute-start(bf16[20,896]{1,0:T(8,128)(2,1)S(1)} %get-tuple-element.80), channel_id=1, source_target_pairs={{0,8},{8,0},{16,24},{24,16},{32,40},{40,32},{48,56},{56,48},{64,72... | collective-permute-start | bytes 107528 | tf_op jit(solution)/shard_map/ppermute | solution.py:333
  99.5 0.3 collective-permute-start.20
  99.8 5.0 %collective-permute-start.21 = (bf16[80,128]{1,0:T(8,128)(2,1)S(1)}, bf16[80,128]{1,0:T(8,128)(2,1)S(1)}, u32[]{:S(2)}, u32[]{:S(2)}) collective-permute-start(bf16[80,128]{1,0:T(8,128)(2,1)S(1)} %get-tuple-element.75), channel_id=1, source_target_pairs={{0,5},{1,4},{2,7},{3,6},{4,1},{5,0},{6,3},{7,2},{8,13},{9,12},{10,... | collective-permute-start | bytes 61448 | tf_op jit(solution)/shard_map/ppermute | solution.py:272
  104.7 1.7 %collective-permute-start.22 = (bf16[80,128]{1,0:T(8,128)(2,1)S(1)}, bf16[80,128]{1,0:T(8,128)(2,1)S(1)}, u32[]{:S(2)}, u32[]{:S(2)}) collective-permute-start(bf16[80,128]{1,0:T(8,128)(2,1)S(1)} %get-tuple-element.76), channel_id=1, source_target_pairs={{0,6},{1,7},{2,4},{3,5},{4,2},{5,3},{6,0},{7,1},{8,14},{9,15},{10,... | collective-permute-start | bytes 61448 | tf_op jit(solution)/shard_map/ppermute | solution.py:272
  106.5 0.4 collective-permute-done.21.refs_5_
  106.8 2.3 %collective-permute-done.22.refs_6_ = bf16[80,128]{1,0:T(8,128)(2,1)S(1)} collective-permute-done((bf16[80,128]{1,0:T(8,128)(2,1)S(1)}, bf16[80,128]{1,0:T(8,128)(2,1)S(1)}, u32[]{:S(2)}, u32[]{:S(2)}) %collective-permute-start.22) | collective-permute-done | bytes 20512 | tf_op jit(solution)/shard_map/ppermute | solution.py:272
  109.2 2.3 %collective-permute-done.23.refs_7_ = bf16[80,128]{1,0:T(8,128)(2,1)S(1)} collective-permute-done((bf16[80,128]{1,0:T(8,128)(2,1)S(1)}, bf16[80,128]{1,0:T(8,128)(2,1)S(1)}, u32[]{:S(2)}, u32[]{:S(2)}) %collective-permute-start.23) | collective-permute-done | bytes 20512 | tf_op jit(solution)/shard_map/ppermute | solution.py:272
  111.5 0.9 shard_map.74
  112.4 0.8 shard_map.76
  (25 shorter events, 0.1 us)
Async XLA Ops:
  0.6 33.8 %copy-start = (bf16[80,9,640]{2,0,1:T(8,128)(2,1)S(1)}, bf16[80,9,640]{2,0,1:T(8,128)(2,1)}, u32[]{:S(2)}) copy-start(bf16[80,9,640]{2,0,1:T(8,128)(2,1)} %param.5) | copy-start | bytes 2764804
  0.6 1.0 copy-start.1
  1.6 0.8 copy-start.2
  2.4 0.9 copy-start.4
  3.8 7.8 %collective-permute-start = (bf16[336,128]{1,0:T(8,128)(2,1)S(1)}, bf16[336,128]{1,0:T(8,128)(2,1)S(1)}, u32[]{:S(2)}, u32[]{:S(2)}) collective-permute-start(bf16[336,128]{1,0:T(8,128)(2,1)S(1)} %get-tuple-element.44), channel_id=1, source_target_pairs={{0,1},{1,0},{2,3},{3,2},{4,5},{5,4},{6,7},{7,6},{8,9},{9,8},{10,11... | collective-permute-start | bytes 258056 | tf_op jit(solution)/shard_map/ppermute | solution.py:272
  7.2 7.0 %collective-permute-start.1 = (bf16[336,128]{1,0:T(8,128)(2,1)S(1)}, bf16[336,128]{1,0:T(8,128)(2,1)S(1)}, u32[]{:S(2)}, u32[]{:S(2)}) collective-permute-start(bf16[336,128]{1,0:T(8,128)(2,1)S(1)} %get-tuple-element.45), channel_id=1, source_target_pairs={{0,2},{1,3},{2,0},{3,1},{4,6},{5,7},{6,4},{7,5},{8,10},{9,11},{10,... | collective-permute-start | bytes 258056 | tf_op jit(solution)/shard_map/ppermute | solution.py:272
  7.2 8.7 %collective-permute-start.2 = (bf16[336,128]{1,0:T(8,128)(2,1)S(1)}, bf16[336,128]{1,0:T(8,128)(2,1)S(1)}, u32[]{:S(2)}, u32[]{:S(2)}) collective-permute-start(bf16[336,128]{1,0:T(8,128)(2,1)S(1)} %get-tuple-element.46), channel_id=1, source_target_pairs={{0,3},{1,2},{2,1},{3,0},{4,7},{5,6},{6,5},{7,4},{8,11},{9,10},{10,... | collective-permute-start | bytes 258056 | tf_op jit(solution)/shard_map/ppermute | solution.py:272
  8.9 6.9 %collective-permute-start.3 = (bf16[336,128]{1,0:T(8,128)(2,1)S(1)}, bf16[336,128]{1,0:T(8,128)(2,1)S(1)}, u32[]{:S(2)}, u32[]{:S(2)}) collective-permute-start(bf16[336,128]{1,0:T(8,128)(2,1)S(1)} %get-tuple-element.47), channel_id=1, source_target_pairs={{0,4},{1,5},{2,6},{3,7},{4,0},{5,1},{6,2},{7,3},{8,12},{9,13},{10,... | collective-permute-start | bytes 258056 | tf_op jit(solution)/shard_map/ppermute | solution.py:272
  10.1 13.3 %collective-permute-start.4 = (bf16[336,128]{1,0:T(8,128)(2,1)S(1)}, bf16[336,128]{1,0:T(8,128)(2,1)S(1)}, u32[]{:S(2)}, u32[]{:S(2)}) collective-permute-start(bf16[336,128]{1,0:T(8,128)(2,1)S(1)} %get-tuple-element.48), channel_id=1, source_target_pairs={{0,5},{1,4},{2,7},{3,6},{4,1},{5,0},{6,3},{7,2},{8,13},{9,12},{10,... | collective-permute-start | bytes 258056 | tf_op jit(solution)/shard_map/ppermute | solution.py:272
  11.6 11.9 %collective-permute-start.5 = (bf16[336,128]{1,0:T(8,128)(2,1)S(1)}, bf16[336,128]{1,0:T(8,128)(2,1)S(1)}, u32[]{:S(2)}, u32[]{:S(2)}) collective-permute-start(bf16[336,128]{1,0:T(8,128)(2,1)S(1)} %get-tuple-element.49), channel_id=1, source_target_pairs={{0,6},{1,7},{2,4},{3,5},{4,2},{5,3},{6,0},{7,1},{8,14},{9,15},{10,... | collective-permute-start | bytes 258056 | tf_op jit(solution)/shard_map/ppermute | solution.py:272
  14.2 9.3 %collective-permute-start.6 = (bf16[336,128]{1,0:T(8,128)(2,1)S(1)}, bf16[336,128]{1,0:T(8,128)(2,1)S(1)}, u32[]{:S(2)}, u32[]{:S(2)}) collective-permute-start(bf16[336,128]{1,0:T(8,128)(2,1)S(1)} %get-tuple-element.50), channel_id=1, source_target_pairs={{0,7},{1,6},{2,5},{3,4},{4,3},{5,2},{6,1},{7,0},{8,15},{9,14},{10,... | collective-permute-start | bytes 258056 | tf_op jit(solution)/shard_map/ppermute | solution.py:272
  23.5 0.8 copy-start.3
  25.1 9.3 %collective-permute-start.7 = (bf16[80,512]{1,0:T(8,128)(2,1)S(1)}, bf16[80,512]{1,0:T(8,128)(2,1)S(1)}, u32[]{:S(2)}, u32[]{:S(2)}) collective-permute-start(bf16[80,512]{1,0:T(8,128)(2,1)S(1)} %get-tuple-element.52), channel_id=1, source_target_pairs={{0,8},{8,16},{16,24},{24,32},{32,40},{40,48},{48,56},{56,64},{64,7... | collective-permute-start | bytes 245768 | tf_op jit(solution)/shard_map/ppermute | solution.py:300
  32.4 10.8 %collective-permute-start.8 = (bf16[80,256]{1,0:T(8,128)(2,1)S(1)}, bf16[80,256]{1,0:T(8,128)(2,1)S(1)}, u32[]{:S(2)}, u32[]{:S(2)}) collective-permute-start(bf16[80,256]{1,0:T(8,128)(2,1)S(1)} %get-tuple-element.53), channel_id=1, source_target_pairs={{8,0},{16,8},{24,16},{32,24},{40,32},{48,40},{56,48},{64,56},{72,6... | collective-permute-start | bytes 122888 | tf_op jit(solution)/shard_map/ppermute | solution.py:307
  34.9 11.8 %collective-permute-start.9 = (bf16[80,256]{1,0:T(8,128)(2,1)S(1)}, bf16[80,256]{1,0:T(8,128)(2,1)S(1)}, u32[]{:S(2)}, u32[]{:S(2)}) collective-permute-start(bf16[80,256]{1,0:T(8,128)(2,1)S(1)} %get-tuple-element.56), channel_id=1, source_target_pairs={{0,1},{1,0},{2,3},{3,2},{4,5},{5,4},{6,7},{7,6},{8,9},{9,8},{10,11... | collective-permute-start | bytes 122888 | tf_op jit(solution)/shard_map/ppermute | solution.py:272
  35.7 12.7 %collective-permute-start.10 = (bf16[80,256]{1,0:T(8,128)(2,1)S(1)}, bf16[80,256]{1,0:T(8,128)(2,1)S(1)}, u32[]{:S(2)}, u32[]{:S(2)}) collective-permute-start(bf16[80,256]{1,0:T(8,128)(2,1)S(1)} %get-tuple-element.57), channel_id=1, source_target_pairs={{0,2},{1,3},{2,0},{3,1},{4,6},{5,7},{6,4},{7,5},{8,10},{9,11},{10,... | collective-permute-start | bytes 122888 | tf_op jit(solution)/shard_map/ppermute | solution.py:272
  39.3 10.2 %collective-permute-start.11 = (bf16[80,256]{1,0:T(8,128)(2,1)S(1)}, bf16[80,256]{1,0:T(8,128)(2,1)S(1)}, u32[]{:S(2)}, u32[]{:S(2)}) collective-permute-start(bf16[80,256]{1,0:T(8,128)(2,1)S(1)} %get-tuple-element.58), channel_id=1, source_target_pairs={{0,3},{1,2},{2,1},{3,0},{4,7},{5,6},{6,5},{7,4},{8,11},{9,10},{10,... | collective-permute-start | bytes 122888 | tf_op jit(solution)/shard_map/ppermute | solution.py:272
  39.3 10.2 %collective-permute-start.12 = (bf16[80,256]{1,0:T(8,128)(2,1)S(1)}, bf16[80,256]{1,0:T(8,128)(2,1)S(1)}, u32[]{:S(2)}, u32[]{:S(2)}) collective-permute-start(bf16[80,256]{1,0:T(8,128)(2,1)S(1)} %get-tuple-element.59), channel_id=1, source_target_pairs={{0,4},{1,5},{2,6},{3,7},{4,0},{5,1},{6,2},{7,3},{8,12},{9,13},{10,... | collective-permute-start | bytes 122888 | tf_op jit(solution)/shard_map/ppermute | solution.py:272
  43.3 6.2 %collective-permute-start.13 = (bf16[80,256]{1,0:T(8,128)(2,1)S(1)}, bf16[80,256]{1,0:T(8,128)(2,1)S(1)}, u32[]{:S(2)}, u32[]{:S(2)}) collective-permute-start(bf16[80,256]{1,0:T(8,128)(2,1)S(1)} %get-tuple-element.60), channel_id=1, source_target_pairs={{0,5},{1,4},{2,7},{3,6},{4,1},{5,0},{6,3},{7,2},{8,13},{9,12},{10,... | collective-permute-start | bytes 122888 | tf_op jit(solution)/shard_map/ppermute | solution.py:272
  46.7 5.0 %collective-permute-start.14 = (bf16[80,256]{1,0:T(8,128)(2,1)S(1)}, bf16[80,256]{1,0:T(8,128)(2,1)S(1)}, u32[]{:S(2)}, u32[]{:S(2)}) collective-permute-start(bf16[80,256]{1,0:T(8,128)(2,1)S(1)} %get-tuple-element.61), channel_id=1, source_target_pairs={{0,6},{1,7},{2,4},{3,5},{4,2},{5,3},{6,0},{7,1},{8,14},{9,15},{10,... | collective-permute-start | bytes 122888 | tf_op jit(solution)/shard_map/ppermute | solution.py:272
  48.3 5.2 %collective-permute-start.15 = (bf16[80,256]{1,0:T(8,128)(2,1)S(1)}, bf16[80,256]{1,0:T(8,128)(2,1)S(1)}, u32[]{:S(2)}, u32[]{:S(2)}) collective-permute-start(bf16[80,256]{1,0:T(8,128)(2,1)S(1)} %get-tuple-element.62), channel_id=1, source_target_pairs={{0,7},{1,6},{2,5},{3,4},{4,3},{5,2},{6,1},{7,0},{8,15},{9,14},{10,... | collective-permute-start | bytes 122888 | tf_op jit(solution)/shard_map/ppermute | solution.py:272
  71.3 24.1 %all-to-all-start = ((bf16[16,40,896]{2,1,0:T(8,128)(2,1)}), bf16[16,40,896]{2,1,0:T(8,128)(2,1)S(1)}, u32[]{:S(2)}, u32[]{:S(2)}) async-start(bf16[16,40,896]{2,1,0:T(8,128)(2,1)} %bitcast.9), calls=%async_computation | async-start | bytes 2293760 | tf_op jit(solution)/shard_map/all_to_all | solution.py:322
  78.6 9.4 %collective-permute-start.16 = (f32[2,80,128]{2,1,0:T(8,128)S(1)}, f32[2,80,128]{2,1,0:T(8,128)S(1)}, u32[]{:S(2)}, u32[]{:S(2)}) collective-permute-start(f32[2,80,128]{2,1,0:T(8,128)S(1)} %get-tuple-element.69), channel_id=1, source_target_pairs={{8,0},{16,8},{24,16},{32,24},{40,32},{48,40},{56,48},{64,56},{72,6... | collective-permute-start | bytes 245768 | tf_op jit(solution)/shard_map/ppermute | solution.py:321
  88.3 11.5 %collective-permute-start.17 = (bf16[80,128]{1,0:T(8,128)(2,1)S(1)}, bf16[80,128]{1,0:T(8,128)(2,1)S(1)}, u32[]{:S(2)}, u32[]{:S(2)}) collective-permute-start(bf16[80,128]{1,0:T(8,128)(2,1)S(1)} %get-tuple-element.71), channel_id=1, source_target_pairs={{0,1},{1,0},{2,3},{3,2},{4,5},{5,4},{6,7},{7,6},{8,9},{9,8},{10,11... | collective-permute-start | bytes 61448 | tf_op jit(solution)/shard_map/ppermute | solution.py:272
  89.7 15.0 %collective-permute-start.18 = (bf16[80,128]{1,0:T(8,128)(2,1)S(1)}, bf16[80,128]{1,0:T(8,128)(2,1)S(1)}, u32[]{:S(2)}, u32[]{:S(2)}) collective-permute-start(bf16[80,128]{1,0:T(8,128)(2,1)S(1)} %get-tuple-element.72), channel_id=1, source_target_pairs={{0,2},{1,3},{2,0},{3,1},{4,6},{5,7},{6,4},{7,5},{8,10},{9,11},{10,... | collective-permute-start | bytes 61448 | tf_op jit(solution)/shard_map/ppermute | solution.py:272
  89.7 16.7 %collective-permute-start.19 = (bf16[80,128]{1,0:T(8,128)(2,1)S(1)}, bf16[80,128]{1,0:T(8,128)(2,1)S(1)}, u32[]{:S(2)}, u32[]{:S(2)}) collective-permute-start(bf16[80,128]{1,0:T(8,128)(2,1)S(1)} %get-tuple-element.73), channel_id=1, source_target_pairs={{0,3},{1,2},{2,1},{3,0},{4,7},{5,6},{6,5},{7,4},{8,11},{9,10},{10,... | collective-permute-start | bytes 61448 | tf_op jit(solution)/shard_map/ppermute | solution.py:272
  95.6 16.8 %collective-permute-start.24 = (bf16[20,896]{1,0:T(8,128)(2,1)S(1)}, bf16[20,896]{1,0:T(8,128)(2,1)S(1)}, u32[]{:S(2)}, u32[]{:S(2)}) collective-permute-start(bf16[20,896]{1,0:T(8,128)(2,1)S(1)} %get-tuple-element.80), channel_id=1, source_target_pairs={{0,8},{8,0},{16,24},{24,16},{32,40},{40,32},{48,56},{56,48},{64,72... | collective-permute-start | bytes 107528 | tf_op jit(solution)/shard_map/ppermute | solution.py:333
  99.5 7.0 %collective-permute-start.20 = (bf16[80,128]{1,0:T(8,128)(2,1)S(1)}, bf16[80,128]{1,0:T(8,128)(2,1)S(1)}, u32[]{:S(2)}, u32[]{:S(2)}) collective-permute-start(bf16[80,128]{1,0:T(8,128)(2,1)S(1)} %get-tuple-element.74), channel_id=1, source_target_pairs={{0,4},{1,5},{2,6},{3,7},{4,0},{5,1},{6,2},{7,3},{8,12},{9,13},{10,... | collective-permute-start | bytes 61448 | tf_op jit(solution)/shard_map/ppermute | solution.py:272
  99.8 7.1 %collective-permute-start.21 = (bf16[80,128]{1,0:T(8,128)(2,1)S(1)}, bf16[80,128]{1,0:T(8,128)(2,1)S(1)}, u32[]{:S(2)}, u32[]{:S(2)}) collective-permute-start(bf16[80,128]{1,0:T(8,128)(2,1)S(1)} %get-tuple-element.75), channel_id=1, source_target_pairs={{0,5},{1,4},{2,7},{3,6},{4,1},{5,0},{6,3},{7,2},{8,13},{9,12},{10,... | collective-permute-start | bytes 61448 | tf_op jit(solution)/shard_map/ppermute | solution.py:272
  104.7 4.4 %collective-permute-start.22 = (bf16[80,128]{1,0:T(8,128)(2,1)S(1)}, bf16[80,128]{1,0:T(8,128)(2,1)S(1)}, u32[]{:S(2)}, u32[]{:S(2)}) collective-permute-start(bf16[80,128]{1,0:T(8,128)(2,1)S(1)} %get-tuple-element.76), channel_id=1, source_target_pairs={{0,6},{1,7},{2,4},{3,5},{4,2},{5,3},{6,0},{7,1},{8,14},{9,15},{10,... | collective-permute-start | bytes 61448 | tf_op jit(solution)/shard_map/ppermute | solution.py:272
  106.4 5.0 %collective-permute-start.23 = (bf16[80,128]{1,0:T(8,128)(2,1)S(1)}, bf16[80,128]{1,0:T(8,128)(2,1)S(1)}, u32[]{:S(2)}, u32[]{:S(2)}) collective-permute-start(bf16[80,128]{1,0:T(8,128)(2,1)S(1)} %get-tuple-element.77), channel_id=1, source_target_pairs={{0,7},{1,6},{2,5},{3,4},{4,3},{5,2},{6,1},{7,0},{8,15},{9,14},{10,... | collective-permute-start | bytes 61448 | tf_op jit(solution)/shard_map/ppermute | solution.py:272

commit v6 on v5

--- a/solution.py
+++ b/solution.py
@@ -10,6 +10,7 @@
 
 F32 = jnp.float32
 BF16 = jnp.bfloat16
+ORDER = (0, 6, 7, 4, 5, 2, 3, 1)
 FORWARD_FLOPS = 12_000_000_000
 
 
@@ -67,16 +68,16 @@
         block_ref[p, 0:80, :] = pixels[80 * p : 80 * p + 80]
         block_ref[p, 80:160, :] = taps[p].astype(BF16)
         block_ref[p, 160:176, :] = last[p].astype(BF16)
-    for k in range(8):
-        send_refs[k][0:176, :] = block_ref[slot_ref[0] ^ k]
+    for n, k in enumerate(ORDER):
+        send_refs[n][0:176, :] = block_ref[slot_ref[0] ^ k]
         for j in range(5):
-            send_refs[k][176 + 32 * j : 208 + 32 * j, :] = cot_ref[:, 128 * j : 128 * j + 128]
-
-
-def spread_kernel(slot_ref, raw_ref, *refs):
+            send_refs[n][176 + 32 * j : 208 + 32 * j, :] = cot_ref[:, 128 * j : 128 * j + 128]
+
+
+def spread_kernel(slot_ref, *refs):
     *recv_refs, win_ref, down_ref, up_ref, own_ref, cot_ref, cell_ref, tap_ref, block_ref = refs
-    for k in range(8):
-        block_ref[slot_ref[0] ^ k] = recv_refs[k][...]
+    for n, k in enumerate(ORDER):
+        block_ref[slot_ref[0] ^ k] = recv_refs[n][...]
     pixels = swap_blocks([block_ref[q, 0:80, :].astype(F32) for q in range(8)])
     for r in range(4):
         columns = (from_left(pixels[2 * r + 1]), pixels[2 * r], pixels[2 * r + 1])
@@ -122,9 +123,9 @@
         own_ref[here, 0:128] = sums[1][0] + sums[0][1]
         own_ref[here, 128:256] = sums[1][1] + sums[2][0]
         up_ref[here, 0:128] = sums[0][0].astype(BF16)
-        up_ref[here, 128:256] = raw_ref[0:16, rows]
+        up_ref[here, 128:256] = recv_refs[0][176 + 32 * g : 192 + 32 * g, :]
         down_ref[here, 256:384] = sums[2][1].astype(BF16)
-        down_ref[here, 384:512] = raw_ref[16:32, rows]
+        down_ref[here, 384:512] = recv_refs[0][192 + 32 * g : 208 + 32 * g, :]
 
 
 def forward_kernel(slot_ref, part_ref, down_ref, weight_ref, *refs):
@@ -138,8 +139,8 @@
     for p in range(8):
         for g in range(5):
             block_ref[p, 16 * g : 16 * g + 16, :] = hidden[128 * g + 16 * p : 128 * g + 16 * p + 16]
-    for k in range(8):
-        hid_refs[k][...] = block_ref[slot_ref[0] ^ k]
+    for n, k in enumerate(ORDER):
+        hid_refs[n][...] = block_ref[slot_ref[0] ^ k]
 
 
 def middle_kernel(own_ref, down_ref, up_ref, *refs):
@@ -220,8 +221,8 @@
     parts[7] = parts[7] + below_ref[1]
     for q, x in enumerate(swap_blocks(parts)):
         slot_blocks[slot_ref[0] ^ q] = x.astype(BF16)
-    for k in range(8):
-        send_refs[k][...] = slot_blocks[k]
+    for n, k in enumerate(ORDER):
+        send_refs[n][...] = slot_blocks[k]
 
 
 def fold_kernel(high_ref, red_ref, keep_ref, give_ref):
@@ -236,8 +237,8 @@
 
 def unpack_kernel(slot_ref, *refs):
     *recv_refs, out_ref, block_ref = refs
-    for k in range(8):
-        block_ref[slot_ref[0] ^ k] = recv_refs[k][...]
+    for n, k in enumerate(ORDER):
+        block_ref[slot_ref[0] ^ k] = recv_refs[n][...]
     lane = iota((128, 128), 1)
     pick = jnp.where(cell_of_lane(lane) == iota((128, 128), 0), 1.0, 0.0).astype(BF16)
     blocks = block_ref[...].reshape(640, 128)
@@ -267,10 +268,11 @@
 
 
 def trade(blocks):
-    devices = range(8)
-    return [blocks[0]] + [
-        lax.ppermute(blocks[k], "fsdp", [(i, i ^ k) for i in devices]) for k in devices[1:]
+    moved = [
+        lax.ppermute(block, "fsdp", [(i, i ^ k) for i in range(8)])
+        for k, block in zip(ORDER[1:], blocks[1:])
     ]
+    return [blocks[0]] + moved
 
 
 def per_device(image, conv_weight, group_weight, cotangent):
@@ -293,7 +295,7 @@
     windows, down, up, own, cot = call(
         spread_kernel,
         [((720, 256), BF16), ((80, 512), BF16), ((80, 256), BF16), ((80, 256), F32), ((640, 256), BF16)],
-        slot, cells, *parts,
+        slot, *parts,
         scratch=[pltpu.VMEM((256, 640), BF16), pltpu.VMEM((640, 256), BF16), pltpu.VMEM((8, 336, 128), BF16)],
         smem=1,
     )

time: 114 us -> 107 us (0.939)
  waiting for transfers between devices: 31.9 us -> 22.9 us
  starting transfers between devices: 54.8 us -> 57 us
    ppermute x21, waiting for transfers between devices: 17.5 us -> 11.4 us  [trade(): lax.ppermute(block, 'fsdp', [(i, i ^ k) for i in range(8)])]
    ppermute x21, starting transfers between devices: 34.2 us -> 32.1 us  [trade(): lax.ppermute(block, 'fsdp', [(i, i ^ k) for i in range(8)])]
    ppermute x1, starting transfers between devices: 3.87 us -> 5.81 us  [per_device(): given = lax.ppermute(give, 'tile', partners)]
    ppermute x1, waiting for transfers between devices: 1.82 us -> 0.01 us  [per_device(): up = lax.ppermute(up, 'tile', upward)]
    all_to_all x1, waiting for transfers between devices: 3.96 us -> 2.26 us  [per_device(): lax.all_to_all(red.reshape(16, 40, 896), 'tile', 0, 0, tiled=True, axis_i...]
    all_to_all x1, starting transfers between devices: 6.71 us -> 8.24 us  [per_device(): lax.all_to_all(red.reshape(16, 40, 896), 'tile', 0, 0, tiled=True, axis_i...]
  transfers between devices with their start and end apart: 26 -> 26, of which waited for: 11 -> 12; matrix products, arithmetic and copies ran while one was open for 0% -> 0% of each run, Pallas kernels for 2% -> 2%
where the time goes in v6:
time: 107 us
  starting transfers between devices  57 us (53%)
  waiting for transfers between devices  22.9 us (21%)
  blocking collectives  15.2 us (14%)
  Pallas kernels  7.21 us (7%)
  local copies, waits for them, and re-layouts  3.79 us (4%)
    ppermute x21, starting transfers between devices, trade(): lax.ppermute(block, 'fsdp', [(i, i ^ k) for i in range(8)])  32.1 us
    all_gather x1, blocking collectives, per_device(): share_all = lax.all_gather(share, 'fsdp', axis=0, tiled=False)  15.2 us
    ppermute x21, waiting for transfers between devices, trade(): lax.ppermute(block, 'fsdp', [(i, i ^ k) for i in range(8)])  11.4 us
    all_to_all x1, starting transfers between devices, per_device(): lax.all_to_all(red.reshape(16, 40, 896), 'tile', 0, 0, tiled=True, axis_i...  8.24 us
    ppermute x1, starting transfers between devices, per_device(): down = lax.ppermute(down, 'tile', downward)  8.07 us
    ppermute x1, waiting for transfers between devices, per_device(): img_below = lax.ppermute(img_up, 'tile', upward)  7.91 us
    pallas_call x10, Pallas kernels, call(): pl.pallas_call(kernel, out_shape=[jax.ShapeDtypeStruct(shape, dtype) for...  7.21 us
    ppermute x1, starting transfers between devices, per_device(): given = lax.ppermute(give, 'tile', partners)  5.81 us
  transfers between devices with their start and end apart: 26, of which 12 were waited for; matrix products, arithmetic and copies ran while one was open for 0% of the time, Pallas kernels for 2%

profile of v6, /device:TPU:1, one launch (start us, length us, event | category | flops | bytes accessed | tf_op | source)
XLA Modules:
  0.0 107.0 jit_solution(2680151146490295126)
XLA Ops:
  0.6 0.9 copy-done.2
  1.6 0.9 copy-done.3
  2.5 0.8 copy-done.4
  3.3 0.5 shard_map.67
  3.7 5.3 %collective-permute-start = (bf16[336,128]{1,0:T(8,128)(2,1)S(1)}, bf16[336,128]{1,0:T(8,128)(2,1)S(1)}, u32[]{:S(2)}, u32[]{:S(2)}) collective-permute-start(bf16[336,128]{1,0:T(8,128)(2,1)S(1)} %get-tuple-element.44), channel_id=1, source_target_pairs={{0,6},{1,7},{2,4},{3,5},{4,2},{5,3},{6,0},{7,1},{8,14},{9,15},{10,... | collective-permute-start | bytes 258056 | tf_op jit(solution)/shard_map/ppermute | solution.py:272
  9.0 1.5 %collective-permute-start.1 = (bf16[336,128]{1,0:T(8,128)(2,1)S(1)}, bf16[336,128]{1,0:T(8,128)(2,1)S(1)}, u32[]{:S(2)}, u32[]{:S(2)}) collective-permute-start(bf16[336,128]{1,0:T(8,128)(2,1)S(1)} %get-tuple-element.45), channel_id=1, source_target_pairs={{0,7},{1,6},{2,5},{3,4},{4,3},{5,2},{6,1},{7,0},{8,15},{9,14},{10,... | collective-permute-start | bytes 258056 | tf_op jit(solution)/shard_map/ppermute | solution.py:272
  10.5 0.0 collective-permute-start.2
  10.5 2.0 %collective-permute-start.3 = (bf16[336,128]{1,0:T(8,128)(2,1)S(1)}, bf16[336,128]{1,0:T(8,128)(2,1)S(1)}, u32[]{:S(2)}, u32[]{:S(2)}) collective-permute-start(bf16[336,128]{1,0:T(8,128)(2,1)S(1)} %get-tuple-element.47), channel_id=1, source_target_pairs={{0,5},{1,4},{2,7},{3,6},{4,1},{5,0},{6,3},{7,2},{8,13},{9,12},{10,... | collective-permute-start | bytes 258056 | tf_op jit(solution)/shard_map/ppermute | solution.py:272
  12.5 0.9 collective-permute-start.4
  13.4 5.1 %collective-permute-start.5 = (bf16[336,128]{1,0:T(8,128)(2,1)S(1)}, bf16[336,128]{1,0:T(8,128)(2,1)S(1)}, u32[]{:S(2)}, u32[]{:S(2)}) collective-permute-start(bf16[336,128]{1,0:T(8,128)(2,1)S(1)} %get-tuple-element.49), channel_id=1, source_target_pairs={{0,3},{1,2},{2,1},{3,0},{4,7},{5,6},{6,5},{7,4},{8,11},{9,10},{10,... | collective-permute-start | bytes 258056 | tf_op jit(solution)/shard_map/ppermute | solution.py:272
  18.5 3.1 %collective-permute-done.2.refs_3_ = bf16[336,128]{1,0:T(8,128)(2,1)S(1)} collective-permute-done((bf16[336,128]{1,0:T(8,128)(2,1)S(1)}, bf16[336,128]{1,0:T(8,128)(2,1)S(1)}, u32[]{:S(2)}, u32[]{:S(2)}) %collective-permute-start.2) | collective-permute-done | bytes 86048 | tf_op jit(solution)/shard_map/ppermute | solution.py:272
  21.6 1.9 %collective-permute-done.3.refs_4_ = bf16[336,128]{1,0:T(8,128)(2,1)S(1)} collective-permute-done((bf16[336,128]{1,0:T(8,128)(2,1)S(1)}, bf16[336,128]{1,0:T(8,128)(2,1)S(1)}, u32[]{:S(2)}, u32[]{:S(2)}) %collective-permute-start.3) | collective-permute-done | bytes 86048 | tf_op jit(solution)/shard_map/ppermute | solution.py:272
  23.5 0.7 collective-permute-done.5.refs_6_
  24.2 0.8 shard_map.68
  25.0 8.1 %collective-permute-start.7 = (bf16[80,512]{1,0:T(8,128)(2,1)S(1)}, bf16[80,512]{1,0:T(8,128)(2,1)S(1)}, u32[]{:S(2)}, u32[]{:S(2)}) collective-permute-start(bf16[80,512]{1,0:T(8,128)(2,1)S(1)} %get-tuple-element.52), channel_id=1, source_target_pairs={{0,8},{8,16},{16,24},{24,32},{32,40},{40,48},{48,56},{56,64},{64,7... | collective-permute-start | bytes 245768 | tf_op jit(solution)/shard_map/ppermute | solution.py:302
  33.1 1.3 %collective-permute-start.8 = (bf16[80,256]{1,0:T(8,128)(2,1)S(1)}, bf16[80,256]{1,0:T(8,128)(2,1)S(1)}, u32[]{:S(2)}, u32[]{:S(2)}) collective-permute-start(bf16[80,256]{1,0:T(8,128)(2,1)S(1)} %get-tuple-element.53), channel_id=1, source_target_pairs={{8,0},{16,8},{24,16},{32,24},{40,32},{48,40},{56,48},{64,56},{72,6... | collective-permute-start | bytes 122888 | tf_op jit(solution)/shard_map/ppermute | solution.py:309
  34.4 1.3 %collective-permute-done.7.down_ref = bf16[80,512]{1,0:T(8,128)(2,1)S(1)} collective-permute-done((bf16[80,512]{1,0:T(8,128)(2,1)S(1)}, bf16[80,512]{1,0:T(8,128)(2,1)S(1)}, u32[]{:S(2)}, u32[]{:S(2)}) %collective-permute-start.7) | collective-permute-done | bytes 81952 | tf_op jit(solution)/shard_map/ppermute | solution.py:302
  35.7 1.2 %copy-done = bf16[80,9,640]{2,0,1:T(8,128)(2,1)S(1)} copy-done((bf16[80,9,640]{2,0,1:T(8,128)(2,1)S(1)}, bf16[80,9,640]{2,0,1:T(8,128)(2,1)}, u32[]{:S(2)}) %copy-start) | copy-done | bytes 921624
  36.9 0.5 shard_map.69
  37.4 1.1 collective-permute-start.9
  38.5 2.0 %collective-permute-start.10 = (bf16[80,256]{1,0:T(8,128)(2,1)S(1)}, bf16[80,256]{1,0:T(8,128)(2,1)S(1)}, u32[]{:S(2)}, u32[]{:S(2)}) collective-permute-start(bf16[80,256]{1,0:T(8,128)(2,1)S(1)} %get-tuple-element.57), channel_id=1, source_target_pairs={{0,7},{1,6},{2,5},{3,4},{4,3},{5,2},{6,1},{7,0},{8,15},{9,14},{10,... | collective-permute-start | bytes 122888 | tf_op jit(solution)/shard_map/ppermute | solution.py:272
  40.5 3.2 %collective-permute-start.12 = (bf16[80,256]{1,0:T(8,128)(2,1)S(1)}, bf16[80,256]{1,0:T(8,128)(2,1)S(1)}, u32[]{:S(2)}, u32[]{:S(2)}) collective-permute-start(bf16[80,256]{1,0:T(8,128)(2,1)S(1)} %get-tuple-element.59), channel_id=1, source_target_pairs={{0,5},{1,4},{2,7},{3,6},{4,1},{5,0},{6,3},{7,2},{8,13},{9,12},{10,... | collective-permute-start | bytes 122888 | tf_op jit(solution)/shard_map/ppermute | solution.py:272
  43.7 1.2 %collective-permute-start.14 = (bf16[80,256]{1,0:T(8,128)(2,1)S(1)}, bf16[80,256]{1,0:T(8,128)(2,1)S(1)}, u32[]{:S(2)}, u32[]{:S(2)}) collective-permute-start(bf16[80,256]{1,0:T(8,128)(2,1)S(1)} %get-tuple-element.61), channel_id=1, source_target_pairs={{0,3},{1,2},{2,1},{3,0},{4,7},{5,6},{6,5},{7,4},{8,11},{9,10},{10,... | collective-permute-start | bytes 122888 | tf_op jit(solution)/shard_map/ppermute | solution.py:272
  44.9 0.7 collective-permute-start.15
  45.6 0.2 collective-permute-done.11.refs_3_
  45.8 1.8 %collective-permute-done.12.refs_4_ = bf16[80,256]{1,0:T(8,128)(2,1)S(1)} collective-permute-done((bf16[80,256]{1,0:T(8,128)(2,1)S(1)}, bf16[80,256]{1,0:T(8,128)(2,1)S(1)}, u32[]{:S(2)}, u32[]{:S(2)}) %collective-permute-start.12) | collective-permute-done | bytes 40992 | tf_op jit(solution)/shard_map/ppermute | solution.py:272
  47.5 0.6 collective-permute-done.13.refs_5_
  48.1 0.9 collective-permute-done.14.refs_6_
  49.0 0.1 shard_map.70
  49.1 15.2 %all-gather = bf16[1280,256]{1,0:T(8,128)(2,1)S(1)} all-gather(bf16[160,256]{1,0:T(8,128)(2,1)S(1)} %get-tuple-element.63), channel_id=2, replica_groups=mesh['tile'=32,'fsdp'=8] {'fsdp'}, dimensions={0}, use_global_device_ids=true | all-gather | bytes 737280 | tf_op jit(solution)/shard_map/all_gather | solution.py:313
  64.3 2.6 %shard_map.71 = (bf16[640,896]{1,0:T(8,128)(2,1)}, bf16[640,256]{1,0:T(8,128)(2,1)S(1)}) custom-call(bf16[8,160,256]{2,1,0:T(8,128)(2,1)S(1)} %bitcast.13, bf16[720,256]{1,0:T(8,128)(2,1)S(1)} %get-tuple-element.64.win_ref, bf16[640,256]{1,0:T(8,128)(2,1)S(1)} %get-tuple-element.65.cot_ref, bf16[80,256]{1,0:T(8,128)(2,1)S(1)} %get-tuple-element.66.act_ref), custom_call_target="tpu_custom_call" | custom-call | tf_op jit(solution)/shard_map/pallas_call | solution.py:259
  66.9 8.2 %all-to-all-start = ((bf16[16,40,896]{2,1,0:T(8,128)(2,1)}), bf16[16,40,896]{2,1,0:T(8,128)(2,1)S(1)}, u32[]{:S(2)}, u32[]{:S(2)}) async-start(bf16[16,40,896]{2,1,0:T(8,128)(2,1)} %bitcast.9), calls=%async_computation | async-start | bytes 2293760 | tf_op jit(solution)/shard_map/all_to_all | solution.py:324
  75.2 0.5 shard_map.72
  75.6 1.5 %collective-permute-start.16 = (f32[2,80,128]{2,1,0:T(8,128)S(1)}, f32[2,80,128]{2,1,0:T(8,128)S(1)}, u32[]{:S(2)}, u32[]{:S(2)}) collective-permute-start(f32[2,80,128]{2,1,0:T(8,128)S(1)} %get-tuple-element.69), channel_id=1, source_target_pairs={{8,0},{16,8},{24,16},{32,24},{40,32},{48,40},{56,48},{64,56},{72,6... | collective-permute-start | bytes 245768 | tf_op jit(solution)/shard_map/ppermute | solution.py:323
  77.1 7.9 %collective-permute-done.16.below_ref = f32[2,80,128]{2,1,0:T(8,128)S(1)} collective-permute-done((f32[2,80,128]{2,1,0:T(8,128)S(1)}, f32[2,80,128]{2,1,0:T(8,128)S(1)}, u32[]{:S(2)}, u32[]{:S(2)}) %collective-permute-start.16) | collective-permute-done | bytes 81952 | tf_op jit(solution)/shard_map/ppermute | solution.py:323
  85.0 0.3 shard_map.73
  85.3 2.0 %collective-permute-start.17 = (bf16[80,128]{1,0:T(8,128)(2,1)S(1)}, bf16[80,128]{1,0:T(8,128)(2,1)S(1)}, u32[]{:S(2)}, u32[]{:S(2)}) collective-permute-start(bf16[80,128]{1,0:T(8,128)(2,1)S(1)} %get-tuple-element.71), channel_id=1, source_target_pairs={{0,6},{1,7},{2,4},{3,5},{4,2},{5,3},{6,0},{7,1},{8,14},{9,15},{10,... | collective-permute-start | bytes 61448 | tf_op jit(solution)/shard_map/ppermute | solution.py:272
  87.4 2.8 %collective-permute-start.18 = (bf16[80,128]{1,0:T(8,128)(2,1)S(1)}, bf16[80,128]{1,0:T(8,128)(2,1)S(1)}, u32[]{:S(2)}, u32[]{:S(2)}) collective-permute-start(bf16[80,128]{1,0:T(8,128)(2,1)S(1)} %get-tuple-element.72), channel_id=1, source_target_pairs={{0,7},{1,6},{2,5},{3,4},{4,3},{5,2},{6,1},{7,0},{8,15},{9,14},{10,... | collective-permute-start | bytes 61448 | tf_op jit(solution)/shard_map/ppermute | solution.py:272
  90.2 2.3 %all-to-all-done.red_ref = bf16[16,40,896]{2,1,0:T(8,128)(2,1)S(1)} async-done(((bf16[16,40,896]{2,1,0:T(8,128)(2,1)}), bf16[16,40,896]{2,1,0:T(8,128)(2,1)S(1)}, u32[]{:S(2)}, u32[]{:S(2)}) %all-to-all-start) | async-done | bytes 1146912 | tf_op jit(solution)/shard_map/all_to_all | solution.py:324
  92.5 0.2 shard_map.75
  92.7 5.8 %collective-permute-start.24 = (bf16[20,896]{1,0:T(8,128)(2,1)S(1)}, bf16[20,896]{1,0:T(8,128)(2,1)S(1)}, u32[]{:S(2)}, u32[]{:S(2)}) collective-permute-start(bf16[20,896]{1,0:T(8,128)(2,1)S(1)} %get-tuple-element.80), channel_id=1, source_target_pairs={{0,8},{8,0},{16,24},{24,16},{32,40},{40,32},{48,56},{56,48},{64,72... | collective-permute-start | bytes 107528 | tf_op jit(solution)/shard_map/ppermute | solution.py:335
  98.5 2.2 %collective-permute-start.20 = (bf16[80,128]{1,0:T(8,128)(2,1)S(1)}, bf16[80,128]{1,0:T(8,128)(2,1)S(1)}, u32[]{:S(2)}, u32[]{:S(2)}) collective-permute-start(bf16[80,128]{1,0:T(8,128)(2,1)S(1)} %get-tuple-element.74), channel_id=1, source_target_pairs={{0,5},{1,4},{2,7},{3,6},{4,1},{5,0},{6,3},{7,2},{8,13},{9,12},{10,... | collective-permute-start | bytes 61448 | tf_op jit(solution)/shard_map/ppermute | solution.py:272
  100.7 1.3 %collective-permute-start.21 = (bf16[80,128]{1,0:T(8,128)(2,1)S(1)}, bf16[80,128]{1,0:T(8,128)(2,1)S(1)}, u32[]{:S(2)}, u32[]{:S(2)}) collective-permute-start(bf16[80,128]{1,0:T(8,128)(2,1)S(1)} %get-tuple-element.75), channel_id=1, source_target_pairs={{0,2},{1,3},{2,0},{3,1},{4,6},{5,7},{6,4},{7,5},{8,10},{9,11},{10,... | collective-permute-start | bytes 61448 | tf_op jit(solution)/shard_map/ppermute | solution.py:272
  102.0 0.9 collective-permute-start.22
  102.9 1.3 %collective-permute-done.20.refs_4_ = bf16[80,128]{1,0:T(8,128)(2,1)S(1)} collective-permute-done((bf16[80,128]{1,0:T(8,128)(2,1)S(1)}, bf16[80,128]{1,0:T(8,128)(2,1)S(1)}, u32[]{:S(2)}, u32[]{:S(2)}) %collective-permute-start.20) | collective-permute-done | bytes 20512 | tf_op jit(solution)/shard_map/ppermute | solution.py:272
  104.1 1.1 %collective-permute-done.22.refs_6_ = bf16[80,128]{1,0:T(8,128)(2,1)S(1)} collective-permute-done((bf16[80,128]{1,0:T(8,128)(2,1)S(1)}, bf16[80,128]{1,0:T(8,128)(2,1)S(1)}, u32[]{:S(2)}, u32[]{:S(2)}) %collective-permute-start.22) | collective-permute-done | bytes 20512 | tf_op jit(solution)/shard_map/ppermute | solution.py:272
  105.2 0.9 shard_map.74
  106.2 0.8 shard_map.76
  (25 shorter events, 0.1 us)
Async XLA Ops:
  0.6 0.9 copy-start.2
  1.6 0.9 copy-start.3
  2.5 0.8 copy-start.4
  3.7 9.7 %collective-permute-start = (bf16[336,128]{1,0:T(8,128)(2,1)S(1)}, bf16[336,128]{1,0:T(8,128)(2,1)S(1)}, u32[]{:S(2)}, u32[]{:S(2)}) collective-permute-start(bf16[336,128]{1,0:T(8,128)(2,1)S(1)} %get-tuple-element.44), channel_id=1, source_target_pairs={{0,6},{1,7},{2,4},{3,5},{4,2},{5,3},{6,0},{7,1},{8,14},{9,15},{10,... | collective-permute-start | bytes 258056 | tf_op jit(solution)/shard_map/ppermute | solution.py:272
  9.0 9.5 %collective-permute-start.1 = (bf16[336,128]{1,0:T(8,128)(2,1)S(1)}, bf16[336,128]{1,0:T(8,128)(2,1)S(1)}, u32[]{:S(2)}, u32[]{:S(2)}) collective-permute-start(bf16[336,128]{1,0:T(8,128)(2,1)S(1)} %get-tuple-element.45), channel_id=1, source_target_pairs={{0,7},{1,6},{2,5},{3,4},{4,3},{5,2},{6,1},{7,0},{8,15},{9,14},{10,... | collective-permute-start | bytes 258056 | tf_op jit(solution)/shard_map/ppermute | solution.py:272
  10.5 11.1 %collective-permute-start.2 = (bf16[336,128]{1,0:T(8,128)(2,1)S(1)}, bf16[336,128]{1,0:T(8,128)(2,1)S(1)}, u32[]{:S(2)}, u32[]{:S(2)}) collective-permute-start(bf16[336,128]{1,0:T(8,128)(2,1)S(1)} %get-tuple-element.46), channel_id=1, source_target_pairs={{0,4},{1,5},{2,6},{3,7},{4,0},{5,1},{6,2},{7,3},{8,12},{9,13},{10,... | collective-permute-start | bytes 258056 | tf_op jit(solution)/shard_map/ppermute | solution.py:272
  10.5 13.0 %collective-permute-start.3 = (bf16[336,128]{1,0:T(8,128)(2,1)S(1)}, bf16[336,128]{1,0:T(8,128)(2,1)S(1)}, u32[]{:S(2)}, u32[]{:S(2)}) collective-permute-start(bf16[336,128]{1,0:T(8,128)(2,1)S(1)} %get-tuple-element.47), channel_id=1, source_target_pairs={{0,5},{1,4},{2,7},{3,6},{4,1},{5,0},{6,3},{7,2},{8,13},{9,12},{10,... | collective-permute-start | bytes 258056 | tf_op jit(solution)/shard_map/ppermute | solution.py:272
  12.5 11.0 %collective-permute-start.4 = (bf16[336,128]{1,0:T(8,128)(2,1)S(1)}, bf16[336,128]{1,0:T(8,128)(2,1)S(1)}, u32[]{:S(2)}, u32[]{:S(2)}) collective-permute-start(bf16[336,128]{1,0:T(8,128)(2,1)S(1)} %get-tuple-element.48), channel_id=1, source_target_pairs={{0,2},{1,3},{2,0},{3,1},{4,6},{5,7},{6,4},{7,5},{8,10},{9,11},{10,... | collective-permute-start | bytes 258056 | tf_op jit(solution)/shard_map/ppermute | solution.py:272
  13.4 10.8 %collective-permute-start.5 = (bf16[336,128]{1,0:T(8,128)(2,1)S(1)}, bf16[336,128]{1,0:T(8,128)(2,1)S(1)}, u32[]{:S(2)}, u32[]{:S(2)}) collective-permute-start(bf16[336,128]{1,0:T(8,128)(2,1)S(1)} %get-tuple-element.49), channel_id=1, source_target_pairs={{0,3},{1,2},{2,1},{3,0},{4,7},{5,6},{6,5},{7,4},{8,11},{9,10},{10,... | collective-permute-start | bytes 258056 | tf_op jit(solution)/shard_map/ppermute | solution.py:272
  18.5 5.7 %collective-permute-start.6 = (bf16[336,128]{1,0:T(8,128)(2,1)S(1)}, bf16[336,128]{1,0:T(8,128)(2,1)S(1)}, u32[]{:S(2)}, u32[]{:S(2)}) collective-permute-start(bf16[336,128]{1,0:T(8,128)(2,1)S(1)} %get-tuple-element.50), channel_id=1, source_target_pairs={{0,1},{1,0},{2,3},{3,2},{4,5},{5,4},{6,7},{7,6},{8,9},{9,8},{10,11... | collective-permute-start | bytes 258056 | tf_op jit(solution)/shard_map/ppermute | solution.py:272
  25.0 10.7 %collective-permute-start.7 = (bf16[80,512]{1,0:T(8,128)(2,1)S(1)}, bf16[80,512]{1,0:T(8,128)(2,1)S(1)}, u32[]{:S(2)}, u32[]{:S(2)}) collective-permute-start(bf16[80,512]{1,0:T(8,128)(2,1)S(1)} %get-tuple-element.52), channel_id=1, source_target_pairs={{0,8},{8,16},{16,24},{24,32},{32,40},{40,48},{48,56},{56,64},{64,7... | collective-permute-start | bytes 245768 | tf_op jit(solution)/shard_map/ppermute | solution.py:302
  33.1 10.6 %collective-permute-start.8 = (bf16[80,256]{1,0:T(8,128)(2,1)S(1)}, bf16[80,256]{1,0:T(8,128)(2,1)S(1)}, u32[]{:S(2)}, u32[]{:S(2)}) collective-permute-start(bf16[80,256]{1,0:T(8,128)(2,1)S(1)} %get-tuple-element.53), channel_id=1, source_target_pairs={{8,0},{16,8},{24,16},{32,24},{40,32},{48,40},{56,48},{64,56},{72,6... | collective-permute-start | bytes 122888 | tf_op jit(solution)/shard_map/ppermute | solution.py:309
  35.7 1.2 %copy-start = (bf16[80,9,640]{2,0,1:T(8,128)(2,1)S(1)}, bf16[80,9,640]{2,0,1:T(8,128)(2,1)}, u32[]{:S(2)}) copy-start(bf16[80,9,640]{2,0,1:T(8,128)(2,1)} %param.5) | copy-start | bytes 2764804
  37.4 6.3 %collective-permute-start.9 = (bf16[80,256]{1,0:T(8,128)(2,1)S(1)}, bf16[80,256]{1,0:T(8,128)(2,1)S(1)}, u32[]{:S(2)}, u32[]{:S(2)}) collective-permute-start(bf16[80,256]{1,0:T(8,128)(2,1)S(1)} %get-tuple-element.56), channel_id=1, source_target_pairs={{0,6},{1,7},{2,4},{3,5},{4,2},{5,3},{6,0},{7,1},{8,14},{9,15},{10,... | collective-permute-start | bytes 122888 | tf_op jit(solution)/shard_map/ppermute | solution.py:272
  38.5 6.4 %collective-permute-start.10 = (bf16[80,256]{1,0:T(8,128)(2,1)S(1)}, bf16[80,256]{1,0:T(8,128)(2,1)S(1)}, u32[]{:S(2)}, u32[]{:S(2)}) collective-permute-start(bf16[80,256]{1,0:T(8,128)(2,1)S(1)} %get-tuple-element.57), channel_id=1, source_target_pairs={{0,7},{1,6},{2,5},{3,4},{4,3},{5,2},{6,1},{7,0},{8,15},{9,14},{10,... | collective-permute-start | bytes 122888 | tf_op jit(solution)/shard_map/ppermute | solution.py:272
  40.5 5.3 %collective-permute-start.11 = (bf16[80,256]{1,0:T(8,128)(2,1)S(1)}, bf16[80,256]{1,0:T(8,128)(2,1)S(1)}, u32[]{:S(2)}, u32[]{:S(2)}) collective-permute-start(bf16[80,256]{1,0:T(8,128)(2,1)S(1)} %get-tuple-element.58), channel_id=1, source_target_pairs={{0,4},{1,5},{2,6},{3,7},{4,0},{5,1},{6,2},{7,3},{8,12},{9,13},{10,... | collective-permute-start | bytes 122888 | tf_op jit(solution)/shard_map/ppermute | solution.py:272
  40.5 7.0 %collective-permute-start.12 = (bf16[80,256]{1,0:T(8,128)(2,1)S(1)}, bf16[80,256]{1,0:T(8,128)(2,1)S(1)}, u32[]{:S(2)}, u32[]{:S(2)}) collective-permute-start(bf16[80,256]{1,0:T(8,128)(2,1)S(1)} %get-tuple-element.59), channel_id=1, source_target_pairs={{0,5},{1,4},{2,7},{3,6},{4,1},{5,0},{6,3},{7,2},{8,13},{9,12},{10,... | collective-permute-start | bytes 122888 | tf_op jit(solution)/shard_map/ppermute | solution.py:272
  43.7 4.4 %collective-permute-start.13 = (bf16[80,256]{1,0:T(8,128)(2,1)S(1)}, bf16[80,256]{1,0:T(8,128)(2,1)S(1)}, u32[]{:S(2)}, u32[]{:S(2)}) collective-permute-start(bf16[80,256]{1,0:T(8,128)(2,1)S(1)} %get-tuple-element.60), channel_id=1, source_target_pairs={{0,2},{1,3},{2,0},{3,1},{4,6},{5,7},{6,4},{7,5},{8,10},{9,11},{10,... | collective-permute-start | bytes 122888 | tf_op jit(solution)/shard_map/ppermute | solution.py:272
  43.7 5.2 %collective-permute-start.14 = (bf16[80,256]{1,0:T(8,128)(2,1)S(1)}, bf16[80,256]{1,0:T(8,128)(2,1)S(1)}, u32[]{:S(2)}, u32[]{:S(2)}) collective-permute-start(bf16[80,256]{1,0:T(8,128)(2,1)S(1)} %get-tuple-element.61), channel_id=1, source_target_pairs={{0,3},{1,2},{2,1},{3,0},{4,7},{5,6},{6,5},{7,4},{8,11},{9,10},{10,... | collective-permute-start | bytes 122888 | tf_op jit(solution)/shard_map/ppermute | solution.py:272
  44.9 4.1 %collective-permute-start.15 = (bf16[80,256]{1,0:T(8,128)(2,1)S(1)}, bf16[80,256]{1,0:T(8,128)(2,1)S(1)}, u32[]{:S(2)}, u32[]{:S(2)}) collective-permute-start(bf16[80,256]{1,0:T(8,128)(2,1)S(1)} %get-tuple-element.62), channel_id=1, source_target_pairs={{0,1},{1,0},{2,3},{3,2},{4,5},{5,4},{6,7},{7,6},{8,9},{9,8},{10,11... | collective-permute-start | bytes 122888 | tf_op jit(solution)/shard_map/ppermute | solution.py:272
  66.9 8.3 %copy-start.1 = (bf16[80,9,640]{2,0,1:T(8,128)(2,1)S(1)}, bf16[80,9,640]{2,0,1:T(8,128)(2,1)}, u32[]{:S(2)}) copy-start(bf16[80,9,640]{2,0,1:T(8,128)(2,1)} %param.5) | copy-start | bytes 2764804
  66.9 25.6 %all-to-all-start = ((bf16[16,40,896]{2,1,0:T(8,128)(2,1)}), bf16[16,40,896]{2,1,0:T(8,128)(2,1)S(1)}, u32[]{:S(2)}, u32[]{:S(2)}) async-start(bf16[16,40,896]{2,1,0:T(8,128)(2,1)} %bitcast.9), calls=%async_computation | async-start | bytes 2293760 | tf_op jit(solution)/shard_map/all_to_all | solution.py:324
  75.6 9.4 %collective-permute-start.16 = (f32[2,80,128]{2,1,0:T(8,128)S(1)}, f32[2,80,128]{2,1,0:T(8,128)S(1)}, u32[]{:S(2)}, u32[]{:S(2)}) collective-permute-start(f32[2,80,128]{2,1,0:T(8,128)S(1)} %get-tuple-element.69), channel_id=1, source_target_pairs={{8,0},{16,8},{24,16},{32,24},{40,32},{48,40},{56,48},{64,56},{72,6... | collective-permute-start | bytes 245768 | tf_op jit(solution)/shard_map/ppermute | solution.py:323
  85.3 15.4 %collective-permute-start.17 = (bf16[80,128]{1,0:T(8,128)(2,1)S(1)}, bf16[80,128]{1,0:T(8,128)(2,1)S(1)}, u32[]{:S(2)}, u32[]{:S(2)}) collective-permute-start(bf16[80,128]{1,0:T(8,128)(2,1)S(1)} %get-tuple-element.71), channel_id=1, source_target_pairs={{0,6},{1,7},{2,4},{3,5},{4,2},{5,3},{6,0},{7,1},{8,14},{9,15},{10,... | collective-permute-start | bytes 61448 | tf_op jit(solution)/shard_map/ppermute | solution.py:272
  87.4 14.6 %collective-permute-start.18 = (bf16[80,128]{1,0:T(8,128)(2,1)S(1)}, bf16[80,128]{1,0:T(8,128)(2,1)S(1)}, u32[]{:S(2)}, u32[]{:S(2)}) collective-permute-start(bf16[80,128]{1,0:T(8,128)(2,1)S(1)} %get-tuple-element.72), channel_id=1, source_target_pairs={{0,7},{1,6},{2,5},{3,4},{4,3},{5,2},{6,1},{7,0},{8,15},{9,14},{10,... | collective-permute-start | bytes 61448 | tf_op jit(solution)/shard_map/ppermute | solution.py:272
  90.2 12.6 %collective-permute-start.19 = (bf16[80,128]{1,0:T(8,128)(2,1)S(1)}, bf16[80,128]{1,0:T(8,128)(2,1)S(1)}, u32[]{:S(2)}, u32[]{:S(2)}) collective-permute-start(bf16[80,128]{1,0:T(8,128)(2,1)S(1)} %get-tuple-element.73), channel_id=1, source_target_pairs={{0,4},{1,5},{2,6},{3,7},{4,0},{5,1},{6,2},{7,3},{8,12},{9,13},{10,... | collective-permute-start | bytes 61448 | tf_op jit(solution)/shard_map/ppermute | solution.py:272
  92.7 13.5 %collective-permute-start.24 = (bf16[20,896]{1,0:T(8,128)(2,1)S(1)}, bf16[20,896]{1,0:T(8,128)(2,1)S(1)}, u32[]{:S(2)}, u32[]{:S(2)}) collective-permute-start(bf16[20,896]{1,0:T(8,128)(2,1)S(1)} %get-tuple-element.80), channel_id=1, source_target_pairs={{0,8},{8,0},{16,24},{24,16},{32,40},{40,32},{48,56},{56,48},{64,72... | collective-permute-start | bytes 107528 | tf_op jit(solution)/shard_map/ppermute | solution.py:335
  98.5 5.7 %collective-permute-start.20 = (bf16[80,128]{1,0:T(8,128)(2,1)S(1)}, bf16[80,128]{1,0:T(8,128)(2,1)S(1)}, u32[]{:S(2)}, u32[]{:S(2)}) collective-permute-start(bf16[80,128]{1,0:T(8,128)(2,1)S(1)} %get-tuple-element.74), channel_id=1, source_target_pairs={{0,5},{1,4},{2,7},{3,6},{4,1},{5,0},{6,3},{7,2},{8,13},{9,12},{10,... | collective-permute-start | bytes 61448 | tf_op jit(solution)/shard_map/ppermute | solution.py:272
  100.7 3.4 %collective-permute-start.21 = (bf16[80,128]{1,0:T(8,128)(2,1)S(1)}, bf16[80,128]{1,0:T(8,128)(2,1)S(1)}, u32[]{:S(2)}, u32[]{:S(2)}) collective-permute-start(bf16[80,128]{1,0:T(8,128)(2,1)S(1)} %get-tuple-element.75), channel_id=1, source_target_pairs={{0,2},{1,3},{2,0},{3,1},{4,6},{5,7},{6,4},{7,5},{8,10},{9,11},{10,... | collective-permute-start | bytes 61448 | tf_op jit(solution)/shard_map/ppermute | solution.py:272
  102.0 3.2 %collective-permute-start.22 = (bf16[80,128]{1,0:T(8,128)(2,1)S(1)}, bf16[80,128]{1,0:T(8,128)(2,1)S(1)}, u32[]{:S(2)}, u32[]{:S(2)}) collective-permute-start(bf16[80,128]{1,0:T(8,128)(2,1)S(1)} %get-tuple-element.76), channel_id=1, source_target_pairs={{0,3},{1,2},{2,1},{3,0},{4,7},{5,6},{6,5},{7,4},{8,11},{9,10},{10,... | collective-permute-start | bytes 61448 | tf_op jit(solution)/shard_map/ppermute | solution.py:272
  102.9 2.4 %collective-permute-start.23 = (bf16[80,128]{1,0:T(8,128)(2,1)S(1)}, bf16[80,128]{1,0:T(8,128)(2,1)S(1)}, u32[]{:S(2)}, u32[]{:S(2)}) collective-permute-start(bf16[80,128]{1,0:T(8,128)(2,1)S(1)} %get-tuple-element.77), channel_id=1, source_target_pairs={{0,1},{1,0},{2,3},{3,2},{4,5},{5,4},{6,7},{7,6},{8,9},{9,8},{10,11... | collective-permute-start | bytes 61448 | tf_op jit(solution)/shard_map/ppermute | solution.py:272

commit v7 on v6

--- a/solution.py
+++ b/solution.py
@@ -10,7 +10,9 @@
 
 F32 = jnp.float32
 BF16 = jnp.bfloat16
-ORDER = (0, 6, 7, 4, 5, 2, 3, 1)
+ORDER = (0, 6, 4, 7, 5, 2, 3, 1)
+GATHERED = (0, 6, 4, 2, 1, 7, 5, 3)
+DIRECT = GATHERED[:5]
 FORWARD_FLOPS = 12_000_000_000
 
 
@@ -70,14 +72,18 @@
         block_ref[p, 160:176, :] = last[p].astype(BF16)
     for n, k in enumerate(ORDER):
         send_refs[n][0:176, :] = block_ref[slot_ref[0] ^ k]
-        for j in range(5):
+        for j in range(5 if k in DIRECT else 0):
             send_refs[n][176 + 32 * j : 208 + 32 * j, :] = cot_ref[:, 128 * j : 128 * j + 128]
 
 
 def spread_kernel(slot_ref, *refs):
     *recv_refs, win_ref, down_ref, up_ref, own_ref, cot_ref, cell_ref, tap_ref, block_ref = refs
     for n, k in enumerate(ORDER):
-        block_ref[slot_ref[0] ^ k] = recv_refs[n][...]
+        if k in DIRECT:
+            block_ref[slot_ref[0] ^ k] = recv_refs[n][...]
+        else:
+            block_ref[slot_ref[0] ^ k, 0:176, :] = recv_refs[n][...]
+            block_ref[slot_ref[0] ^ k, 176:336, :] = recv_refs[3 + GATHERED.index(k)][176:336, :]
     pixels = swap_blocks([block_ref[q, 0:80, :].astype(F32) for q in range(8)])
     for r in range(4):
         columns = (from_left(pixels[2 * r + 1]), pixels[2 * r], pixels[2 * r + 1])
@@ -160,10 +166,16 @@
     share_ref[80:160, 128:256] = up_ref[:, 128:256]
 
 
-def weight_grad_kernel(all_ref, win_ref, cot_ref, act_ref, red_ref, pre_ref, shift_ref, cell_ref):
-    for p in range(8):
+def weight_grad_kernel(slot_ref, win_ref, cot_ref, act_ref, *refs):
+    *all_refs, red_ref, pre_ref, shift_ref, cell_ref = refs
+    for n, k in enumerate(GATHERED):
+        start = pl.multiple_of(16 * (slot_ref[0] ^ k), 16)
         for g in range(5):
-            pre_ref[128 * g + 16 * p : 128 * g + 16 * p + 16, :] = all_ref[p, 16 * g : 16 * g + 16, :]
+            pre_ref[pl.ds(128 * g + start, 16), :] = all_refs[n][16 * g : 16 * g + 16, :]
+            for side in range(2):
+                cell_ref[pl.ds(128 * side + start, 16), 128 * g : 128 * g + 128] = all_refs[n][
+                    80 + 16 * g : 96 + 16 * g, 128 * side : 128 * side + 128
+                ]
     pre = pre_ref[...]
     red_ref[:, 0:640] = nt(pre, win_ref[0:640, :]).astype(BF16)
     rows = [act_ref[:, 128 * i : 128 * i + 128].astype(F32) for i in range(2)]
@@ -176,12 +188,6 @@
                 for i in range(2):
                     lanes = slice(128 * (i + 2 - u), 128 * (i + 2 - u) + 128)
                     shift_ref[g, base : base + 16, lanes] = moved[v][i][16 * g : 16 * g + 16]
-    for q in range(8):
-        for k in range(5):
-            for side in range(2):
-                cell_ref[128 * side + 16 * q : 128 * side + 16 * q + 16, 128 * k : 128 * k + 128] = all_ref[
-                    q, 80 + 16 * k : 96 + 16 * k, 128 * side : 128 * side + 128
-                ]
     eye = jnp.where(iota((128, 128), 0) == iota((128, 128), 1), 1.0, 0.0).astype(BF16)
     tail = jnp.concatenate([win_ref[640:720, :], jnp.zeros((176, 256), BF16)], axis=0)
     last = nt(pre, tail)
@@ -210,15 +216,15 @@
     img_ref[3] = lower_odd[0] + upper_odd[1]
     img_ref[6] = term(2, 1, 1)
     img_ref[7] = lower_odd[1]
-    up_ref[0] = upper_even[0]
-    up_ref[1] = upper_odd[0]
+    up_ref[0] = upper_even[0].astype(BF16)
+    up_ref[1] = upper_odd[0].astype(BF16)
 
 
 def return_kernel(slot_ref, img_ref, below_ref, *refs):
     *send_refs, slot_blocks = refs
     parts = [img_ref[k] for k in range(8)]
-    parts[6] = parts[6] + below_ref[0]
-    parts[7] = parts[7] + below_ref[1]
+    parts[6] = parts[6] + below_ref[0].astype(F32)
+    parts[7] = parts[7] + below_ref[1].astype(F32)
     for q, x in enumerate(swap_blocks(parts)):
         slot_blocks[slot_ref[0] ^ q] = x.astype(BF16)
     for n, k in enumerate(ORDER):
@@ -275,6 +281,15 @@
     return [blocks[0]] + moved
 
 
+def swap(block, k):
+    return lax.ppermute(block, "fsdp", [(i, i ^ k) for i in range(8)])
+
+
+def gather(block):
+    direct = [swap(block, k) for k in GATHERED[1:5]]
+    return [block] + direct + [swap(got, 1) for got in direct[:3]]
+
+
 def per_device(image, conv_weight, group_weight, cotangent):
     tiles = lax.axis_size("tile")
     downward = [(i, i + 1) for i in range(tiles - 1)]
@@ -287,15 +302,16 @@
     weights = conv_weight.transpose(1, 0, 2).reshape(720, 640)
     parts = trade(
         call(
-            pack_kernel, [((336, 128), BF16)] * 8,
+            pack_kernel, [((336 if k in DIRECT else 176, 128), BF16) for k in ORDER],
             slot, image.reshape(128, 640), group_weight.transpose(0, 2, 1), cells,
             scratch=[pltpu.VMEM((8, 176, 128), BF16)], smem=1,
         )
     )
+    passed = [swap(parts[ORDER.index(k)], 1) for k in GATHERED[1:4]]
     windows, down, up, own, cot = call(
         spread_kernel,
         [((720, 256), BF16), ((80, 512), BF16), ((80, 256), BF16), ((80, 256), F32), ((640, 256), BF16)],
-        slot, *parts,
+        slot, *parts, *passed,
         scratch=[pltpu.VMEM((256, 640), BF16), pltpu.VMEM((640, 256), BF16), pltpu.VMEM((8, 336, 128), BF16)],
         smem=1,
     )
@@ -310,15 +326,14 @@
     act, share = call(
         middle_kernel, [((80, 256), BF16), ((160, 256), BF16)], own, down, up, *hid
     )
-    share_all = lax.all_gather(share, "fsdp", axis=0, tiled=False)
     red, pre = call(
         weight_grad_kernel,
         [((640, 896), BF16), ((640, 256), BF16)],
-        share_all, windows, cot, act,
-        scratch=[pltpu.VMEM((5, 256, 512), BF16), pltpu.VMEM((256, 640), BF16)],
+        slot, windows, cot, act, *gather(share),
+        scratch=[pltpu.VMEM((5, 256, 512), BF16), pltpu.VMEM((256, 640), BF16)], smem=1,
     )
     img, img_up = call(
-        image_grad_kernel, [((8, 80, 128), F32), ((2, 80, 128), F32)], pre, weights
+        image_grad_kernel, [((8, 80, 128), F32), ((2, 80, 128), BF16)], pre, weights
     )
     img_below = lax.ppermute(img_up, "tile", upward)
     red = lax.all_to_all(

time: 107 us -> 103 us (0.963)
  blocking collectives: 15.2 us -> 0 us
  starting transfers between devices: 57 us -> 70.1 us
  waiting for transfers between devices: 22.9 us -> 21.4 us
  local copies, waits for them, and re-layouts: 3.79 us -> 2.69 us
    all_gather x1 -> x0, blocking collectives: 15.2 us -> none  [per_device(): share_all = lax.all_gather(share, 'fsdp', axis=0, tiled=False)]
    ppermute x0 -> x10, starting transfers between devices: none -> 11.9 us  [swap(): return lax.ppermute(block, 'fsdp', [(i, i ^ k) for i in range(8)])]
    ppermute x21, starting transfers between devices: 32.1 us -> 34.5 us  [trade(): lax.ppermute(block, 'fsdp', [(i, i ^ k) for i in range(8)])]
    all_to_all x1, waiting for transfers between devices: 2.26 us -> 0.9 us  [per_device(): lax.all_to_all(red.reshape(16, 40, 896), 'tile', 0, 0, tiled=True, axis_i...]
    ppermute x0 -> x10, waiting for transfers between devices: none -> 1.28 us  [swap(): return lax.ppermute(block, 'fsdp', [(i, i ^ k) for i in range(8)])]
    ppermute x21, waiting for transfers between devices: 11.4 us -> 10.3 us  [trade(): lax.ppermute(block, 'fsdp', [(i, i ^ k) for i in range(8)])]
    unnamed x10 -> x8, local copies, waits for them, and re-layouts: 3.79 us -> 2.69 us
  transfers between devices with their start and end apart: 26 -> 36, of which waited for: 12 -> 14; matrix products, arithmetic and copies ran while one was open for 0% -> 0% of each run, Pallas kernels for 2% -> 2%
where the time goes in v7:
time: 103 us; the launch traced here: 102 us
  starting transfers between devices  70.1 us (68%)
  waiting for transfers between devices  21.4 us (21%)
  Pallas kernels  7.21 us (7%)
  local copies, waits for them, and re-layouts  2.69 us (3%)
    ppermute x21, starting transfers between devices, trade(): lax.ppermute(block, 'fsdp', [(i, i ^ k) for i in range(8)])  34.5 us
    ppermute x10, starting transfers between devices, swap(): return lax.ppermute(block, 'fsdp', [(i, i ^ k) for i in range(8)])  11.9 us
    ppermute x21, waiting for transfers between devices, trade(): lax.ppermute(block, 'fsdp', [(i, i ^ k) for i in range(8)])  10.3 us
    all_to_all x1, starting transfers between devices, per_device(): lax.all_to_all(red.reshape(16, 40, 896), 'tile', 0, 0, tiled=True, axis_i...  7.77 us
    ppermute x1, starting transfers between devices, per_device(): down = lax.ppermute(down, 'tile', downward)  7.77 us
    ppermute x1, waiting for transfers between devices, per_device(): img_below = lax.ppermute(img_up, 'tile', upward)  7.65 us
    pallas_call x10, Pallas kernels, call(): pl.pallas_call(kernel, out_shape=[jax.ShapeDtypeStruct(shape, dtype) for...  7.21 us
    ppermute x1, starting transfers between devices, per_device(): given = lax.ppermute(give, 'tile', partners)  5.64 us
  transfers between devices with their start and end apart: 36, of which 14 were waited for; matrix products, arithmetic and copies ran while one was open for 0% of the time, Pallas kernels for 2%

profile of v7, /device:TPU:1, one launch (start us, length us, event | category | flops | bytes accessed | tf_op | source)
XLA Modules:
  0.0 102.2 jit_solution(10771666881865268928)
XLA Ops:
  0.7 1.0 copy-done.1
  1.7 0.9 copy-done.2
  2.6 0.8 copy-done.3
  3.3 0.5 shard_map.67
  3.8 5.3 %collective-permute-start = (bf16[336,128]{1,0:T(8,128)(2,1)S(1)}, bf16[336,128]{1,0:T(8,128)(2,1)S(1)}, u32[]{:S(2)}, u32[]{:S(2)}) collective-permute-start(bf16[336,128]{1,0:T(8,128)(2,1)S(1)} %get-tuple-element.44), channel_id=1, source_target_pairs={{0,6},{1,7},{2,4},{3,5},{4,2},{5,3},{6,0},{7,1},{8,14},{9,15},{10,... | collective-permute-start | bytes 258056 | tf_op jit(solution)/shard_map/ppermute | solution.py:278
  9.1 0.4 collective-permute-start.4
  9.5 4.6 %collective-permute-start.2 = (bf16[176,128]{1,0:T(8,128)(2,1)S(1)}, bf16[176,128]{1,0:T(8,128)(2,1)S(1)}, u32[]{:S(2)}, u32[]{:S(2)}) collective-permute-start(bf16[176,128]{1,0:T(8,128)(2,1)S(1)} %get-tuple-element.46), channel_id=1, source_target_pairs={{0,7},{1,6},{2,5},{3,4},{4,3},{5,2},{6,1},{7,0},{8,15},{9,14},{10,... | collective-permute-start | bytes 135176 | tf_op jit(solution)/shard_map/ppermute | solution.py:278
  14.0 3.6 %collective-permute-done.2.refs_3_ = bf16[176,128]{1,0:T(8,128)(2,1)S(1)} collective-permute-done((bf16[176,128]{1,0:T(8,128)(2,1)S(1)}, bf16[176,128]{1,0:T(8,128)(2,1)S(1)}, u32[]{:S(2)}, u32[]{:S(2)}) %collective-permute-start.2) | collective-permute-done | bytes 45088 | tf_op jit(solution)/shard_map/ppermute | solution.py:278
  17.7 0.5 collective-permute-start.7
  18.2 0.9 collective-permute-start.8
  19.1 0.9 collective-permute-done.3.refs_4_
  20.0 0.8 collective-permute-start.5
  20.8 2.8 %collective-permute-done.5.refs_6_ = bf16[176,128]{1,0:T(8,128)(2,1)S(1)} collective-permute-done((bf16[176,128]{1,0:T(8,128)(2,1)S(1)}, bf16[176,128]{1,0:T(8,128)(2,1)S(1)}, u32[]{:S(2)}, u32[]{:S(2)}) %collective-permute-start.5) | collective-permute-done | bytes 45088 | tf_op jit(solution)/shard_map/ppermute | solution.py:278
  23.6 0.8 shard_map.68
  24.5 7.8 %collective-permute-start.10 = (bf16[80,512]{1,0:T(8,128)(2,1)S(1)}, bf16[80,512]{1,0:T(8,128)(2,1)S(1)}, u32[]{:S(2)}, u32[]{:S(2)}) collective-permute-start(bf16[80,512]{1,0:T(8,128)(2,1)S(1)} %get-tuple-element.52), channel_id=1, source_target_pairs={{0,8},{8,16},{16,24},{24,32},{32,40},{40,48},{48,56},{56,64},{64,7... | collective-permute-start | bytes 245768 | tf_op jit(solution)/shard_map/ppermute | solution.py:318
  32.2 1.3 %collective-permute-start.11 = (bf16[80,256]{1,0:T(8,128)(2,1)S(1)}, bf16[80,256]{1,0:T(8,128)(2,1)S(1)}, u32[]{:S(2)}, u32[]{:S(2)}) collective-permute-start(bf16[80,256]{1,0:T(8,128)(2,1)S(1)} %get-tuple-element.56), channel_id=1, source_target_pairs={{8,0},{16,8},{24,16},{32,24},{40,32},{48,40},{56,48},{64,56},{72,6... | collective-permute-start | bytes 122888 | tf_op jit(solution)/shard_map/ppermute | solution.py:325
  33.5 0.7 collective-permute-done.10.down_ref
  34.2 0.5 shard_map.69
  34.8 2.9 %collective-permute-start.12 = (bf16[80,256]{1,0:T(8,128)(2,1)S(1)}, bf16[80,256]{1,0:T(8,128)(2,1)S(1)}, u32[]{:S(2)}, u32[]{:S(2)}) collective-permute-start(bf16[80,256]{1,0:T(8,128)(2,1)S(1)} %get-tuple-element.58), channel_id=1, source_target_pairs={{0,6},{1,7},{2,4},{3,5},{4,2},{5,3},{6,0},{7,1},{8,14},{9,15},{10,... | collective-permute-start | bytes 122888 | tf_op jit(solution)/shard_map/ppermute | solution.py:278
  37.7 3.7 %collective-permute-start.14 = (bf16[80,256]{1,0:T(8,128)(2,1)S(1)}, bf16[80,256]{1,0:T(8,128)(2,1)S(1)}, u32[]{:S(2)}, u32[]{:S(2)}) collective-permute-start(bf16[80,256]{1,0:T(8,128)(2,1)S(1)} %get-tuple-element.60), channel_id=1, source_target_pairs={{0,7},{1,6},{2,5},{3,4},{4,3},{5,2},{6,1},{7,0},{8,15},{9,14},{10,... | collective-permute-start | bytes 122888 | tf_op jit(solution)/shard_map/ppermute | solution.py:278
  41.4 0.5 collective-permute-done.11.up_ref
  41.9 2.3 %collective-permute-start.17 = (bf16[80,256]{1,0:T(8,128)(2,1)S(1)}, bf16[80,256]{1,0:T(8,128)(2,1)S(1)}, u32[]{:S(2)}, u32[]{:S(2)}) collective-permute-start(bf16[80,256]{1,0:T(8,128)(2,1)S(1)} %get-tuple-element.63), channel_id=1, source_target_pairs={{0,3},{1,2},{2,1},{3,0},{4,7},{5,6},{6,5},{7,4},{8,11},{9,10},{10,... | collective-permute-start | bytes 122888 | tf_op jit(solution)/shard_map/ppermute | solution.py:278
  44.2 2.1 %collective-permute-start.18 = (bf16[80,256]{1,0:T(8,128)(2,1)S(1)}, bf16[80,256]{1,0:T(8,128)(2,1)S(1)}, u32[]{:S(2)}, u32[]{:S(2)}) collective-permute-start(bf16[80,256]{1,0:T(8,128)(2,1)S(1)} %get-tuple-element.64), channel_id=1, source_target_pairs={{0,1},{1,0},{2,3},{3,2},{4,5},{5,4},{6,7},{7,6},{8,9},{9,8},{10,11... | collective-permute-start | bytes 122888 | tf_op jit(solution)/shard_map/ppermute | solution.py:278
  46.4 0.8 collective-permute-done.15.refs_4_
  47.1 0.5 collective-permute-done.17.refs_6_
  47.7 0.4 collective-permute-start.21
  48.1 1.9 %collective-permute-start.20 = (bf16[160,256]{1,0:T(8,128)(2,1)S(1)}, bf16[160,256]{1,0:T(8,128)(2,1)S(1)}, u32[]{:S(2)}, u32[]{:S(2)}) collective-permute-start(bf16[160,256]{1,0:T(8,128)(2,1)S(1)} %get-tuple-element.66.refs_0_), channel_id=1, source_target_pairs={{0,4},{1,5},{2,6},{3,7},{4,0},{5,1},{6,2},{7,3},{8,12},{9,13},{10,... | collective-permute-start | bytes 245768 | tf_op jit(solution)/shard_map/ppermute | solution.py:285
  50.1 1.3 %collective-permute-start.19 = (bf16[160,256]{1,0:T(8,128)(2,1)S(1)}, bf16[160,256]{1,0:T(8,128)(2,1)S(1)}, u32[]{:S(2)}, u32[]{:S(2)}) collective-permute-start(bf16[160,256]{1,0:T(8,128)(2,1)S(1)} %get-tuple-element.66.refs_0_), channel_id=1, source_target_pairs={{0,6},{1,7},{2,4},{3,5},{4,2},{5,3},{6,0},{7,1},{8,14},{9,15},{10,... | collective-permute-start | bytes 245768 | tf_op jit(solution)/shard_map/ppermute | solution.py:285
  51.4 1.6 %collective-permute-start.22 = (bf16[160,256]{1,0:T(8,128)(2,1)S(1)}, bf16[160,256]{1,0:T(8,128)(2,1)S(1)}, u32[]{:S(2)}, u32[]{:S(2)}) collective-permute-start(bf16[160,256]{1,0:T(8,128)(2,1)S(1)} %get-tuple-element.66.refs_0_), channel_id=1, source_target_pairs={{0,1},{1,0},{2,3},{3,2},{4,5},{5,4},{6,7},{7,6},{8,9},{9,8},{10,11... | collective-permute-start | bytes 245768 | tf_op jit(solution)/shard_map/ppermute | solution.py:285
  53.0 1.0 collective-permute-start.25
  53.9 4.3 %collective-permute-start.24 = (bf16[160,256]{1,0:T(8,128)(2,1)S(1)}, bf16[160,256]{1,0:T(8,128)(2,1)S(1)}, u32[]{:S(2)}, u32[]{:S(2)}) collective-permute-start(bf16[160,256]{1,0:T(8,128)(2,1)S(1)} %collective-permute-done.20.refs_2_), channel_id=1, source_target_pairs={{0,1},{1,0},{2,3},{3,2},{4,5},{5,4},{6,7},{7,6},{8,9},{9,8},{10,11... | collective-permute-start | bytes 245768 | tf_op jit(solution)/shard_map/ppermute | solution.py:285
  58.3 0.9 collective-permute-done.24.refs_6_
  59.2 0.4 collective-permute-done.23.refs_5_
  59.6 2.6 %shard_map.71 = (bf16[640,896]{1,0:T(8,128)(2,1)}, bf16[640,256]{1,0:T(8,128)(2,1)S(1)}) custom-call(s32[1]{0:T(128)} %bitcast.slot_ref, bf16[720,256]{1,0:T(8,128)(2,1)S(1)} %get-tuple-element.53.win_ref, bf16[640,256]{1,0:T(8,128)(2,1)S(1)} %get-tuple-element.54.cot_ref, bf16[80,256]{1,0:T(8,128)(2,1)S(1)} %get-tuple-element.65.act_ref, ...), custom_call_target="tpu_custom_call" | custom-call | tf_op jit(solution)/shard_map/pallas_call | solution.py:265
  62.2 7.8 %all-to-all-start = ((bf16[16,40,896]{2,1,0:T(8,128)(2,1)}), bf16[16,40,896]{2,1,0:T(8,128)(2,1)S(1)}, u32[]{:S(2)}, u32[]{:S(2)}) async-start(bf16[16,40,896]{2,1,0:T(8,128)(2,1)} %bitcast.8), calls=%async_computation | async-start | bytes 2293760 | tf_op jit(solution)/shard_map/all_to_all | solution.py:339
  69.9 0.5 shard_map.72
  70.4 1.3 %collective-permute-start.26 = (bf16[2,80,128]{2,1,0:T(8,128)(2,1)S(1)}, bf16[2,80,128]{2,1,0:T(8,128)(2,1)S(1)}, u32[]{:S(2)}, u32[]{:S(2)}) collective-permute-start(bf16[2,80,128]{2,1,0:T(8,128)(2,1)S(1)} %get-tuple-element.69), channel_id=1, source_target_pairs={{8,0},{16,8},{24,16},{32,24},{40,32},{48,40},{56,48},{64,56},{72,6... | collective-permute-start | bytes 122888 | tf_op jit(solution)/shard_map/ppermute | solution.py:338
  71.7 7.6 %collective-permute-done.26.below_ref = bf16[2,80,128]{2,1,0:T(8,128)(2,1)S(1)} collective-permute-done((bf16[2,80,128]{2,1,0:T(8,128)(2,1)S(1)}, bf16[2,80,128]{2,1,0:T(8,128)(2,1)S(1)}, u32[]{:S(2)}, u32[]{:S(2)}) %collective-permute-start.26) | collective-permute-done | bytes 40992 | tf_op jit(solution)/shard_map/ppermute | solution.py:338
  79.7 2.3 %collective-permute-start.27 = (bf16[80,128]{1,0:T(8,128)(2,1)S(1)}, bf16[80,128]{1,0:T(8,128)(2,1)S(1)}, u32[]{:S(2)}, u32[]{:S(2)}) collective-permute-start(bf16[80,128]{1,0:T(8,128)(2,1)S(1)} %get-tuple-element.71), channel_id=1, source_target_pairs={{0,6},{1,7},{2,4},{3,5},{4,2},{5,3},{6,0},{7,1},{8,14},{9,15},{10,... | collective-permute-start | bytes 61448 | tf_op jit(solution)/shard_map/ppermute | solution.py:278
  82.2 4.2 %collective-permute-start.29 = (bf16[80,128]{1,0:T(8,128)(2,1)S(1)}, bf16[80,128]{1,0:T(8,128)(2,1)S(1)}, u32[]{:S(2)}, u32[]{:S(2)}) collective-permute-start(bf16[80,128]{1,0:T(8,128)(2,1)S(1)} %get-tuple-element.73), channel_id=1, source_target_pairs={{0,7},{1,6},{2,5},{3,4},{4,3},{5,2},{6,1},{7,0},{8,15},{9,14},{10,... | collective-permute-start | bytes 61448 | tf_op jit(solution)/shard_map/ppermute | solution.py:278
  86.4 0.9 all-to-all-done.red_ref
  87.4 5.6 %collective-permute-start.34 = (bf16[20,896]{1,0:T(8,128)(2,1)S(1)}, bf16[20,896]{1,0:T(8,128)(2,1)S(1)}, u32[]{:S(2)}, u32[]{:S(2)}) collective-permute-start(bf16[20,896]{1,0:T(8,128)(2,1)S(1)} %get-tuple-element.80), channel_id=1, source_target_pairs={{0,8},{8,0},{16,24},{24,16},{32,40},{40,32},{48,56},{56,48},{64,72... | collective-permute-start | bytes 107528 | tf_op jit(solution)/shard_map/ppermute | solution.py:350
  93.1 3.8 %collective-permute-start.30 = (bf16[80,128]{1,0:T(8,128)(2,1)S(1)}, bf16[80,128]{1,0:T(8,128)(2,1)S(1)}, u32[]{:S(2)}, u32[]{:S(2)}) collective-permute-start(bf16[80,128]{1,0:T(8,128)(2,1)S(1)} %get-tuple-element.74), channel_id=1, source_target_pairs={{0,5},{1,4},{2,7},{3,6},{4,1},{5,0},{6,3},{7,2},{8,13},{9,12},{10,... | collective-permute-start | bytes 61448 | tf_op jit(solution)/shard_map/ppermute | solution.py:278
  97.3 1.5 %collective-permute-start.33 = (bf16[80,128]{1,0:T(8,128)(2,1)S(1)}, bf16[80,128]{1,0:T(8,128)(2,1)S(1)}, u32[]{:S(2)}, u32[]{:S(2)}) collective-permute-start(bf16[80,128]{1,0:T(8,128)(2,1)S(1)} %get-tuple-element.77), channel_id=1, source_target_pairs={{0,1},{1,0},{2,3},{3,2},{4,5},{5,4},{6,7},{7,6},{8,9},{9,8},{10,11... | collective-permute-start | bytes 61448 | tf_op jit(solution)/shard_map/ppermute | solution.py:278
  98.8 0.6 collective-permute-done.30.refs_4_
  99.5 0.9 collective-permute-done.32.refs_6_
  100.5 0.9 shard_map.74
  101.4 0.8 shard_map.76
  (42 shorter events, 1.3 us)
Async XLA Ops:
  0.6 33.6 %copy-start = (bf16[80,9,640]{2,0,1:T(8,128)(2,1)S(1)}, bf16[80,9,640]{2,0,1:T(8,128)(2,1)}, u32[]{:S(2)}) copy-start(bf16[80,9,640]{2,0,1:T(8,128)(2,1)} %param.5) | copy-start | bytes 2764804
  0.6 1.0 copy-start.1
  1.6 0.9 copy-start.2
  2.6 0.8 copy-start.3
  3.8 13.8 %collective-permute-start = (bf16[336,128]{1,0:T(8,128)(2,1)S(1)}, bf16[336,128]{1,0:T(8,128)(2,1)S(1)}, u32[]{:S(2)}, u32[]{:S(2)}) collective-permute-start(bf16[336,128]{1,0:T(8,128)(2,1)S(1)} %get-tuple-element.44), channel_id=1, source_target_pairs={{0,6},{1,7},{2,4},{3,5},{4,2},{5,3},{6,0},{7,1},{8,14},{9,15},{10,... | collective-permute-start | bytes 258056 | tf_op jit(solution)/shard_map/ppermute | solution.py:278
  9.1 9.1 %collective-permute-start.1 = (bf16[336,128]{1,0:T(8,128)(2,1)S(1)}, bf16[336,128]{1,0:T(8,128)(2,1)S(1)}, u32[]{:S(2)}, u32[]{:S(2)}) collective-permute-start(bf16[336,128]{1,0:T(8,128)(2,1)S(1)} %get-tuple-element.45), channel_id=1, source_target_pairs={{0,4},{1,5},{2,6},{3,7},{4,0},{5,1},{6,2},{7,3},{8,12},{9,13},{10,... | collective-permute-start | bytes 258056 | tf_op jit(solution)/shard_map/ppermute | solution.py:278
  9.1 10.0 %collective-permute-start.4 = (bf16[336,128]{1,0:T(8,128)(2,1)S(1)}, bf16[336,128]{1,0:T(8,128)(2,1)S(1)}, u32[]{:S(2)}, u32[]{:S(2)}) collective-permute-start(bf16[336,128]{1,0:T(8,128)(2,1)S(1)} %get-tuple-element.48), channel_id=1, source_target_pairs={{0,2},{1,3},{2,0},{3,1},{4,6},{5,7},{6,4},{7,5},{8,10},{9,11},{10,... | collective-permute-start | bytes 258056 | tf_op jit(solution)/shard_map/ppermute | solution.py:278
  9.5 8.2 %collective-permute-start.2 = (bf16[176,128]{1,0:T(8,128)(2,1)S(1)}, bf16[176,128]{1,0:T(8,128)(2,1)S(1)}, u32[]{:S(2)}, u32[]{:S(2)}) collective-permute-start(bf16[176,128]{1,0:T(8,128)(2,1)S(1)} %get-tuple-element.46), channel_id=1, source_target_pairs={{0,7},{1,6},{2,5},{3,4},{4,3},{5,2},{6,1},{7,0},{8,15},{9,14},{10,... | collective-permute-start | bytes 135176 | tf_op jit(solution)/shard_map/ppermute | solution.py:278
  14.0 5.9 %collective-permute-start.3 = (bf16[176,128]{1,0:T(8,128)(2,1)S(1)}, bf16[176,128]{1,0:T(8,128)(2,1)S(1)}, u32[]{:S(2)}, u32[]{:S(2)}) collective-permute-start(bf16[176,128]{1,0:T(8,128)(2,1)S(1)} %get-tuple-element.47), channel_id=1, source_target_pairs={{0,5},{1,4},{2,7},{3,6},{4,1},{5,0},{6,3},{7,2},{8,13},{9,12},{10,... | collective-permute-start | bytes 135176 | tf_op jit(solution)/shard_map/ppermute | solution.py:278
  17.7 5.9 %collective-permute-start.6 = (bf16[336,128]{1,0:T(8,128)(2,1)S(1)}, bf16[336,128]{1,0:T(8,128)(2,1)S(1)}, u32[]{:S(2)}, u32[]{:S(2)}) collective-permute-start(bf16[336,128]{1,0:T(8,128)(2,1)S(1)} %get-tuple-element.50), channel_id=1, source_target_pairs={{0,1},{1,0},{2,3},{3,2},{4,5},{5,4},{6,7},{7,6},{8,9},{9,8},{10,11... | collective-permute-start | bytes 258056 | tf_op jit(solution)/shard_map/ppermute | solution.py:278
  17.7 5.9 %collective-permute-start.7 = (bf16[336,128]{1,0:T(8,128)(2,1)S(1)}, bf16[336,128]{1,0:T(8,128)(2,1)S(1)}, u32[]{:S(2)}, u32[]{:S(2)}) collective-permute-start(bf16[336,128]{1,0:T(8,128)(2,1)S(1)} %collective-permute-done.refs_1_), channel_id=1, source_target_pairs={{0,1},{1,0},{2,3},{3,2},{4,5},{5,4},{6,7},{7,6},{8,9},{9,8},{10,11... | collective-permute-start | bytes 258056 | tf_op jit(solution)/shard_map/ppermute | solution.py:285
  18.2 5.4 %collective-permute-start.8 = (bf16[336,128]{1,0:T(8,128)(2,1)S(1)}, bf16[336,128]{1,0:T(8,128)(2,1)S(1)}, u32[]{:S(2)}, u32[]{:S(2)}) collective-permute-start(bf16[336,128]{1,0:T(8,128)(2,1)S(1)} %collective-permute-done.1.refs_2_), channel_id=1, source_target_pairs={{0,1},{1,0},{2,3},{3,2},{4,5},{5,4},{6,7},{7,6},{8,9},{9,8},{10,11... | collective-permute-start | bytes 258056 | tf_op jit(solution)/shard_map/ppermute | solution.py:285
  19.1 4.6 %collective-permute-start.9 = (bf16[336,128]{1,0:T(8,128)(2,1)S(1)}, bf16[336,128]{1,0:T(8,128)(2,1)S(1)}, u32[]{:S(2)}, u32[]{:S(2)}) collective-permute-start(bf16[336,128]{1,0:T(8,128)(2,1)S(1)} %collective-permute-done.4.refs_5_), channel_id=1, source_target_pairs={{0,1},{1,0},{2,3},{3,2},{4,5},{5,4},{6,7},{7,6},{8,9},{9,8},{10,11... | collective-permute-start | bytes 258056 | tf_op jit(solution)/shard_map/ppermute | solution.py:285
  20.0 3.6 %collective-permute-start.5 = (bf16[176,128]{1,0:T(8,128)(2,1)S(1)}, bf16[176,128]{1,0:T(8,128)(2,1)S(1)}, u32[]{:S(2)}, u32[]{:S(2)}) collective-permute-start(bf16[176,128]{1,0:T(8,128)(2,1)S(1)} %get-tuple-element.49), channel_id=1, source_target_pairs={{0,3},{1,2},{2,1},{3,0},{4,7},{5,6},{6,5},{7,4},{8,11},{9,10},{10,... | collective-permute-start | bytes 135176 | tf_op jit(solution)/shard_map/ppermute | solution.py:278
  24.5 9.8 %collective-permute-start.10 = (bf16[80,512]{1,0:T(8,128)(2,1)S(1)}, bf16[80,512]{1,0:T(8,128)(2,1)S(1)}, u32[]{:S(2)}, u32[]{:S(2)}) collective-permute-start(bf16[80,512]{1,0:T(8,128)(2,1)S(1)} %get-tuple-element.52), channel_id=1, source_target_pairs={{0,8},{8,16},{16,24},{24,32},{32,40},{40,48},{48,56},{56,64},{64,7... | collective-permute-start | bytes 245768 | tf_op jit(solution)/shard_map/ppermute | solution.py:318
  32.2 9.7 %collective-permute-start.11 = (bf16[80,256]{1,0:T(8,128)(2,1)S(1)}, bf16[80,256]{1,0:T(8,128)(2,1)S(1)}, u32[]{:S(2)}, u32[]{:S(2)}) collective-permute-start(bf16[80,256]{1,0:T(8,128)(2,1)S(1)} %get-tuple-element.56), channel_id=1, source_target_pairs={{8,0},{16,8},{24,16},{32,24},{40,32},{48,40},{56,48},{64,56},{72,6... | collective-permute-start | bytes 122888 | tf_op jit(solution)/shard_map/ppermute | solution.py:325
  34.8 7.2 %collective-permute-start.12 = (bf16[80,256]{1,0:T(8,128)(2,1)S(1)}, bf16[80,256]{1,0:T(8,128)(2,1)S(1)}, u32[]{:S(2)}, u32[]{:S(2)}) collective-permute-start(bf16[80,256]{1,0:T(8,128)(2,1)S(1)} %get-tuple-element.58), channel_id=1, source_target_pairs={{0,6},{1,7},{2,4},{3,5},{4,2},{5,3},{6,0},{7,1},{8,14},{9,15},{10,... | collective-permute-start | bytes 122888 | tf_op jit(solution)/shard_map/ppermute | solution.py:278
  37.7 6.6 %collective-permute-start.13 = (bf16[80,256]{1,0:T(8,128)(2,1)S(1)}, bf16[80,256]{1,0:T(8,128)(2,1)S(1)}, u32[]{:S(2)}, u32[]{:S(2)}) collective-permute-start(bf16[80,256]{1,0:T(8,128)(2,1)S(1)} %get-tuple-element.59), channel_id=1, source_target_pairs={{0,4},{1,5},{2,6},{3,7},{4,0},{5,1},{6,2},{7,3},{8,12},{9,13},{10,... | collective-permute-start | bytes 122888 | tf_op jit(solution)/shard_map/ppermute | solution.py:278
  37.7 8.7 %collective-permute-start.14 = (bf16[80,256]{1,0:T(8,128)(2,1)S(1)}, bf16[80,256]{1,0:T(8,128)(2,1)S(1)}, u32[]{:S(2)}, u32[]{:S(2)}) collective-permute-start(bf16[80,256]{1,0:T(8,128)(2,1)S(1)} %get-tuple-element.60), channel_id=1, source_target_pairs={{0,7},{1,6},{2,5},{3,4},{4,3},{5,2},{6,1},{7,0},{8,15},{9,14},{10,... | collective-permute-start | bytes 122888 | tf_op jit(solution)/shard_map/ppermute | solution.py:278
  41.4 5.8 %collective-permute-start.15 = (bf16[80,256]{1,0:T(8,128)(2,1)S(1)}, bf16[80,256]{1,0:T(8,128)(2,1)S(1)}, u32[]{:S(2)}, u32[]{:S(2)}) collective-permute-start(bf16[80,256]{1,0:T(8,128)(2,1)S(1)} %get-tuple-element.61), channel_id=1, source_target_pairs={{0,5},{1,4},{2,7},{3,6},{4,1},{5,0},{6,3},{7,2},{8,13},{9,12},{10,... | collective-permute-start | bytes 122888 | tf_op jit(solution)/shard_map/ppermute | solution.py:278
  41.9 5.2 %collective-permute-start.16 = (bf16[80,256]{1,0:T(8,128)(2,1)S(1)}, bf16[80,256]{1,0:T(8,128)(2,1)S(1)}, u32[]{:S(2)}, u32[]{:S(2)}) collective-permute-start(bf16[80,256]{1,0:T(8,128)(2,1)S(1)} %get-tuple-element.62), channel_id=1, source_target_pairs={{0,2},{1,3},{2,0},{3,1},{4,6},{5,7},{6,4},{7,5},{8,10},{9,11},{10,... | collective-permute-start | bytes 122888 | tf_op jit(solution)/shard_map/ppermute | solution.py:278
  41.9 5.7 %collective-permute-start.17 = (bf16[80,256]{1,0:T(8,128)(2,1)S(1)}, bf16[80,256]{1,0:T(8,128)(2,1)S(1)}, u32[]{:S(2)}, u32[]{:S(2)}) collective-permute-start(bf16[80,256]{1,0:T(8,128)(2,1)S(1)} %get-tuple-element.63), channel_id=1, source_target_pairs={{0,3},{1,2},{2,1},{3,0},{4,7},{5,6},{6,5},{7,4},{8,11},{9,10},{10,... | collective-permute-start | bytes 122888 | tf_op jit(solution)/shard_map/ppermute | solution.py:278
  44.2 3.4 %collective-permute-start.18 = (bf16[80,256]{1,0:T(8,128)(2,1)S(1)}, bf16[80,256]{1,0:T(8,128)(2,1)S(1)}, u32[]{:S(2)}, u32[]{:S(2)}) collective-permute-start(bf16[80,256]{1,0:T(8,128)(2,1)S(1)} %get-tuple-element.64), channel_id=1, source_target_pairs={{0,1},{1,0},{2,3},{3,2},{4,5},{5,4},{6,7},{7,6},{8,9},{9,8},{10,11... | collective-permute-start | bytes 122888 | tf_op jit(solution)/shard_map/ppermute | solution.py:278
  47.7 5.2 %collective-permute-start.21 = (bf16[160,256]{1,0:T(8,128)(2,1)S(1)}, bf16[160,256]{1,0:T(8,128)(2,1)S(1)}, u32[]{:S(2)}, u32[]{:S(2)}) collective-permute-start(bf16[160,256]{1,0:T(8,128)(2,1)S(1)} %get-tuple-element.66.refs_0_), channel_id=1, source_target_pairs={{0,2},{1,3},{2,0},{3,1},{4,6},{5,7},{6,4},{7,5},{8,10},{9,11},{10,... | collective-permute-start | bytes 245768 | tf_op jit(solution)/shard_map/ppermute | solution.py:285
  48.1 5.8 %collective-permute-start.20 = (bf16[160,256]{1,0:T(8,128)(2,1)S(1)}, bf16[160,256]{1,0:T(8,128)(2,1)S(1)}, u32[]{:S(2)}, u32[]{:S(2)}) collective-permute-start(bf16[160,256]{1,0:T(8,128)(2,1)S(1)} %get-tuple-element.66.refs_0_), channel_id=1, source_target_pairs={{0,4},{1,5},{2,6},{3,7},{4,0},{5,1},{6,2},{7,3},{8,12},{9,13},{10,... | collective-permute-start | bytes 245768 | tf_op jit(solution)/shard_map/ppermute | solution.py:285
  50.1 8.2 %collective-permute-start.19 = (bf16[160,256]{1,0:T(8,128)(2,1)S(1)}, bf16[160,256]{1,0:T(8,128)(2,1)S(1)}, u32[]{:S(2)}, u32[]{:S(2)}) collective-permute-start(bf16[160,256]{1,0:T(8,128)(2,1)S(1)} %get-tuple-element.66.refs_0_), channel_id=1, source_target_pairs={{0,6},{1,7},{2,4},{3,5},{4,2},{5,3},{6,0},{7,1},{8,14},{9,15},{10,... | collective-permute-start | bytes 245768 | tf_op jit(solution)/shard_map/ppermute | solution.py:285
  51.4 6.9 %collective-permute-start.22 = (bf16[160,256]{1,0:T(8,128)(2,1)S(1)}, bf16[160,256]{1,0:T(8,128)(2,1)S(1)}, u32[]{:S(2)}, u32[]{:S(2)}) collective-permute-start(bf16[160,256]{1,0:T(8,128)(2,1)S(1)} %get-tuple-element.66.refs_0_), channel_id=1, source_target_pairs={{0,1},{1,0},{2,3},{3,2},{4,5},{5,4},{6,7},{7,6},{8,9},{9,8},{10,11... | collective-permute-start | bytes 245768 | tf_op jit(solution)/shard_map/ppermute | solution.py:285
  53.0 5.3 %collective-permute-start.25 = (bf16[160,256]{1,0:T(8,128)(2,1)S(1)}, bf16[160,256]{1,0:T(8,128)(2,1)S(1)}, u32[]{:S(2)}, u32[]{:S(2)}) collective-permute-start(bf16[160,256]{1,0:T(8,128)(2,1)S(1)} %collective-permute-done.21.refs_3_), channel_id=1, source_target_pairs={{0,1},{1,0},{2,3},{3,2},{4,5},{5,4},{6,7},{7,6},{8,9},{9,8},{10,11... | collective-permute-start | bytes 245768 | tf_op jit(solution)/shard_map/ppermute | solution.py:285
  53.9 5.3 %collective-permute-start.24 = (bf16[160,256]{1,0:T(8,128)(2,1)S(1)}, bf16[160,256]{1,0:T(8,128)(2,1)S(1)}, u32[]{:S(2)}, u32[]{:S(2)}) collective-permute-start(bf16[160,256]{1,0:T(8,128)(2,1)S(1)} %collective-permute-done.20.refs_2_), channel_id=1, source_target_pairs={{0,1},{1,0},{2,3},{3,2},{4,5},{5,4},{6,7},{7,6},{8,9},{9,8},{10,11... | collective-permute-start | bytes 245768 | tf_op jit(solution)/shard_map/ppermute | solution.py:285
  58.3 1.3 %collective-permute-start.23 = (bf16[160,256]{1,0:T(8,128)(2,1)S(1)}, bf16[160,256]{1,0:T(8,128)(2,1)S(1)}, u32[]{:S(2)}, u32[]{:S(2)}) collective-permute-start(bf16[160,256]{1,0:T(8,128)(2,1)S(1)} %collective-permute-done.19.refs_1_), channel_id=1, source_target_pairs={{0,1},{1,0},{2,3},{3,2},{4,5},{5,4},{6,7},{7,6},{8,9},{9,8},{10,11... | collective-permute-start | bytes 245768 | tf_op jit(solution)/shard_map/ppermute | solution.py:285
  62.2 25.1 %all-to-all-start = ((bf16[16,40,896]{2,1,0:T(8,128)(2,1)}), bf16[16,40,896]{2,1,0:T(8,128)(2,1)S(1)}, u32[]{:S(2)}, u32[]{:S(2)}) async-start(bf16[16,40,896]{2,1,0:T(8,128)(2,1)} %bitcast.8), calls=%async_computation | async-start | bytes 2293760 | tf_op jit(solution)/shard_map/all_to_all | solution.py:339
  70.4 8.9 %collective-permute-start.26 = (bf16[2,80,128]{2,1,0:T(8,128)(2,1)S(1)}, bf16[2,80,128]{2,1,0:T(8,128)(2,1)S(1)}, u32[]{:S(2)}, u32[]{:S(2)}) collective-permute-start(bf16[2,80,128]{2,1,0:T(8,128)(2,1)S(1)} %get-tuple-element.69), channel_id=1, source_target_pairs={{8,0},{16,8},{24,16},{32,24},{40,32},{48,40},{56,48},{64,56},{72,6... | collective-permute-start | bytes 122888 | tf_op jit(solution)/shard_map/ppermute | solution.py:338
  79.7 17.2 %collective-permute-start.27 = (bf16[80,128]{1,0:T(8,128)(2,1)S(1)}, bf16[80,128]{1,0:T(8,128)(2,1)S(1)}, u32[]{:S(2)}, u32[]{:S(2)}) collective-permute-start(bf16[80,128]{1,0:T(8,128)(2,1)S(1)} %get-tuple-element.71), channel_id=1, source_target_pairs={{0,6},{1,7},{2,4},{3,5},{4,2},{5,3},{6,0},{7,1},{8,14},{9,15},{10,... | collective-permute-start | bytes 61448 | tf_op jit(solution)/shard_map/ppermute | solution.py:278
  82.0 15.2 %collective-permute-start.28 = (bf16[80,128]{1,0:T(8,128)(2,1)S(1)}, bf16[80,128]{1,0:T(8,128)(2,1)S(1)}, u32[]{:S(2)}, u32[]{:S(2)}) collective-permute-start(bf16[80,128]{1,0:T(8,128)(2,1)S(1)} %get-tuple-element.72), channel_id=1, source_target_pairs={{0,4},{1,5},{2,6},{3,7},{4,0},{5,1},{6,2},{7,3},{8,12},{9,13},{10,... | collective-permute-start | bytes 61448 | tf_op jit(solution)/shard_map/ppermute | solution.py:278
  82.2 15.1 %collective-permute-start.29 = (bf16[80,128]{1,0:T(8,128)(2,1)S(1)}, bf16[80,128]{1,0:T(8,128)(2,1)S(1)}, u32[]{:S(2)}, u32[]{:S(2)}) collective-permute-start(bf16[80,128]{1,0:T(8,128)(2,1)S(1)} %get-tuple-element.73), channel_id=1, source_target_pairs={{0,7},{1,6},{2,5},{3,4},{4,3},{5,2},{6,1},{7,0},{8,15},{9,14},{10,... | collective-permute-start | bytes 61448 | tf_op jit(solution)/shard_map/ppermute | solution.py:278
  87.4 13.9 %collective-permute-start.34 = (bf16[20,896]{1,0:T(8,128)(2,1)S(1)}, bf16[20,896]{1,0:T(8,128)(2,1)S(1)}, u32[]{:S(2)}, u32[]{:S(2)}) collective-permute-start(bf16[20,896]{1,0:T(8,128)(2,1)S(1)} %get-tuple-element.80), channel_id=1, source_target_pairs={{0,8},{8,0},{16,24},{24,16},{32,40},{40,32},{48,56},{56,48},{64,72... | collective-permute-start | bytes 107528 | tf_op jit(solution)/shard_map/ppermute | solution.py:350
  93.1 6.3 %collective-permute-start.30 = (bf16[80,128]{1,0:T(8,128)(2,1)S(1)}, bf16[80,128]{1,0:T(8,128)(2,1)S(1)}, u32[]{:S(2)}, u32[]{:S(2)}) collective-permute-start(bf16[80,128]{1,0:T(8,128)(2,1)S(1)} %get-tuple-element.74), channel_id=1, source_target_pairs={{0,5},{1,4},{2,7},{3,6},{4,1},{5,0},{6,3},{7,2},{8,13},{9,12},{10,... | collective-permute-start | bytes 61448 | tf_op jit(solution)/shard_map/ppermute | solution.py:278
  96.9 2.7 %collective-permute-start.31 = (bf16[80,128]{1,0:T(8,128)(2,1)S(1)}, bf16[80,128]{1,0:T(8,128)(2,1)S(1)}, u32[]{:S(2)}, u32[]{:S(2)}) collective-permute-start(bf16[80,128]{1,0:T(8,128)(2,1)S(1)} %get-tuple-element.75), channel_id=1, source_target_pairs={{0,2},{1,3},{2,0},{3,1},{4,6},{5,7},{6,4},{7,5},{8,10},{9,11},{10,... | collective-permute-start | bytes 61448 | tf_op jit(solution)/shard_map/ppermute | solution.py:278
  97.2 3.2 %collective-permute-start.32 = (bf16[80,128]{1,0:T(8,128)(2,1)S(1)}, bf16[80,128]{1,0:T(8,128)(2,1)S(1)}, u32[]{:S(2)}, u32[]{:S(2)}) collective-permute-start(bf16[80,128]{1,0:T(8,128)(2,1)S(1)} %get-tuple-element.76), channel_id=1, source_target_pairs={{0,3},{1,2},{2,1},{3,0},{4,7},{5,6},{6,5},{7,4},{8,11},{9,10},{10,... | collective-permute-start | bytes 61448 | tf_op jit(solution)/shard_map/ppermute | solution.py:278
  97.3 3.2 %collective-permute-start.33 = (bf16[80,128]{1,0:T(8,128)(2,1)S(1)}, bf16[80,128]{1,0:T(8,128)(2,1)S(1)}, u32[]{:S(2)}, u32[]{:S(2)}) collective-permute-start(bf16[80,128]{1,0:T(8,128)(2,1)S(1)} %get-tuple-element.77), channel_id=1, source_target_pairs={{0,1},{1,0},{2,3},{3,2},{4,5},{5,4},{6,7},{7,6},{8,9},{9,8},{10,11... | collective-permute-start | bytes 61448 | tf_op jit(solution)/shard_map/ppermute | solution.py:278

commit v8 on v7

--- a/solution.py
+++ b/solution.py
@@ -10,10 +10,10 @@
 
 F32 = jnp.float32
 BF16 = jnp.bfloat16
+SOURCE = (0, 2, 4, 6, 1, 3, 5, 7)
+HEIGHTS = (80, 160, 160, 160, 80)
 ORDER = (0, 6, 4, 7, 5, 2, 3, 1)
-GATHERED = (0, 6, 4, 2, 1, 7, 5, 3)
-DIRECT = GATHERED[:5]
-FORWARD_FLOPS = 12_000_000_000
+HEAVY = 12_000_000_000
 
 
 def nn(a, b):
@@ -70,20 +70,23 @@
         block_ref[p, 0:80, :] = pixels[80 * p : 80 * p + 80]
         block_ref[p, 80:160, :] = taps[p].astype(BF16)
         block_ref[p, 160:176, :] = last[p].astype(BF16)
-    for n, k in enumerate(ORDER):
-        send_refs[n][0:176, :] = block_ref[slot_ref[0] ^ k]
-        for j in range(5 if k in DIRECT else 0):
-            send_refs[n][176 + 32 * j : 208 + 32 * j, :] = cot_ref[:, 128 * j : 128 * j + 128]
+    for n in range(5):
+        send_refs[n][0:176, :] = block_ref[slot_ref[0] ^ SOURCE[n]]
+        shared = 176
+        if 0 < n < 4:
+            send_refs[n][176:352, :] = block_ref[slot_ref[0] ^ SOURCE[n] ^ 1]
+            shared = 352
+        for j in range(5):
+            start = shared + 32 * j
+            send_refs[n][start : start + 32, :] = cot_ref[:, 128 * j : 128 * j + 128]
 
 
 def spread_kernel(slot_ref, *refs):
     *recv_refs, win_ref, down_ref, up_ref, own_ref, cot_ref, cell_ref, tap_ref, block_ref = refs
-    for n, k in enumerate(ORDER):
-        if k in DIRECT:
-            block_ref[slot_ref[0] ^ k] = recv_refs[n][...]
-        else:
-            block_ref[slot_ref[0] ^ k, 0:176, :] = recv_refs[n][...]
-            block_ref[slot_ref[0] ^ k, 176:336, :] = recv_refs[3 + GATHERED.index(k)][176:336, :]
+    for n, k in enumerate(SOURCE):
+        shared = 176 if n in (0, 4) else 352
+        block_ref[slot_ref[0] ^ k, 0:176, :] = recv_refs[n][rows_for(n, 176), :]
+        block_ref[slot_ref[0] ^ k, 176:336, :] = recv_refs[n][shared : shared + 160, :]
     pixels = swap_blocks([block_ref[q, 0:80, :].astype(F32) for q in range(8)])
     for r in range(4):
         columns = (from_left(pixels[2 * r + 1]), pixels[2 * r], pixels[2 * r + 1])
@@ -152,8 +155,8 @@
 def middle_kernel(own_ref, down_ref, up_ref, *refs):
     *hid_refs, act_ref, share_ref = refs
     hidden = hid_refs[0][...].astype(F32)
-    for k in range(1, 8):
-        hidden = hidden + hid_refs[k][...].astype(F32)
+    for n in range(1, 8):
+        hidden = hidden + hid_refs[n][...].astype(F32)
     cumul = 0.5 * (1.0 + lax.erf(hidden * (1.0 / math.sqrt(2.0))))
     density = jnp.exp(-0.5 * hidden * hidden) * (1.0 / math.sqrt(2.0 * math.pi))
     act_ref[...] = (hidden * cumul).astype(BF16)
@@ -168,7 +171,7 @@
 
 def weight_grad_kernel(slot_ref, win_ref, cot_ref, act_ref, *refs):
     *all_refs, red_ref, pre_ref, shift_ref, cell_ref = refs
-    for n, k in enumerate(GATHERED):
+    for n, k in enumerate(SOURCE):
         start = pl.multiple_of(16 * (slot_ref[0] ^ k), 16)
         for g in range(5):
             pre_ref[pl.ds(128 * g + start, 16), :] = all_refs[n][16 * g : 16 * g + 16, :]
@@ -226,9 +229,11 @@
     parts[6] = parts[6] + below_ref[0].astype(F32)
     parts[7] = parts[7] + below_ref[1].astype(F32)
     for q, x in enumerate(swap_blocks(parts)):
-        slot_blocks[slot_ref[0] ^ q] = x.astype(BF16)
-    for n, k in enumerate(ORDER):
-        send_refs[n][...] = slot_blocks[k]
+        slot_blocks[q] = x.astype(BF16)
+    for n in range(5):
+        send_refs[n][0:80, :] = slot_blocks[slot_ref[0] ^ SOURCE[n]]
+        if 0 < n < 4:
+            send_refs[n][80:160, :] = slot_blocks[slot_ref[0] ^ SOURCE[n] ^ 1]
 
 
 def fold_kernel(high_ref, red_ref, keep_ref, give_ref):
@@ -241,10 +246,19 @@
     give_ref[...] = jnp.where(high, first, second).astype(BF16)
 
 
+def join_kernel(keep_ref, own_ref, *refs):
+    *line_refs, out_ref = refs
+    out_ref[0:80, :] = own_ref[...]
+    for n, line_ref in enumerate(line_refs):
+        out_ref[80 * n + 80 : 80 * n + 160, :] = line_ref[80:160, :]
+
+
 def unpack_kernel(slot_ref, *refs):
-    *recv_refs, out_ref, block_ref = refs
-    for n, k in enumerate(ORDER):
-        block_ref[slot_ref[0] ^ k] = recv_refs[n][...]
+    *recv_refs, joined_ref, out_ref, token_ref, block_ref = refs
+    token_ref[...] = joined_ref[0:16, :]
+    for n in range(4):
+        block_ref[slot_ref[0] ^ SOURCE[n]] = recv_refs[n][0:80, :]
+        block_ref[slot_ref[0] ^ SOURCE[n] ^ 1] = joined_ref[80 * n : 80 * n + 80, :]
     lane = iota((128, 128), 1)
     pick = jnp.where(cell_of_lane(lane) == iota((128, 128), 0), 1.0, 0.0).astype(BF16)
     blocks = block_ref[...].reshape(640, 128)
@@ -252,7 +266,7 @@
         out_ref[:, 128 * p : 128 * p + 128] = nt(pick, blocks[128 * p : 128 * p + 128]).astype(BF16)
 
 
-def finish_kernel(keep_ref, given_ref, conv_ref, group_ref):
+def finish_kernel(keep_ref, given_ref, token_ref, conv_ref, group_ref):
     total = keep_ref[...] + given_ref[...].astype(F32)
     for t in range(9):
         conv_ref[t] = total[:, 80 * t : 80 * t + 80]
@@ -273,21 +287,17 @@
     )(*args)
 
 
-def trade(blocks):
-    moved = [
-        lax.ppermute(block, "fsdp", [(i, i ^ k) for i in range(8)])
-        for k, block in zip(ORDER[1:], blocks[1:])
-    ]
-    return [blocks[0]] + moved
-
-
 def swap(block, k):
     return lax.ppermute(block, "fsdp", [(i, i ^ k) for i in range(8)])
 
 
-def gather(block):
-    direct = [swap(block, k) for k in GATHERED[1:5]]
-    return [block] + direct + [swap(got, 1) for got in direct[:3]]
+def exchange(blocks):
+    direct = [swap(block, k) for block, k in zip(blocks[1:], SOURCE[1:5])]
+    return [blocks[0]] + direct + [swap(got, 1) for got in direct[:3]]
+
+
+def rows_for(n, height):
+    return slice(height, 2 * height) if n > 4 else slice(0, height)
 
 
 def per_device(image, conv_weight, group_weight, cotangent):
@@ -300,18 +310,17 @@
     cells = cotangent.reshape(32, 640)
     slot = lax.axis_index("fsdp").astype(jnp.int32).reshape(1)
     weights = conv_weight.transpose(1, 0, 2).reshape(720, 640)
-    parts = trade(
+    parts = exchange(
         call(
-            pack_kernel, [((336 if k in DIRECT else 176, 128), BF16) for k in ORDER],
+            pack_kernel, [((height, 128), BF16) for height in (336, 512, 512, 512, 336)],
             slot, image.reshape(128, 640), group_weight.transpose(0, 2, 1), cells,
             scratch=[pltpu.VMEM((8, 176, 128), BF16)], smem=1,
         )
     )
-    passed = [swap(parts[ORDER.index(k)], 1) for k in GATHERED[1:4]]
     windows, down, up, own, cot = call(
         spread_kernel,
         [((720, 256), BF16), ((80, 512), BF16), ((80, 256), BF16), ((80, 256), F32), ((640, 256), BF16)],
-        slot, *parts, *passed,
+        slot, *parts,
         scratch=[pltpu.VMEM((256, 640), BF16), pltpu.VMEM((640, 256), BF16), pltpu.VMEM((8, 336, 128), BF16)],
         smem=1,
     )
@@ -319,9 +328,9 @@
     *hid, windows = call(
         forward_kernel, [((80, 256), BF16)] * 8 + [((720, 256), BF16)],
         slot, windows, down, weights,
-        scratch=[pltpu.VMEM((8, 80, 256), BF16)], smem=1, flops=FORWARD_FLOPS,
-    )
-    hid = trade(hid)
+        scratch=[pltpu.VMEM((8, 80, 256), BF16)], smem=1, flops=HEAVY,
+    )
+    hid = [hid[0]] + [swap(block, k) for k, block in zip(ORDER[1:], hid[1:])]
     up = lax.ppermute(up, "tile", upward)
     act, share = call(
         middle_kernel, [((80, 256), BF16), ((160, 256), BF16)], own, down, up, *hid
@@ -329,7 +338,7 @@
     red, pre = call(
         weight_grad_kernel,
         [((640, 896), BF16), ((640, 256), BF16)],
-        slot, windows, cot, act, *gather(share),
+        slot, windows, cot, act, *exchange([share] * 5),
         scratch=[pltpu.VMEM((5, 256, 512), BF16), pltpu.VMEM((256, 640), BF16)], smem=1,
     )
     img, img_up = call(
@@ -339,21 +348,22 @@
     red = lax.all_to_all(
         red.reshape(16, 40, 896), "tile", 0, 0, tiled=True, axis_index_groups=planes
     )
-    back = trade(
-        call(
-            return_kernel, [((80, 128), BF16)] * 8, slot, img, img_below,
-            scratch=[pltpu.VMEM((8, 80, 128), BF16)], smem=1,
-        )
-    )
+    own, *others, core = call(
+        return_kernel, [((height, 128), BF16) for height in HEIGHTS], slot, img, img_below,
+        scratch=[pltpu.VMEM((8, 80, 128), BF16)], smem=1,
+    )
+    others = [swap(block, k) for block, k in zip(others, SOURCE[1:4])]
     high = (lax.axis_index("tile") % 2).astype(jnp.int32).reshape(1)
     keep, give = call(fold_kernel, [((20, 896), F32), ((20, 896), BF16)], high, red, smem=1)
     given = lax.ppermute(give, "tile", partners)
-    (image_grad,) = call(
-        unpack_kernel, [((128, 640), BF16)], slot, *back,
+    (core,) = call(join_kernel, [((320, 128), BF16)], keep, core, *others)
+    core = swap(core, 1)
+    image_grad, token = call(
+        unpack_kernel, [((128, 640), BF16), ((16, 128), BF16)], slot, own, *others, core,
         scratch=[pltpu.VMEM((8, 80, 128), BF16)], smem=1,
     )
     conv_weight_grad, group_weight_grad = call(
-        finish_kernel, [((9, 20, 80), F32), ((144, 20), F32)], keep, given
+        finish_kernel, [((9, 20, 80), F32), ((144, 20), F32)], keep, given, token
     )
     conv_weight_grad = conv_weight_grad.transpose(2, 0, 1)
     group_weight_grad = group_weight_grad.reshape(9, 16, 20)

time: 103 us -> 99.1 us (0.962)
  starting transfers between devices: 70.1 us -> 66.8 us
  waiting for transfers between devices: 21.4 us -> 19.9 us
    ppermute x21 -> x0, starting transfers between devices: 34.5 us -> none  [trade(): lax.ppermute(block, 'fsdp', [(i, i ^ k) for i in range(8)])]
    ppermute x10 -> x25, starting transfers between devices: 11.9 us -> 43.3 us  [swap(): return lax.ppermute(block, 'fsdp', [(i, i ^ k) for i in range(8)])]
    ppermute x21 -> x0, waiting for transfers between devices: 10.3 us -> none  [trade(): lax.ppermute(block, 'fsdp', [(i, i ^ k) for i in range(8)])]
    ppermute x10 -> x25, waiting for transfers between devices: 1.28 us -> 6.51 us  [swap(): return lax.ppermute(block, 'fsdp', [(i, i ^ k) for i in range(8)])]
    all_to_all x1, waiting for transfers between devices: 0.9 us -> 3.85 us  [per_device(): lax.all_to_all(red.reshape(16, 40, 896), 'tile', 0, 0, tiled=True, axis_i...]
    pallas_call x10 -> x11, Pallas kernels: 7.21 us -> 7.19 us  [call(): pl.pallas_call(kernel, out_shape=[jax.ShapeDtypeStruct(shape, dtype) for...]
  transfers between devices with their start and end apart: 36 -> 30, of which waited for: 14 -> 12; matrix products, arithmetic and copies ran while one was open for 0% -> 0% of each run, Pallas kernels for 2% -> 2%
where the time goes in v8:
time: 99.1 us; the launch traced here: 97.4 us
  starting transfers between devices  66.8 us (67%)
  waiting for transfers between devices  19.9 us (20%)
  Pallas kernels  7.19 us (7%)
  local copies, waits for them, and re-layouts  2.69 us (3%)
    ppermute x25, starting transfers between devices, swap(): return lax.ppermute(block, 'fsdp', [(i, i ^ k) for i in range(8)])  43.3 us
    ppermute x1, waiting for transfers between devices, per_device(): img_below = lax.ppermute(img_up, 'tile', upward)  7.77 us
    all_to_all x1, starting transfers between devices, per_device(): lax.all_to_all(red.reshape(16, 40, 896), 'tile', 0, 0, tiled=True, axis_i...  7.7 us
    ppermute x1, starting transfers between devices, per_device(): down = lax.ppermute(down, 'tile', downward)  7.36 us
    pallas_call x11, Pallas kernels, call(): pl.pallas_call(kernel, out_shape=[jax.ShapeDtypeStruct(shape, dtype) for...  7.19 us
    ppermute x25, waiting for transfers between devices, swap(): return lax.ppermute(block, 'fsdp', [(i, i ^ k) for i in range(8)])  6.51 us
    ppermute x1, starting transfers between devices, per_device(): given = lax.ppermute(give, 'tile', partners)  5.84 us
    all_to_all x1, waiting for transfers between devices, per_device(): lax.all_to_all(red.reshape(16, 40, 896), 'tile', 0, 0, tiled=True, axis_i...  3.85 us
  transfers between devices with their start and end apart: 30, of which 12 were waited for; matrix products, arithmetic and copies ran while one was open for 0% of the time, Pallas kernels for 2%

profile of v8, /device:TPU:1, one launch (start us, length us, event | category | flops | bytes accessed | tf_op | source)
XLA Modules:
  0.0 97.4 jit_solution(6446712944226183169)
XLA Ops:
  0.7 1.0 %copy-done.1 = bf16[9,128,80]{1,2,0:T(8,128)(2,1)S(1)} copy-done((bf16[9,128,80]{1,2,0:T(8,128)(2,1)S(1)}, bf16[9,128,80]{1,2,0:T(8,128)(2,1)}, u32[]{:S(2)}) %copy-start.1) | copy-done | bytes 184344
  1.7 0.9 copy-done.2
  2.6 0.8 copy-done.3
  3.3 0.5 shard_map.67
  3.8 2.6 %collective-permute-start = (bf16[512,128]{1,0:T(8,128)(2,1)S(1)}, bf16[512,128]{1,0:T(8,128)(2,1)S(1)}, u32[]{:S(2)}, u32[]{:S(2)}) collective-permute-start(bf16[512,128]{1,0:T(8,128)(2,1)S(1)} %get-tuple-element.40), channel_id=1, source_target_pairs={{0,2},{1,3},{2,0},{3,1},{4,6},{5,7},{6,4},{7,5},{8,10},{9,11},{10,... | collective-permute-start | bytes 393224 | tf_op jit(solution)/shard_map/ppermute | solution.py:291
  6.4 3.0 %collective-permute-start.1 = (bf16[512,128]{1,0:T(8,128)(2,1)S(1)}, bf16[512,128]{1,0:T(8,128)(2,1)S(1)}, u32[]{:S(2)}, u32[]{:S(2)}) collective-permute-start(bf16[512,128]{1,0:T(8,128)(2,1)S(1)} %get-tuple-element.41), channel_id=1, source_target_pairs={{0,4},{1,5},{2,6},{3,7},{4,0},{5,1},{6,2},{7,3},{8,12},{9,13},{10,... | collective-permute-start | bytes 393224 | tf_op jit(solution)/shard_map/ppermute | solution.py:291
  9.4 4.7 %collective-permute-start.4 = (bf16[512,128]{1,0:T(8,128)(2,1)S(1)}, bf16[512,128]{1,0:T(8,128)(2,1)S(1)}, u32[]{:S(2)}, u32[]{:S(2)}) collective-permute-start(bf16[512,128]{1,0:T(8,128)(2,1)S(1)} %collective-permute-done.refs_1_), channel_id=1, source_target_pairs={{0,1},{1,0},{2,3},{3,2},{4,5},{5,4},{6,7},{7,6},{8,9},{9,8},{10,11... | collective-permute-start | bytes 393224 | tf_op jit(solution)/shard_map/ppermute | solution.py:291
  14.1 6.5 %collective-permute-start.5 = (bf16[512,128]{1,0:T(8,128)(2,1)S(1)}, bf16[512,128]{1,0:T(8,128)(2,1)S(1)}, u32[]{:S(2)}, u32[]{:S(2)}) collective-permute-start(bf16[512,128]{1,0:T(8,128)(2,1)S(1)} %collective-permute-done.1.refs_2_), channel_id=1, source_target_pairs={{0,1},{1,0},{2,3},{3,2},{4,5},{5,4},{6,7},{7,6},{8,9},{9,8},{10,11... | collective-permute-start | bytes 393224 | tf_op jit(solution)/shard_map/ppermute | solution.py:291
  20.6 0.5 collective-permute-start.3
  21.1 1.0 collective-permute-done.3.refs_4_
  22.1 0.8 shard_map.68
  22.9 7.4 %collective-permute-start.7 = (bf16[80,512]{1,0:T(8,128)(2,1)S(1)}, bf16[80,512]{1,0:T(8,128)(2,1)S(1)}, u32[]{:S(2)}, u32[]{:S(2)}) collective-permute-start(bf16[80,512]{1,0:T(8,128)(2,1)S(1)} %get-tuple-element.45), channel_id=1, source_target_pairs={{0,8},{8,16},{16,24},{24,32},{32,40},{40,48},{48,56},{56,64},{64,7... | collective-permute-start | bytes 245768 | tf_op jit(solution)/shard_map/ppermute | solution.py:327
  30.3 1.3 %collective-permute-start.8 = (bf16[80,256]{1,0:T(8,128)(2,1)S(1)}, bf16[80,256]{1,0:T(8,128)(2,1)S(1)}, u32[]{:S(2)}, u32[]{:S(2)}) collective-permute-start(bf16[80,256]{1,0:T(8,128)(2,1)S(1)} %get-tuple-element.49), channel_id=1, source_target_pairs={{8,0},{16,8},{24,16},{32,24},{40,32},{48,40},{56,48},{64,56},{72,6... | collective-permute-start | bytes 122888 | tf_op jit(solution)/shard_map/ppermute | solution.py:334
  31.6 0.2 collective-permute-done.7.down_ref
  31.8 0.5 shard_map.69
  32.3 1.7 %collective-permute-start.9 = (bf16[80,256]{1,0:T(8,128)(2,1)S(1)}, bf16[80,256]{1,0:T(8,128)(2,1)S(1)}, u32[]{:S(2)}, u32[]{:S(2)}) collective-permute-start(bf16[80,256]{1,0:T(8,128)(2,1)S(1)} %get-tuple-element.51), channel_id=1, source_target_pairs={{0,6},{1,7},{2,4},{3,5},{4,2},{5,3},{6,0},{7,1},{8,14},{9,15},{10,... | collective-permute-start | bytes 122888 | tf_op jit(solution)/shard_map/ppermute | solution.py:291
  34.0 3.7 %collective-permute-start.10 = (bf16[80,256]{1,0:T(8,128)(2,1)S(1)}, bf16[80,256]{1,0:T(8,128)(2,1)S(1)}, u32[]{:S(2)}, u32[]{:S(2)}) collective-permute-start(bf16[80,256]{1,0:T(8,128)(2,1)S(1)} %get-tuple-element.52), channel_id=1, source_target_pairs={{0,4},{1,5},{2,6},{3,7},{4,0},{5,1},{6,2},{7,3},{8,12},{9,13},{10,... | collective-permute-start | bytes 122888 | tf_op jit(solution)/shard_map/ppermute | solution.py:291
  37.7 2.5 %collective-permute-start.11 = (bf16[80,256]{1,0:T(8,128)(2,1)S(1)}, bf16[80,256]{1,0:T(8,128)(2,1)S(1)}, u32[]{:S(2)}, u32[]{:S(2)}) collective-permute-start(bf16[80,256]{1,0:T(8,128)(2,1)S(1)} %get-tuple-element.53), channel_id=1, source_target_pairs={{0,7},{1,6},{2,5},{3,4},{4,3},{5,2},{6,1},{7,0},{8,15},{9,14},{10,... | collective-permute-start | bytes 122888 | tf_op jit(solution)/shard_map/ppermute | solution.py:291
  40.2 0.7 collective-permute-done.8.up_ref
  40.9 0.6 collective-permute-start.13
  41.5 1.5 %collective-permute-start.14 = (bf16[80,256]{1,0:T(8,128)(2,1)S(1)}, bf16[80,256]{1,0:T(8,128)(2,1)S(1)}, u32[]{:S(2)}, u32[]{:S(2)}) collective-permute-start(bf16[80,256]{1,0:T(8,128)(2,1)S(1)} %get-tuple-element.56), channel_id=1, source_target_pairs={{0,3},{1,2},{2,1},{3,0},{4,7},{5,6},{6,5},{7,4},{8,11},{9,10},{10,... | collective-permute-start | bytes 122888 | tf_op jit(solution)/shard_map/ppermute | solution.py:291
  43.0 2.2 %collective-permute-start.15 = (bf16[80,256]{1,0:T(8,128)(2,1)S(1)}, bf16[80,256]{1,0:T(8,128)(2,1)S(1)}, u32[]{:S(2)}, u32[]{:S(2)}) collective-permute-start(bf16[80,256]{1,0:T(8,128)(2,1)S(1)} %get-tuple-element.57), channel_id=1, source_target_pairs={{0,1},{1,0},{2,3},{3,2},{4,5},{5,4},{6,7},{7,6},{8,9},{9,8},{10,11... | collective-permute-start | bytes 122888 | tf_op jit(solution)/shard_map/ppermute | solution.py:291
  45.3 0.5 collective-permute-done.12.refs_4_
  45.8 1.0 %collective-permute-done.14.refs_6_ = bf16[80,256]{1,0:T(8,128)(2,1)S(1)} collective-permute-done((bf16[80,256]{1,0:T(8,128)(2,1)S(1)}, bf16[80,256]{1,0:T(8,128)(2,1)S(1)}, u32[]{:S(2)}, u32[]{:S(2)}) %collective-permute-start.14) | collective-permute-done | bytes 40992 | tf_op jit(solution)/shard_map/ppermute | solution.py:291
  46.9 1.8 %collective-permute-start.18 = (bf16[160,256]{1,0:T(8,128)(2,1)S(1)}, bf16[160,256]{1,0:T(8,128)(2,1)S(1)}, u32[]{:S(2)}, u32[]{:S(2)}) collective-permute-start(bf16[160,256]{1,0:T(8,128)(2,1)S(1)} %get-tuple-element.59.refs_0_), channel_id=1, source_target_pairs={{0,6},{1,7},{2,4},{3,5},{4,2},{5,3},{6,0},{7,1},{8,14},{9,15},{10,... | collective-permute-start | bytes 245768 | tf_op jit(solution)/shard_map/ppermute | solution.py:291
  48.7 1.8 %collective-permute-start.16 = (bf16[160,256]{1,0:T(8,128)(2,1)S(1)}, bf16[160,256]{1,0:T(8,128)(2,1)S(1)}, u32[]{:S(2)}, u32[]{:S(2)}) collective-permute-start(bf16[160,256]{1,0:T(8,128)(2,1)S(1)} %get-tuple-element.59.refs_0_), channel_id=1, source_target_pairs={{0,2},{1,3},{2,0},{3,1},{4,6},{5,7},{6,4},{7,5},{8,10},{9,11},{10,... | collective-permute-start | bytes 245768 | tf_op jit(solution)/shard_map/ppermute | solution.py:291
  50.5 1.2 %collective-permute-start.19 = (bf16[160,256]{1,0:T(8,128)(2,1)S(1)}, bf16[160,256]{1,0:T(8,128)(2,1)S(1)}, u32[]{:S(2)}, u32[]{:S(2)}) collective-permute-start(bf16[160,256]{1,0:T(8,128)(2,1)S(1)} %get-tuple-element.59.refs_0_), channel_id=1, source_target_pairs={{0,1},{1,0},{2,3},{3,2},{4,5},{5,4},{6,7},{7,6},{8,9},{9,8},{10,11... | collective-permute-start | bytes 245768 | tf_op jit(solution)/shard_map/ppermute | solution.py:291
  51.8 0.6 collective-permute-done.18.refs_3_
  52.4 2.2 %collective-permute-start.22 = (bf16[160,256]{1,0:T(8,128)(2,1)S(1)}, bf16[160,256]{1,0:T(8,128)(2,1)S(1)}, u32[]{:S(2)}, u32[]{:S(2)}) collective-permute-start(bf16[160,256]{1,0:T(8,128)(2,1)S(1)} %collective-permute-done.18.refs_3_), channel_id=1, source_target_pairs={{0,1},{1,0},{2,3},{3,2},{4,5},{5,4},{6,7},{7,6},{8,9},{9,8},{10,11... | collective-permute-start | bytes 245768 | tf_op jit(solution)/shard_map/ppermute | solution.py:291
  54.6 2.1 %collective-permute-done.17.refs_2_ = bf16[160,256]{1,0:T(8,128)(2,1)S(1)} collective-permute-done((bf16[160,256]{1,0:T(8,128)(2,1)S(1)}, bf16[160,256]{1,0:T(8,128)(2,1)S(1)}, u32[]{:S(2)}, u32[]{:S(2)}) %collective-permute-start.17) | collective-permute-done | bytes 81952 | tf_op jit(solution)/shard_map/ppermute | solution.py:291
  56.6 0.5 collective-permute-start.21
  57.2 0.9 collective-permute-done.21.refs_6_
  58.1 0.4 collective-permute-done.20.refs_5_
  58.4 2.6 %shard_map.71 = (bf16[640,896]{1,0:T(8,128)(2,1)}, bf16[640,256]{1,0:T(8,128)(2,1)S(1)}) custom-call(s32[1]{0:T(128)} %bitcast.slot_ref, bf16[720,256]{1,0:T(8,128)(2,1)S(1)} %get-tuple-element.46.win_ref, bf16[640,256]{1,0:T(8,128)(2,1)S(1)} %get-tuple-element.47.cot_ref, bf16[80,256]{1,0:T(8,128)(2,1)S(1)} %get-tuple-element.58.act_ref, ...), custom_call_target="tpu_custom_call" | custom-call | tf_op jit(solution)/shard_map/pallas_call | solution.py:279
  61.0 7.7 %all-to-all-start = ((bf16[16,40,896]{2,1,0:T(8,128)(2,1)}), bf16[16,40,896]{2,1,0:T(8,128)(2,1)S(1)}, u32[]{:S(2)}, u32[]{:S(2)}) async-start(bf16[16,40,896]{2,1,0:T(8,128)(2,1)} %bitcast.7), calls=%async_computation | async-start | bytes 2293760 | tf_op jit(solution)/shard_map/all_to_all | solution.py:348
  68.7 0.5 shard_map.72
  69.2 1.3 %collective-permute-start.23 = (bf16[2,80,128]{2,1,0:T(8,128)(2,1)S(1)}, bf16[2,80,128]{2,1,0:T(8,128)(2,1)S(1)}, u32[]{:S(2)}, u32[]{:S(2)}) collective-permute-start(bf16[2,80,128]{2,1,0:T(8,128)(2,1)S(1)} %get-tuple-element.62), channel_id=1, source_target_pairs={{8,0},{16,8},{24,16},{32,24},{40,32},{48,40},{56,48},{64,56},{72,6... | collective-permute-start | bytes 122888 | tf_op jit(solution)/shard_map/ppermute | solution.py:347
  70.5 7.8 %collective-permute-done.23.below_ref = bf16[2,80,128]{2,1,0:T(8,128)(2,1)S(1)} collective-permute-done((bf16[2,80,128]{2,1,0:T(8,128)(2,1)S(1)}, bf16[2,80,128]{2,1,0:T(8,128)(2,1)S(1)}, u32[]{:S(2)}, u32[]{:S(2)}) %collective-permute-start.23) | collective-permute-done | bytes 40992 | tf_op jit(solution)/shard_map/ppermute | solution.py:347
  78.3 0.3 shard_map.73
  78.7 1.7 %collective-permute-start.25 = (bf16[160,128]{1,0:T(8,128)(2,1)S(1)}, bf16[160,128]{1,0:T(8,128)(2,1)S(1)}, u32[]{:S(2)}, u32[]{:S(2)}) collective-permute-start(bf16[160,128]{1,0:T(8,128)(2,1)S(1)} %get-tuple-element.65), channel_id=1, source_target_pairs={{0,4},{1,5},{2,6},{3,7},{4,0},{5,1},{6,2},{7,3},{8,12},{9,13},{10,... | collective-permute-start | bytes 122888 | tf_op jit(solution)/shard_map/ppermute | solution.py:291
  80.3 1.9 %collective-permute-start.26 = (bf16[160,128]{1,0:T(8,128)(2,1)S(1)}, bf16[160,128]{1,0:T(8,128)(2,1)S(1)}, u32[]{:S(2)}, u32[]{:S(2)}) collective-permute-start(bf16[160,128]{1,0:T(8,128)(2,1)S(1)} %get-tuple-element.66), channel_id=1, source_target_pairs={{0,6},{1,7},{2,4},{3,5},{4,2},{5,3},{6,0},{7,1},{8,14},{9,15},{10,... | collective-permute-start | bytes 122888 | tf_op jit(solution)/shard_map/ppermute | solution.py:291
  82.2 3.8 %all-to-all-done.red_ref = bf16[16,40,896]{2,1,0:T(8,128)(2,1)S(1)} async-done(((bf16[16,40,896]{2,1,0:T(8,128)(2,1)}), bf16[16,40,896]{2,1,0:T(8,128)(2,1)S(1)}, u32[]{:S(2)}, u32[]{:S(2)}) %all-to-all-start) | async-done | bytes 1146912 | tf_op jit(solution)/shard_map/all_to_all | solution.py:348
  86.0 0.2 shard_map.74
  86.3 2.6 %collective-permute-start.27 = (bf16[320,128]{1,0:T(8,128)(2,1)S(1)}, bf16[320,128]{1,0:T(8,128)(2,1)S(1)}, u32[]{:S(2)}, u32[]{:S(2)}) collective-permute-start(bf16[320,128]{1,0:T(8,128)(2,1)S(1)} %shard_map.75), channel_id=1, source_target_pairs={{0,1},{1,0},{2,3},{3,2},{4,5},{5,4},{6,7},{7,6},{8,9},{9,8},{10,11... | collective-permute-start | bytes 245768 | tf_op jit(solution)/shard_map/ppermute | solution.py:291
  88.9 5.8 %collective-permute-start.28 = (bf16[20,896]{1,0:T(8,128)(2,1)S(1)}, bf16[20,896]{1,0:T(8,128)(2,1)S(1)}, u32[]{:S(2)}, u32[]{:S(2)}) collective-permute-start(bf16[20,896]{1,0:T(8,128)(2,1)S(1)} %get-tuple-element.71), channel_id=1, source_target_pairs={{0,8},{8,0},{16,24},{24,16},{32,40},{40,32},{48,56},{56,48},{64,72... | collective-permute-start | bytes 107528 | tf_op jit(solution)/shard_map/ppermute | solution.py:358
  94.7 0.9 shard_map.76
  95.7 0.9 collective-permute-done.28.given_ref
  96.6 0.8 shard_map.77
  (31 shorter events, 0.3 us)
Async XLA Ops:
  0.6 31.1 %copy-start = (bf16[80,9,640]{2,0,1:T(8,128)(2,1)S(1)}, bf16[80,9,640]{2,0,1:T(8,128)(2,1)}, u32[]{:S(2)}) copy-start(bf16[80,9,640]{2,0,1:T(8,128)(2,1)} %param.5) | copy-start | bytes 2764804
  0.6 1.0 %copy-start.1 = (bf16[9,128,80]{1,2,0:T(8,128)(2,1)S(1)}, bf16[9,128,80]{1,2,0:T(8,128)(2,1)}, u32[]{:S(2)}) copy-start(bf16[9,128,80]{1,2,0:T(8,128)(2,1)} %param.6) | copy-start | bytes 552964
  1.6 0.9 copy-start.2
  2.6 0.8 copy-start.3
  3.8 5.6 %collective-permute-start = (bf16[512,128]{1,0:T(8,128)(2,1)S(1)}, bf16[512,128]{1,0:T(8,128)(2,1)S(1)}, u32[]{:S(2)}, u32[]{:S(2)}) collective-permute-start(bf16[512,128]{1,0:T(8,128)(2,1)S(1)} %get-tuple-element.40), channel_id=1, source_target_pairs={{0,2},{1,3},{2,0},{3,1},{4,6},{5,7},{6,4},{7,5},{8,10},{9,11},{10,... | collective-permute-start | bytes 393224 | tf_op jit(solution)/shard_map/ppermute | solution.py:291
  6.4 7.7 %collective-permute-start.1 = (bf16[512,128]{1,0:T(8,128)(2,1)S(1)}, bf16[512,128]{1,0:T(8,128)(2,1)S(1)}, u32[]{:S(2)}, u32[]{:S(2)}) collective-permute-start(bf16[512,128]{1,0:T(8,128)(2,1)S(1)} %get-tuple-element.41), channel_id=1, source_target_pairs={{0,4},{1,5},{2,6},{3,7},{4,0},{5,1},{6,2},{7,3},{8,12},{9,13},{10,... | collective-permute-start | bytes 393224 | tf_op jit(solution)/shard_map/ppermute | solution.py:291
  9.4 11.2 %collective-permute-start.2 = (bf16[512,128]{1,0:T(8,128)(2,1)S(1)}, bf16[512,128]{1,0:T(8,128)(2,1)S(1)}, u32[]{:S(2)}, u32[]{:S(2)}) collective-permute-start(bf16[512,128]{1,0:T(8,128)(2,1)S(1)} %get-tuple-element.42), channel_id=1, source_target_pairs={{0,6},{1,7},{2,4},{3,5},{4,2},{5,3},{6,0},{7,1},{8,14},{9,15},{10,... | collective-permute-start | bytes 393224 | tf_op jit(solution)/shard_map/ppermute | solution.py:291
  9.4 12.7 %collective-permute-start.4 = (bf16[512,128]{1,0:T(8,128)(2,1)S(1)}, bf16[512,128]{1,0:T(8,128)(2,1)S(1)}, u32[]{:S(2)}, u32[]{:S(2)}) collective-permute-start(bf16[512,128]{1,0:T(8,128)(2,1)S(1)} %collective-permute-done.refs_1_), channel_id=1, source_target_pairs={{0,1},{1,0},{2,3},{3,2},{4,5},{5,4},{6,7},{7,6},{8,9},{9,8},{10,11... | collective-permute-start | bytes 393224 | tf_op jit(solution)/shard_map/ppermute | solution.py:291
  14.1 7.9 %collective-permute-start.5 = (bf16[512,128]{1,0:T(8,128)(2,1)S(1)}, bf16[512,128]{1,0:T(8,128)(2,1)S(1)}, u32[]{:S(2)}, u32[]{:S(2)}) collective-permute-start(bf16[512,128]{1,0:T(8,128)(2,1)S(1)} %collective-permute-done.1.refs_2_), channel_id=1, source_target_pairs={{0,1},{1,0},{2,3},{3,2},{4,5},{5,4},{6,7},{7,6},{8,9},{9,8},{10,11... | collective-permute-start | bytes 393224 | tf_op jit(solution)/shard_map/ppermute | solution.py:291
  20.6 1.5 %collective-permute-start.6 = (bf16[512,128]{1,0:T(8,128)(2,1)S(1)}, bf16[512,128]{1,0:T(8,128)(2,1)S(1)}, u32[]{:S(2)}, u32[]{:S(2)}) collective-permute-start(bf16[512,128]{1,0:T(8,128)(2,1)S(1)} %collective-permute-done.2.refs_3_), channel_id=1, source_target_pairs={{0,1},{1,0},{2,3},{3,2},{4,5},{5,4},{6,7},{7,6},{8,9},{9,8},{10,11... | collective-permute-start | bytes 393224 | tf_op jit(solution)/shard_map/ppermute | solution.py:291
  20.6 1.5 %collective-permute-start.3 = (bf16[336,128]{1,0:T(8,128)(2,1)S(1)}, bf16[336,128]{1,0:T(8,128)(2,1)S(1)}, u32[]{:S(2)}, u32[]{:S(2)}) collective-permute-start(bf16[336,128]{1,0:T(8,128)(2,1)S(1)} %get-tuple-element.43), channel_id=1, source_target_pairs={{0,1},{1,0},{2,3},{3,2},{4,5},{5,4},{6,7},{7,6},{8,9},{9,8},{10,11... | collective-permute-start | bytes 258056 | tf_op jit(solution)/shard_map/ppermute | solution.py:291
  22.9 8.8 %collective-permute-start.7 = (bf16[80,512]{1,0:T(8,128)(2,1)S(1)}, bf16[80,512]{1,0:T(8,128)(2,1)S(1)}, u32[]{:S(2)}, u32[]{:S(2)}) collective-permute-start(bf16[80,512]{1,0:T(8,128)(2,1)S(1)} %get-tuple-element.45), channel_id=1, source_target_pairs={{0,8},{8,16},{16,24},{24,32},{32,40},{40,48},{48,56},{56,64},{64,7... | collective-permute-start | bytes 245768 | tf_op jit(solution)/shard_map/ppermute | solution.py:327
  30.3 10.6 %collective-permute-start.8 = (bf16[80,256]{1,0:T(8,128)(2,1)S(1)}, bf16[80,256]{1,0:T(8,128)(2,1)S(1)}, u32[]{:S(2)}, u32[]{:S(2)}) collective-permute-start(bf16[80,256]{1,0:T(8,128)(2,1)S(1)} %get-tuple-element.49), channel_id=1, source_target_pairs={{8,0},{16,8},{24,16},{32,24},{40,32},{48,40},{56,48},{64,56},{72,6... | collective-permute-start | bytes 122888 | tf_op jit(solution)/shard_map/ppermute | solution.py:334
  32.3 9.2 %collective-permute-start.9 = (bf16[80,256]{1,0:T(8,128)(2,1)S(1)}, bf16[80,256]{1,0:T(8,128)(2,1)S(1)}, u32[]{:S(2)}, u32[]{:S(2)}) collective-permute-start(bf16[80,256]{1,0:T(8,128)(2,1)S(1)} %get-tuple-element.51), channel_id=1, source_target_pairs={{0,6},{1,7},{2,4},{3,5},{4,2},{5,3},{6,0},{7,1},{8,14},{9,15},{10,... | collective-permute-start | bytes 122888 | tf_op jit(solution)/shard_map/ppermute | solution.py:291
  34.0 9.0 %collective-permute-start.10 = (bf16[80,256]{1,0:T(8,128)(2,1)S(1)}, bf16[80,256]{1,0:T(8,128)(2,1)S(1)}, u32[]{:S(2)}, u32[]{:S(2)}) collective-permute-start(bf16[80,256]{1,0:T(8,128)(2,1)S(1)} %get-tuple-element.52), channel_id=1, source_target_pairs={{0,4},{1,5},{2,6},{3,7},{4,0},{5,1},{6,2},{7,3},{8,12},{9,13},{10,... | collective-permute-start | bytes 122888 | tf_op jit(solution)/shard_map/ppermute | solution.py:291
  37.7 7.6 %collective-permute-start.11 = (bf16[80,256]{1,0:T(8,128)(2,1)S(1)}, bf16[80,256]{1,0:T(8,128)(2,1)S(1)}, u32[]{:S(2)}, u32[]{:S(2)}) collective-permute-start(bf16[80,256]{1,0:T(8,128)(2,1)S(1)} %get-tuple-element.53), channel_id=1, source_target_pairs={{0,7},{1,6},{2,5},{3,4},{4,3},{5,2},{6,1},{7,0},{8,15},{9,14},{10,... | collective-permute-start | bytes 122888 | tf_op jit(solution)/shard_map/ppermute | solution.py:291
  40.2 5.6 %collective-permute-start.12 = (bf16[80,256]{1,0:T(8,128)(2,1)S(1)}, bf16[80,256]{1,0:T(8,128)(2,1)S(1)}, u32[]{:S(2)}, u32[]{:S(2)}) collective-permute-start(bf16[80,256]{1,0:T(8,128)(2,1)S(1)} %get-tuple-element.54), channel_id=1, source_target_pairs={{0,5},{1,4},{2,7},{3,6},{4,1},{5,0},{6,3},{7,2},{8,13},{9,12},{10,... | collective-permute-start | bytes 122888 | tf_op jit(solution)/shard_map/ppermute | solution.py:291
  40.9 4.9 %collective-permute-start.13 = (bf16[80,256]{1,0:T(8,128)(2,1)S(1)}, bf16[80,256]{1,0:T(8,128)(2,1)S(1)}, u32[]{:S(2)}, u32[]{:S(2)}) collective-permute-start(bf16[80,256]{1,0:T(8,128)(2,1)S(1)} %get-tuple-element.55), channel_id=1, source_target_pairs={{0,2},{1,3},{2,0},{3,1},{4,6},{5,7},{6,4},{7,5},{8,10},{9,11},{10,... | collective-permute-start | bytes 122888 | tf_op jit(solution)/shard_map/ppermute | solution.py:291
  41.5 5.3 %collective-permute-start.14 = (bf16[80,256]{1,0:T(8,128)(2,1)S(1)}, bf16[80,256]{1,0:T(8,128)(2,1)S(1)}, u32[]{:S(2)}, u32[]{:S(2)}) collective-permute-start(bf16[80,256]{1,0:T(8,128)(2,1)S(1)} %get-tuple-element.56), channel_id=1, source_target_pairs={{0,3},{1,2},{2,1},{3,0},{4,7},{5,6},{6,5},{7,4},{8,11},{9,10},{10,... | collective-permute-start | bytes 122888 | tf_op jit(solution)/shard_map/ppermute | solution.py:291
  43.0 3.7 %collective-permute-start.15 = (bf16[80,256]{1,0:T(8,128)(2,1)S(1)}, bf16[80,256]{1,0:T(8,128)(2,1)S(1)}, u32[]{:S(2)}, u32[]{:S(2)}) collective-permute-start(bf16[80,256]{1,0:T(8,128)(2,1)S(1)} %get-tuple-element.57), channel_id=1, source_target_pairs={{0,1},{1,0},{2,3},{3,2},{4,5},{5,4},{6,7},{7,6},{8,9},{9,8},{10,11... | collective-permute-start | bytes 122888 | tf_op jit(solution)/shard_map/ppermute | solution.py:291
  46.9 5.5 %collective-permute-start.18 = (bf16[160,256]{1,0:T(8,128)(2,1)S(1)}, bf16[160,256]{1,0:T(8,128)(2,1)S(1)}, u32[]{:S(2)}, u32[]{:S(2)}) collective-permute-start(bf16[160,256]{1,0:T(8,128)(2,1)S(1)} %get-tuple-element.59.refs_0_), channel_id=1, source_target_pairs={{0,6},{1,7},{2,4},{3,5},{4,2},{5,3},{6,0},{7,1},{8,14},{9,15},{10,... | collective-permute-start | bytes 245768 | tf_op jit(solution)/shard_map/ppermute | solution.py:291
  48.7 7.9 %collective-permute-start.17 = (bf16[160,256]{1,0:T(8,128)(2,1)S(1)}, bf16[160,256]{1,0:T(8,128)(2,1)S(1)}, u32[]{:S(2)}, u32[]{:S(2)}) collective-permute-start(bf16[160,256]{1,0:T(8,128)(2,1)S(1)} %get-tuple-element.59.refs_0_), channel_id=1, source_target_pairs={{0,4},{1,5},{2,6},{3,7},{4,0},{5,1},{6,2},{7,3},{8,12},{9,13},{10,... | collective-permute-start | bytes 245768 | tf_op jit(solution)/shard_map/ppermute | solution.py:291
  48.7 8.4 %collective-permute-start.16 = (bf16[160,256]{1,0:T(8,128)(2,1)S(1)}, bf16[160,256]{1,0:T(8,128)(2,1)S(1)}, u32[]{:S(2)}, u32[]{:S(2)}) collective-permute-start(bf16[160,256]{1,0:T(8,128)(2,1)S(1)} %get-tuple-element.59.refs_0_), channel_id=1, source_target_pairs={{0,2},{1,3},{2,0},{3,1},{4,6},{5,7},{6,4},{7,5},{8,10},{9,11},{10,... | collective-permute-start | bytes 245768 | tf_op jit(solution)/shard_map/ppermute | solution.py:291
  50.5 6.6 %collective-permute-start.19 = (bf16[160,256]{1,0:T(8,128)(2,1)S(1)}, bf16[160,256]{1,0:T(8,128)(2,1)S(1)}, u32[]{:S(2)}, u32[]{:S(2)}) collective-permute-start(bf16[160,256]{1,0:T(8,128)(2,1)S(1)} %get-tuple-element.59.refs_0_), channel_id=1, source_target_pairs={{0,1},{1,0},{2,3},{3,2},{4,5},{5,4},{6,7},{7,6},{8,9},{9,8},{10,11... | collective-permute-start | bytes 245768 | tf_op jit(solution)/shard_map/ppermute | solution.py:291
  52.4 4.8 %collective-permute-start.22 = (bf16[160,256]{1,0:T(8,128)(2,1)S(1)}, bf16[160,256]{1,0:T(8,128)(2,1)S(1)}, u32[]{:S(2)}, u32[]{:S(2)}) collective-permute-start(bf16[160,256]{1,0:T(8,128)(2,1)S(1)} %collective-permute-done.18.refs_3_), channel_id=1, source_target_pairs={{0,1},{1,0},{2,3},{3,2},{4,5},{5,4},{6,7},{7,6},{8,9},{9,8},{10,11... | collective-permute-start | bytes 245768 | tf_op jit(solution)/shard_map/ppermute | solution.py:291
  56.6 1.4 %collective-permute-start.21 = (bf16[160,256]{1,0:T(8,128)(2,1)S(1)}, bf16[160,256]{1,0:T(8,128)(2,1)S(1)}, u32[]{:S(2)}, u32[]{:S(2)}) collective-permute-start(bf16[160,256]{1,0:T(8,128)(2,1)S(1)} %collective-permute-done.17.refs_2_), channel_id=1, source_target_pairs={{0,1},{1,0},{2,3},{3,2},{4,5},{5,4},{6,7},{7,6},{8,9},{9,8},{10,11... | collective-permute-start | bytes 245768 | tf_op jit(solution)/shard_map/ppermute | solution.py:291
  57.1 1.3 %collective-permute-start.20 = (bf16[160,256]{1,0:T(8,128)(2,1)S(1)}, bf16[160,256]{1,0:T(8,128)(2,1)S(1)}, u32[]{:S(2)}, u32[]{:S(2)}) collective-permute-start(bf16[160,256]{1,0:T(8,128)(2,1)S(1)} %collective-permute-done.16.refs_1_), channel_id=1, source_target_pairs={{0,1},{1,0},{2,3},{3,2},{4,5},{5,4},{6,7},{7,6},{8,9},{9,8},{10,11... | collective-permute-start | bytes 245768 | tf_op jit(solution)/shard_map/ppermute | solution.py:291
  61.0 25.0 %all-to-all-start = ((bf16[16,40,896]{2,1,0:T(8,128)(2,1)}), bf16[16,40,896]{2,1,0:T(8,128)(2,1)S(1)}, u32[]{:S(2)}, u32[]{:S(2)}) async-start(bf16[16,40,896]{2,1,0:T(8,128)(2,1)} %bitcast.7), calls=%async_computation | async-start | bytes 2293760 | tf_op jit(solution)/shard_map/all_to_all | solution.py:348
  69.2 9.1 %collective-permute-start.23 = (bf16[2,80,128]{2,1,0:T(8,128)(2,1)S(1)}, bf16[2,80,128]{2,1,0:T(8,128)(2,1)S(1)}, u32[]{:S(2)}, u32[]{:S(2)}) collective-permute-start(bf16[2,80,128]{2,1,0:T(8,128)(2,1)S(1)} %get-tuple-element.62), channel_id=1, source_target_pairs={{8,0},{16,8},{24,16},{32,24},{40,32},{48,40},{56,48},{64,56},{72,6... | collective-permute-start | bytes 122888 | tf_op jit(solution)/shard_map/ppermute | solution.py:347
  78.6 7.7 %collective-permute-start.24 = (bf16[160,128]{1,0:T(8,128)(2,1)S(1)}, bf16[160,128]{1,0:T(8,128)(2,1)S(1)}, u32[]{:S(2)}, u32[]{:S(2)}) collective-permute-start(bf16[160,128]{1,0:T(8,128)(2,1)S(1)} %get-tuple-element.64), channel_id=1, source_target_pairs={{0,2},{1,3},{2,0},{3,1},{4,6},{5,7},{6,4},{7,5},{8,10},{9,11},{10,... | collective-permute-start | bytes 122888 | tf_op jit(solution)/shard_map/ppermute | solution.py:291
  78.7 7.6 %collective-permute-start.25 = (bf16[160,128]{1,0:T(8,128)(2,1)S(1)}, bf16[160,128]{1,0:T(8,128)(2,1)S(1)}, u32[]{:S(2)}, u32[]{:S(2)}) collective-permute-start(bf16[160,128]{1,0:T(8,128)(2,1)S(1)} %get-tuple-element.65), channel_id=1, source_target_pairs={{0,4},{1,5},{2,6},{3,7},{4,0},{5,1},{6,2},{7,3},{8,12},{9,13},{10,... | collective-permute-start | bytes 122888 | tf_op jit(solution)/shard_map/ppermute | solution.py:291
  80.3 5.9 %collective-permute-start.26 = (bf16[160,128]{1,0:T(8,128)(2,1)S(1)}, bf16[160,128]{1,0:T(8,128)(2,1)S(1)}, u32[]{:S(2)}, u32[]{:S(2)}) collective-permute-start(bf16[160,128]{1,0:T(8,128)(2,1)S(1)} %get-tuple-element.66), channel_id=1, source_target_pairs={{0,6},{1,7},{2,4},{3,5},{4,2},{5,3},{6,0},{7,1},{8,14},{9,15},{10,... | collective-permute-start | bytes 122888 | tf_op jit(solution)/shard_map/ppermute | solution.py:291
  86.3 8.5 %collective-permute-start.27 = (bf16[320,128]{1,0:T(8,128)(2,1)S(1)}, bf16[320,128]{1,0:T(8,128)(2,1)S(1)}, u32[]{:S(2)}, u32[]{:S(2)}) collective-permute-start(bf16[320,128]{1,0:T(8,128)(2,1)S(1)} %shard_map.75), channel_id=1, source_target_pairs={{0,1},{1,0},{2,3},{3,2},{4,5},{5,4},{6,7},{7,6},{8,9},{9,8},{10,11... | collective-permute-start | bytes 245768 | tf_op jit(solution)/shard_map/ppermute | solution.py:291
  88.9 7.7 %collective-permute-start.28 = (bf16[20,896]{1,0:T(8,128)(2,1)S(1)}, bf16[20,896]{1,0:T(8,128)(2,1)S(1)}, u32[]{:S(2)}, u32[]{:S(2)}) collective-permute-start(bf16[20,896]{1,0:T(8,128)(2,1)S(1)} %get-tuple-element.71), channel_id=1, source_target_pairs={{0,8},{8,0},{16,24},{24,16},{32,40},{40,32},{48,56},{56,48},{64,72... | collective-permute-start | bytes 107528 | tf_op jit(solution)/shard_map/ppermute | solution.py:358

commit v9 on v8

--- a/solution.py
+++ b/solution.py
@@ -10,7 +10,8 @@
 
 F32 = jnp.float32
 BF16 = jnp.bfloat16
-SOURCE = (0, 2, 4, 6, 1, 3, 5, 7)
+SOURCE = (0, 6, 4, 2, 1, 7, 5, 3)
+GATHERED = (0, 2, 4, 6, 1, 3, 5, 7)
 HEIGHTS = (80, 160, 160, 160, 80)
 ORDER = (0, 6, 4, 7, 5, 2, 3, 1)
 HEAVY = 12_000_000_000
@@ -169,9 +170,28 @@
     share_ref[80:160, 128:256] = up_ref[:, 128:256]
 
 
-def weight_grad_kernel(slot_ref, win_ref, cot_ref, act_ref, *refs):
-    *all_refs, red_ref, pre_ref, shift_ref, cell_ref = refs
-    for n, k in enumerate(SOURCE):
+def group_grad_kernel(act_ref, cot_ref, part_ref, edge_ref, inner_ref):
+    rows = [act_ref[:, 128 * i : 128 * i + 128].astype(F32) for i in range(2)]
+    moved = [[move(x).astype(BF16) for x in rows] for move in (from_left, lambda x: x, from_right)]
+    edge_ref[...] = jnp.zeros((5, 256, 256), BF16)
+    inner_ref[...] = jnp.zeros((5, 256, 256), BF16)
+    for g in range(5):
+        for u in range(3):
+            for v in range(3):
+                base = 80 + 16 * (3 * u + v)
+                for i in range(2):
+                    row = i + 1 - u
+                    target_ref = inner_ref if 0 <= row < 2 else edge_ref
+                    lanes = slice(0, 128) if row in (0, -1) else slice(128, 256)
+                    target_ref[g, base : base + 16, lanes] = moved[v][i][16 * g : 16 * g + 16]
+    for g in range(5):
+        here = slice(128 * g, 128 * g + 128)
+        part_ref[here, :] = nt(cot_ref[here, :], inner_ref[g])
+
+
+def weight_grad_kernel(slot_ref, win_ref, part_ref, shift_ref, *refs):
+    *all_refs, red_ref, pre_ref, cell_ref = refs
+    for n, k in enumerate(GATHERED):
         start = pl.multiple_of(16 * (slot_ref[0] ^ k), 16)
         for g in range(5):
             pre_ref[pl.ds(128 * g + start, 16), :] = all_refs[n][16 * g : 16 * g + 16, :]
@@ -181,24 +201,14 @@
                 ]
     pre = pre_ref[...]
     red_ref[:, 0:640] = nt(pre, win_ref[0:640, :]).astype(BF16)
-    rows = [act_ref[:, 128 * i : 128 * i + 128].astype(F32) for i in range(2)]
-    moved = [[move(x).astype(BF16) for x in rows] for move in (from_left, lambda x: x, from_right)]
-    shift_ref[...] = jnp.zeros((5, 256, 512), BF16)
-    for g in range(5):
-        for u in range(3):
-            for v in range(3):
-                base = 80 + 16 * (3 * u + v)
-                for i in range(2):
-                    lanes = slice(128 * (i + 2 - u), 128 * (i + 2 - u) + 128)
-                    shift_ref[g, base : base + 16, lanes] = moved[v][i][16 * g : 16 * g + 16]
     eye = jnp.where(iota((128, 128), 0) == iota((128, 128), 1), 1.0, 0.0).astype(BF16)
     tail = jnp.concatenate([win_ref[640:720, :], jnp.zeros((176, 256), BF16)], axis=0)
     last = nt(pre, tail)
     for g in range(5):
         here = slice(128 * g, 128 * g + 128)
         rims = nt(eye, cell_ref[:, here]).astype(BF16)
-        cot = jnp.concatenate([rims[:, 0:128], cot_ref[here, :], rims[:, 128:256]], axis=1)
-        red_ref[here, 640:896] = (last[here] + nt(cot, shift_ref[g])).astype(BF16)
+        group = part_ref[here, :] + nt(rims, shift_ref[g])
+        red_ref[here, 640:896] = (last[here] + group).astype(BF16)
 
 
 def image_grad_kernel(pre_ref, weight_ref, img_ref, up_ref):
@@ -291,8 +301,8 @@
     return lax.ppermute(block, "fsdp", [(i, i ^ k) for i in range(8)])
 
 
-def exchange(blocks):
-    direct = [swap(block, k) for block, k in zip(blocks[1:], SOURCE[1:5])]
+def exchange(blocks, source=SOURCE):
+    direct = [swap(block, k) for block, k in zip(blocks[1:], source[1:5])]
     return [blocks[0]] + direct + [swap(got, 1) for got in direct[:3]]
 
 
@@ -335,11 +345,15 @@
     act, share = call(
         middle_kernel, [((80, 256), BF16), ((160, 256), BF16)], own, down, up, *hid
     )
+    part, edge = call(
+        group_grad_kernel, [((640, 256), F32), ((5, 256, 256), BF16)], act, cot,
+        scratch=[pltpu.VMEM((5, 256, 256), BF16)],
+    )
     red, pre = call(
         weight_grad_kernel,
         [((640, 896), BF16), ((640, 256), BF16)],
-        slot, windows, cot, act, *exchange([share] * 5),
-        scratch=[pltpu.VMEM((5, 256, 512), BF16), pltpu.VMEM((256, 640), BF16)], smem=1,
+        slot, windows, part, edge, *exchange([share] * 5, GATHERED),
+        scratch=[pltpu.VMEM((256, 640), BF16)], smem=1,
     )
     img, img_up = call(
         image_grad_kernel, [((8, 80, 128), F32), ((2, 80, 128), BF16)], pre, weights

time: 99.1 us -> 95.7 us (0.966); the launches traced: 97.4 us -> 95.1 us
  starting transfers between devices: 66.8 us -> 55.9 us
  waiting for transfers between devices: 19.9 us -> 28.6 us
    ppermute x25, starting transfers between devices: 43.3 us -> 33.9 us  [swap(): return lax.ppermute(block, 'fsdp', [(i, i ^ k) for i in range(8)])]
    ppermute x25, waiting for transfers between devices: 6.51 us -> 13.8 us  [swap(): return lax.ppermute(block, 'fsdp', [(i, i ^ k) for i in range(8)])]
    ppermute x1, starting transfers between devices: 5.84 us -> 3.63 us  [per_device(): given = lax.ppermute(give, 'tile', partners)]
    ppermute x1, waiting for transfers between devices: 0.94 us -> 2.24 us  [per_device(): given = lax.ppermute(give, 'tile', partners)]
    pallas_call x11 -> x12, Pallas kernels: 7.19 us -> 7.14 us  [call(): pl.pallas_call(kernel, out_shape=[jax.ShapeDtypeStruct(shape, dtype) for...]
  transfers between devices with their start and end apart: 30 -> 30, of which waited for: 12 -> 14; matrix products, arithmetic and copies ran while one was open for 0% -> 0% of each run, Pallas kernels for 2% -> 3%
where the time goes in v9:
time: 95.7 us; the launch traced here: 95.1 us
  starting transfers between devices  55.9 us (58%)
  waiting for transfers between devices  28.6 us (30%)
  Pallas kernels  7.14 us (7%)
  local copies, waits for them, and re-layouts  2.69 us (3%)
    ppermute x25, starting transfers between devices, swap(): return lax.ppermute(block, 'fsdp', [(i, i ^ k) for i in range(8)])  33.9 us
    ppermute x25, waiting for transfers between devices, swap(): return lax.ppermute(block, 'fsdp', [(i, i ^ k) for i in range(8)])  13.8 us
    all_to_all x1, starting transfers between devices, per_device(): lax.all_to_all(red.reshape(16, 40, 896), 'tile', 0, 0, tiled=True, axis_i...  7.98 us
    ppermute x1, starting transfers between devices, per_device(): down = lax.ppermute(down, 'tile', downward)  7.74 us
    ppermute x1, waiting for transfers between devices, per_device(): img_below = lax.ppermute(img_up, 'tile', upward)  7.65 us
    pallas_call x12, Pallas kernels, call(): pl.pallas_call(kernel, out_shape=[jax.ShapeDtypeStruct(shape, dtype) for...  7.14 us
    all_to_all x1, waiting for transfers between devices, per_device(): lax.all_to_all(red.reshape(16, 40, 896), 'tile', 0, 0, tiled=True, axis_i...  4.03 us
    ppermute x1, starting transfers between devices, per_device(): given = lax.ppermute(give, 'tile', partners)  3.63 us
  transfers between devices with their start and end apart: 30, of which 14 were waited for; matrix products, arithmetic and copies ran while one was open for 0% of the time, Pallas kernels for 3%

profile of v9, /device:TPU:1, one launch (start us, length us, event | category | flops | bytes accessed | tf_op | source)
XLA Modules:
  0.0 95.1 jit_solution(4660794167716651960)
XLA Ops:
  0.7 1.0 %copy-done.1 = bf16[9,128,80]{1,2,0:T(8,128)(2,1)S(1)} copy-done((bf16[9,128,80]{1,2,0:T(8,128)(2,1)S(1)}, bf16[9,128,80]{1,2,0:T(8,128)(2,1)}, u32[]{:S(2)}) %copy-start.1) | copy-done | bytes 184344
  1.7 0.9 copy-done.2
  2.6 0.8 copy-done.3
  3.3 0.5 shard_map.67
  3.8 5.3 %collective-permute-start = (bf16[512,128]{1,0:T(8,128)(2,1)S(1)}, bf16[512,128]{1,0:T(8,128)(2,1)S(1)}, u32[]{:S(2)}, u32[]{:S(2)}) collective-permute-start(bf16[512,128]{1,0:T(8,128)(2,1)S(1)} %get-tuple-element.42), channel_id=1, source_target_pairs={{0,6},{1,7},{2,4},{3,5},{4,2},{5,3},{6,0},{7,1},{8,14},{9,15},{10,... | collective-permute-start | bytes 393224 | tf_op jit(solution)/shard_map/ppermute | solution.py:301
  9.1 0.4 collective-permute-start.2
  9.5 2.1 %collective-permute-done.refs_1_ = bf16[512,128]{1,0:T(8,128)(2,1)S(1)} collective-permute-done((bf16[512,128]{1,0:T(8,128)(2,1)S(1)}, bf16[512,128]{1,0:T(8,128)(2,1)S(1)}, u32[]{:S(2)}, u32[]{:S(2)}) %collective-permute-start) | collective-permute-done | bytes 131104 | tf_op jit(solution)/shard_map/ppermute | solution.py:301
  11.6 3.8 %collective-permute-start.4 = (bf16[512,128]{1,0:T(8,128)(2,1)S(1)}, bf16[512,128]{1,0:T(8,128)(2,1)S(1)}, u32[]{:S(2)}, u32[]{:S(2)}) collective-permute-start(bf16[512,128]{1,0:T(8,128)(2,1)S(1)} %collective-permute-done.refs_1_), channel_id=1, source_target_pairs={{0,1},{1,0},{2,3},{3,2},{4,5},{5,4},{6,7},{7,6},{8,9},{9,8},{10,11... | collective-permute-start | bytes 393224 | tf_op jit(solution)/shard_map/ppermute | solution.py:301
  15.4 3.9 %collective-permute-done.1.refs_2_ = bf16[512,128]{1,0:T(8,128)(2,1)S(1)} collective-permute-done((bf16[512,128]{1,0:T(8,128)(2,1)S(1)}, bf16[512,128]{1,0:T(8,128)(2,1)S(1)}, u32[]{:S(2)}, u32[]{:S(2)}) %collective-permute-start.1) | collective-permute-done | bytes 131104 | tf_op jit(solution)/shard_map/ppermute | solution.py:301
  19.3 1.3 %collective-permute-start.5 = (bf16[512,128]{1,0:T(8,128)(2,1)S(1)}, bf16[512,128]{1,0:T(8,128)(2,1)S(1)}, u32[]{:S(2)}, u32[]{:S(2)}) collective-permute-start(bf16[512,128]{1,0:T(8,128)(2,1)S(1)} %collective-permute-done.1.refs_2_), channel_id=1, source_target_pairs={{0,1},{1,0},{2,3},{3,2},{4,5},{5,4},{6,7},{7,6},{8,9},{9,8},{10,11... | collective-permute-start | bytes 393224 | tf_op jit(solution)/shard_map/ppermute | solution.py:301
  20.6 0.5 collective-permute-start.3
  21.1 1.0 %collective-permute-done.3.refs_4_ = bf16[336,128]{1,0:T(8,128)(2,1)S(1)} collective-permute-done((bf16[336,128]{1,0:T(8,128)(2,1)S(1)}, bf16[336,128]{1,0:T(8,128)(2,1)S(1)}, u32[]{:S(2)}, u32[]{:S(2)}) %collective-permute-start.3) | collective-permute-done | bytes 86048 | tf_op jit(solution)/shard_map/ppermute | solution.py:301
  22.1 0.8 shard_map.68
  23.0 7.7 %collective-permute-start.7 = (bf16[80,512]{1,0:T(8,128)(2,1)S(1)}, bf16[80,512]{1,0:T(8,128)(2,1)S(1)}, u32[]{:S(2)}, u32[]{:S(2)}) collective-permute-start(bf16[80,512]{1,0:T(8,128)(2,1)S(1)} %get-tuple-element.47), channel_id=1, source_target_pairs={{0,8},{8,16},{16,24},{24,32},{32,40},{40,48},{48,56},{56,64},{64,7... | collective-permute-start | bytes 245768 | tf_op jit(solution)/shard_map/ppermute | solution.py:337
  30.7 1.3 %collective-permute-start.8 = (bf16[80,256]{1,0:T(8,128)(2,1)S(1)}, bf16[80,256]{1,0:T(8,128)(2,1)S(1)}, u32[]{:S(2)}, u32[]{:S(2)}) collective-permute-start(bf16[80,256]{1,0:T(8,128)(2,1)S(1)} %get-tuple-element.50), channel_id=1, source_target_pairs={{8,0},{16,8},{24,16},{32,24},{40,32},{48,40},{56,48},{64,56},{72,6... | collective-permute-start | bytes 122888 | tf_op jit(solution)/shard_map/ppermute | solution.py:344
  32.2 0.5 shard_map.69
  32.7 2.3 %collective-permute-start.9 = (bf16[80,256]{1,0:T(8,128)(2,1)S(1)}, bf16[80,256]{1,0:T(8,128)(2,1)S(1)}, u32[]{:S(2)}, u32[]{:S(2)}) collective-permute-start(bf16[80,256]{1,0:T(8,128)(2,1)S(1)} %get-tuple-element.52), channel_id=1, source_target_pairs={{0,6},{1,7},{2,4},{3,5},{4,2},{5,3},{6,0},{7,1},{8,14},{9,15},{10,... | collective-permute-start | bytes 122888 | tf_op jit(solution)/shard_map/ppermute | solution.py:301
  35.0 2.5 %collective-permute-start.11 = (bf16[80,256]{1,0:T(8,128)(2,1)S(1)}, bf16[80,256]{1,0:T(8,128)(2,1)S(1)}, u32[]{:S(2)}, u32[]{:S(2)}) collective-permute-start(bf16[80,256]{1,0:T(8,128)(2,1)S(1)} %get-tuple-element.54), channel_id=1, source_target_pairs={{0,7},{1,6},{2,5},{3,4},{4,3},{5,2},{6,1},{7,0},{8,15},{9,14},{10,... | collective-permute-start | bytes 122888 | tf_op jit(solution)/shard_map/ppermute | solution.py:301
  37.5 1.2 %collective-permute-start.12 = (bf16[80,256]{1,0:T(8,128)(2,1)S(1)}, bf16[80,256]{1,0:T(8,128)(2,1)S(1)}, u32[]{:S(2)}, u32[]{:S(2)}) collective-permute-start(bf16[80,256]{1,0:T(8,128)(2,1)S(1)} %get-tuple-element.55), channel_id=1, source_target_pairs={{0,5},{1,4},{2,7},{3,6},{4,1},{5,0},{6,3},{7,2},{8,13},{9,12},{10,... | collective-permute-start | bytes 122888 | tf_op jit(solution)/shard_map/ppermute | solution.py:301
  38.7 0.7 collective-permute-done.8.up_ref
  39.4 3.4 %collective-permute-start.14 = (bf16[80,256]{1,0:T(8,128)(2,1)S(1)}, bf16[80,256]{1,0:T(8,128)(2,1)S(1)}, u32[]{:S(2)}, u32[]{:S(2)}) collective-permute-start(bf16[80,256]{1,0:T(8,128)(2,1)S(1)} %get-tuple-element.57), channel_id=1, source_target_pairs={{0,3},{1,2},{2,1},{3,0},{4,7},{5,6},{6,5},{7,4},{8,11},{9,10},{10,... | collective-permute-start | bytes 122888 | tf_op jit(solution)/shard_map/ppermute | solution.py:301
  42.8 1.3 %collective-permute-done.12.refs_4_ = bf16[80,256]{1,0:T(8,128)(2,1)S(1)} collective-permute-done((bf16[80,256]{1,0:T(8,128)(2,1)S(1)}, bf16[80,256]{1,0:T(8,128)(2,1)S(1)}, u32[]{:S(2)}, u32[]{:S(2)}) %collective-permute-start.12) | collective-permute-done | bytes 40992 | tf_op jit(solution)/shard_map/ppermute | solution.py:301
  44.1 1.2 %collective-permute-done.14.refs_6_ = bf16[80,256]{1,0:T(8,128)(2,1)S(1)} collective-permute-done((bf16[80,256]{1,0:T(8,128)(2,1)S(1)}, bf16[80,256]{1,0:T(8,128)(2,1)S(1)}, u32[]{:S(2)}, u32[]{:S(2)}) %collective-permute-start.14) | collective-permute-done | bytes 40992 | tf_op jit(solution)/shard_map/ppermute | solution.py:301
  45.4 2.0 %collective-permute-start.18 = (bf16[160,256]{1,0:T(8,128)(2,1)S(1)}, bf16[160,256]{1,0:T(8,128)(2,1)S(1)}, u32[]{:S(2)}, u32[]{:S(2)}) collective-permute-start(bf16[160,256]{1,0:T(8,128)(2,1)S(1)} %get-tuple-element.63.refs_0_), channel_id=1, source_target_pairs={{0,6},{1,7},{2,4},{3,5},{4,2},{5,3},{6,0},{7,1},{8,14},{9,15},{10,... | collective-permute-start | bytes 245768 | tf_op jit(solution)/shard_map/ppermute | solution.py:301
  47.5 1.6 %collective-permute-start.16 = (bf16[160,256]{1,0:T(8,128)(2,1)S(1)}, bf16[160,256]{1,0:T(8,128)(2,1)S(1)}, u32[]{:S(2)}, u32[]{:S(2)}) collective-permute-start(bf16[160,256]{1,0:T(8,128)(2,1)S(1)} %get-tuple-element.63.refs_0_), channel_id=1, source_target_pairs={{0,2},{1,3},{2,0},{3,1},{4,6},{5,7},{6,4},{7,5},{8,10},{9,11},{10,... | collective-permute-start | bytes 245768 | tf_op jit(solution)/shard_map/ppermute | solution.py:301
  49.1 1.1 %collective-permute-start.19 = (bf16[160,256]{1,0:T(8,128)(2,1)S(1)}, bf16[160,256]{1,0:T(8,128)(2,1)S(1)}, u32[]{:S(2)}, u32[]{:S(2)}) collective-permute-start(bf16[160,256]{1,0:T(8,128)(2,1)S(1)} %get-tuple-element.63.refs_0_), channel_id=1, source_target_pairs={{0,1},{1,0},{2,3},{3,2},{4,5},{5,4},{6,7},{7,6},{8,9},{9,8},{10,11... | collective-permute-start | bytes 245768 | tf_op jit(solution)/shard_map/ppermute | solution.py:301
  50.2 1.0 %collective-permute-done.18.refs_3_ = bf16[160,256]{1,0:T(8,128)(2,1)S(1)} collective-permute-done((bf16[160,256]{1,0:T(8,128)(2,1)S(1)}, bf16[160,256]{1,0:T(8,128)(2,1)S(1)}, u32[]{:S(2)}, u32[]{:S(2)}) %collective-permute-start.18) | collective-permute-done | bytes 81952 | tf_op jit(solution)/shard_map/ppermute | solution.py:301
  51.2 1.8 %collective-permute-start.22 = (bf16[160,256]{1,0:T(8,128)(2,1)S(1)}, bf16[160,256]{1,0:T(8,128)(2,1)S(1)}, u32[]{:S(2)}, u32[]{:S(2)}) collective-permute-start(bf16[160,256]{1,0:T(8,128)(2,1)S(1)} %collective-permute-done.18.refs_3_), channel_id=1, source_target_pairs={{0,1},{1,0},{2,3},{3,2},{4,5},{5,4},{6,7},{7,6},{8,9},{9,8},{10,11... | collective-permute-start | bytes 245768 | tf_op jit(solution)/shard_map/ppermute | solution.py:301
  53.0 2.5 %collective-permute-done.17.refs_2_ = bf16[160,256]{1,0:T(8,128)(2,1)S(1)} collective-permute-done((bf16[160,256]{1,0:T(8,128)(2,1)S(1)}, bf16[160,256]{1,0:T(8,128)(2,1)S(1)}, u32[]{:S(2)}, u32[]{:S(2)}) %collective-permute-start.17) | collective-permute-done | bytes 81952 | tf_op jit(solution)/shard_map/ppermute | solution.py:301
  55.5 0.5 collective-permute-start.21
  56.0 0.4 shard_map.71
  56.4 0.4 collective-permute-done.21.refs_6_
  56.9 0.4 collective-permute-done.20.refs_5_
  57.2 2.1 %shard_map.72 = (bf16[640,896]{1,0:T(8,128)(2,1)}, bf16[640,256]{1,0:T(8,128)(2,1)S(1)}) custom-call(s32[1]{0:T(128)} %bitcast.slot_ref, bf16[720,256]{1,0:T(8,128)(2,1)S(1)} %get-tuple-element.48.win_ref, f32[640,256]{1,0:T(8,128)S(1)} %get-tuple-element.61.part_ref, bf16[5,256,256]{2,1,0:T(8,128)(2,1)S(1)} %get-tuple-element.62.shift_ref, ...), custom_call_target="tpu_custom_call" | custom-call | tf_op jit(solution)/shard_map/pallas_call | solution.py:289
  59.3 8.0 %all-to-all-start = ((bf16[16,40,896]{2,1,0:T(8,128)(2,1)}), bf16[16,40,896]{2,1,0:T(8,128)(2,1)S(1)}, u32[]{:S(2)}, u32[]{:S(2)}) async-start(bf16[16,40,896]{2,1,0:T(8,128)(2,1)} %bitcast.7), calls=%async_computation | async-start | bytes 2293760 | tf_op jit(solution)/shard_map/all_to_all | solution.py:362
  67.3 0.5 shard_map.73
  67.8 1.3 %collective-permute-start.23 = (bf16[2,80,128]{2,1,0:T(8,128)(2,1)S(1)}, bf16[2,80,128]{2,1,0:T(8,128)(2,1)S(1)}, u32[]{:S(2)}, u32[]{:S(2)}) collective-permute-start(bf16[2,80,128]{2,1,0:T(8,128)(2,1)S(1)} %get-tuple-element.66), channel_id=1, source_target_pairs={{8,0},{16,8},{24,16},{32,24},{40,32},{48,40},{56,48},{64,56},{72,6... | collective-permute-start | bytes 122888 | tf_op jit(solution)/shard_map/ppermute | solution.py:361
  69.1 7.6 %collective-permute-done.23.below_ref = bf16[2,80,128]{2,1,0:T(8,128)(2,1)S(1)} collective-permute-done((bf16[2,80,128]{2,1,0:T(8,128)(2,1)S(1)}, bf16[2,80,128]{2,1,0:T(8,128)(2,1)S(1)}, u32[]{:S(2)}, u32[]{:S(2)}) %collective-permute-start.23) | collective-permute-done | bytes 40992 | tf_op jit(solution)/shard_map/ppermute | solution.py:361
  76.7 0.3 shard_map.74
  77.0 2.6 %collective-permute-start.24 = (bf16[160,128]{1,0:T(8,128)(2,1)S(1)}, bf16[160,128]{1,0:T(8,128)(2,1)S(1)}, u32[]{:S(2)}, u32[]{:S(2)}) collective-permute-start(bf16[160,128]{1,0:T(8,128)(2,1)S(1)} %get-tuple-element.68), channel_id=1, source_target_pairs={{0,6},{1,7},{2,4},{3,5},{4,2},{5,3},{6,0},{7,1},{8,14},{9,15},{10,... | collective-permute-start | bytes 122888 | tf_op jit(solution)/shard_map/ppermute | solution.py:301
  79.6 1.1 %collective-permute-start.26 = (bf16[160,128]{1,0:T(8,128)(2,1)S(1)}, bf16[160,128]{1,0:T(8,128)(2,1)S(1)}, u32[]{:S(2)}, u32[]{:S(2)}) collective-permute-start(bf16[160,128]{1,0:T(8,128)(2,1)S(1)} %get-tuple-element.70), channel_id=1, source_target_pairs={{0,2},{1,3},{2,0},{3,1},{4,6},{5,7},{6,4},{7,5},{8,10},{9,11},{10,... | collective-permute-start | bytes 122888 | tf_op jit(solution)/shard_map/ppermute | solution.py:301
  80.7 4.0 %all-to-all-done.red_ref = bf16[16,40,896]{2,1,0:T(8,128)(2,1)S(1)} async-done(((bf16[16,40,896]{2,1,0:T(8,128)(2,1)}), bf16[16,40,896]{2,1,0:T(8,128)(2,1)S(1)}, u32[]{:S(2)}, u32[]{:S(2)}) %all-to-all-start) | async-done | bytes 1146912 | tf_op jit(solution)/shard_map/all_to_all | solution.py:362
  84.7 0.2 shard_map.75
  84.9 2.6 %collective-permute-start.27 = (bf16[320,128]{1,0:T(8,128)(2,1)S(1)}, bf16[320,128]{1,0:T(8,128)(2,1)S(1)}, u32[]{:S(2)}, u32[]{:S(2)}) collective-permute-start(bf16[320,128]{1,0:T(8,128)(2,1)S(1)} %shard_map.76), channel_id=1, source_target_pairs={{0,1},{1,0},{2,3},{3,2},{4,5},{5,4},{6,7},{7,6},{8,9},{9,8},{10,11... | collective-permute-start | bytes 245768 | tf_op jit(solution)/shard_map/ppermute | solution.py:301
  87.5 3.6 %collective-permute-start.28 = (bf16[20,896]{1,0:T(8,128)(2,1)S(1)}, bf16[20,896]{1,0:T(8,128)(2,1)S(1)}, u32[]{:S(2)}, u32[]{:S(2)}) collective-permute-start(bf16[20,896]{1,0:T(8,128)(2,1)S(1)} %get-tuple-element.75), channel_id=1, source_target_pairs={{0,8},{8,0},{16,24},{24,16},{32,40},{40,32},{48,56},{56,48},{64,72... | collective-permute-start | bytes 107528 | tf_op jit(solution)/shard_map/ppermute | solution.py:372
  91.1 0.9 shard_map.77
  92.1 2.2 %collective-permute-done.28.given_ref = bf16[20,896]{1,0:T(8,128)(2,1)S(1)} collective-permute-done((bf16[20,896]{1,0:T(8,128)(2,1)S(1)}, bf16[20,896]{1,0:T(8,128)(2,1)S(1)}, u32[]{:S(2)}, u32[]{:S(2)}) %collective-permute-start.28) | collective-permute-done | bytes 35872 | tf_op jit(solution)/shard_map/ppermute | solution.py:372
  94.3 0.8 shard_map.78
  (32 shorter events, 0.4 us)
Async XLA Ops:
  0.6 31.5 %copy-start = (bf16[80,9,640]{2,0,1:T(8,128)(2,1)S(1)}, bf16[80,9,640]{2,0,1:T(8,128)(2,1)}, u32[]{:S(2)}) copy-start(bf16[80,9,640]{2,0,1:T(8,128)(2,1)} %param.5) | copy-start | bytes 2764804
  0.6 1.0 %copy-start.1 = (bf16[9,128,80]{1,2,0:T(8,128)(2,1)S(1)}, bf16[9,128,80]{1,2,0:T(8,128)(2,1)}, u32[]{:S(2)}) copy-start(bf16[9,128,80]{1,2,0:T(8,128)(2,1)} %param.6) | copy-start | bytes 552964
  1.6 0.9 copy-start.2
  2.6 0.8 copy-start.3
  3.8 7.7 %collective-permute-start = (bf16[512,128]{1,0:T(8,128)(2,1)S(1)}, bf16[512,128]{1,0:T(8,128)(2,1)S(1)}, u32[]{:S(2)}, u32[]{:S(2)}) collective-permute-start(bf16[512,128]{1,0:T(8,128)(2,1)S(1)} %get-tuple-element.42), channel_id=1, source_target_pairs={{0,6},{1,7},{2,4},{3,5},{4,2},{5,3},{6,0},{7,1},{8,14},{9,15},{10,... | collective-permute-start | bytes 393224 | tf_op jit(solution)/shard_map/ppermute | solution.py:301
  9.1 10.2 %collective-permute-start.1 = (bf16[512,128]{1,0:T(8,128)(2,1)S(1)}, bf16[512,128]{1,0:T(8,128)(2,1)S(1)}, u32[]{:S(2)}, u32[]{:S(2)}) collective-permute-start(bf16[512,128]{1,0:T(8,128)(2,1)S(1)} %get-tuple-element.43), channel_id=1, source_target_pairs={{0,4},{1,5},{2,6},{3,7},{4,0},{5,1},{6,2},{7,3},{8,12},{9,13},{10,... | collective-permute-start | bytes 393224 | tf_op jit(solution)/shard_map/ppermute | solution.py:301
  9.1 11.5 %collective-permute-start.2 = (bf16[512,128]{1,0:T(8,128)(2,1)S(1)}, bf16[512,128]{1,0:T(8,128)(2,1)S(1)}, u32[]{:S(2)}, u32[]{:S(2)}) collective-permute-start(bf16[512,128]{1,0:T(8,128)(2,1)S(1)} %get-tuple-element.44), channel_id=1, source_target_pairs={{0,2},{1,3},{2,0},{3,1},{4,6},{5,7},{6,4},{7,5},{8,10},{9,11},{10,... | collective-permute-start | bytes 393224 | tf_op jit(solution)/shard_map/ppermute | solution.py:301
  11.6 10.5 %collective-permute-start.4 = (bf16[512,128]{1,0:T(8,128)(2,1)S(1)}, bf16[512,128]{1,0:T(8,128)(2,1)S(1)}, u32[]{:S(2)}, u32[]{:S(2)}) collective-permute-start(bf16[512,128]{1,0:T(8,128)(2,1)S(1)} %collective-permute-done.refs_1_), channel_id=1, source_target_pairs={{0,1},{1,0},{2,3},{3,2},{4,5},{5,4},{6,7},{7,6},{8,9},{9,8},{10,11... | collective-permute-start | bytes 393224 | tf_op jit(solution)/shard_map/ppermute | solution.py:301
  19.3 2.8 %collective-permute-start.5 = (bf16[512,128]{1,0:T(8,128)(2,1)S(1)}, bf16[512,128]{1,0:T(8,128)(2,1)S(1)}, u32[]{:S(2)}, u32[]{:S(2)}) collective-permute-start(bf16[512,128]{1,0:T(8,128)(2,1)S(1)} %collective-permute-done.1.refs_2_), channel_id=1, source_target_pairs={{0,1},{1,0},{2,3},{3,2},{4,5},{5,4},{6,7},{7,6},{8,9},{9,8},{10,11... | collective-permute-start | bytes 393224 | tf_op jit(solution)/shard_map/ppermute | solution.py:301
  20.6 1.5 %collective-permute-start.6 = (bf16[512,128]{1,0:T(8,128)(2,1)S(1)}, bf16[512,128]{1,0:T(8,128)(2,1)S(1)}, u32[]{:S(2)}, u32[]{:S(2)}) collective-permute-start(bf16[512,128]{1,0:T(8,128)(2,1)S(1)} %collective-permute-done.2.refs_3_), channel_id=1, source_target_pairs={{0,1},{1,0},{2,3},{3,2},{4,5},{5,4},{6,7},{7,6},{8,9},{9,8},{10,11... | collective-permute-start | bytes 393224 | tf_op jit(solution)/shard_map/ppermute | solution.py:301
  20.6 1.5 %collective-permute-start.3 = (bf16[336,128]{1,0:T(8,128)(2,1)S(1)}, bf16[336,128]{1,0:T(8,128)(2,1)S(1)}, u32[]{:S(2)}, u32[]{:S(2)}) collective-permute-start(bf16[336,128]{1,0:T(8,128)(2,1)S(1)} %get-tuple-element.45), channel_id=1, source_target_pairs={{0,1},{1,0},{2,3},{3,2},{4,5},{5,4},{6,7},{7,6},{8,9},{9,8},{10,11... | collective-permute-start | bytes 258056 | tf_op jit(solution)/shard_map/ppermute | solution.py:301
  23.0 9.2 %collective-permute-start.7 = (bf16[80,512]{1,0:T(8,128)(2,1)S(1)}, bf16[80,512]{1,0:T(8,128)(2,1)S(1)}, u32[]{:S(2)}, u32[]{:S(2)}) collective-permute-start(bf16[80,512]{1,0:T(8,128)(2,1)S(1)} %get-tuple-element.47), channel_id=1, source_target_pairs={{0,8},{8,16},{16,24},{24,32},{32,40},{40,48},{48,56},{56,64},{64,7... | collective-permute-start | bytes 245768 | tf_op jit(solution)/shard_map/ppermute | solution.py:337
  30.7 8.7 %collective-permute-start.8 = (bf16[80,256]{1,0:T(8,128)(2,1)S(1)}, bf16[80,256]{1,0:T(8,128)(2,1)S(1)}, u32[]{:S(2)}, u32[]{:S(2)}) collective-permute-start(bf16[80,256]{1,0:T(8,128)(2,1)S(1)} %get-tuple-element.50), channel_id=1, source_target_pairs={{8,0},{16,8},{24,16},{32,24},{40,32},{48,40},{56,48},{64,56},{72,6... | collective-permute-start | bytes 122888 | tf_op jit(solution)/shard_map/ppermute | solution.py:344
  32.7 6.7 %collective-permute-start.9 = (bf16[80,256]{1,0:T(8,128)(2,1)S(1)}, bf16[80,256]{1,0:T(8,128)(2,1)S(1)}, u32[]{:S(2)}, u32[]{:S(2)}) collective-permute-start(bf16[80,256]{1,0:T(8,128)(2,1)S(1)} %get-tuple-element.52), channel_id=1, source_target_pairs={{0,6},{1,7},{2,4},{3,5},{4,2},{5,3},{6,0},{7,1},{8,14},{9,15},{10,... | collective-permute-start | bytes 122888 | tf_op jit(solution)/shard_map/ppermute | solution.py:301
  35.0 7.8 %collective-permute-start.10 = (bf16[80,256]{1,0:T(8,128)(2,1)S(1)}, bf16[80,256]{1,0:T(8,128)(2,1)S(1)}, u32[]{:S(2)}, u32[]{:S(2)}) collective-permute-start(bf16[80,256]{1,0:T(8,128)(2,1)S(1)} %get-tuple-element.53), channel_id=1, source_target_pairs={{0,4},{1,5},{2,6},{3,7},{4,0},{5,1},{6,2},{7,3},{8,12},{9,13},{10,... | collective-permute-start | bytes 122888 | tf_op jit(solution)/shard_map/ppermute | solution.py:301
  35.0 7.8 %collective-permute-start.11 = (bf16[80,256]{1,0:T(8,128)(2,1)S(1)}, bf16[80,256]{1,0:T(8,128)(2,1)S(1)}, u32[]{:S(2)}, u32[]{:S(2)}) collective-permute-start(bf16[80,256]{1,0:T(8,128)(2,1)S(1)} %get-tuple-element.54), channel_id=1, source_target_pairs={{0,7},{1,6},{2,5},{3,4},{4,3},{5,2},{6,1},{7,0},{8,15},{9,14},{10,... | collective-permute-start | bytes 122888 | tf_op jit(solution)/shard_map/ppermute | solution.py:301
  37.5 6.7 %collective-permute-start.12 = (bf16[80,256]{1,0:T(8,128)(2,1)S(1)}, bf16[80,256]{1,0:T(8,128)(2,1)S(1)}, u32[]{:S(2)}, u32[]{:S(2)}) collective-permute-start(bf16[80,256]{1,0:T(8,128)(2,1)S(1)} %get-tuple-element.55), channel_id=1, source_target_pairs={{0,5},{1,4},{2,7},{3,6},{4,1},{5,0},{6,3},{7,2},{8,13},{9,12},{10,... | collective-permute-start | bytes 122888 | tf_op jit(solution)/shard_map/ppermute | solution.py:301
  39.4 4.7 %collective-permute-start.13 = (bf16[80,256]{1,0:T(8,128)(2,1)S(1)}, bf16[80,256]{1,0:T(8,128)(2,1)S(1)}, u32[]{:S(2)}, u32[]{:S(2)}) collective-permute-start(bf16[80,256]{1,0:T(8,128)(2,1)S(1)} %get-tuple-element.56), channel_id=1, source_target_pairs={{0,2},{1,3},{2,0},{3,1},{4,6},{5,7},{6,4},{7,5},{8,10},{9,11},{10,... | collective-permute-start | bytes 122888 | tf_op jit(solution)/shard_map/ppermute | solution.py:301
  39.4 5.9 %collective-permute-start.14 = (bf16[80,256]{1,0:T(8,128)(2,1)S(1)}, bf16[80,256]{1,0:T(8,128)(2,1)S(1)}, u32[]{:S(2)}, u32[]{:S(2)}) collective-permute-start(bf16[80,256]{1,0:T(8,128)(2,1)S(1)} %get-tuple-element.57), channel_id=1, source_target_pairs={{0,3},{1,2},{2,1},{3,0},{4,7},{5,6},{6,5},{7,4},{8,11},{9,10},{10,... | collective-permute-start | bytes 122888 | tf_op jit(solution)/shard_map/ppermute | solution.py:301
  42.8 2.6 %collective-permute-start.15 = (bf16[80,256]{1,0:T(8,128)(2,1)S(1)}, bf16[80,256]{1,0:T(8,128)(2,1)S(1)}, u32[]{:S(2)}, u32[]{:S(2)}) collective-permute-start(bf16[80,256]{1,0:T(8,128)(2,1)S(1)} %get-tuple-element.58), channel_id=1, source_target_pairs={{0,1},{1,0},{2,3},{3,2},{4,5},{5,4},{6,7},{7,6},{8,9},{9,8},{10,11... | collective-permute-start | bytes 122888 | tf_op jit(solution)/shard_map/ppermute | solution.py:301
  45.4 5.7 %collective-permute-start.18 = (bf16[160,256]{1,0:T(8,128)(2,1)S(1)}, bf16[160,256]{1,0:T(8,128)(2,1)S(1)}, u32[]{:S(2)}, u32[]{:S(2)}) collective-permute-start(bf16[160,256]{1,0:T(8,128)(2,1)S(1)} %get-tuple-element.63.refs_0_), channel_id=1, source_target_pairs={{0,6},{1,7},{2,4},{3,5},{4,2},{5,3},{6,0},{7,1},{8,14},{9,15},{10,... | collective-permute-start | bytes 245768 | tf_op jit(solution)/shard_map/ppermute | solution.py:301
  47.5 8.0 %collective-permute-start.17 = (bf16[160,256]{1,0:T(8,128)(2,1)S(1)}, bf16[160,256]{1,0:T(8,128)(2,1)S(1)}, u32[]{:S(2)}, u32[]{:S(2)}) collective-permute-start(bf16[160,256]{1,0:T(8,128)(2,1)S(1)} %get-tuple-element.63.refs_0_), channel_id=1, source_target_pairs={{0,4},{1,5},{2,6},{3,7},{4,0},{5,1},{6,2},{7,3},{8,12},{9,13},{10,... | collective-permute-start | bytes 245768 | tf_op jit(solution)/shard_map/ppermute | solution.py:301
  47.5 8.5 %collective-permute-start.16 = (bf16[160,256]{1,0:T(8,128)(2,1)S(1)}, bf16[160,256]{1,0:T(8,128)(2,1)S(1)}, u32[]{:S(2)}, u32[]{:S(2)}) collective-permute-start(bf16[160,256]{1,0:T(8,128)(2,1)S(1)} %get-tuple-element.63.refs_0_), channel_id=1, source_target_pairs={{0,2},{1,3},{2,0},{3,1},{4,6},{5,7},{6,4},{7,5},{8,10},{9,11},{10,... | collective-permute-start | bytes 245768 | tf_op jit(solution)/shard_map/ppermute | solution.py:301
  49.1 7.3 %collective-permute-start.19 = (bf16[160,256]{1,0:T(8,128)(2,1)S(1)}, bf16[160,256]{1,0:T(8,128)(2,1)S(1)}, u32[]{:S(2)}, u32[]{:S(2)}) collective-permute-start(bf16[160,256]{1,0:T(8,128)(2,1)S(1)} %get-tuple-element.63.refs_0_), channel_id=1, source_target_pairs={{0,1},{1,0},{2,3},{3,2},{4,5},{5,4},{6,7},{7,6},{8,9},{9,8},{10,11... | collective-permute-start | bytes 245768 | tf_op jit(solution)/shard_map/ppermute | solution.py:301
  51.2 5.3 %collective-permute-start.22 = (bf16[160,256]{1,0:T(8,128)(2,1)S(1)}, bf16[160,256]{1,0:T(8,128)(2,1)S(1)}, u32[]{:S(2)}, u32[]{:S(2)}) collective-permute-start(bf16[160,256]{1,0:T(8,128)(2,1)S(1)} %collective-permute-done.18.refs_3_), channel_id=1, source_target_pairs={{0,1},{1,0},{2,3},{3,2},{4,5},{5,4},{6,7},{7,6},{8,9},{9,8},{10,11... | collective-permute-start | bytes 245768 | tf_op jit(solution)/shard_map/ppermute | solution.py:301
  55.5 1.4 %collective-permute-start.21 = (bf16[160,256]{1,0:T(8,128)(2,1)S(1)}, bf16[160,256]{1,0:T(8,128)(2,1)S(1)}, u32[]{:S(2)}, u32[]{:S(2)}) collective-permute-start(bf16[160,256]{1,0:T(8,128)(2,1)S(1)} %collective-permute-done.17.refs_2_), channel_id=1, source_target_pairs={{0,1},{1,0},{2,3},{3,2},{4,5},{5,4},{6,7},{7,6},{8,9},{9,8},{10,11... | collective-permute-start | bytes 245768 | tf_op jit(solution)/shard_map/ppermute | solution.py:301
  56.0 1.3 %collective-permute-start.20 = (bf16[160,256]{1,0:T(8,128)(2,1)S(1)}, bf16[160,256]{1,0:T(8,128)(2,1)S(1)}, u32[]{:S(2)}, u32[]{:S(2)}) collective-permute-start(bf16[160,256]{1,0:T(8,128)(2,1)S(1)} %collective-permute-done.16.refs_1_), channel_id=1, source_target_pairs={{0,1},{1,0},{2,3},{3,2},{4,5},{5,4},{6,7},{7,6},{8,9},{9,8},{10,11... | collective-permute-start | bytes 245768 | tf_op jit(solution)/shard_map/ppermute | solution.py:301
  59.3 25.4 %all-to-all-start = ((bf16[16,40,896]{2,1,0:T(8,128)(2,1)}), bf16[16,40,896]{2,1,0:T(8,128)(2,1)S(1)}, u32[]{:S(2)}, u32[]{:S(2)}) async-start(bf16[16,40,896]{2,1,0:T(8,128)(2,1)} %bitcast.7), calls=%async_computation | async-start | bytes 2293760 | tf_op jit(solution)/shard_map/all_to_all | solution.py:362
  67.8 8.9 %collective-permute-start.23 = (bf16[2,80,128]{2,1,0:T(8,128)(2,1)S(1)}, bf16[2,80,128]{2,1,0:T(8,128)(2,1)S(1)}, u32[]{:S(2)}, u32[]{:S(2)}) collective-permute-start(bf16[2,80,128]{2,1,0:T(8,128)(2,1)S(1)} %get-tuple-element.66), channel_id=1, source_target_pairs={{8,0},{16,8},{24,16},{32,24},{40,32},{48,40},{56,48},{64,56},{72,6... | collective-permute-start | bytes 122888 | tf_op jit(solution)/shard_map/ppermute | solution.py:361
  77.0 7.8 %collective-permute-start.24 = (bf16[160,128]{1,0:T(8,128)(2,1)S(1)}, bf16[160,128]{1,0:T(8,128)(2,1)S(1)}, u32[]{:S(2)}, u32[]{:S(2)}) collective-permute-start(bf16[160,128]{1,0:T(8,128)(2,1)S(1)} %get-tuple-element.68), channel_id=1, source_target_pairs={{0,6},{1,7},{2,4},{3,5},{4,2},{5,3},{6,0},{7,1},{8,14},{9,15},{10,... | collective-permute-start | bytes 122888 | tf_op jit(solution)/shard_map/ppermute | solution.py:301
  79.6 5.3 %collective-permute-start.25 = (bf16[160,128]{1,0:T(8,128)(2,1)S(1)}, bf16[160,128]{1,0:T(8,128)(2,1)S(1)}, u32[]{:S(2)}, u32[]{:S(2)}) collective-permute-start(bf16[160,128]{1,0:T(8,128)(2,1)S(1)} %get-tuple-element.69), channel_id=1, source_target_pairs={{0,4},{1,5},{2,6},{3,7},{4,0},{5,1},{6,2},{7,3},{8,12},{9,13},{10,... | collective-permute-start | bytes 122888 | tf_op jit(solution)/shard_map/ppermute | solution.py:301
  79.6 5.3 %collective-permute-start.26 = (bf16[160,128]{1,0:T(8,128)(2,1)S(1)}, bf16[160,128]{1,0:T(8,128)(2,1)S(1)}, u32[]{:S(2)}, u32[]{:S(2)}) collective-permute-start(bf16[160,128]{1,0:T(8,128)(2,1)S(1)} %get-tuple-element.70), channel_id=1, source_target_pairs={{0,2},{1,3},{2,0},{3,1},{4,6},{5,7},{6,4},{7,5},{8,10},{9,11},{10,... | collective-permute-start | bytes 122888 | tf_op jit(solution)/shard_map/ppermute | solution.py:301
  84.9 6.2 %collective-permute-start.27 = (bf16[320,128]{1,0:T(8,128)(2,1)S(1)}, bf16[320,128]{1,0:T(8,128)(2,1)S(1)}, u32[]{:S(2)}, u32[]{:S(2)}) collective-permute-start(bf16[320,128]{1,0:T(8,128)(2,1)S(1)} %shard_map.76), channel_id=1, source_target_pairs={{0,1},{1,0},{2,3},{3,2},{4,5},{5,4},{6,7},{7,6},{8,9},{9,8},{10,11... | collective-permute-start | bytes 245768 | tf_op jit(solution)/shard_map/ppermute | solution.py:301
  87.5 6.8 %collective-permute-start.28 = (bf16[20,896]{1,0:T(8,128)(2,1)S(1)}, bf16[20,896]{1,0:T(8,128)(2,1)S(1)}, u32[]{:S(2)}, u32[]{:S(2)}) collective-permute-start(bf16[20,896]{1,0:T(8,128)(2,1)S(1)} %get-tuple-element.75), channel_id=1, source_target_pairs={{0,8},{8,0},{16,24},{24,16},{32,40},{40,32},{48,56},{56,48},{64,72... | collective-permute-start | bytes 107528 | tf_op jit(solution)/shard_map/ppermute | solution.py:372

commit v10 on v9

--- a/solution.py
+++ b/solution.py
@@ -13,7 +13,7 @@
 SOURCE = (0, 6, 4, 2, 1, 7, 5, 3)
 GATHERED = (0, 2, 4, 6, 1, 3, 5, 7)
 HEIGHTS = (80, 160, 160, 160, 80)
-ORDER = (0, 6, 4, 7, 5, 2, 3, 1)
+ORDER = (0, 4, 6, 5, 7, 2, 3, 1)
 HEAVY = 12_000_000_000
 
 

time: 95.7 us -> 95.4 us (level)
  starting transfers between devices: 55.9 us -> 54.8 us
  waiting for transfers between devices: 28.6 us -> 29.7 us
where the time goes in v10:
time: 95.4 us; the launch traced here: 95.1 us
  starting transfers between devices  54.8 us (57%)
  waiting for transfers between devices  29.7 us (31%)
  Pallas kernels  7.13 us (7%)
  local copies, waits for them, and re-layouts  2.69 us (3%)
    ppermute x25, starting transfers between devices, swap(): return lax.ppermute(block, 'fsdp', [(i, i ^ k) for i in range(8)])  33.5 us
    ppermute x25, waiting for transfers between devices, swap(): return lax.ppermute(block, 'fsdp', [(i, i ^ k) for i in range(8)])  13.8 us
    ppermute x1, starting transfers between devices, per_device(): down = lax.ppermute(down, 'tile', downward)  7.74 us
    ppermute x1, waiting for transfers between devices, per_device(): img_below = lax.ppermute(img_up, 'tile', upward)  7.65 us
    all_to_all x1, starting transfers between devices, per_device(): lax.all_to_all(red.reshape(16, 40, 896), 'tile', 0, 0, tiled=True, axis_i...  7.64 us
    pallas_call x12, Pallas kernels, call(): pl.pallas_call(kernel, out_shape=[jax.ShapeDtypeStruct(shape, dtype) for...  7.13 us
    all_to_all x1, waiting for transfers between devices, per_device(): lax.all_to_all(red.reshape(16, 40, 896), 'tile', 0, 0, tiled=True, axis_i...  4.03 us
    ppermute x1, starting transfers between devices, per_device(): given = lax.ppermute(give, 'tile', partners)  3.34 us
  transfers between devices with their start and end apart: 30, of which 14 were waited for; matrix products, arithmetic and copies ran while one was open for 0% of the time, Pallas kernels for 3%

profile of v10, /device:TPU:1, one launch (start us, length us, event | category | flops | bytes accessed | tf_op | source)
XLA Modules:
  0.0 95.1 jit_solution(5505300709758898517)
XLA Ops:
  0.7 1.0 %copy-done.1 = bf16[9,128,80]{1,2,0:T(8,128)(2,1)S(1)} copy-done((bf16[9,128,80]{1,2,0:T(8,128)(2,1)S(1)}, bf16[9,128,80]{1,2,0:T(8,128)(2,1)}, u32[]{:S(2)}) %copy-start.1) | copy-done | bytes 184344
  1.7 0.9 copy-done.2
  2.6 0.8 copy-done.3
  3.3 0.5 shard_map.67
  3.8 5.3 %collective-permute-start = (bf16[512,128]{1,0:T(8,128)(2,1)S(1)}, bf16[512,128]{1,0:T(8,128)(2,1)S(1)}, u32[]{:S(2)}, u32[]{:S(2)}) collective-permute-start(bf16[512,128]{1,0:T(8,128)(2,1)S(1)} %get-tuple-element.42), channel_id=1, source_target_pairs={{0,6},{1,7},{2,4},{3,5},{4,2},{5,3},{6,0},{7,1},{8,14},{9,15},{10,... | collective-permute-start | bytes 393224 | tf_op jit(solution)/shard_map/ppermute | solution.py:301
  9.1 0.4 collective-permute-start.2
  9.5 2.1 %collective-permute-done.refs_1_ = bf16[512,128]{1,0:T(8,128)(2,1)S(1)} collective-permute-done((bf16[512,128]{1,0:T(8,128)(2,1)S(1)}, bf16[512,128]{1,0:T(8,128)(2,1)S(1)}, u32[]{:S(2)}, u32[]{:S(2)}) %collective-permute-start) | collective-permute-done | bytes 131104 | tf_op jit(solution)/shard_map/ppermute | solution.py:301
  11.6 3.8 %collective-permute-start.4 = (bf16[512,128]{1,0:T(8,128)(2,1)S(1)}, bf16[512,128]{1,0:T(8,128)(2,1)S(1)}, u32[]{:S(2)}, u32[]{:S(2)}) collective-permute-start(bf16[512,128]{1,0:T(8,128)(2,1)S(1)} %collective-permute-done.refs_1_), channel_id=1, source_target_pairs={{0,1},{1,0},{2,3},{3,2},{4,5},{5,4},{6,7},{7,6},{8,9},{9,8},{10,11... | collective-permute-start | bytes 393224 | tf_op jit(solution)/shard_map/ppermute | solution.py:301
  15.4 3.9 %collective-permute-done.1.refs_2_ = bf16[512,128]{1,0:T(8,128)(2,1)S(1)} collective-permute-done((bf16[512,128]{1,0:T(8,128)(2,1)S(1)}, bf16[512,128]{1,0:T(8,128)(2,1)S(1)}, u32[]{:S(2)}, u32[]{:S(2)}) %collective-permute-start.1) | collective-permute-done | bytes 131104 | tf_op jit(solution)/shard_map/ppermute | solution.py:301
  19.3 1.3 %collective-permute-start.5 = (bf16[512,128]{1,0:T(8,128)(2,1)S(1)}, bf16[512,128]{1,0:T(8,128)(2,1)S(1)}, u32[]{:S(2)}, u32[]{:S(2)}) collective-permute-start(bf16[512,128]{1,0:T(8,128)(2,1)S(1)} %collective-permute-done.1.refs_2_), channel_id=1, source_target_pairs={{0,1},{1,0},{2,3},{3,2},{4,5},{5,4},{6,7},{7,6},{8,9},{9,8},{10,11... | collective-permute-start | bytes 393224 | tf_op jit(solution)/shard_map/ppermute | solution.py:301
  20.6 0.5 collective-permute-start.3
  21.1 1.0 %collective-permute-done.3.refs_4_ = bf16[336,128]{1,0:T(8,128)(2,1)S(1)} collective-permute-done((bf16[336,128]{1,0:T(8,128)(2,1)S(1)}, bf16[336,128]{1,0:T(8,128)(2,1)S(1)}, u32[]{:S(2)}, u32[]{:S(2)}) %collective-permute-start.3) | collective-permute-done | bytes 86048 | tf_op jit(solution)/shard_map/ppermute | solution.py:301
  22.1 0.8 shard_map.68
  23.0 7.7 %collective-permute-start.7 = (bf16[80,512]{1,0:T(8,128)(2,1)S(1)}, bf16[80,512]{1,0:T(8,128)(2,1)S(1)}, u32[]{:S(2)}, u32[]{:S(2)}) collective-permute-start(bf16[80,512]{1,0:T(8,128)(2,1)S(1)} %get-tuple-element.47), channel_id=1, source_target_pairs={{0,8},{8,16},{16,24},{24,32},{32,40},{40,48},{48,56},{56,64},{64,7... | collective-permute-start | bytes 245768 | tf_op jit(solution)/shard_map/ppermute | solution.py:337
  30.7 1.3 %collective-permute-start.8 = (bf16[80,256]{1,0:T(8,128)(2,1)S(1)}, bf16[80,256]{1,0:T(8,128)(2,1)S(1)}, u32[]{:S(2)}, u32[]{:S(2)}) collective-permute-start(bf16[80,256]{1,0:T(8,128)(2,1)S(1)} %get-tuple-element.50), channel_id=1, source_target_pairs={{8,0},{16,8},{24,16},{32,24},{40,32},{48,40},{56,48},{64,56},{72,6... | collective-permute-start | bytes 122888 | tf_op jit(solution)/shard_map/ppermute | solution.py:344
  32.0 0.2 collective-permute-done.7.down_ref
  32.2 0.5 shard_map.69
  32.8 2.3 %collective-permute-start.10 = (bf16[80,256]{1,0:T(8,128)(2,1)S(1)}, bf16[80,256]{1,0:T(8,128)(2,1)S(1)}, u32[]{:S(2)}, u32[]{:S(2)}) collective-permute-start(bf16[80,256]{1,0:T(8,128)(2,1)S(1)} %get-tuple-element.53), channel_id=1, source_target_pairs={{0,6},{1,7},{2,4},{3,5},{4,2},{5,3},{6,0},{7,1},{8,14},{9,15},{10,... | collective-permute-start | bytes 122888 | tf_op jit(solution)/shard_map/ppermute | solution.py:301
  35.1 2.7 %collective-permute-start.11 = (bf16[80,256]{1,0:T(8,128)(2,1)S(1)}, bf16[80,256]{1,0:T(8,128)(2,1)S(1)}, u32[]{:S(2)}, u32[]{:S(2)}) collective-permute-start(bf16[80,256]{1,0:T(8,128)(2,1)S(1)} %get-tuple-element.54), channel_id=1, source_target_pairs={{0,5},{1,4},{2,7},{3,6},{4,1},{5,0},{6,3},{7,2},{8,13},{9,12},{10,... | collective-permute-start | bytes 122888 | tf_op jit(solution)/shard_map/ppermute | solution.py:301
  37.8 1.6 %collective-permute-done.8.up_ref = bf16[80,256]{1,0:T(8,128)(2,1)S(1)} collective-permute-done((bf16[80,256]{1,0:T(8,128)(2,1)S(1)}, bf16[80,256]{1,0:T(8,128)(2,1)S(1)}, u32[]{:S(2)}, u32[]{:S(2)}) %collective-permute-start.8) | collective-permute-done | bytes 40992 | tf_op jit(solution)/shard_map/ppermute | solution.py:344
  39.4 3.8 %collective-permute-start.14 = (bf16[80,256]{1,0:T(8,128)(2,1)S(1)}, bf16[80,256]{1,0:T(8,128)(2,1)S(1)}, u32[]{:S(2)}, u32[]{:S(2)}) collective-permute-start(bf16[80,256]{1,0:T(8,128)(2,1)S(1)} %get-tuple-element.57), channel_id=1, source_target_pairs={{0,3},{1,2},{2,1},{3,0},{4,7},{5,6},{6,5},{7,4},{8,11},{9,10},{10,... | collective-permute-start | bytes 122888 | tf_op jit(solution)/shard_map/ppermute | solution.py:301
  43.2 0.4 collective-permute-done.11.refs_3_
  43.6 2.1 %collective-permute-done.14.refs_6_ = bf16[80,256]{1,0:T(8,128)(2,1)S(1)} collective-permute-done((bf16[80,256]{1,0:T(8,128)(2,1)S(1)}, bf16[80,256]{1,0:T(8,128)(2,1)S(1)}, u32[]{:S(2)}, u32[]{:S(2)}) %collective-permute-start.14) | collective-permute-done | bytes 40992 | tf_op jit(solution)/shard_map/ppermute | solution.py:301
  45.8 1.7 %collective-permute-start.18 = (bf16[160,256]{1,0:T(8,128)(2,1)S(1)}, bf16[160,256]{1,0:T(8,128)(2,1)S(1)}, u32[]{:S(2)}, u32[]{:S(2)}) collective-permute-start(bf16[160,256]{1,0:T(8,128)(2,1)S(1)} %get-tuple-element.63.refs_0_), channel_id=1, source_target_pairs={{0,6},{1,7},{2,4},{3,5},{4,2},{5,3},{6,0},{7,1},{8,14},{9,15},{10,... | collective-permute-start | bytes 245768 | tf_op jit(solution)/shard_map/ppermute | solution.py:301
  47.5 1.9 %collective-permute-start.16 = (bf16[160,256]{1,0:T(8,128)(2,1)S(1)}, bf16[160,256]{1,0:T(8,128)(2,1)S(1)}, u32[]{:S(2)}, u32[]{:S(2)}) collective-permute-start(bf16[160,256]{1,0:T(8,128)(2,1)S(1)} %get-tuple-element.63.refs_0_), channel_id=1, source_target_pairs={{0,2},{1,3},{2,0},{3,1},{4,6},{5,7},{6,4},{7,5},{8,10},{9,11},{10,... | collective-permute-start | bytes 245768 | tf_op jit(solution)/shard_map/ppermute | solution.py:301
  49.4 1.1 %collective-permute-start.19 = (bf16[160,256]{1,0:T(8,128)(2,1)S(1)}, bf16[160,256]{1,0:T(8,128)(2,1)S(1)}, u32[]{:S(2)}, u32[]{:S(2)}) collective-permute-start(bf16[160,256]{1,0:T(8,128)(2,1)S(1)} %get-tuple-element.63.refs_0_), channel_id=1, source_target_pairs={{0,1},{1,0},{2,3},{3,2},{4,5},{5,4},{6,7},{7,6},{8,9},{9,8},{10,11... | collective-permute-start | bytes 245768 | tf_op jit(solution)/shard_map/ppermute | solution.py:301
  50.5 1.0 %collective-permute-done.18.refs_3_ = bf16[160,256]{1,0:T(8,128)(2,1)S(1)} collective-permute-done((bf16[160,256]{1,0:T(8,128)(2,1)S(1)}, bf16[160,256]{1,0:T(8,128)(2,1)S(1)}, u32[]{:S(2)}, u32[]{:S(2)}) %collective-permute-start.18) | collective-permute-done | bytes 81952 | tf_op jit(solution)/shard_map/ppermute | solution.py:301
  51.5 1.8 %collective-permute-start.22 = (bf16[160,256]{1,0:T(8,128)(2,1)S(1)}, bf16[160,256]{1,0:T(8,128)(2,1)S(1)}, u32[]{:S(2)}, u32[]{:S(2)}) collective-permute-start(bf16[160,256]{1,0:T(8,128)(2,1)S(1)} %collective-permute-done.18.refs_3_), channel_id=1, source_target_pairs={{0,1},{1,0},{2,3},{3,2},{4,5},{5,4},{6,7},{7,6},{8,9},{9,8},{10,11... | collective-permute-start | bytes 245768 | tf_op jit(solution)/shard_map/ppermute | solution.py:301
  53.3 2.5 %collective-permute-done.17.refs_2_ = bf16[160,256]{1,0:T(8,128)(2,1)S(1)} collective-permute-done((bf16[160,256]{1,0:T(8,128)(2,1)S(1)}, bf16[160,256]{1,0:T(8,128)(2,1)S(1)}, u32[]{:S(2)}, u32[]{:S(2)}) %collective-permute-start.17) | collective-permute-done | bytes 81952 | tf_op jit(solution)/shard_map/ppermute | solution.py:301
  55.8 0.5 collective-permute-start.21
  56.3 0.4 shard_map.71
  56.8 0.4 collective-permute-done.21.refs_6_
  57.2 0.4 collective-permute-done.20.refs_5_
  57.6 2.1 %shard_map.72 = (bf16[640,896]{1,0:T(8,128)(2,1)}, bf16[640,256]{1,0:T(8,128)(2,1)S(1)}) custom-call(s32[1]{0:T(128)} %bitcast.slot_ref, bf16[720,256]{1,0:T(8,128)(2,1)S(1)} %get-tuple-element.48.win_ref, f32[640,256]{1,0:T(8,128)S(1)} %get-tuple-element.61.part_ref, bf16[5,256,256]{2,1,0:T(8,128)(2,1)S(1)} %get-tuple-element.62.shift_ref, ...), custom_call_target="tpu_custom_call" | custom-call | tf_op jit(solution)/shard_map/pallas_call | solution.py:289
  59.7 7.6 %all-to-all-start = ((bf16[16,40,896]{2,1,0:T(8,128)(2,1)}), bf16[16,40,896]{2,1,0:T(8,128)(2,1)S(1)}, u32[]{:S(2)}, u32[]{:S(2)}) async-start(bf16[16,40,896]{2,1,0:T(8,128)(2,1)} %bitcast.7), calls=%async_computation | async-start | bytes 2293760 | tf_op jit(solution)/shard_map/all_to_all | solution.py:362
  67.3 0.5 shard_map.73
  67.8 1.3 %collective-permute-start.23 = (bf16[2,80,128]{2,1,0:T(8,128)(2,1)S(1)}, bf16[2,80,128]{2,1,0:T(8,128)(2,1)S(1)}, u32[]{:S(2)}, u32[]{:S(2)}) collective-permute-start(bf16[2,80,128]{2,1,0:T(8,128)(2,1)S(1)} %get-tuple-element.66), channel_id=1, source_target_pairs={{8,0},{16,8},{24,16},{32,24},{40,32},{48,40},{56,48},{64,56},{72,6... | collective-permute-start | bytes 122888 | tf_op jit(solution)/shard_map/ppermute | solution.py:361
  69.1 7.6 %collective-permute-done.23.below_ref = bf16[2,80,128]{2,1,0:T(8,128)(2,1)S(1)} collective-permute-done((bf16[2,80,128]{2,1,0:T(8,128)(2,1)S(1)}, bf16[2,80,128]{2,1,0:T(8,128)(2,1)S(1)}, u32[]{:S(2)}, u32[]{:S(2)}) %collective-permute-start.23) | collective-permute-done | bytes 40992 | tf_op jit(solution)/shard_map/ppermute | solution.py:361
  76.8 0.3 shard_map.74
  77.1 2.5 %collective-permute-start.24 = (bf16[160,128]{1,0:T(8,128)(2,1)S(1)}, bf16[160,128]{1,0:T(8,128)(2,1)S(1)}, u32[]{:S(2)}, u32[]{:S(2)}) collective-permute-start(bf16[160,128]{1,0:T(8,128)(2,1)S(1)} %get-tuple-element.68), channel_id=1, source_target_pairs={{0,6},{1,7},{2,4},{3,5},{4,2},{5,3},{6,0},{7,1},{8,14},{9,15},{10,... | collective-permute-start | bytes 122888 | tf_op jit(solution)/shard_map/ppermute | solution.py:301
  79.6 1.1 %collective-permute-start.26 = (bf16[160,128]{1,0:T(8,128)(2,1)S(1)}, bf16[160,128]{1,0:T(8,128)(2,1)S(1)}, u32[]{:S(2)}, u32[]{:S(2)}) collective-permute-start(bf16[160,128]{1,0:T(8,128)(2,1)S(1)} %get-tuple-element.70), channel_id=1, source_target_pairs={{0,2},{1,3},{2,0},{3,1},{4,6},{5,7},{6,4},{7,5},{8,10},{9,11},{10,... | collective-permute-start | bytes 122888 | tf_op jit(solution)/shard_map/ppermute | solution.py:301
  80.7 4.0 %all-to-all-done.red_ref = bf16[16,40,896]{2,1,0:T(8,128)(2,1)S(1)} async-done(((bf16[16,40,896]{2,1,0:T(8,128)(2,1)}), bf16[16,40,896]{2,1,0:T(8,128)(2,1)S(1)}, u32[]{:S(2)}, u32[]{:S(2)}) %all-to-all-start) | async-done | bytes 1146912 | tf_op jit(solution)/shard_map/all_to_all | solution.py:362
  84.7 0.2 shard_map.75
  85.0 2.6 %collective-permute-start.27 = (bf16[320,128]{1,0:T(8,128)(2,1)S(1)}, bf16[320,128]{1,0:T(8,128)(2,1)S(1)}, u32[]{:S(2)}, u32[]{:S(2)}) collective-permute-start(bf16[320,128]{1,0:T(8,128)(2,1)S(1)} %shard_map.76), channel_id=1, source_target_pairs={{0,1},{1,0},{2,3},{3,2},{4,5},{5,4},{6,7},{7,6},{8,9},{9,8},{10,11... | collective-permute-start | bytes 245768 | tf_op jit(solution)/shard_map/ppermute | solution.py:301
  87.5 3.3 %collective-permute-start.28 = (bf16[20,896]{1,0:T(8,128)(2,1)S(1)}, bf16[20,896]{1,0:T(8,128)(2,1)S(1)}, u32[]{:S(2)}, u32[]{:S(2)}) collective-permute-start(bf16[20,896]{1,0:T(8,128)(2,1)S(1)} %get-tuple-element.75), channel_id=1, source_target_pairs={{0,8},{8,0},{16,24},{24,16},{32,40},{40,32},{48,56},{56,48},{64,72... | collective-permute-start | bytes 107528 | tf_op jit(solution)/shard_map/ppermute | solution.py:372
  90.9 0.9 shard_map.77
  91.8 2.5 %collective-permute-done.28.given_ref = bf16[20,896]{1,0:T(8,128)(2,1)S(1)} collective-permute-done((bf16[20,896]{1,0:T(8,128)(2,1)S(1)}, bf16[20,896]{1,0:T(8,128)(2,1)S(1)}, u32[]{:S(2)}, u32[]{:S(2)}) %collective-permute-start.28) | collective-permute-done | bytes 35872 | tf_op jit(solution)/shard_map/ppermute | solution.py:372
  94.3 0.8 shard_map.78
  (32 shorter events, 0.3 us)
Async XLA Ops:
  0.6 31.5 %copy-start = (bf16[80,9,640]{2,0,1:T(8,128)(2,1)S(1)}, bf16[80,9,640]{2,0,1:T(8,128)(2,1)}, u32[]{:S(2)}) copy-start(bf16[80,9,640]{2,0,1:T(8,128)(2,1)} %param.5) | copy-start | bytes 2764804
  0.6 1.0 %copy-start.1 = (bf16[9,128,80]{1,2,0:T(8,128)(2,1)S(1)}, bf16[9,128,80]{1,2,0:T(8,128)(2,1)}, u32[]{:S(2)}) copy-start(bf16[9,128,80]{1,2,0:T(8,128)(2,1)} %param.6) | copy-start | bytes 552964
  1.6 0.9 copy-start.2
  2.6 0.8 copy-start.3
  3.8 7.7 %collective-permute-start = (bf16[512,128]{1,0:T(8,128)(2,1)S(1)}, bf16[512,128]{1,0:T(8,128)(2,1)S(1)}, u32[]{:S(2)}, u32[]{:S(2)}) collective-permute-start(bf16[512,128]{1,0:T(8,128)(2,1)S(1)} %get-tuple-element.42), channel_id=1, source_target_pairs={{0,6},{1,7},{2,4},{3,5},{4,2},{5,3},{6,0},{7,1},{8,14},{9,15},{10,... | collective-permute-start | bytes 393224 | tf_op jit(solution)/shard_map/ppermute | solution.py:301
  9.1 10.2 %collective-permute-start.1 = (bf16[512,128]{1,0:T(8,128)(2,1)S(1)}, bf16[512,128]{1,0:T(8,128)(2,1)S(1)}, u32[]{:S(2)}, u32[]{:S(2)}) collective-permute-start(bf16[512,128]{1,0:T(8,128)(2,1)S(1)} %get-tuple-element.43), channel_id=1, source_target_pairs={{0,4},{1,5},{2,6},{3,7},{4,0},{5,1},{6,2},{7,3},{8,12},{9,13},{10,... | collective-permute-start | bytes 393224 | tf_op jit(solution)/shard_map/ppermute | solution.py:301
  9.1 11.5 %collective-permute-start.2 = (bf16[512,128]{1,0:T(8,128)(2,1)S(1)}, bf16[512,128]{1,0:T(8,128)(2,1)S(1)}, u32[]{:S(2)}, u32[]{:S(2)}) collective-permute-start(bf16[512,128]{1,0:T(8,128)(2,1)S(1)} %get-tuple-element.44), channel_id=1, source_target_pairs={{0,2},{1,3},{2,0},{3,1},{4,6},{5,7},{6,4},{7,5},{8,10},{9,11},{10,... | collective-permute-start | bytes 393224 | tf_op jit(solution)/shard_map/ppermute | solution.py:301
  11.6 10.5 %collective-permute-start.4 = (bf16[512,128]{1,0:T(8,128)(2,1)S(1)}, bf16[512,128]{1,0:T(8,128)(2,1)S(1)}, u32[]{:S(2)}, u32[]{:S(2)}) collective-permute-start(bf16[512,128]{1,0:T(8,128)(2,1)S(1)} %collective-permute-done.refs_1_), channel_id=1, source_target_pairs={{0,1},{1,0},{2,3},{3,2},{4,5},{5,4},{6,7},{7,6},{8,9},{9,8},{10,11... | collective-permute-start | bytes 393224 | tf_op jit(solution)/shard_map/ppermute | solution.py:301
  19.3 2.8 %collective-permute-start.5 = (bf16[512,128]{1,0:T(8,128)(2,1)S(1)}, bf16[512,128]{1,0:T(8,128)(2,1)S(1)}, u32[]{:S(2)}, u32[]{:S(2)}) collective-permute-start(bf16[512,128]{1,0:T(8,128)(2,1)S(1)} %collective-permute-done.1.refs_2_), channel_id=1, source_target_pairs={{0,1},{1,0},{2,3},{3,2},{4,5},{5,4},{6,7},{7,6},{8,9},{9,8},{10,11... | collective-permute-start | bytes 393224 | tf_op jit(solution)/shard_map/ppermute | solution.py:301
  20.6 1.5 %collective-permute-start.6 = (bf16[512,128]{1,0:T(8,128)(2,1)S(1)}, bf16[512,128]{1,0:T(8,128)(2,1)S(1)}, u32[]{:S(2)}, u32[]{:S(2)}) collective-permute-start(bf16[512,128]{1,0:T(8,128)(2,1)S(1)} %collective-permute-done.2.refs_3_), channel_id=1, source_target_pairs={{0,1},{1,0},{2,3},{3,2},{4,5},{5,4},{6,7},{7,6},{8,9},{9,8},{10,11... | collective-permute-start | bytes 393224 | tf_op jit(solution)/shard_map/ppermute | solution.py:301
  20.6 1.5 %collective-permute-start.3 = (bf16[336,128]{1,0:T(8,128)(2,1)S(1)}, bf16[336,128]{1,0:T(8,128)(2,1)S(1)}, u32[]{:S(2)}, u32[]{:S(2)}) collective-permute-start(bf16[336,128]{1,0:T(8,128)(2,1)S(1)} %get-tuple-element.45), channel_id=1, source_target_pairs={{0,1},{1,0},{2,3},{3,2},{4,5},{5,4},{6,7},{7,6},{8,9},{9,8},{10,11... | collective-permute-start | bytes 258056 | tf_op jit(solution)/shard_map/ppermute | solution.py:301
  23.0 9.2 %collective-permute-start.7 = (bf16[80,512]{1,0:T(8,128)(2,1)S(1)}, bf16[80,512]{1,0:T(8,128)(2,1)S(1)}, u32[]{:S(2)}, u32[]{:S(2)}) collective-permute-start(bf16[80,512]{1,0:T(8,128)(2,1)S(1)} %get-tuple-element.47), channel_id=1, source_target_pairs={{0,8},{8,16},{16,24},{24,32},{32,40},{40,48},{48,56},{56,64},{64,7... | collective-permute-start | bytes 245768 | tf_op jit(solution)/shard_map/ppermute | solution.py:337
  30.7 8.7 %collective-permute-start.8 = (bf16[80,256]{1,0:T(8,128)(2,1)S(1)}, bf16[80,256]{1,0:T(8,128)(2,1)S(1)}, u32[]{:S(2)}, u32[]{:S(2)}) collective-permute-start(bf16[80,256]{1,0:T(8,128)(2,1)S(1)} %get-tuple-element.50), channel_id=1, source_target_pairs={{8,0},{16,8},{24,16},{32,24},{40,32},{48,40},{56,48},{64,56},{72,6... | collective-permute-start | bytes 122888 | tf_op jit(solution)/shard_map/ppermute | solution.py:344
  32.7 6.7 %collective-permute-start.9 = (bf16[80,256]{1,0:T(8,128)(2,1)S(1)}, bf16[80,256]{1,0:T(8,128)(2,1)S(1)}, u32[]{:S(2)}, u32[]{:S(2)}) collective-permute-start(bf16[80,256]{1,0:T(8,128)(2,1)S(1)} %get-tuple-element.52), channel_id=1, source_target_pairs={{0,4},{1,5},{2,6},{3,7},{4,0},{5,1},{6,2},{7,3},{8,12},{9,13},{10,... | collective-permute-start | bytes 122888 | tf_op jit(solution)/shard_map/ppermute | solution.py:301
  32.8 10.3 %collective-permute-start.10 = (bf16[80,256]{1,0:T(8,128)(2,1)S(1)}, bf16[80,256]{1,0:T(8,128)(2,1)S(1)}, u32[]{:S(2)}, u32[]{:S(2)}) collective-permute-start(bf16[80,256]{1,0:T(8,128)(2,1)S(1)} %get-tuple-element.53), channel_id=1, source_target_pairs={{0,6},{1,7},{2,4},{3,5},{4,2},{5,3},{6,0},{7,1},{8,14},{9,15},{10,... | collective-permute-start | bytes 122888 | tf_op jit(solution)/shard_map/ppermute | solution.py:301
  35.1 8.5 %collective-permute-start.11 = (bf16[80,256]{1,0:T(8,128)(2,1)S(1)}, bf16[80,256]{1,0:T(8,128)(2,1)S(1)}, u32[]{:S(2)}, u32[]{:S(2)}) collective-permute-start(bf16[80,256]{1,0:T(8,128)(2,1)S(1)} %get-tuple-element.54), channel_id=1, source_target_pairs={{0,5},{1,4},{2,7},{3,6},{4,1},{5,0},{6,3},{7,2},{8,13},{9,12},{10,... | collective-permute-start | bytes 122888 | tf_op jit(solution)/shard_map/ppermute | solution.py:301
  37.8 5.8 %collective-permute-start.12 = (bf16[80,256]{1,0:T(8,128)(2,1)S(1)}, bf16[80,256]{1,0:T(8,128)(2,1)S(1)}, u32[]{:S(2)}, u32[]{:S(2)}) collective-permute-start(bf16[80,256]{1,0:T(8,128)(2,1)S(1)} %get-tuple-element.55), channel_id=1, source_target_pairs={{0,7},{1,6},{2,5},{3,4},{4,3},{5,2},{6,1},{7,0},{8,15},{9,14},{10,... | collective-permute-start | bytes 122888 | tf_op jit(solution)/shard_map/ppermute | solution.py:301
  39.4 4.2 %collective-permute-start.13 = (bf16[80,256]{1,0:T(8,128)(2,1)S(1)}, bf16[80,256]{1,0:T(8,128)(2,1)S(1)}, u32[]{:S(2)}, u32[]{:S(2)}) collective-permute-start(bf16[80,256]{1,0:T(8,128)(2,1)S(1)} %get-tuple-element.56), channel_id=1, source_target_pairs={{0,2},{1,3},{2,0},{3,1},{4,6},{5,7},{6,4},{7,5},{8,10},{9,11},{10,... | collective-permute-start | bytes 122888 | tf_op jit(solution)/shard_map/ppermute | solution.py:301
  39.4 6.3 %collective-permute-start.14 = (bf16[80,256]{1,0:T(8,128)(2,1)S(1)}, bf16[80,256]{1,0:T(8,128)(2,1)S(1)}, u32[]{:S(2)}, u32[]{:S(2)}) collective-permute-start(bf16[80,256]{1,0:T(8,128)(2,1)S(1)} %get-tuple-element.57), channel_id=1, source_target_pairs={{0,3},{1,2},{2,1},{3,0},{4,7},{5,6},{6,5},{7,4},{8,11},{9,10},{10,... | collective-permute-start | bytes 122888 | tf_op jit(solution)/shard_map/ppermute | solution.py:301
  43.2 2.6 %collective-permute-start.15 = (bf16[80,256]{1,0:T(8,128)(2,1)S(1)}, bf16[80,256]{1,0:T(8,128)(2,1)S(1)}, u32[]{:S(2)}, u32[]{:S(2)}) collective-permute-start(bf16[80,256]{1,0:T(8,128)(2,1)S(1)} %get-tuple-element.58), channel_id=1, source_target_pairs={{0,1},{1,0},{2,3},{3,2},{4,5},{5,4},{6,7},{7,6},{8,9},{9,8},{10,11... | collective-permute-start | bytes 122888 | tf_op jit(solution)/shard_map/ppermute | solution.py:301
  45.8 5.7 %collective-permute-start.18 = (bf16[160,256]{1,0:T(8,128)(2,1)S(1)}, bf16[160,256]{1,0:T(8,128)(2,1)S(1)}, u32[]{:S(2)}, u32[]{:S(2)}) collective-permute-start(bf16[160,256]{1,0:T(8,128)(2,1)S(1)} %get-tuple-element.63.refs_0_), channel_id=1, source_target_pairs={{0,6},{1,7},{2,4},{3,5},{4,2},{5,3},{6,0},{7,1},{8,14},{9,15},{10,... | collective-permute-start | bytes 245768 | tf_op jit(solution)/shard_map/ppermute | solution.py:301
  47.5 8.3 %collective-permute-start.17 = (bf16[160,256]{1,0:T(8,128)(2,1)S(1)}, bf16[160,256]{1,0:T(8,128)(2,1)S(1)}, u32[]{:S(2)}, u32[]{:S(2)}) collective-permute-start(bf16[160,256]{1,0:T(8,128)(2,1)S(1)} %get-tuple-element.63.refs_0_), channel_id=1, source_target_pairs={{0,4},{1,5},{2,6},{3,7},{4,0},{5,1},{6,2},{7,3},{8,12},{9,13},{10,... | collective-permute-start | bytes 245768 | tf_op jit(solution)/shard_map/ppermute | solution.py:301
  47.5 8.8 %collective-permute-start.16 = (bf16[160,256]{1,0:T(8,128)(2,1)S(1)}, bf16[160,256]{1,0:T(8,128)(2,1)S(1)}, u32[]{:S(2)}, u32[]{:S(2)}) collective-permute-start(bf16[160,256]{1,0:T(8,128)(2,1)S(1)} %get-tuple-element.63.refs_0_), channel_id=1, source_target_pairs={{0,2},{1,3},{2,0},{3,1},{4,6},{5,7},{6,4},{7,5},{8,10},{9,11},{10,... | collective-permute-start | bytes 245768 | tf_op jit(solution)/shard_map/ppermute | solution.py:301
  49.4 7.3 %collective-permute-start.19 = (bf16[160,256]{1,0:T(8,128)(2,1)S(1)}, bf16[160,256]{1,0:T(8,128)(2,1)S(1)}, u32[]{:S(2)}, u32[]{:S(2)}) collective-permute-start(bf16[160,256]{1,0:T(8,128)(2,1)S(1)} %get-tuple-element.63.refs_0_), channel_id=1, source_target_pairs={{0,1},{1,0},{2,3},{3,2},{4,5},{5,4},{6,7},{7,6},{8,9},{9,8},{10,11... | collective-permute-start | bytes 245768 | tf_op jit(solution)/shard_map/ppermute | solution.py:301
  51.5 5.3 %collective-permute-start.22 = (bf16[160,256]{1,0:T(8,128)(2,1)S(1)}, bf16[160,256]{1,0:T(8,128)(2,1)S(1)}, u32[]{:S(2)}, u32[]{:S(2)}) collective-permute-start(bf16[160,256]{1,0:T(8,128)(2,1)S(1)} %collective-permute-done.18.refs_3_), channel_id=1, source_target_pairs={{0,1},{1,0},{2,3},{3,2},{4,5},{5,4},{6,7},{7,6},{8,9},{9,8},{10,11... | collective-permute-start | bytes 245768 | tf_op jit(solution)/shard_map/ppermute | solution.py:301
  55.8 1.4 %collective-permute-start.21 = (bf16[160,256]{1,0:T(8,128)(2,1)S(1)}, bf16[160,256]{1,0:T(8,128)(2,1)S(1)}, u32[]{:S(2)}, u32[]{:S(2)}) collective-permute-start(bf16[160,256]{1,0:T(8,128)(2,1)S(1)} %collective-permute-done.17.refs_2_), channel_id=1, source_target_pairs={{0,1},{1,0},{2,3},{3,2},{4,5},{5,4},{6,7},{7,6},{8,9},{9,8},{10,11... | collective-permute-start | bytes 245768 | tf_op jit(solution)/shard_map/ppermute | solution.py:301
  56.3 1.3 %collective-permute-start.20 = (bf16[160,256]{1,0:T(8,128)(2,1)S(1)}, bf16[160,256]{1,0:T(8,128)(2,1)S(1)}, u32[]{:S(2)}, u32[]{:S(2)}) collective-permute-start(bf16[160,256]{1,0:T(8,128)(2,1)S(1)} %collective-permute-done.16.refs_1_), channel_id=1, source_target_pairs={{0,1},{1,0},{2,3},{3,2},{4,5},{5,4},{6,7},{7,6},{8,9},{9,8},{10,11... | collective-permute-start | bytes 245768 | tf_op jit(solution)/shard_map/ppermute | solution.py:301
  59.7 25.1 %all-to-all-start = ((bf16[16,40,896]{2,1,0:T(8,128)(2,1)}), bf16[16,40,896]{2,1,0:T(8,128)(2,1)S(1)}, u32[]{:S(2)}, u32[]{:S(2)}) async-start(bf16[16,40,896]{2,1,0:T(8,128)(2,1)} %bitcast.7), calls=%async_computation | async-start | bytes 2293760 | tf_op jit(solution)/shard_map/all_to_all | solution.py:362
  67.8 8.9 %collective-permute-start.23 = (bf16[2,80,128]{2,1,0:T(8,128)(2,1)S(1)}, bf16[2,80,128]{2,1,0:T(8,128)(2,1)S(1)}, u32[]{:S(2)}, u32[]{:S(2)}) collective-permute-start(bf16[2,80,128]{2,1,0:T(8,128)(2,1)S(1)} %get-tuple-element.66), channel_id=1, source_target_pairs={{8,0},{16,8},{24,16},{32,24},{40,32},{48,40},{56,48},{64,56},{72,6... | collective-permute-start | bytes 122888 | tf_op jit(solution)/shard_map/ppermute | solution.py:361
  77.1 7.8 %collective-permute-start.24 = (bf16[160,128]{1,0:T(8,128)(2,1)S(1)}, bf16[160,128]{1,0:T(8,128)(2,1)S(1)}, u32[]{:S(2)}, u32[]{:S(2)}) collective-permute-start(bf16[160,128]{1,0:T(8,128)(2,1)S(1)} %get-tuple-element.68), channel_id=1, source_target_pairs={{0,6},{1,7},{2,4},{3,5},{4,2},{5,3},{6,0},{7,1},{8,14},{9,15},{10,... | collective-permute-start | bytes 122888 | tf_op jit(solution)/shard_map/ppermute | solution.py:301
  79.6 5.3 %collective-permute-start.25 = (bf16[160,128]{1,0:T(8,128)(2,1)S(1)}, bf16[160,128]{1,0:T(8,128)(2,1)S(1)}, u32[]{:S(2)}, u32[]{:S(2)}) collective-permute-start(bf16[160,128]{1,0:T(8,128)(2,1)S(1)} %get-tuple-element.69), channel_id=1, source_target_pairs={{0,4},{1,5},{2,6},{3,7},{4,0},{5,1},{6,2},{7,3},{8,12},{9,13},{10,... | collective-permute-start | bytes 122888 | tf_op jit(solution)/shard_map/ppermute | solution.py:301
  79.6 5.3 %collective-permute-start.26 = (bf16[160,128]{1,0:T(8,128)(2,1)S(1)}, bf16[160,128]{1,0:T(8,128)(2,1)S(1)}, u32[]{:S(2)}, u32[]{:S(2)}) collective-permute-start(bf16[160,128]{1,0:T(8,128)(2,1)S(1)} %get-tuple-element.70), channel_id=1, source_target_pairs={{0,2},{1,3},{2,0},{3,1},{4,6},{5,7},{6,4},{7,5},{8,10},{9,11},{10,... | collective-permute-start | bytes 122888 | tf_op jit(solution)/shard_map/ppermute | solution.py:301
  85.0 5.9 %collective-permute-start.27 = (bf16[320,128]{1,0:T(8,128)(2,1)S(1)}, bf16[320,128]{1,0:T(8,128)(2,1)S(1)}, u32[]{:S(2)}, u32[]{:S(2)}) collective-permute-start(bf16[320,128]{1,0:T(8,128)(2,1)S(1)} %shard_map.76), channel_id=1, source_target_pairs={{0,1},{1,0},{2,3},{3,2},{4,5},{5,4},{6,7},{7,6},{8,9},{9,8},{10,11... | collective-permute-start | bytes 245768 | tf_op jit(solution)/shard_map/ppermute | solution.py:301
  87.5 6.8 %collective-permute-start.28 = (bf16[20,896]{1,0:T(8,128)(2,1)S(1)}, bf16[20,896]{1,0:T(8,128)(2,1)S(1)}, u32[]{:S(2)}, u32[]{:S(2)}) collective-permute-start(bf16[20,896]{1,0:T(8,128)(2,1)S(1)} %get-tuple-element.75), channel_id=1, source_target_pairs={{0,8},{8,0},{16,24},{24,16},{32,40},{40,32},{48,56},{56,48},{64,72... | collective-permute-start | bytes 107528 | tf_op jit(solution)/shard_map/ppermute | solution.py:372
